TPU v7x, 32 devices: a whole 2x2x4 slice. The times are simulated.
32 devices in a mesh: loop: 2 (over x), inner: 16 (over z, y, core).
Axes of the slice: x: 2, y: 2, z: 4, core: 2. Of those that a mesh axis runs over, the one named last changes fastest.
Arguments:
- site_blocks: bfloat16 [2, 16, 4, 256, 256], P('loop', 'inner'), may hold values from -6 to 6
- bond_weights: float32 [2, 16, 256], P('loop', 'inner'), may hold values from 0.2 to 2
- bond_gates: float32 [2, 16, 16], P('loop'), may hold values from -3 to 3
- kept_slots: int32 [2, 16], P('loop', 'inner'), may hold values from 64 to 256, as said below
Outputs:
- new_sites: bfloat16 [2, 16, 4, 256, 256], P('loop', 'inner')
- new_weights: float32 [2, 16, 256], P('loop', 'inner')
Inputs may be any that keep to these rules, and one draw needn't show every extreme that they name: `kept_slots`: every bond has at least one sector block with all 256 slots kept.
All inputs are finite; a program needn't handle non-finite values.
Results may differ from a plain program's by a relative error of at most 0.015.
The roundings to bfloat16 on the way count: a program that leaves them out, or rounds other values in their place, can miss the bound.
Values may be sent and summed in bfloat16 or wider, within the bound.
No kernel may reach another device: no remote copies, remote signals or barrier semaphores. Data moves between devices by JAX's collectives and lax.ppermute only.
A program may use at most 64 MiB of HBM per device.

v0:
```python
import functools
import math

import jax
import jax.numpy as jnp
import numpy as np
from jax import lax
from jax.experimental import pallas as pl
from jax.experimental.pallas import tpu as pltpu
from jax.sharding import PartitionSpec as P

CHARGE = (0, 1, 1, 2)
AXES = ("loop", "inner")
BF16, F32 = jnp.bfloat16, jnp.float32
VMEM_BYTES = 40 << 20
HIGHEST = lax.Precision.HIGHEST


def gate_terms():
    table = {}
    for a in range(4):
        for b in range(4):
            table[a, b] = [
                (CHARGE[p] - CHARGE[a], p, q)
                for p in range(4)
                for q in range(4)
                if CHARGE[p] + CHARGE[q] == CHARGE[a] + CHARGE[b]
                and abs(CHARGE[p] - CHARGE[a]) <= 1
            ]
    return table


TERMS = gate_terms()
PIECES = {
    (0, 0): (0, 3, 4, 0),
    (0, 1): (4, 3, 4, 0),
    (0, 2): (5, 3, 4, 0),
    (0, 3): (9, 3, 4, 0),
    (-1, 1): (1, 0, 3, 0),
    (-1, 2): (2, 0, 3, 0),
    (-1, 3): (6, 0, 3, 0),
    (1, 0): (3, 7, 3, 1),
    (1, 1): (7, 7, 3, 1),
    (1, 2): (8, 7, 3, 1),
}


def theta_slots():
    slots, count = {}, 0
    for (distance, q), (_, _, rows, first) in PIECES.items():
        for p in range(rows):
            slots[distance, first + p, q] = count
            count += 1
    return slots, count


SLOTS, SLOT_COUNT = theta_slots()


def dot(a, b, dims, precision=None):
    return lax.dot_general(a, b, (dims, ((), ())), precision=precision, preferred_element_type=F32)


def split3(a):
    h = a.astype(BF16)
    r = a - h.astype(F32)
    m = r.astype(BF16)
    return h, m, (r - m.astype(F32)).astype(BF16)


def factor_rows(work, size, panel=32):
    rowid = lax.broadcasted_iota(jnp.int32, (panel, 128), 0)
    for start in range(0, size, panel):
        low = start < size // 2
        chunks = [0, 1, 2] if low else [1, 2, 3]
        rows = [work[start : start + panel, 128 * c : 128 * c + 128] for c in chunks]
        pivots = jnp.ones((panel, 128), F32)
        for group in range(panel // 8):
            base = start % 128 + 8 * group
            cols = [
                jnp.broadcast_to(rows[0][:, base + k : base + k + 1], (panel, 128))
                for k in range(8)
            ]
            for j in range(8):
                at = 8 * group + j
                pivot = cols[j][at : at + 1, :]
                factor = jnp.where(rowid > at, cols[j], 0.0) * (1.0 / pivot)
                for k in range(j + 1, 8):
                    cols[k] = cols[k] - factor * cols[k][at : at + 1, :]
                rows = [x - factor * x[at : at + 1, :] for x in rows]
                pivots = jnp.where(rowid == at, pivot, pivots)
        scale = lax.rsqrt(pivots)
        rows = [x * scale for x in rows]
        for c, x in zip(chunks, rows):
            work[start : start + panel, 128 * c : 128 * c + 128] = x
        after = start + panel
        if after < size:
            h, m, l = split3(jnp.concatenate(rows, axis=1))
            right = jnp.concatenate([h, m, h, l, h, m], axis=0)
            left = jnp.concatenate([h, h, m, h, l, m], axis=0)
            first = 128 * chunks[0]
            for lo, hi in ((after, after + panel), (after + panel, size)):
                if lo < hi:
                    update = dot(left[:, lo - first : hi - first], right, ((0,), (0,)))
                    for i, c in enumerate(chunks):
                        work[lo:hi, 128 * c : 128 * c + 128] -= update[:, 128 * i : 128 * i + 128]


def bond_body(bond, x, c, table, gates, sem, a_ref, b_ref, scaled, theta, matrix, proj, work, iso):
    def row(core, which):
        return table.at[jnp.where(core == c, 0, 1), which]

    def weights(core, which):
        ref = row(core, which)
        return jnp.concatenate([ref[0:1, :], ref[1:2, :]], axis=1)

    plain = jnp.where(x == bond, 0, 1)
    across = jnp.where(x == bond, 2, 3)
    holder = jnp.where(x == bond, 1 - x, x)
    at_even, at_odd, beyond = weights(0, plain), weights(1, plain), weights(holder, across)
    even_role = x == 0
    below = jnp.where(even_role, beyond, at_even)
    here = jnp.where(even_role, at_even, at_odd)
    above = jnp.where(even_role, at_odd, beyond)
    copy = pltpu.make_async_copy(table.at[0, plain], gates, sem)
    copy.start()
    copy.wait()
    kept = table[0, plain, 4:5, 0:1]
    kept = jnp.where(even_role, row(0, plain)[4:5, 0:1], row(1, plain)[4:5, 0:1])

    for slot, w in [(s, below) for s in range(3)] + [(s, here) for s in range(3, 7)] + [
        (s, above) for s in range(7, 10)
    ]:
        scaled[slot] = (a_ref[slot].astype(F32) * w).astype(BF16)
    blocks = a_ref.shape[-1]
    for (distance, q), (right, left, count, first) in PIECES.items():
        product = dot(
            scaled[left : left + count].reshape(count * blocks, blocks), b_ref[right], ((1,), (0,))
        )
        product = (product * (1.0 / math.sqrt(blocks))).astype(BF16)
        slot = SLOTS[distance, first, q]
        theta[slot : slot + count] = product.reshape(count, blocks, blocks)

    def gate(a, b, p, q):
        flat = (4 * a + b) * 16 + 4 * p + q
        return gates[2 + flat // 128, flat % 128]

    step = 16

    @pl.loop(0, blocks // step)
    def mix(chunk):
        at = pl.multiple_of(chunk * step, step)
        for half in range(blocks // 128):
            cut = slice(128 * half, 128 * half + 128)
            held = {}

            def term(distance, p, q):
                slot = SLOTS[distance, p, q]
                if slot not in held:
                    held[slot] = theta[slot, pl.ds(at, step), cut].astype(F32)
                return held[slot]

            for total in range(5):
                for a in range(4):
                    for b in range(4):
                        if CHARGE[a] + CHARGE[b] != total:
                            continue
                        value = None
                        for distance, p, q in TERMS[a, b]:
                            part = gate(a, b, p, q) * term(distance, p, q)
                            value = part if value is None else value + part
                        matrix[
                            pl.ds(pl.multiple_of(a * blocks + at, step), step),
                            b * blocks + 128 * half : b * blocks + 128 * half + 128,
                        ] = value.astype(BF16)
                held.clear()

    basis = a_ref[3:7].reshape(4 * blocks, blocks)
    projected = dot(basis, matrix[...], ((0,), (0,)))
    slot_id = lax.broadcasted_iota(jnp.int32, projected.shape, 0).astype(F32)
    projected = jnp.where(slot_id < kept, projected, 0.0)
    proj[...] = projected
    work[:, :blocks] = dot(projected, projected, ((1,), (1,)), HIGHEST)
    ri = lax.broadcasted_iota(jnp.int32, (blocks, blocks), 0)
    ci = lax.broadcasted_iota(jnp.int32, (blocks, blocks), 1)
    eye = jnp.where(ri == ci, 1.0, 0.0).astype(F32)
    work[:, :blocks] += eye
    work[:, blocks:] = eye
    factor_rows(work, blocks)
    ortho = dot(work[:, blocks:], proj[...], ((1,), (0,)), HIGHEST)
    ortho = (ortho * math.sqrt(4 * blocks)).astype(BF16)
    for p in range(4):
        iso[p] = ortho[:, p * blocks : (p + 1) * blocks]


def finish_iso(c, iso, iso_half, iso_three):
    half = iso.shape[1] // 2
    mine = iso[:, pl.ds(pl.multiple_of(c * half, half), half), :]
    iso_half[...] = mine
    iso_three[...] = mine[1:]


def first_kernel(
    table, own, far, near, cross, own_s, far_s, near_s, cross_s,
    matrix, iso, iso_half, iso_three,
    a_ref, b_ref, scaled, theta, proj, work, gates, sems, sem,
):
    x = lax.axis_index("loop") % 2
    c = lax.axis_index("inner") % 2
    pairs = {"own": (own, own_s), "far": (far, far_s), "near": (near, near_s), "cross": (cross, cross_s)}
    plans = {
        0: [
            (a_ref, 0, "near", 1, 0, 3),
            (a_ref, 3, "own", 0, 0, 4),
            (a_ref, 7, "own", 1, 1, 3),
            (b_ref, 0, "far", 0, 0, 3),
            (b_ref, 3, "far", 1, 0, 4),
            (b_ref, 7, "cross", 0, 0, 3),
        ],
        1: [
            (a_ref, 0, "far", 0, 0, 3),
            (a_ref, 3, "far", 1, 0, 4),
            (a_ref, 7, "cross", 1, 0, 3),
            (b_ref, 0, "own", 1, 0, 3),
            (b_ref, 3, "near", 0, 0, 4),
            (b_ref, 7, "near", 1, 1, 3),
        ],
    }
    for role, plan in plans.items():
        for core in (0, 1):

            @pl.when(jnp.logical_and(x == role, c == core))
            def _(plan=plan, core=core):
                for n, (target, at, name, holder, first, count) in enumerate(plan):
                    source = pairs[name][0 if holder == core else 1]
                    pltpu.make_async_copy(
                        source.at[pl.ds(first, count)], target.at[pl.ds(at, count)], sems.at[n]
                    ).start()

    for n, (target, at, _, _, _, count) in enumerate(plans[0]):
        pltpu.make_async_copy(
            own.at[pl.ds(0, count)], target.at[pl.ds(at, count)], sems.at[n]
        ).wait()
    bond_body(0, x, c, table, gates, sem, a_ref, b_ref, scaled, theta, matrix, proj, work, iso)
    finish_iso(c, iso, iso_half, iso_three)


def second_kernel(
    table, iso_0, iso_1, iso_2, left_0, left_1, left_2, iso_1s, iso_2s, left_1s, left_2s,
    matrix, iso,
    a_ref, b_ref, scaled, theta, proj, work, gates, sems, sem,
):
    x = lax.axis_index("loop") % 2
    c = lax.axis_index("inner") % 2
    half = iso_1.shape[1]
    mine = pl.ds(pl.multiple_of(c * half, half), half)
    other = pl.ds(pl.multiple_of((1 - c) * half, half), half)
    copies = []

    def move(source, target):
        copy = pltpu.make_async_copy(source, target, sems.at[len(copies)])
        copy.start()
        copies.append(copy)

    move(iso_0.at[pl.ds(0, 1)], a_ref.at[pl.ds(3, 1)])
    move(iso_0.at[pl.ds(1, 2)], a_ref.at[pl.ds(7, 2)])
    move(left_0.at[pl.ds(0, 3)], b_ref.at[pl.ds(0, 3)])
    for rows, one, two, three, four in (
        (mine, iso_1, iso_2, left_1, left_2),
        (other, iso_1s, iso_2s, left_1s, left_2s),
    ):
        move(one.at[pl.ds(0, 1)], a_ref.at[pl.ds(0, 1), rows])
        move(one.at[pl.ds(1, 2)], a_ref.at[pl.ds(4, 2), rows])
        move(one.at[pl.ds(3, 1)], a_ref.at[pl.ds(9, 1), rows])
        move(two.at[pl.ds(0, 2)], a_ref.at[pl.ds(1, 2), rows])
        move(two.at[pl.ds(2, 1)], a_ref.at[pl.ds(6, 1), rows])
        move(three, b_ref.at[pl.ds(3, 4), rows])
        move(four, b_ref.at[pl.ds(7, 3), rows])
    for copy in copies:
        copy.wait()
    bond_body(1, x, c, table, gates, sem, a_ref, b_ref, scaled, theta, matrix, proj, work, iso)


def carry(matrix, iso):
    blocks = iso.shape[-1]
    total = None
    for p in range(4):
        part = dot(matrix[:, p * blocks : (p + 1) * blocks], iso[p], ((1,), (1,)))
        total = part if total is None else total + part
    carried = total * (1.0 / math.sqrt(4 * blocks))
    level = jnp.sqrt(jnp.mean(carried * carried, axis=0, keepdims=True) + 1e-06)
    return (carried / level).astype(BF16).reshape(4, blocks, blocks), level


def first_carry(matrix, iso, left, left_half, left_three, level_ref):
    c = lax.axis_index("inner") % 2
    new_left, level = carry(matrix, iso)
    left[...] = new_left
    half = left.shape[1] // 2
    mine = left[:, pl.ds(pl.multiple_of(c * half, half), half), :]
    left_half[...] = mine
    left_three[...] = mine[1:]
    level_ref[...] = jnp.broadcast_to(level, level_ref.shape)


def as_column(row):
    return jnp.broadcast_to(row, (row.shape[1], row.shape[1])).T


def second_carry(
    matrix, iso, level_0, level_1, level_2, left_out, iso_out, iso_mid, iso_last, iso_first, level_ref
):
    x = lax.axis_index("loop") % 2
    new_left, level = carry(matrix, iso)
    scales = [as_column(ref[0:1, :]) for ref in (level_0, level_1, level_2)]
    for p in range(4):
        left_out[p] = (new_left[p].astype(F32) * scales[CHARGE[p]]).astype(BF16)
    column = as_column(level)
    for p in range(4):
        iso_out[p] = (iso[p].astype(F32) * column).astype(BF16)
    iso_first[...] = iso_out[0:1]
    iso_mid[...] = iso_out[1:3]
    iso_last[...] = iso_out[3:4]
    level_ref[0:8, :] = jnp.broadcast_to(level, (8, level.shape[1]))
    level_ref[8:16, :] = jnp.where(x == 1, level_0[...], level_ref[0:8, :])


def final_kernel(left_out, iso_out, mid, last, first, whole, out, sems):
    x = lax.axis_index("loop") % 2
    c = lax.axis_index("inner") % 2
    plans = {
        (0, 0): [(iso_out, 0, 0, 1), (mid, 0, 1, 2), (last, 0, 3, 1)],
        (0, 1): [(first, 0, 0, 1), (iso_out, 1, 1, 2), (last, 0, 3, 1)],
        (1, 0): [(whole, 0, 0, 4)],
        (1, 1): [(left_out, 0, 0, 4)],
    }
    for (role, core), plan in plans.items():

        @pl.when(jnp.logical_and(x == role, c == core))
        def _(plan=plan):
            copies = [
                pltpu.make_async_copy(
                    source.at[pl.ds(at, count)], out.at[pl.ds(to, count)], sems.at[n]
                )
                for n, (source, at, to, count) in enumerate(plan)
            ]
            for copy in copies:
                copy.start()
            for copy in copies:
                copy.wait()


def scratch(blocks):
    return [
        pltpu.VMEM((10, blocks, blocks), BF16),
        pltpu.VMEM((10, blocks, blocks), BF16),
        pltpu.VMEM((10, blocks, blocks), BF16),
        pltpu.VMEM((SLOT_COUNT, blocks, blocks), BF16),
        pltpu.VMEM((blocks, 4 * blocks), F32),
        pltpu.VMEM((blocks, 2 * blocks), F32),
        pltpu.SMEM((8, 128), F32),
        pltpu.SemaphoreType.DMA((20,)),
        pltpu.SemaphoreType.DMA,
    ]


def vmem():
    return pl.BlockSpec(memory_space=pltpu.VMEM)


def hbm():
    return pl.BlockSpec(memory_space=pl.ANY)


def params():
    return pltpu.CompilerParams(vmem_limit_bytes=VMEM_BYTES)


def cost(flops, nbytes):
    return pl.CostEstimate(flops=flops, bytes_accessed=nbytes, transcendentals=0)


def per_device(loops, inners, site_blocks, bond_weights, bond_gates, kept_slots):
    blocks = site_blocks.shape[-1]

    def send(value, where):
        route = []
        for l in range(loops):
            for i in range(inners):
                source = where(l, i)
                if source is not None:
                    sl, si = source
                    route.append(((sl % loops) * inners + si % inners, l * inners + i))
        return lax.ppermute(value, AXES, route)

    def mirror(l, i):
        return (l ^ 1, i)

    def swap(l, i):
        return (l, i ^ 1)

    def near(l, i):
        if l % 2 == 0:
            return (l, i - 2) if i % 2 == 1 else None
        return (l, i + 2)

    def cross(l, i):
        if l % 2 == 0:
            return (l + 1, i + 2) if i % 2 == 0 else None
        return (l - 1, i + 1) if i % 2 == 1 else None

    def cross_weights(l, i):
        if l % 2 == 0:
            return (l + 1, i - 1) if i % 2 == 0 else None
        return (l - 1, i + 1) if i % 2 == 1 else None

    def below_one(l, i):
        return (l + 1, i - 2) if l % 2 == 0 else (l - 1, i)

    def below_two(l, i):
        return (l, i - 2)

    def above_none(l, i):
        return (l + 2, i)

    def above_one(l, i):
        return (l + 3, i) if l % 2 == 0 else (l + 1, i + 2)

    def above_two(l, i):
        return (l + 2, i + 2)

    block = site_blocks[0, 0]
    pack = jnp.concatenate(
        [
            bond_weights.reshape(2, 128),
            lax.reduce_precision(bond_gates.reshape(2, 128), 8, 7),
            jnp.broadcast_to(kept_slots.astype(F32).reshape(1, 1), (1, 128)),
            jnp.zeros((3, 128), F32),
        ],
        axis=0,
    )
    far_r = send(block, mirror)
    near_r = send(block, near)
    cross_r = send(block[1:], cross)
    own_s = send(block, swap)
    pack_far = send(pack, mirror)
    pack_near = send(pack, near)
    pack_cross = send(pack, cross_weights)
    mine = jnp.stack([pack, pack_far, pack_near, pack_cross])
    table = jnp.stack([mine, send(mine, swap)])
    far_s = send(far_r, swap)
    near_s = send(near_r, swap)
    cross_s = send(cross_r, swap)

    four = jax.ShapeDtypeStruct((4, blocks, blocks), BF16)
    four_half = jax.ShapeDtypeStruct((4, blocks // 2, blocks), BF16)
    three_half = jax.ShapeDtypeStruct((3, blocks // 2, blocks), BF16)
    square = jax.ShapeDtypeStruct((4 * blocks, 4 * blocks), BF16)
    level_shape = jax.ShapeDtypeStruct((8, blocks), F32)

    matrix, iso, iso_half, iso_three = pl.pallas_call(
        first_kernel,
        out_shape=(square, four, four_half, three_half),
        in_specs=[vmem()] + [hbm()] * 8,
        out_specs=(vmem(),) * 4,
        scratch_shapes=scratch(blocks),
        compiler_params=params(),
        name="first_bond",
    )(table, block, far_r, near_r, cross_r, own_s, far_s, near_s, cross_s)

    iso_1 = send(iso_half, below_one)
    iso_2 = send(iso_three, below_two)
    left, left_half, left_three, level = pl.pallas_call(
        first_carry,
        out_shape=(four, four_half, three_half, level_shape),
        in_specs=[vmem()] * 2,
        out_specs=(vmem(),) * 4,
        compiler_params=params(),
        cost_estimate=cost(2 * 1024 * 1024 * 256, 4 << 20),
        name="first_carry",
    )(matrix, iso)
    left_1 = send(left_half, above_one)
    left_2 = send(left_three, above_two)
    left_0 = left if loops == 2 else send(left, above_none)
    iso_1s = send(iso_1, swap)
    iso_2s = send(iso_2, swap)
    left_1s = send(left_1, swap)
    left_2s = send(left_2, swap)
    level_1 = send(level, below_one)
    level_2 = send(level, below_two)

    matrix, iso = pl.pallas_call(
        second_kernel,
        out_shape=(square, four),
        in_specs=[vmem()] + [hbm()] * 10,
        out_specs=(vmem(),) * 2,
        scratch_shapes=scratch(blocks),
        compiler_params=params(),
        cost_estimate=cost(8 * 1024 * 1024 * 256, 8 << 20),
        name="second_bond",
    )(table, iso, iso_1, iso_2, left_0, left_1, left_2, iso_1s, iso_2s, left_1s, left_2s)

    left_out, iso_out, iso_mid, iso_last, iso_first, levels = pl.pallas_call(
        second_carry,
        out_shape=(
            four,
            four,
            jax.ShapeDtypeStruct((2, blocks, blocks), BF16),
            jax.ShapeDtypeStruct((1, blocks, blocks), BF16),
            jax.ShapeDtypeStruct((1, blocks, blocks), BF16),
            jax.ShapeDtypeStruct((16, blocks), F32),
        ),
        in_specs=[vmem()] * 5,
        out_specs=(vmem(),) * 6,
        compiler_params=params(),
        name="second_carry",
    )(matrix, iso, level, level_1, level_2)

    def mid_from(l, i):
        return (l - 1, i - 2) if l % 2 == 0 and i % 2 == 0 else None

    def last_from(l, i):
        if l % 2:
            return None
        return (l - 2, i - 2) if i % 2 == 0 else (l - 1, i - 2)

    def first_from(l, i):
        return (l - 1, i - 1) if l % 2 == 0 and i % 2 == 1 else None

    def whole_from(l, i):
        return (l - 1, i) if l % 2 == 1 and i % 2 == 0 else None

    def level_from(l, i):
        if l % 2 == 0:
            return (l + 1, i - 1) if i % 2 == 1 else None
        return (l - 1, i) if i % 2 == 0 else None

    mid = send(iso_mid, mid_from)
    last = send(iso_last, last_from)
    first = send(iso_first, first_from)
    whole = send(left_out, whole_from)
    level_got = send(levels[8:9], level_from)
    iso_mine = iso_out if loops == 2 else send(iso_out, lambda l, i: (l - 2, i))
    sites = pl.pallas_call(
        final_kernel,
        out_shape=four,
        in_specs=[hbm()] * 6,
        out_specs=hbm(),
        scratch_shapes=[pltpu.SemaphoreType.DMA((3,))],
        name="assemble",
    )(left_out, iso_mine, mid, last, first, whole)
    x = lax.axis_index("loop") % 2
    c = lax.axis_index("inner") % 2
    local = jnp.where(x == 0, level[0:1], levels[0:1])
    weights = jnp.where(x == c, local, level_got)
    return sites[None, None], weights[None]


def solution(mesh):
    return jax.shard_map(
        functools.partial(per_device, mesh.shape["loop"], mesh.shape["inner"]),
        mesh=mesh,
        in_specs=(
            P("loop", "inner", None, None, None),
            P("loop", "inner", None),
            P("loop", None, None),
            P("loop", "inner"),
        ),
        out_specs=(P("loop", "inner", None, None, None), P("loop", "inner", None)),
        check_vma=False,
    )
```

profile of v0, /device:TPU:0, one launch (start us, length us, event | category | flops | bytes accessed | tf_op | source)
XLA Modules:
  0.0 147.9 jit_solution(13146078022122498685)
XLA Ops:
  0.6 3.0 %collective-permute-start.4 = (bf16[4,256,256]{2,1,0:T(8,128)(2,1)}, bf16[4,256,256]{2,1,0:T(8,128)(2,1)S(1)}, u32[]{:S(2)}, u32[]{:S(2)}) collective-permute-start(bf16[4,256,256]{2,1,0:T(8,128)(2,1)} %bitcast.18), channel_id=1, source_target_pairs={{16,0},{17,1},{18,2},{19,3},{20,4},{21,5},{22,6},{23,7},{24,8},{25... | collective-permute-start | bytes 1572872 | tf_op jit(solution)/shard_map/ppermute | solution.py:394
  3.6 0.7 collective-permute-start.5
  4.3 1.0 slice_bitcast_fusion
  5.4 7.0 %collective-permute-start.6 = (bf16[3,256,256]{2,1,0:T(8,128)(2,1)S(1)}, bf16[3,256,256]{2,1,0:T(8,128)(2,1)S(1)}, u32[]{:S(2)}, u32[]{:S(2)}) collective-permute-start(bf16[3,256,256]{2,1,0:T(8,128)(2,1)S(1)} %slice_bitcast_fusion), channel_id=1, source_target_pairs={{18,0},{20,2},{22,4},{24,6},{26,8},{28,10},{30,12},{16,14},{2,17},... | collective-permute-start | bytes 1179656 | tf_op jit(solution)/shard_map/ppermute | solution.py:394
  12.4 0.1 collective-permute-start.7
  12.5 6.9 %collective-permute-done.4.far = bf16[4,256,256]{2,1,0:T(8,128)(2,1)S(1)} collective-permute-done((bf16[4,256,256]{2,1,0:T(8,128)(2,1)}, bf16[4,256,256]{2,1,0:T(8,128)(2,1)S(1)}, u32[]{:S(2)}, u32[]{:S(2)}) %collective-permute-start.4) | collective-permute-done | bytes 524320 | tf_op jit(solution)/shard_map/ppermute | solution.py:394
  19.4 0.5 collective-permute-start.9
  19.9 0.7 reduce_precision.6
  20.6 0.1 reduce_precision.7
  21.3 0.1 pad.8.clone
  21.4 0.1 pad.9.clone
  21.5 0.0 collective-permute-start.10
  21.5 0.8 fusion.1
  22.2 8.5 %collective-permute-start = (f32[8,128]{1,0:T(8,128)S(1)}, f32[8,128]{1,0:T(8,128)S(1)}, u32[]{:S(2)}, u32[]{:S(2)}) collective-permute-start(f32[8,128]{1,0:T(8,128)S(1)} %get-tuple-element.37), channel_id=1, source_target_pairs={{16,0},{17,1},{18,2},{19,3},{20,4},{21,5},{22,6},{23,7},{24,8},{25... | collective-permute-start | bytes 12296 | tf_op jit(solution)/shard_map/ppermute | solution.py:394
  30.7 1.6 %collective-permute-done = f32[8,128]{1,0:T(8,128)S(1)} collective-permute-done((f32[8,128]{1,0:T(8,128)S(1)}, f32[8,128]{1,0:T(8,128)S(1)}, u32[]{:S(2)}, u32[]{:S(2)}) %collective-permute-start) | collective-permute-done | bytes 4128 | tf_op jit(solution)/shard_map/ppermute | solution.py:394
  32.3 0.7 collective-permute-start.1
  33.0 13.8 %collective-permute-start.2 = (f32[8,128]{1,0:T(8,128)S(1)}, f32[8,128]{1,0:T(8,128)S(1)}, u32[]{:S(2)}, u32[]{:S(2)}) collective-permute-start(f32[8,128]{1,0:T(8,128)S(1)} %get-tuple-element.37), channel_id=1, source_target_pairs={{31,0},{17,2},{19,4},{21,6},{23,8},{25,10},{27,12},{29,14},{2,17},... | collective-permute-start | bytes 12296 | tf_op jit(solution)/shard_map/ppermute | solution.py:394
  46.8 1.3 collective-permute-done.2
  48.1 0.0 collective-permute-start.3
  48.1 1.2 collective-permute-done.3
  49.3 0.0 copy-start
  49.3 1.0 copy-done
  50.4 16.4 %first_bond.1 = (bf16[1024,1024]{1,0:T(8,128)(2,1)S(1)}, bf16[4,256,256]{2,1,0:T(8,128)(2,1)S(1)}, bf16[4,128,256]{2,1,0:T(8,128)(2,1)S(1)}, bf16[3,128,256]{2,1,0:T(8,128)(2,1)S(1)}) custom-call(f32[2,4,8,128]{3,2,1,0:T(8,128)S(1)} %pad_maximum_fusion.table, bf16[4,256,256]{2,1,0:T(8,128)(2,1)S(1)} %bitcast.21, ...), custom_call_target="tpu_custom_call" | custom-call | tf_op jit(solution)/shard_map/first_bond/pallas_call | solution.py:461
  66.7 1.0 first_carry.1
  67.7 5.4 %collective-permute-start.13 = (bf16[4,128,256]{2,1,0:T(8,128)(2,1)S(1)}, bf16[4,128,256]{2,1,0:T(8,128)(2,1)S(1)}, u32[]{:S(2)}, u32[]{:S(2)}) collective-permute-start(bf16[4,128,256]{2,1,0:T(8,128)(2,1)S(1)} %get-tuple-element.23), channel_id=1, source_target_pairs={{16,0},{17,1},{18,2},{19,3},{20,4},{21,5},{22,6},{23,7},{24,8},{25... | collective-permute-start | bytes 786440 | tf_op jit(solution)/shard_map/ppermute | solution.py:394
  73.1 0.6 collective-permute-start.14
  73.7 1.4 collective-permute-start.12
  75.1 4.6 %collective-permute-done.13.left_1 = bf16[4,128,256]{2,1,0:T(8,128)(2,1)S(1)} collective-permute-done((bf16[4,128,256]{2,1,0:T(8,128)(2,1)S(1)}, bf16[4,128,256]{2,1,0:T(8,128)(2,1)S(1)}, u32[]{:S(2)}, u32[]{:S(2)}) %collective-permute-start.13) | collective-permute-done | bytes 262176 | tf_op jit(solution)/shard_map/ppermute | solution.py:394
  79.7 9.0 %collective-permute-done.11.iso_1 = bf16[4,128,256]{2,1,0:T(8,128)(2,1)S(1)} collective-permute-done((bf16[4,128,256]{2,1,0:T(8,128)(2,1)S(1)}, bf16[4,128,256]{2,1,0:T(8,128)(2,1)S(1)}, u32[]{:S(2)}, u32[]{:S(2)}) %collective-permute-start.11) | collective-permute-done | bytes 262176 | tf_op jit(solution)/shard_map/ppermute | solution.py:394
  88.7 1.1 collective-permute-done.14.left_2
  89.8 0.5 collective-permute-start.16
  90.3 2.2 %collective-permute-start.19 = (f32[8,256]{1,0:T(8,128)S(1)}, f32[8,256]{1,0:T(8,128)S(1)}, u32[]{:S(2)}, u32[]{:S(2)}) collective-permute-start(f32[8,256]{1,0:T(8,128)S(1)} %get-tuple-element.27.level_0), channel_id=1, source_target_pairs={{30,0},{31,1},{16,2},{17,3},{18,4},{19,5},{20,6},{21,7},{22,8},{23... | collective-permute-start | bytes 24584 | tf_op jit(solution)/shard_map/ppermute | solution.py:394
  92.6 17.0 %second_bond.1 = (bf16[1024,1024]{1,0:T(8,128)(2,1)S(1)}, bf16[4,256,256]{2,1,0:T(8,128)(2,1)S(1)}) custom-call(f32[2,4,8,128]{3,2,1,0:T(8,128)S(1)} %pad_maximum_fusion.table, bf16[4,256,256]{2,1,0:T(8,128)(2,1)S(1)} %get-tuple-element.18.iso.iso_0, bf16[4,128,256]{2,1,0:T(8,128)(2,1)S(1)} %collective-permute-done.11.iso_1, ...), custom_call_target="tpu_custom_call" | custom-call | flops 2147483648 | bytes 8388608 | tf_op jit(solution)/shard_map/second_bond/pallas_call | solution.py:492
  109.6 1.1 second_carry.1
  110.7 0.8 copy-done.2
  111.5 3.3 %collective-permute-start.24 = (bf16[4,256,256]{2,1,0:T(8,128)(2,1)S(1)}, bf16[4,256,256]{2,1,0:T(8,128)(2,1)S(1)}, u32[]{:S(2)}, u32[]{:S(2)}) collective-permute-start(bf16[4,256,256]{2,1,0:T(8,128)(2,1)S(1)} %get-tuple-element.28.left_out), channel_id=1, source_target_pairs={{0,16},{2,18},{4,20},{6,22},{8,24},{10,26},{12,28},{14,30}} | collective-permute-start | bytes 1572872 | tf_op jit(solution)/shard_map/ppermute | solution.py:394
  114.8 1.3 collective-permute-start.21
  116.1 1.3 collective-permute-start.25
  117.5 1.9 %collective-permute-start.22 = (bf16[1,256,256]{2,1,0:T(8,128)(2,1)S(1)}, bf16[1,256,256]{2,1,0:T(8,128)(2,1)S(1)}, u32[]{:S(2)}, u32[]{:S(2)}) collective-permute-start(bf16[1,256,256]{2,1,0:T(8,128)(2,1)S(1)} %get-tuple-element.31), channel_id=1, source_target_pairs={{14,0},{31,1},{0,2},{17,3},{2,4},{19,5},{4,6},{21,7},{6,8},{23,9},... | collective-permute-start | bytes 393224 | tf_op jit(solution)/shard_map/ppermute | solution.py:394
  119.4 0.7 collective-permute-start.23
  120.1 1.4 collective-permute-done.25
  121.5 0.6 fusion
  122.1 7.7 %collective-permute-done.22.last = bf16[1,256,256]{2,1,0:T(8,128)(2,1)S(1)} collective-permute-done((bf16[1,256,256]{2,1,0:T(8,128)(2,1)S(1)}, bf16[1,256,256]{2,1,0:T(8,128)(2,1)S(1)}, u32[]{:S(2)}, u32[]{:S(2)}) %collective-permute-start.22) | collective-permute-done | bytes 131104 | tf_op jit(solution)/shard_map/ppermute | solution.py:394
  129.8 0.6 copy-done.5
  130.4 0.1 copy-done.6
  130.4 0.1 copy-done.4
  130.5 0.2 copy-done.3
  130.7 17.0 %assemble.1 = bf16[4,256,256]{2,1,0:T(8,128)(2,1)} custom-call(bf16[4,256,256]{2,1,0:T(8,128)(2,1)} %copy-done.1, bf16[4,256,256]{2,1,0:T(8,128)(2,1)} %copy-done.2, bf16[2,256,256]{2,1,0:T(8,128)(2,1)} %copy-done.4, bf16[1,256,256]{2,1,0:T(8,128)(2,1)} %copy-done.5, bf16[1,256,256]{2,1,0:T(8,128)(2,1)} %copy-done.6, bf16[4,256,256]{2,1,0:T(8,128)(2,1)} %copy-done.3), custom_call_target="tpu_custom_call" | custom-call | tf_op jit(solution)/shard_map/assemble/pallas_call | solution.py:544
  (34 shorter events, 0.1 us)
Async XLA Ops:
  0.6 18.7 %collective-permute-start.4 = (bf16[4,256,256]{2,1,0:T(8,128)(2,1)}, bf16[4,256,256]{2,1,0:T(8,128)(2,1)S(1)}, u32[]{:S(2)}, u32[]{:S(2)}) collective-permute-start(bf16[4,256,256]{2,1,0:T(8,128)(2,1)} %bitcast.18), channel_id=1, source_target_pairs={{16,0},{17,1},{18,2},{19,3},{20,4},{21,5},{22,6},{23,7},{24,8},{25... | collective-permute-start | bytes 1572872 | tf_op jit(solution)/shard_map/ppermute | solution.py:394
  3.6 15.7 %collective-permute-start.5 = (bf16[4,256,256]{2,1,0:T(8,128)(2,1)}, bf16[4,256,256]{2,1,0:T(8,128)(2,1)S(1)}, u32[]{:S(2)}, u32[]{:S(2)}) collective-permute-start(bf16[4,256,256]{2,1,0:T(8,128)(2,1)} %bitcast.19), channel_id=1, source_target_pairs={{15,1},{1,3},{3,5},{5,7},{7,9},{9,11},{11,13},{13,15},{18,16},{19,... | collective-permute-start | bytes 1572872 | tf_op jit(solution)/shard_map/ppermute | solution.py:394
  5.4 16.1 %collective-permute-start.6 = (bf16[3,256,256]{2,1,0:T(8,128)(2,1)S(1)}, bf16[3,256,256]{2,1,0:T(8,128)(2,1)S(1)}, u32[]{:S(2)}, u32[]{:S(2)}) collective-permute-start(bf16[3,256,256]{2,1,0:T(8,128)(2,1)S(1)} %slice_bitcast_fusion), channel_id=1, source_target_pairs={{18,0},{20,2},{22,4},{24,6},{26,8},{28,10},{30,12},{16,14},{2,17},... | collective-permute-start | bytes 1179656 | tf_op jit(solution)/shard_map/ppermute | solution.py:394
  12.4 36.9 %collective-permute-start.7 = (bf16[4,256,256]{2,1,0:T(8,128)(2,1)}, bf16[4,256,256]{2,1,0:T(8,128)(2,1)S(1)}, u32[]{:S(2)}, u32[]{:S(2)}) collective-permute-start(bf16[4,256,256]{2,1,0:T(8,128)(2,1)} %bitcast.20), channel_id=1, source_target_pairs={{1,0},{0,1},{3,2},{2,3},{5,4},{4,5},{7,6},{6,7},{9,8},{8,9},{11,10... | collective-permute-start | bytes 1572872 | tf_op jit(solution)/shard_map/ppermute | solution.py:394
  19.3 29.9 %collective-permute-start.8 = (bf16[4,256,256]{2,1,0:T(8,128)(2,1)S(1)}, bf16[4,256,256]{2,1,0:T(8,128)(2,1)S(1)}, u32[]{:S(2)}, u32[]{:S(2)}) collective-permute-start(bf16[4,256,256]{2,1,0:T(8,128)(2,1)S(1)} %collective-permute-done.4.far), channel_id=1, source_target_pairs={{1,0},{0,1},{3,2},{2,3},{5,4},{4,5},{7,6},{6,7},{9,8},{8,9},{11,10... | collective-permute-start | bytes 1572872 | tf_op jit(solution)/shard_map/ppermute | solution.py:394
  19.4 30.0 %collective-permute-start.9 = (bf16[4,256,256]{2,1,0:T(8,128)(2,1)S(1)}, bf16[4,256,256]{2,1,0:T(8,128)(2,1)S(1)}, u32[]{:S(2)}, u32[]{:S(2)}) collective-permute-start(bf16[4,256,256]{2,1,0:T(8,128)(2,1)S(1)} %collective-permute-done.5.near), channel_id=1, source_target_pairs={{1,0},{0,1},{3,2},{2,3},{5,4},{4,5},{7,6},{6,7},{9,8},{8,9},{11,10... | collective-permute-start | bytes 1572872 | tf_op jit(solution)/shard_map/ppermute | solution.py:394
  21.5 27.8 %collective-permute-start.10 = (bf16[3,256,256]{2,1,0:T(8,128)(2,1)S(1)}, bf16[3,256,256]{2,1,0:T(8,128)(2,1)S(1)}, u32[]{:S(2)}, u32[]{:S(2)}) collective-permute-start(bf16[3,256,256]{2,1,0:T(8,128)(2,1)S(1)} %collective-permute-done.6.cross), channel_id=1, source_target_pairs={{1,0},{0,1},{3,2},{2,3},{5,4},{4,5},{7,6},{6,7},{9,8},{8,9},{11,10... | collective-permute-start | bytes 1179656 | tf_op jit(solution)/shard_map/ppermute | solution.py:394
  22.2 10.1 %collective-permute-start = (f32[8,128]{1,0:T(8,128)S(1)}, f32[8,128]{1,0:T(8,128)S(1)}, u32[]{:S(2)}, u32[]{:S(2)}) collective-permute-start(f32[8,128]{1,0:T(8,128)S(1)} %get-tuple-element.37), channel_id=1, source_target_pairs={{16,0},{17,1},{18,2},{19,3},{20,4},{21,5},{22,6},{23,7},{24,8},{25... | collective-permute-start | bytes 12296 | tf_op jit(solution)/shard_map/ppermute | solution.py:394
  32.3 0.7 collective-permute-start.1
  33.0 15.1 %collective-permute-start.2 = (f32[8,128]{1,0:T(8,128)S(1)}, f32[8,128]{1,0:T(8,128)S(1)}, u32[]{:S(2)}, u32[]{:S(2)}) collective-permute-start(f32[8,128]{1,0:T(8,128)S(1)} %get-tuple-element.37), channel_id=1, source_target_pairs={{31,0},{17,2},{19,4},{21,6},{23,8},{25,10},{27,12},{29,14},{2,17},... | collective-permute-start | bytes 12296 | tf_op jit(solution)/shard_map/ppermute | solution.py:394
  48.1 1.2 collective-permute-start.3
  49.3 1.0 copy-start
  67.7 12.0 %collective-permute-start.13 = (bf16[4,128,256]{2,1,0:T(8,128)(2,1)S(1)}, bf16[4,128,256]{2,1,0:T(8,128)(2,1)S(1)}, u32[]{:S(2)}, u32[]{:S(2)}) collective-permute-start(bf16[4,128,256]{2,1,0:T(8,128)(2,1)S(1)} %get-tuple-element.23), channel_id=1, source_target_pairs={{16,0},{17,1},{18,2},{19,3},{20,4},{21,5},{22,6},{23,7},{24,8},{25... | collective-permute-start | bytes 786440 | tf_op jit(solution)/shard_map/ppermute | solution.py:394
  73.1 15.6 %collective-permute-start.11 = (bf16[4,128,256]{2,1,0:T(8,128)(2,1)S(1)}, bf16[4,128,256]{2,1,0:T(8,128)(2,1)S(1)}, u32[]{:S(2)}, u32[]{:S(2)}) collective-permute-start(bf16[4,128,256]{2,1,0:T(8,128)(2,1)S(1)} %get-tuple-element.19), channel_id=1, source_target_pairs={{30,0},{31,1},{16,2},{17,3},{18,4},{19,5},{20,6},{21,7},{22,8},{23... | collective-permute-start | bytes 786440 | tf_op jit(solution)/shard_map/ppermute | solution.py:394
  73.1 16.7 %collective-permute-start.14 = (bf16[3,128,256]{2,1,0:T(8,128)(2,1)S(1)}, bf16[3,128,256]{2,1,0:T(8,128)(2,1)S(1)}, u32[]{:S(2)}, u32[]{:S(2)}) collective-permute-start(bf16[3,128,256]{2,1,0:T(8,128)(2,1)S(1)} %get-tuple-element.24), channel_id=1, source_target_pairs={{2,0},{3,1},{4,2},{5,3},{6,4},{7,5},{8,6},{9,7},{10,8},{11,9},{12,... | collective-permute-start | bytes 589832 | tf_op jit(solution)/shard_map/ppermute | solution.py:394
  73.7 16.1 %collective-permute-start.12 = (bf16[3,128,256]{2,1,0:T(8,128)(2,1)S(1)}, bf16[3,128,256]{2,1,0:T(8,128)(2,1)S(1)}, u32[]{:S(2)}, u32[]{:S(2)}) collective-permute-start(bf16[3,128,256]{2,1,0:T(8,128)(2,1)S(1)} %get-tuple-element.20), channel_id=1, source_target_pairs={{14,0},{15,1},{0,2},{1,3},{2,4},{3,5},{4,6},{5,7},{6,8},{7,9},{8,1... | collective-permute-start | bytes 589832 | tf_op jit(solution)/shard_map/ppermute | solution.py:394
  79.7 12.8 %collective-permute-start.17 = (bf16[4,128,256]{2,1,0:T(8,128)(2,1)S(1)}, bf16[4,128,256]{2,1,0:T(8,128)(2,1)S(1)}, u32[]{:S(2)}, u32[]{:S(2)}) collective-permute-start(bf16[4,128,256]{2,1,0:T(8,128)(2,1)S(1)} %collective-permute-done.13.left_1), channel_id=1, source_target_pairs={{1,0},{0,1},{3,2},{2,3},{5,4},{4,5},{7,6},{6,7},{9,8},{8,9},{11,10... | collective-permute-start | bytes 786440 | tf_op jit(solution)/shard_map/ppermute | solution.py:394
  88.7 3.9 %collective-permute-start.15 = (bf16[4,128,256]{2,1,0:T(8,128)(2,1)S(1)}, bf16[4,128,256]{2,1,0:T(8,128)(2,1)S(1)}, u32[]{:S(2)}, u32[]{:S(2)}) collective-permute-start(bf16[4,128,256]{2,1,0:T(8,128)(2,1)S(1)} %collective-permute-done.11.iso_1), channel_id=1, source_target_pairs={{1,0},{0,1},{3,2},{2,3},{5,4},{4,5},{7,6},{6,7},{9,8},{8,9},{11,10... | collective-permute-start | bytes 786440 | tf_op jit(solution)/shard_map/ppermute | solution.py:394
  89.8 2.8 %collective-permute-start.18 = (bf16[3,128,256]{2,1,0:T(8,128)(2,1)S(1)}, bf16[3,128,256]{2,1,0:T(8,128)(2,1)S(1)}, u32[]{:S(2)}, u32[]{:S(2)}) collective-permute-start(bf16[3,128,256]{2,1,0:T(8,128)(2,1)S(1)} %collective-permute-done.14.left_2), channel_id=1, source_target_pairs={{1,0},{0,1},{3,2},{2,3},{5,4},{4,5},{7,6},{6,7},{9,8},{8,9},{11,10... | collective-permute-start | bytes 589832 | tf_op jit(solution)/shard_map/ppermute | solution.py:394
  89.8 2.8 %collective-permute-start.16 = (bf16[3,128,256]{2,1,0:T(8,128)(2,1)S(1)}, bf16[3,128,256]{2,1,0:T(8,128)(2,1)S(1)}, u32[]{:S(2)}, u32[]{:S(2)}) collective-permute-start(bf16[3,128,256]{2,1,0:T(8,128)(2,1)S(1)} %collective-permute-done.12.iso_2), channel_id=1, source_target_pairs={{1,0},{0,1},{3,2},{2,3},{5,4},{4,5},{7,6},{6,7},{9,8},{8,9},{11,10... | collective-permute-start | bytes 589832 | tf_op jit(solution)/shard_map/ppermute | solution.py:394
  90.3 19.2 %collective-permute-start.19 = (f32[8,256]{1,0:T(8,128)S(1)}, f32[8,256]{1,0:T(8,128)S(1)}, u32[]{:S(2)}, u32[]{:S(2)}) collective-permute-start(f32[8,256]{1,0:T(8,128)S(1)} %get-tuple-element.27.level_0), channel_id=1, source_target_pairs={{30,0},{31,1},{16,2},{17,3},{18,4},{19,5},{20,6},{21,7},{22,8},{23... | collective-permute-start | bytes 24584 | tf_op jit(solution)/shard_map/ppermute | solution.py:394
  92.6 17.0 %collective-permute-start.20 = (f32[8,256]{1,0:T(8,128)S(1)}, f32[8,256]{1,0:T(8,128)S(1)}, u32[]{:S(2)}, u32[]{:S(2)}) collective-permute-start(f32[8,256]{1,0:T(8,128)S(1)} %get-tuple-element.27.level_0), channel_id=1, source_target_pairs={{14,0},{15,1},{0,2},{1,3},{2,4},{3,5},{4,6},{5,7},{6,8},{7,9},{8,1... | collective-permute-start | bytes 24584 | tf_op jit(solution)/shard_map/ppermute | solution.py:394
  110.7 0.8 copy-start.2
  111.5 18.3 %copy-start.1 = (bf16[4,256,256]{2,1,0:T(8,128)(2,1)}, bf16[4,256,256]{2,1,0:T(8,128)(2,1)S(1)}, u32[]{:S(2)}) copy-start(bf16[4,256,256]{2,1,0:T(8,128)(2,1)S(1)} %get-tuple-element.28.left_out) | copy-start | bytes 1572868
  111.5 18.3 %collective-permute-start.24 = (bf16[4,256,256]{2,1,0:T(8,128)(2,1)S(1)}, bf16[4,256,256]{2,1,0:T(8,128)(2,1)S(1)}, u32[]{:S(2)}, u32[]{:S(2)}) collective-permute-start(bf16[4,256,256]{2,1,0:T(8,128)(2,1)S(1)} %get-tuple-element.28.left_out), channel_id=1, source_target_pairs={{0,16},{2,18},{4,20},{6,22},{8,24},{10,26},{12,28},{14,30}} | collective-permute-start | bytes 1572872 | tf_op jit(solution)/shard_map/ppermute | solution.py:394
  114.8 14.9 %collective-permute-start.21 = (bf16[2,256,256]{2,1,0:T(8,128)(2,1)S(1)}, bf16[2,256,256]{2,1,0:T(8,128)(2,1)S(1)}, u32[]{:S(2)}, u32[]{:S(2)}) collective-permute-start(bf16[2,256,256]{2,1,0:T(8,128)(2,1)S(1)} %get-tuple-element.30), channel_id=1, source_target_pairs={{30,0},{16,2},{18,4},{20,6},{22,8},{24,10},{26,12},{28,14}} | collective-permute-start | bytes 786440 | tf_op jit(solution)/shard_map/ppermute | solution.py:394
  116.1 5.4 %collective-permute-start.25 = (f32[1,256]{1,0:T(1,128)S(1)}, f32[1,256]{1,0:T(1,128)S(1)}, u32[]{:S(2)}, u32[]{:S(2)}) collective-permute-start(f32[1,256]{1,0:T(1,128)S(1)} %slice.19), channel_id=1, source_target_pairs={{16,1},{18,3},{20,5},{22,7},{24,9},{26,11},{28,13},{30,15},{0,16},... | collective-permute-start | bytes 3080 | tf_op jit(solution)/shard_map/ppermute | solution.py:394
  117.5 12.3 %collective-permute-start.22 = (bf16[1,256,256]{2,1,0:T(8,128)(2,1)S(1)}, bf16[1,256,256]{2,1,0:T(8,128)(2,1)S(1)}, u32[]{:S(2)}, u32[]{:S(2)}) collective-permute-start(bf16[1,256,256]{2,1,0:T(8,128)(2,1)S(1)} %get-tuple-element.31), channel_id=1, source_target_pairs={{14,0},{31,1},{0,2},{17,3},{2,4},{19,5},{4,6},{21,7},{6,8},{23,9},... | collective-permute-start | bytes 393224 | tf_op jit(solution)/shard_map/ppermute | solution.py:394
  119.4 10.4 %collective-permute-start.23 = (bf16[1,256,256]{2,1,0:T(8,128)(2,1)S(1)}, bf16[1,256,256]{2,1,0:T(8,128)(2,1)S(1)}, u32[]{:S(2)}, u32[]{:S(2)}) collective-permute-start(bf16[1,256,256]{2,1,0:T(8,128)(2,1)S(1)} %get-tuple-element.32), channel_id=1, source_target_pairs={{16,1},{18,3},{20,5},{22,7},{24,9},{26,11},{28,13},{30,15}} | collective-permute-start | bytes 393224 | tf_op jit(solution)/shard_map/ppermute | solution.py:394
  129.7 0.7 copy-start.5
  129.7 0.7 copy-start.6
  129.7 0.8 copy-start.4
  129.8 0.9 copy-start.3
where the time goes:
time: 148 us
  starting transfers between devices  52.9 us (36%)
  Pallas kernels  52.4 us (35%)
  waiting for transfers between devices  34.8 us (24%)
  local copies, waits for them, and re-layouts  4.03 us (3%)
  other arithmetic  2.02 us (1%)
  between operations  1.74 us (1%)
    ppermute x26, starting transfers between devices, send(): return lax.ppermute(value, AXES, route)  52.9 us
    ppermute x26, waiting for transfers between devices, send(): return lax.ppermute(value, AXES, route)  34.8 us
    pallas_call x1, Pallas kernels, per_device(): pl.pallas_call(final_kernel, out_shape=four, in_specs=[hbm()] * 6, out_sp...  17 us
    pallas_call x1, Pallas kernels, per_device(): pl.pallas_call(second_kernel, out_shape=(square, four), in_specs=[vmem()]...  17 us
    pallas_call x1, Pallas kernels, per_device(): pl.pallas_call(first_kernel, out_shape=(square, four, four_half, three_ha...  16.4 us
  transfers between devices with their start and end apart: 26, of which 9 were waited for; matrix products, arithmetic and copies ran while one was open for 2% of the time, Pallas kernels for 11%

commit v1 on v0

v1 whole, which is shorter than its diff:
```python
import functools
import math

import jax
import jax.numpy as jnp
import numpy as np
from jax import lax
from jax.experimental import pallas as pl
from jax.experimental.pallas import tpu as pltpu
from jax.sharding import PartitionSpec as P

CHARGE = (0, 1, 1, 2)
AXES = ("loop", "inner")
BF16, F32 = jnp.bfloat16, jnp.float32
VMEM_BYTES = 40 << 20
HIGHEST = lax.Precision.HIGHEST


def gate_terms():
    table = {}
    for a in range(4):
        for b in range(4):
            table[a, b] = [
                (CHARGE[p] - CHARGE[a], p, q)
                for p in range(4)
                for q in range(4)
                if CHARGE[p] + CHARGE[q] == CHARGE[a] + CHARGE[b]
                and abs(CHARGE[p] - CHARGE[a]) <= 1
            ]
    return table


TERMS = gate_terms()
PIECES = {
    (0, 0): (0, 3, 4, 0),
    (0, 1): (4, 3, 4, 0),
    (0, 2): (5, 3, 4, 0),
    (0, 3): (9, 3, 4, 0),
    (-1, 1): (1, 0, 3, 0),
    (-1, 2): (2, 0, 3, 0),
    (-1, 3): (6, 0, 3, 0),
    (1, 0): (3, 7, 3, 1),
    (1, 1): (7, 7, 3, 1),
    (1, 2): (8, 7, 3, 1),
}


def theta_slots():
    slots, count = {}, 0
    for (distance, q), (_, _, rows, first) in PIECES.items():
        for p in range(rows):
            slots[distance, first + p, q] = count
            count += 1
    return slots, count


SLOTS, SLOT_COUNT = theta_slots()


def dot(a, b, dims, precision=None):
    return lax.dot_general(a, b, (dims, ((), ())), precision=precision, preferred_element_type=F32)


def split3(a):
    h = a.astype(BF16)
    r = a - h.astype(F32)
    m = r.astype(BF16)
    return h, m, (r - m.astype(F32)).astype(BF16)


def factor_rows(work, size, panel=32):
    rowid = lax.broadcasted_iota(jnp.int32, (panel, 128), 0)
    for start in range(0, size, panel):
        low = start < size // 2
        chunks = [0, 1, 2] if low else [1, 2, 3]
        rows = [work[start : start + panel, 128 * c : 128 * c + 128] for c in chunks]
        pivots = jnp.ones((panel, 128), F32)
        for group in range(panel // 8):
            base = start % 128 + 8 * group
            cols = [
                jnp.broadcast_to(rows[0][:, base + k : base + k + 1], (panel, 128))
                for k in range(8)
            ]
            for j in range(8):
                at = 8 * group + j
                pivot = cols[j][at : at + 1, :]
                factor = jnp.where(rowid > at, cols[j], 0.0) * (1.0 / pivot)
                for k in range(j + 1, 8):
                    cols[k] = cols[k] - factor * cols[k][at : at + 1, :]
                rows = [x - factor * x[at : at + 1, :] for x in rows]
                pivots = jnp.where(rowid == at, pivot, pivots)
        scale = lax.rsqrt(pivots)
        rows = [x * scale for x in rows]
        for c, x in zip(chunks, rows):
            work[start : start + panel, 128 * c : 128 * c + 128] = x
        after = start + panel
        if after < size:
            h, m, l = split3(jnp.concatenate(rows, axis=1))
            right = jnp.concatenate([h, m, h, l, h, m], axis=0)
            left = jnp.concatenate([h, h, m, h, l, m], axis=0)
            first = 128 * chunks[0]
            for lo, hi in ((after, after + panel), (after + panel, size)):
                if lo < hi:
                    update = dot(left[:, lo - first : hi - first], right, ((0,), (0,)))
                    for i, c in enumerate(chunks):
                        work[lo:hi, 128 * c : 128 * c + 128] -= update[:, 128 * i : 128 * i + 128]


SMALL = 32
W_ROW, K_ROW = 16, 19
LEVEL_ROW = 3


def put_split(ref, at, row):
    for n, part in enumerate(split3(row)):
        ref[at + n : at + n + 1, :] = part


def get_split(ref, at):
    h, m, l = (ref[at + n : at + n + 1, :].astype(F32) for n in range(3))
    return (h + m) + l


def prepare(block_ref, weight_ref, gate_ref, kept_ref, full, head, tail):
    blocks = block_ref.shape[-1]
    rows = block_ref[...].reshape(4 * blocks, blocks)
    small = jnp.zeros((SMALL, blocks), F32)
    rowid = lax.broadcasted_iota(jnp.int32, (SMALL, blocks), 0)
    for n, part in enumerate(split3(weight_ref[...])):
        small = jnp.where(rowid == W_ROW + n, part.astype(F32), small)
    small = jnp.where(rowid == K_ROW, kept_ref[...].astype(F32), small).astype(BF16)
    for ref, lo, hi in ((full, 0, 4), (head, 0, 3), (tail, 1, 4)):
        size = (hi - lo) * blocks
        ref[0:size, :] = rows[lo * blocks : hi * blocks]
        ref[size : size + SMALL, :] = small
        ref[size : size + 16, 0:16] = gate_ref[...].astype(BF16)


def bond_body(
    a_ref, b_ref, below, here, above, kept, gate_rows, scaled, theta, matrix, proj, work, iso, left,
    gate_stage, gates, sem
):
    blocks = b_ref.shape[-1]
    gate_stage[...] = gate_rows.astype(F32)
    copy = pltpu.make_async_copy(gate_stage, gates, sem)
    copy.start()
    copy.wait()
    for first, count, w in ((0, 3, below), (3, 4, here), (7, 3, above)):
        rows = slice(first * blocks, (first + count) * blocks)
        scaled[rows, :] = (a_ref[rows, :].astype(F32) * w).astype(BF16)
    for (distance, q), (right, first_row, count, first) in PIECES.items():
        product = dot(
            scaled[first_row * blocks : (first_row + count) * blocks, :],
            b_ref[right * blocks : (right + 1) * blocks, :],
            ((1,), (0,)),
        )
        slot = SLOTS[distance, first, q]
        theta[slot * blocks : (slot + count) * blocks, :] = (
            product * (1.0 / math.sqrt(blocks))
        ).astype(BF16)

    def gate(a, b, p, q):
        return gates[4 * a + b, 4 * p + q]

    step = 16

    @pl.loop(0, blocks // step)
    def mix(chunk):
        at = pl.multiple_of(chunk * step, step)
        for half in range(blocks // 128):
            cut = slice(128 * half, 128 * half + 128)
            held = {}

            def term(distance, p, q):
                slot = SLOTS[distance, p, q]
                if slot not in held:
                    place = pl.ds(pl.multiple_of(slot * blocks + at, step), step)
                    held[slot] = theta[place, cut].astype(F32)
                return held[slot]

            for total in range(5):
                for a in range(4):
                    for b in range(4):
                        if CHARGE[a] + CHARGE[b] != total:
                            continue
                        value = None
                        for distance, p, q in TERMS[a, b]:
                            part = gate(a, b, p, q) * term(distance, p, q)
                            value = part if value is None else value + part
                        matrix[
                            pl.ds(pl.multiple_of(a * blocks + at, step), step),
                            b * blocks + 128 * half : b * blocks + 128 * half + 128,
                        ] = value.astype(BF16)
                held.clear()

    basis = a_ref[3 * blocks : 7 * blocks, :]
    projected = dot(basis, matrix[...], ((0,), (0,)))
    slot_id = lax.broadcasted_iota(jnp.int32, projected.shape, 0).astype(F32)
    projected = jnp.where(slot_id < kept, projected, 0.0)
    proj[...] = projected
    ri = lax.broadcasted_iota(jnp.int32, (blocks, blocks), 0)
    ci = lax.broadcasted_iota(jnp.int32, (blocks, blocks), 1)
    eye = jnp.where(ri == ci, 1.0, 0.0).astype(F32)
    work[:, :blocks] = dot(projected, projected, ((1,), (1,)), HIGHEST) + eye
    work[:, blocks:] = eye
    factor_rows(work, blocks)
    ortho = dot(work[:, blocks:], proj[...], ((1,), (0,)), HIGHEST)
    ortho = (ortho * math.sqrt(4 * blocks)).astype(BF16)
    for p in range(4):
        iso[p * blocks : (p + 1) * blocks, :] = ortho[:, p * blocks : (p + 1) * blocks]
    carried = dot(matrix[...], ortho, ((1,), (1,))) * (1.0 / math.sqrt(4 * blocks))
    level = jnp.sqrt(jnp.mean(carried * carried, axis=0, keepdims=True) + 1e-06)
    left[...] = (carried / level).astype(BF16)
    return level


def first_kernel(
    own, core, mirror, mirror_core, near, next_one, next_two,
    iso_msg, iso_three, left, left_three, small_out,
    a_ref, b_ref, small, scaled, theta, matrix, proj, work, gate_stage, gates, sems, sem,
):
    x = lax.axis_index("loop") % 2
    c = lax.axis_index("inner") % 2
    blocks = a_ref.shape[-1]
    plans = {
        0: [
            (a_ref, 0, near, 0, 3), (a_ref, 3, own, 0, 4), (a_ref, 7, core, 1, 3),
            (b_ref, 0, mirror, 0, 3), (b_ref, 3, mirror_core, 0, 4), (b_ref, 7, next_one, 0, 3),
        ],
        1: [
            (a_ref, 0, mirror, 0, 3), (a_ref, 3, mirror_core, 0, 4), (a_ref, 7, next_two, 0, 3),
            (b_ref, 0, core, 0, 3), (b_ref, 3, near, 0, 4), (b_ref, 7, next_one, 0, 3),
        ],
    }
    smalls = {
        0: [near, own, core, mirror, mirror_core],
        1: [mirror, mirror_core, next_two, core, near],
    }

    def move(source, at, target, to, rows, n):
        return pltpu.make_async_copy(
            source.at[pl.ds(at, rows)], target.at[pl.ds(to, rows)], sems.at[n]
        )

    @pl.when(c == 0)
    def _():
        for role in (0, 1):

            @pl.when(x == role)
            def _(role=role):
                for n, (target, to, source, at, count) in enumerate(plans[role]):
                    move(source, at * blocks, target, to * blocks, count * blocks, n).start()
                for n, source in enumerate(smalls[role]):
                    move(source, source.shape[0] - SMALL, small, n * SMALL, SMALL, 6 + n).start()

        for n, (target, to, _, _, count) in enumerate(plans[0]):
            move(own, 0, target, to * blocks, count * blocks, n).wait()
        for n in range(5):
            move(own, 0, small, n * SMALL, SMALL, 6 + n).wait()
        below, here, above = (get_split(small, n * SMALL + W_ROW) for n in range(3))
        kept = small[SMALL + K_ROW : SMALL + K_ROW + 1, 0:1].astype(F32)
        level = bond_body(
            a_ref, b_ref, below, here, above, kept, small[SMALL : SMALL + 16, 0:128],
            scaled, theta, matrix, proj, work, iso_msg, left, gate_stage, gates, sem,
        )
        iso_three[0 : 3 * blocks, :] = iso_msg[blocks : 4 * blocks, :]
        left_three[...] = left[blocks : 4 * blocks, :]
        for ref in (iso_msg, iso_three):
            base = ref.shape[0] - SMALL
            ref[base : base + SMALL, :] = jnp.zeros((SMALL, blocks), BF16)
            put_split(ref, base, get_split(small, 3 * SMALL + W_ROW))
            put_split(ref, base + LEVEL_ROW, level)
        small_out[...] = small[3 * SMALL : 5 * SMALL, :]


def as_column(row):
    return jnp.broadcast_to(row, (row.shape[1], row.shape[1])).T


def second_kernel(
    iso_0, iso_1, iso_2, left_0, left_1, left_2, small_in,
    mid, last, first, whole,
    a_ref, b_ref, small, scaled, theta, matrix, proj, work, gate_stage, gates, sems, sem,
    iso, left,
):
    c = lax.axis_index("inner") % 2
    blocks = a_ref.shape[-1]
    moves = [
        (iso_1, 0, a_ref, 0, 1), (iso_2, 0, a_ref, 1, 2), (iso_0, 0, a_ref, 3, 1),
        (iso_1, 1, a_ref, 4, 2), (iso_2, 2, a_ref, 6, 1), (iso_0, 1, a_ref, 7, 2),
        (iso_1, 3, a_ref, 9, 1), (left_0, 0, b_ref, 0, 3), (left_1, 0, b_ref, 3, 4),
        (left_2, 0, b_ref, 7, 3),
    ]

    @pl.when(c == 0)
    def _():
        copies = [
            pltpu.make_async_copy(
                source.at[pl.ds(at * blocks, count * blocks)],
                target.at[pl.ds(to * blocks, count * blocks)],
                sems.at[n],
            )
            for n, (source, at, target, to, count) in enumerate(moves)
        ]
        for n, source in enumerate((iso_0, iso_1, iso_2)):
            copies.append(
                pltpu.make_async_copy(
                    source.at[pl.ds(source.shape[0] - SMALL, SMALL)],
                    small.at[pl.ds(n * SMALL, SMALL)],
                    sems.at[10 + n],
                )
            )
        for copy in copies:
            copy.start()
        for copy in copies:
            copy.wait()
        below = get_split(small, SMALL)
        here, above = (get_split(small_in, n * SMALL + W_ROW) for n in range(2))
        kept = small_in[K_ROW : K_ROW + 1, 0:1].astype(F32)
        level = bond_body(
            a_ref, b_ref, below, here, above, kept, small_in[0:16, 0:128],
            scaled, theta, matrix, proj, work, iso, left, gate_stage, gates, sem,
        )
        scales = [as_column(get_split(small, n * SMALL + LEVEL_ROW)) for n in range(3)]
        column = as_column(level)
        for p in range(4):
            rows = slice(p * blocks, (p + 1) * blocks)
            whole[rows, :] = (left[rows, :].astype(F32) * scales[CHARGE[p]]).astype(BF16)
        for ref, lo, hi in ((first, 0, 1), (mid, 1, 3), (last, 3, 4)):
            for p in range(lo, hi):
                value = iso[p * blocks : (p + 1) * blocks, :].astype(F32) * column
                ref[(p - lo) * blocks : (p - lo + 1) * blocks, :] = value.astype(BF16)
        for ref, value in ((first, get_split(small, LEVEL_ROW)), (whole, level)):
            base = ref.shape[0] - SMALL
            ref[base : base + SMALL, :] = jnp.zeros((SMALL, blocks), BF16)
            put_split(ref, base + LEVEL_ROW, value)


def final_kernel(first_mine, mid, last, first, whole, level_mine, level_far, out, weights, small, sems):
    x = lax.axis_index("loop") % 2
    c = lax.axis_index("inner") % 2
    blocks = out.shape[-1]
    plans = {
        (0, 0): [(first_mine, 0, 1), (mid, 1, 2), (last, 3, 1), (level_mine, 0, 0)],
        (0, 1): [(first, 0, 1), (mid, 1, 2), (last, 3, 1), (level_far, 0, 0)],
        (1, 0): [(whole, 0, 4), (whole, 0, 0)],
        (1, 1): [(whole, 0, 4), (whole, 0, 0)],
    }
    for (role, core), plan in plans.items():

        @pl.when(jnp.logical_and(x == role, c == core))
        def _(plan=plan):
            copies = []
            for n, (source, to, count) in enumerate(plan):
                if count:
                    rows, goal = pl.ds(0, count * blocks), out.at[pl.ds(to * blocks, count * blocks)]
                else:
                    rows, goal = pl.ds(source.shape[0] - SMALL, SMALL), small
                copies.append(pltpu.make_async_copy(source.at[rows], goal, sems.at[n]))
            for copy in copies:
                copy.start()
            for copy in copies:
                copy.wait()

    weights[...] = get_split(small, LEVEL_ROW)


def scratch(blocks):
    return [
        pltpu.VMEM((10 * blocks, blocks), BF16),
        pltpu.VMEM((10 * blocks, blocks), BF16),
        pltpu.VMEM((5 * SMALL, blocks), BF16),
        pltpu.VMEM((10 * blocks, blocks), BF16),
        pltpu.VMEM((SLOT_COUNT * blocks, blocks), BF16),
        pltpu.VMEM((4 * blocks, 4 * blocks), BF16),
        pltpu.VMEM((blocks, 4 * blocks), F32),
        pltpu.VMEM((blocks, 2 * blocks), F32),
        pltpu.VMEM((16, 128), F32),
        pltpu.SMEM((16, 128), F32),
        pltpu.SemaphoreType.DMA((13,)),
        pltpu.SemaphoreType.DMA,
    ]


def vmem():
    return pl.BlockSpec(memory_space=pltpu.VMEM)


def hbm():
    return pl.BlockSpec(memory_space=pl.ANY)


def params():
    return pltpu.CompilerParams(vmem_limit_bytes=VMEM_BYTES)


def per_device(loops, inners, site_blocks, bond_weights, bond_gates, kept_slots):
    blocks = site_blocks.shape[-1]

    def rows(count, small=0):
        return jax.ShapeDtypeStruct((count * blocks + small, blocks), BF16)

    def send(value, where):
        route = []
        for l in range(loops):
            for i in range(inners):
                source = where(l, i)
                if source is not None:
                    sl, si = source
                    route.append(((sl % loops) * inners + si % inners, l * inners + i))
        return lax.ppermute(value, AXES, route)

    def worker(where):
        return lambda l, i: where(l, i) if i % 2 == 0 else None

    full, head, tail = pl.pallas_call(
        prepare,
        out_shape=(rows(4, SMALL), rows(3, SMALL), rows(3, SMALL)),
        in_specs=[vmem()] * 4,
        out_specs=(vmem(),) * 3,
        name="prepare",
    )(site_blocks[0, 0], bond_weights[0], bond_gates[0], kept_slots)

    core = send(full, worker(lambda l, i: (l, i + 1)))
    mirror = send(head, worker(lambda l, i: (l ^ 1, i)))
    mirror_core = send(full, worker(lambda l, i: (l ^ 1, i + 1)))
    near = send(full, worker(lambda l, i: (l, i - 1) if l % 2 == 0 else (l, i + 2)))
    next_one = send(tail, worker(lambda l, i: (l + 1, i + 2) if l % 2 == 0 else (l, i + 3)))
    next_two = send(tail, worker(lambda l, i: None if l % 2 == 0 else (l - 1, i + 2)))

    iso_msg, iso_three, left, left_three, small = pl.pallas_call(
        first_kernel,
        out_shape=(
            rows(4, SMALL), rows(3, SMALL), rows(4), rows(3),
            jax.ShapeDtypeStruct((2 * SMALL, blocks), BF16),
        ),
        in_specs=[hbm()] * 7,
        out_specs=(vmem(),) * 5,
        scratch_shapes=scratch(blocks),
        compiler_params=params(),
        name="first_bond",
    )(full, core, mirror, mirror_core, near, next_one, next_two)

    iso_1 = send(iso_msg, worker(lambda l, i: (l + 1, i - 2) if l % 2 == 0 else (l - 1, i)))
    iso_2 = send(iso_three, worker(lambda l, i: (l, i - 2)))
    left_1 = send(left, worker(lambda l, i: (l + 3, i) if l % 2 == 0 else (l + 1, i + 2)))
    left_2 = send(left_three, worker(lambda l, i: (l + 2, i + 2)))
    left_0 = left if loops == 2 else send(left, worker(lambda l, i: (l + 2, i)))

    mid, last, first, whole = pl.pallas_call(
        second_kernel,
        out_shape=(rows(2), rows(1), rows(1, SMALL), rows(4, SMALL)),
        in_specs=[hbm()] * 6 + [vmem()],
        out_specs=(vmem(),) * 4,
        scratch_shapes=scratch(blocks)
        + [pltpu.VMEM((4 * blocks, blocks), BF16), pltpu.VMEM((4 * blocks, blocks), BF16)],
        compiler_params=params(),
        name="second_bond",
    )(iso_msg, iso_1, iso_2, left_0, left_1, left_2, small)

    def mid_from(l, i):
        if l % 2:
            return None
        return (l - 1, i - 2) if i % 2 == 0 else (l - 2, i - 1)

    def last_from(l, i):
        if l % 2:
            return None
        return (l - 2, i - 2) if i % 2 == 0 else (l - 1, i - 3)

    def first_from(l, i):
        return (l - 1, i - 1) if l % 2 == 0 and i % 2 else None

    def whole_from(l, i):
        if l % 2 == 0:
            return None
        return (l - 1, i) if i % 2 == 0 else (l, i - 1)

    mid_r = send(mid, mid_from)
    last_r = send(last, last_from)
    first_r = send(first, first_from)
    whole_r = send(whole, whole_from)
    if loops == 2:
        first_mine, level_far = first, first_r
    else:
        first_mine = send(first, worker(lambda l, i: (l - 2, i) if l % 2 == 0 else None))
        level_far = send(
            iso_msg[4 * blocks :], lambda l, i: (l + 1, i - 1) if l % 2 == 0 and i % 2 else None
        )
    sites, weights = pl.pallas_call(
        final_kernel,
        out_shape=(rows(4), jax.ShapeDtypeStruct((1, blocks), F32)),
        in_specs=[hbm()] * 7,
        out_specs=(vmem(),) * 2,
        scratch_shapes=[pltpu.VMEM((SMALL, blocks), BF16), pltpu.SemaphoreType.DMA((4,))],
        name="assemble",
    )(first_mine, mid_r, last_r, first_r, whole_r, iso_msg, level_far)
    return sites.reshape(1, 1, 4, blocks, blocks), weights[None]


def solution(mesh):
    return jax.shard_map(
        functools.partial(per_device, mesh.shape["loop"], mesh.shape["inner"]),
        mesh=mesh,
        in_specs=(
            P("loop", "inner", None, None, None),
            P("loop", "inner", None),
            P("loop", None, None),
            P("loop", "inner"),
        ),
        out_specs=(P("loop", "inner", None, None, None), P("loop", "inner", None)),
        check_vma=False,
    )
```

time: 148 us -> 117 us (0.79)
  the two profiles are of different devices: /device:TPU:0 before, /device:TPU:1 now
where the time goes in v1:
time: 117 us; the launch traced here: 116 us
  waiting for transfers between devices  84 us (72%)
  starting transfers between devices  23.5 us (20%)
  Pallas kernels  4.56 us (4%)
  local copies, waits for them, and re-layouts  2.65 us (2%)
  between operations  1.69 us (1%)
    ppermute x14, waiting for transfers between devices, send(): return lax.ppermute(value, AXES, route)  84 us
    ppermute x14, starting transfers between devices, send(): return lax.ppermute(value, AXES, route)  23.5 us
    unnamed x14, local copies, waits for them, and re-layouts  2.65 us
  transfers between devices with their start and end apart: 14, of which 2 were waited for; matrix products, arithmetic and copies ran while one was open for 0% of the time, Pallas kernels for 0%

profile of v1, /device:TPU:1, one launch (start us, length us, event | category | flops | bytes accessed | tf_op | source)
XLA Modules:
  0.0 116.3 jit_solution(2995381517861359473)
XLA Ops:
  1.3 2.2 %prepare.1 = (bf16[1056,256]{1,0:T(8,128)(2,1)}, bf16[800,256]{1,0:T(8,128)(2,1)}, bf16[800,256]{1,0:T(8,128)(2,1)}) custom-call(bf16[4,256,256]{2,1,0:T(8,128)(2,1)} %bitcast.5, f32[1,256]{1,0:T(1,128)} %bitcast.7, f32[16,16]{1,0:T(8,128)} %bitcast.6, s32[1,1]{1,0:T(1,128)S(6)} %copy.6.kept_ref), custom_call_target="tpu_custom_call" | custom-call | tf_op jit(solution)/shard_map/prepare/pallas_call | solution.py:416
  3.5 0.7 collective-permute-start.1
  4.2 7.3 %collective-permute-start.3 = (bf16[1056,256]{1,0:T(8,128)(2,1)}, bf16[1056,256]{1,0:T(8,128)(2,1)S(1)}, u32[]{:S(2)}, u32[]{:S(2)}) collective-permute-start(bf16[1056,256]{1,0:T(8,128)(2,1)} %get-tuple-element.16.own), channel_id=1, source_target_pairs={{15,0},{1,2},{3,4},{5,6},{7,8},{9,10},{11,12},{13,14},{18,16},{20,... | collective-permute-start | bytes 1622024 | tf_op jit(solution)/shard_map/ppermute | solution.py:411
  11.5 5.5 %collective-permute-start.2 = (bf16[1056,256]{1,0:T(8,128)(2,1)}, bf16[1056,256]{1,0:T(8,128)(2,1)S(1)}, u32[]{:S(2)}, u32[]{:S(2)}) collective-permute-start(bf16[1056,256]{1,0:T(8,128)(2,1)} %get-tuple-element.16.own), channel_id=1, source_target_pairs={{17,0},{19,2},{21,4},{23,6},{25,8},{27,10},{29,12},{31,14},{1,16},... | collective-permute-start | bytes 1622024 | tf_op jit(solution)/shard_map/ppermute | solution.py:411
  17.0 1.3 %collective-permute-start = (bf16[1056,256]{1,0:T(8,128)(2,1)}, bf16[1056,256]{1,0:T(8,128)(2,1)S(1)}, u32[]{:S(2)}, u32[]{:S(2)}) collective-permute-start(bf16[1056,256]{1,0:T(8,128)(2,1)} %get-tuple-element.16.own), channel_id=1, source_target_pairs={{1,0},{3,2},{5,4},{7,6},{9,8},{11,10},{13,12},{15,14},{17,16},{19,... | collective-permute-start | bytes 1622024 | tf_op jit(solution)/shard_map/ppermute | solution.py:411
  18.3 0.7 collective-permute-start.5
  19.0 0.0 collective-permute-done.1.mirror
  19.0 0.7 collective-permute-start.4
  19.7 0.0 collective-permute-done.5.next_two
  19.7 0.0 collective-permute-done.4.next_one
  19.7 0.0 collective-permute-done.3.near
  19.7 8.2 %collective-permute-done.2.mirror_core = bf16[1056,256]{1,0:T(8,128)(2,1)S(1)} collective-permute-done((bf16[1056,256]{1,0:T(8,128)(2,1)}, bf16[1056,256]{1,0:T(8,128)(2,1)S(1)}, u32[]{:S(2)}, u32[]{:S(2)}) %collective-permute-start.2) | collective-permute-done | bytes 540704 | tf_op jit(solution)/shard_map/ppermute | solution.py:411
  27.9 0.0 collective-permute-done.core
  27.9 0.0 copy-start.1
  27.9 1.0 copy-done.1
  29.0 0.1 first_bond.1
  29.1 0.0 copy-start
  29.1 0.7 collective-permute-start.6
  29.8 0.7 collective-permute-start.8
  30.5 0.7 collective-permute-start.7
  31.2 0.7 collective-permute-start.9
  31.9 0.0 collective-permute-done.9.left_2
  31.9 0.0 collective-permute-done.7.iso_2
  31.9 0.0 collective-permute-done.8.left_1
  31.9 0.0 collective-permute-done.6.iso_1
  31.9 0.3 second_bond.1
  32.3 0.0 copy-done
  32.3 0.0 copy-start.2
  32.3 0.7 collective-permute-start.13
  33.0 1.3 %collective-permute-start.10 = (bf16[512,256]{1,0:T(8,128)(2,1)S(1)}, bf16[512,256]{1,0:T(8,128)(2,1)S(1)}, u32[]{:S(2)}, u32[]{:S(2)}) collective-permute-start(bf16[512,256]{1,0:T(8,128)(2,1)S(1)} %get-tuple-element.25), channel_id=1, source_target_pairs={{30,0},{0,1},{16,2},{2,3},{18,4},{4,5},{20,6},{6,7},{22,8},{8,9},{... | collective-permute-start | bytes 786440 | tf_op jit(solution)/shard_map/ppermute | solution.py:411
  34.3 1.3 %collective-permute-start.12 = (bf16[288,256]{1,0:T(8,128)(2,1)S(1)}, bf16[288,256]{1,0:T(8,128)(2,1)S(1)}, u32[]{:S(2)}, u32[]{:S(2)}) collective-permute-start(bf16[288,256]{1,0:T(8,128)(2,1)S(1)} %get-tuple-element.24.first_mine), channel_id=1, source_target_pairs={{16,1},{18,3},{20,5},{22,7},{24,9},{26,11},{28,13},{30,15}} | collective-permute-start | bytes 442376 | tf_op jit(solution)/shard_map/ppermute | solution.py:411
  35.6 1.3 %collective-permute-start.11 = (bf16[256,256]{1,0:T(8,128)(2,1)S(1)}, bf16[256,256]{1,0:T(8,128)(2,1)S(1)}, u32[]{:S(2)}, u32[]{:S(2)}) collective-permute-start(bf16[256,256]{1,0:T(8,128)(2,1)S(1)} %get-tuple-element.26), channel_id=1, source_target_pairs={{14,0},{30,1},{0,2},{16,3},{2,4},{18,5},{4,6},{20,7},{6,8},{22,9},... | collective-permute-start | bytes 393224 | tf_op jit(solution)/shard_map/ppermute | solution.py:411
  36.9 75.8 %collective-permute-done.11.last = bf16[256,256]{1,0:T(8,128)(2,1)S(1)} collective-permute-done((bf16[256,256]{1,0:T(8,128)(2,1)S(1)}, bf16[256,256]{1,0:T(8,128)(2,1)S(1)}, u32[]{:S(2)}, u32[]{:S(2)}) %collective-permute-start.11) | collective-permute-done | bytes 131104 | tf_op jit(solution)/shard_map/ppermute | solution.py:411
  112.7 0.0 copy-start.6
  112.7 0.0 collective-permute-done.12.first.level_far
  112.7 0.0 copy-start.3
  112.7 0.0 collective-permute-done.10.mid
  112.7 0.0 copy-start.5
  112.7 0.0 collective-permute-done.13.whole
  112.7 0.0 copy-done.2
  112.7 0.6 copy-done.6
  113.3 0.1 copy-done.3
  113.4 0.1 copy-done.5
  113.5 0.0 copy-start.4
  113.5 0.8 copy-done.4
  114.3 1.9 %assemble.1 = (bf16[1024,256]{1,0:T(8,128)(2,1)}, f32[1,256]{1,0:T(1,128)}) custom-call(bf16[288,256]{1,0:T(8,128)(2,1)} %copy-done.2, bf16[512,256]{1,0:T(8,128)(2,1)} %copy-done.5, bf16[256,256]{1,0:T(8,128)(2,1)} %copy-done.6, bf16[288,256]{1,0:T(8,128)(2,1)} %copy-done.3, bf16[1056,256]{1,0:T(8,128)(2,1)} %copy-done.4, bf16[1056,256]{1,0:T(8,128)(2,1)} %copy-done, ...), custom_call_target="tpu_custom_call" | custom-call | tf_op jit(solution)/shard_map/assemble/pallas_call | solution.py:490
Async XLA Ops:
  3.5 15.5 %collective-permute-start.1 = (bf16[800,256]{1,0:T(8,128)(2,1)}, bf16[800,256]{1,0:T(8,128)(2,1)S(1)}, u32[]{:S(2)}, u32[]{:S(2)}) collective-permute-start(bf16[800,256]{1,0:T(8,128)(2,1)} %get-tuple-element.17), channel_id=1, source_target_pairs={{16,0},{18,2},{20,4},{22,6},{24,8},{26,10},{28,12},{30,14},{0,16},... | collective-permute-start | bytes 1228808 | tf_op jit(solution)/shard_map/ppermute | solution.py:411
  4.2 15.5 %collective-permute-start.3 = (bf16[1056,256]{1,0:T(8,128)(2,1)}, bf16[1056,256]{1,0:T(8,128)(2,1)S(1)}, u32[]{:S(2)}, u32[]{:S(2)}) collective-permute-start(bf16[1056,256]{1,0:T(8,128)(2,1)} %get-tuple-element.16.own), channel_id=1, source_target_pairs={{15,0},{1,2},{3,4},{5,6},{7,8},{9,10},{11,12},{13,14},{18,16},{20,... | collective-permute-start | bytes 1622024 | tf_op jit(solution)/shard_map/ppermute | solution.py:411
  11.5 16.4 %collective-permute-start.2 = (bf16[1056,256]{1,0:T(8,128)(2,1)}, bf16[1056,256]{1,0:T(8,128)(2,1)S(1)}, u32[]{:S(2)}, u32[]{:S(2)}) collective-permute-start(bf16[1056,256]{1,0:T(8,128)(2,1)} %get-tuple-element.16.own), channel_id=1, source_target_pairs={{17,0},{19,2},{21,4},{23,6},{25,8},{27,10},{29,12},{31,14},{1,16},... | collective-permute-start | bytes 1622024 | tf_op jit(solution)/shard_map/ppermute | solution.py:411
  17.0 11.0 %collective-permute-start = (bf16[1056,256]{1,0:T(8,128)(2,1)}, bf16[1056,256]{1,0:T(8,128)(2,1)S(1)}, u32[]{:S(2)}, u32[]{:S(2)}) collective-permute-start(bf16[1056,256]{1,0:T(8,128)(2,1)} %get-tuple-element.16.own), channel_id=1, source_target_pairs={{1,0},{3,2},{5,4},{7,6},{9,8},{11,10},{13,12},{15,14},{17,16},{19,... | collective-permute-start | bytes 1622024 | tf_op jit(solution)/shard_map/ppermute | solution.py:411
  18.3 1.4 %collective-permute-start.5 = (bf16[800,256]{1,0:T(8,128)(2,1)}, bf16[800,256]{1,0:T(8,128)(2,1)S(1)}, u32[]{:S(2)}, u32[]{:S(2)}) collective-permute-start(bf16[800,256]{1,0:T(8,128)(2,1)} %get-tuple-element.18), channel_id=1, source_target_pairs={{2,16},{4,18},{6,20},{8,22},{10,24},{12,26},{14,28},{0,30}} | collective-permute-start | bytes 1228808 | tf_op jit(solution)/shard_map/ppermute | solution.py:411
  19.0 0.7 collective-permute-start.4
  27.9 1.0 copy-start.1
  29.1 3.2 %copy-start = (bf16[1056,256]{1,0:T(8,128)(2,1)}, bf16[1056,256]{1,0:T(8,128)(2,1)S(1)}, u32[]{:S(2)}) copy-start(bf16[1056,256]{1,0:T(8,128)(2,1)S(1)} %get-tuple-element.19.iso_0.level_mine) | copy-start | bytes 1622020
  29.1 2.8 %collective-permute-start.6 = (bf16[1056,256]{1,0:T(8,128)(2,1)S(1)}, bf16[1056,256]{1,0:T(8,128)(2,1)S(1)}, u32[]{:S(2)}, u32[]{:S(2)}) collective-permute-start(bf16[1056,256]{1,0:T(8,128)(2,1)S(1)} %get-tuple-element.19.iso_0.level_mine), channel_id=1, source_target_pairs={{30,0},{16,2},{18,4},{20,6},{22,8},{24,10},{26,12},{28,14},{0,16},... | collective-permute-start | bytes 1622024 | tf_op jit(solution)/shard_map/ppermute | solution.py:411
  29.8 2.1 %collective-permute-start.8 = (bf16[1024,256]{1,0:T(8,128)(2,1)S(1)}, bf16[1024,256]{1,0:T(8,128)(2,1)S(1)}, u32[]{:S(2)}, u32[]{:S(2)}) collective-permute-start(bf16[1024,256]{1,0:T(8,128)(2,1)S(1)} %get-tuple-element.21.left_0), channel_id=1, source_target_pairs={{16,0},{18,2},{20,4},{22,6},{24,8},{26,10},{28,12},{30,14},{2,16},... | collective-permute-start | bytes 1572872 | tf_op jit(solution)/shard_map/ppermute | solution.py:411
  30.5 1.4 %collective-permute-start.7 = (bf16[800,256]{1,0:T(8,128)(2,1)S(1)}, bf16[800,256]{1,0:T(8,128)(2,1)S(1)}, u32[]{:S(2)}, u32[]{:S(2)}) collective-permute-start(bf16[800,256]{1,0:T(8,128)(2,1)S(1)} %get-tuple-element.20), channel_id=1, source_target_pairs={{14,0},{0,2},{2,4},{4,6},{6,8},{8,10},{10,12},{12,14},{30,16},{16,... | collective-permute-start | bytes 1228808 | tf_op jit(solution)/shard_map/ppermute | solution.py:411
  31.2 0.7 collective-permute-start.9
  32.3 80.4 %copy-start.2 = (bf16[288,256]{1,0:T(8,128)(2,1)}, bf16[288,256]{1,0:T(8,128)(2,1)S(1)}, u32[]{:S(2)}) copy-start(bf16[288,256]{1,0:T(8,128)(2,1)S(1)} %get-tuple-element.24.first_mine) | copy-start | bytes 442372
  32.3 80.4 %collective-permute-start.13 = (bf16[1056,256]{1,0:T(8,128)(2,1)S(1)}, bf16[1056,256]{1,0:T(8,128)(2,1)S(1)}, u32[]{:S(2)}, u32[]{:S(2)}) collective-permute-start(bf16[1056,256]{1,0:T(8,128)(2,1)S(1)} %get-tuple-element.27), channel_id=1, source_target_pairs={{0,16},{16,17},{2,18},{18,19},{4,20},{20,21},{6,22},{22,23},{8,24}... | collective-permute-start | bytes 1622024 | tf_op jit(solution)/shard_map/ppermute | solution.py:411
  33.0 79.7 %collective-permute-start.10 = (bf16[512,256]{1,0:T(8,128)(2,1)S(1)}, bf16[512,256]{1,0:T(8,128)(2,1)S(1)}, u32[]{:S(2)}, u32[]{:S(2)}) collective-permute-start(bf16[512,256]{1,0:T(8,128)(2,1)S(1)} %get-tuple-element.25), channel_id=1, source_target_pairs={{30,0},{0,1},{16,2},{2,3},{18,4},{4,5},{20,6},{6,7},{22,8},{8,9},{... | collective-permute-start | bytes 786440 | tf_op jit(solution)/shard_map/ppermute | solution.py:411
  34.3 78.4 %collective-permute-start.12 = (bf16[288,256]{1,0:T(8,128)(2,1)S(1)}, bf16[288,256]{1,0:T(8,128)(2,1)S(1)}, u32[]{:S(2)}, u32[]{:S(2)}) collective-permute-start(bf16[288,256]{1,0:T(8,128)(2,1)S(1)} %get-tuple-element.24.first_mine), channel_id=1, source_target_pairs={{16,1},{18,3},{20,5},{22,7},{24,9},{26,11},{28,13},{30,15}} | collective-permute-start | bytes 442376 | tf_op jit(solution)/shard_map/ppermute | solution.py:411
  35.6 77.1 %collective-permute-start.11 = (bf16[256,256]{1,0:T(8,128)(2,1)S(1)}, bf16[256,256]{1,0:T(8,128)(2,1)S(1)}, u32[]{:S(2)}, u32[]{:S(2)}) collective-permute-start(bf16[256,256]{1,0:T(8,128)(2,1)S(1)} %get-tuple-element.26), channel_id=1, source_target_pairs={{14,0},{30,1},{0,2},{16,3},{2,4},{18,5},{4,6},{20,7},{6,8},{22,9},... | collective-permute-start | bytes 393224 | tf_op jit(solution)/shard_map/ppermute | solution.py:411
  112.7 0.7 copy-start.6
  112.7 0.7 copy-start.3
  112.7 0.8 copy-start.5
  113.5 0.8 copy-start.4

commit v2 on v1

--- a/solution.py
+++ b/solution.py
@@ -12,7 +12,7 @@
 CHARGE = (0, 1, 1, 2)
 AXES = ("loop", "inner")
 BF16, F32 = jnp.bfloat16, jnp.float32
-VMEM_BYTES = 40 << 20
+VMEM_BYTES = 60 << 20
 HIGHEST = lax.Precision.HIGHEST
 
 
@@ -121,19 +121,25 @@
     return (h + m) + l
 
 
-def prepare(block_ref, weight_ref, gate_ref, kept_ref, full, head, tail):
+def prepare(block_ref, weight_ref, gate_ref, kept_ref, full, three_a, three_b):
+    x = lax.axis_index("loop") % 2
+    c = lax.axis_index("inner") % 2
     blocks = block_ref.shape[-1]
-    rows = block_ref[...].reshape(4 * blocks, blocks)
     small = jnp.zeros((SMALL, blocks), F32)
     rowid = lax.broadcasted_iota(jnp.int32, (SMALL, blocks), 0)
     for n, part in enumerate(split3(weight_ref[...])):
         small = jnp.where(rowid == W_ROW + n, part.astype(F32), small)
     small = jnp.where(rowid == K_ROW, kept_ref[...].astype(F32), small).astype(BF16)
-    for ref, lo, hi in ((full, 0, 4), (head, 0, 3), (tail, 1, 4)):
-        size = (hi - lo) * blocks
-        ref[0:size, :] = rows[lo * blocks : hi * blocks]
-        ref[size : size + SMALL, :] = small
-        ref[size : size + 16, 0:16] = gate_ref[...].astype(BF16)
+    shift = jnp.where(jnp.logical_and(x == 1, c == 1), 1, 0)
+    for n in range(4):
+        full[n * blocks : (n + 1) * blocks, :] = block_ref[n]
+    for n in range(3):
+        three_a[n * blocks : (n + 1) * blocks, :] = block_ref[n + shift]
+        three_b[n * blocks : (n + 1) * blocks, :] = block_ref[n + 1]
+    for ref in (full, three_a, three_b):
+        base = ref.shape[0] - SMALL
+        ref[base : base + SMALL, :] = small
+        ref[base : base + 16, 0:16] = gate_ref[...].astype(BF16)
 
 
 def bond_body(
@@ -215,8 +221,8 @@
 
 
 def first_kernel(
-    own, core, mirror, mirror_core, near, next_one, next_two,
-    iso_msg, iso_three, left, left_three, small_out,
+    own, edge, cross, mirror_odd, mirror_even, beside,
+    iso_msg, iso_three, left, left_three, local,
     a_ref, b_ref, small, scaled, theta, matrix, proj, work, gate_stage, gates, sems, sem,
 ):
     x = lax.axis_index("loop") % 2
@@ -224,17 +230,17 @@
     blocks = a_ref.shape[-1]
     plans = {
         0: [
-            (a_ref, 0, near, 0, 3), (a_ref, 3, own, 0, 4), (a_ref, 7, core, 1, 3),
-            (b_ref, 0, mirror, 0, 3), (b_ref, 3, mirror_core, 0, 4), (b_ref, 7, next_one, 0, 3),
+            (a_ref, 0, edge, 0, 3), (a_ref, 3, own, 0, 4), (a_ref, 7, beside, 1, 3),
+            (b_ref, 0, mirror_even, 0, 3), (b_ref, 3, mirror_odd, 0, 4), (b_ref, 7, cross, 0, 3),
         ],
         1: [
-            (a_ref, 0, mirror, 0, 3), (a_ref, 3, mirror_core, 0, 4), (a_ref, 7, next_two, 0, 3),
-            (b_ref, 0, core, 0, 3), (b_ref, 3, near, 0, 4), (b_ref, 7, next_one, 0, 3),
+            (a_ref, 0, mirror_even, 0, 3), (a_ref, 3, mirror_odd, 0, 4), (a_ref, 7, cross, 0, 3),
+            (b_ref, 0, own, 0, 3), (b_ref, 3, beside, 0, 4), (b_ref, 7, edge, 0, 3),
         ],
     }
     smalls = {
-        0: [near, own, core, mirror, mirror_core],
-        1: [mirror, mirror_core, next_two, core, near],
+        0: [edge, own, beside, mirror_even, mirror_odd],
+        1: [mirror_even, mirror_odd, cross, own, beside],
     }
 
     def move(source, at, target, to, rows, n):
@@ -242,7 +248,7 @@
             source.at[pl.ds(at, rows)], target.at[pl.ds(to, rows)], sems.at[n]
         )
 
-    @pl.when(c == 0)
+    @pl.when(x == c)
     def _():
         for role in (0, 1):
 
@@ -265,12 +271,14 @@
         )
         iso_three[0 : 3 * blocks, :] = iso_msg[blocks : 4 * blocks, :]
         left_three[...] = left[blocks : 4 * blocks, :]
-        for ref in (iso_msg, iso_three):
+        local[0 : 3 * blocks, :] = iso_msg[0 : 3 * blocks, :]
+        local[3 * blocks : 6 * blocks, :] = left[0 : 3 * blocks, :]
+        local[6 * blocks : 6 * blocks + 2 * SMALL, :] = small[3 * SMALL : 5 * SMALL, :]
+        for ref in (iso_msg, iso_three, local):
             base = ref.shape[0] - SMALL
             ref[base : base + SMALL, :] = jnp.zeros((SMALL, blocks), BF16)
             put_split(ref, base, get_split(small, 3 * SMALL + W_ROW))
             put_split(ref, base + LEVEL_ROW, level)
-        small_out[...] = small[3 * SMALL : 5 * SMALL, :]
 
 
 def as_column(row):
@@ -278,50 +286,47 @@
 
 
 def second_kernel(
-    iso_0, iso_1, iso_2, left_0, left_1, left_2, small_in,
+    local, iso_1, iso_2, left_0, left_1, left_2,
     mid, last, first, whole,
     a_ref, b_ref, small, scaled, theta, matrix, proj, work, gate_stage, gates, sems, sem,
     iso, left,
 ):
+    x = lax.axis_index("loop") % 2
     c = lax.axis_index("inner") % 2
     blocks = a_ref.shape[-1]
     moves = [
-        (iso_1, 0, a_ref, 0, 1), (iso_2, 0, a_ref, 1, 2), (iso_0, 0, a_ref, 3, 1),
-        (iso_1, 1, a_ref, 4, 2), (iso_2, 2, a_ref, 6, 1), (iso_0, 1, a_ref, 7, 2),
-        (iso_1, 3, a_ref, 9, 1), (left_0, 0, b_ref, 0, 3), (left_1, 0, b_ref, 3, 4),
-        (left_2, 0, b_ref, 7, 3),
+        (source, at * blocks, target, to * blocks, count * blocks)
+        for source, at, target, to, count in (
+            (iso_1, 0, a_ref, 0, 1), (iso_2, 0, a_ref, 1, 2), (local, 0, a_ref, 3, 1),
+            (iso_1, 1, a_ref, 4, 2), (iso_2, 2, a_ref, 6, 1), (local, 1, a_ref, 7, 2),
+            (iso_1, 3, a_ref, 9, 1), (left_0, left_0.shape[0] // blocks - 3, b_ref, 0, 3),
+            (left_1, 0, b_ref, 3, 4), (left_2, 0, b_ref, 7, 3),
+        )
     ]
-
-    @pl.when(c == 0)
+    moves.append((local, 6 * blocks, small, 0, 3 * SMALL))
+    for n, source in enumerate((iso_1, iso_2)):
+        moves.append((source, source.shape[0] - SMALL, small, (3 + n) * SMALL, SMALL))
+
+    @pl.when(x != c)
     def _():
         copies = [
             pltpu.make_async_copy(
-                source.at[pl.ds(at * blocks, count * blocks)],
-                target.at[pl.ds(to * blocks, count * blocks)],
-                sems.at[n],
+                source.at[pl.ds(at, rows)], target.at[pl.ds(to, rows)], sems.at[n]
             )
-            for n, (source, at, target, to, count) in enumerate(moves)
+            for n, (source, at, target, to, rows) in enumerate(moves)
         ]
-        for n, source in enumerate((iso_0, iso_1, iso_2)):
-            copies.append(
-                pltpu.make_async_copy(
-                    source.at[pl.ds(source.shape[0] - SMALL, SMALL)],
-                    small.at[pl.ds(n * SMALL, SMALL)],
-                    sems.at[10 + n],
-                )
-            )
         for copy in copies:
             copy.start()
         for copy in copies:
             copy.wait()
-        below = get_split(small, SMALL)
-        here, above = (get_split(small_in, n * SMALL + W_ROW) for n in range(2))
-        kept = small_in[K_ROW : K_ROW + 1, 0:1].astype(F32)
+        below = get_split(small, 3 * SMALL)
+        here, above = (get_split(small, n * SMALL + W_ROW) for n in range(2))
+        kept = small[K_ROW : K_ROW + 1, 0:1].astype(F32)
         level = bond_body(
-            a_ref, b_ref, below, here, above, kept, small_in[0:16, 0:128],
+            a_ref, b_ref, below, here, above, kept, small[0:16, 0:128],
             scaled, theta, matrix, proj, work, iso, left, gate_stage, gates, sem,
         )
-        scales = [as_column(get_split(small, n * SMALL + LEVEL_ROW)) for n in range(3)]
+        scales = [as_column(get_split(small, n * SMALL + LEVEL_ROW)) for n in range(2, 5)]
         column = as_column(level)
         for p in range(4):
             rows = slice(p * blocks, (p + 1) * blocks)
@@ -330,19 +335,21 @@
             for p in range(lo, hi):
                 value = iso[p * blocks : (p + 1) * blocks, :].astype(F32) * column
                 ref[(p - lo) * blocks : (p - lo + 1) * blocks, :] = value.astype(BF16)
-        for ref, value in ((first, get_split(small, LEVEL_ROW)), (whole, level)):
+        for ref, value in ((first, get_split(small, 2 * SMALL + LEVEL_ROW)), (whole, level)):
             base = ref.shape[0] - SMALL
             ref[base : base + SMALL, :] = jnp.zeros((SMALL, blocks), BF16)
             put_split(ref, base + LEVEL_ROW, value)
 
 
-def final_kernel(first_mine, mid, last, first, whole, level_mine, level_far, out, weights, small, sems):
+def final_kernel(
+    first, mid_mine, mid, last, whole, level_mine, level_far, out, weights, small, sems
+):
     x = lax.axis_index("loop") % 2
     c = lax.axis_index("inner") % 2
     blocks = out.shape[-1]
     plans = {
-        (0, 0): [(first_mine, 0, 1), (mid, 1, 2), (last, 3, 1), (level_mine, 0, 0)],
-        (0, 1): [(first, 0, 1), (mid, 1, 2), (last, 3, 1), (level_far, 0, 0)],
+        (0, 0): [(first, 0, 1), (mid, 1, 2), (last, 3, 1), (level_mine, 0, 0)],
+        (0, 1): [(first, 0, 1), (mid_mine, 1, 2), (last, 3, 1), (level_far, 0, 0)],
         (1, 0): [(whole, 0, 4), (whole, 0, 0)],
         (1, 1): [(whole, 0, 4), (whole, 0, 0)],
     }
@@ -410,82 +417,86 @@
                     route.append(((sl % loops) * inners + si % inners, l * inners + i))
         return lax.ppermute(value, AXES, route)
 
-    def worker(where):
-        return lambda l, i: where(l, i) if i % 2 == 0 else None
-
-    full, head, tail = pl.pallas_call(
+    def to_first(where):
+        return lambda l, i: where(l, i // 2) if i % 2 == l % 2 else None
+
+    def to_second(where):
+        return lambda l, i: where(l, i // 2) if i % 2 != l % 2 else None
+
+    full, three_a, three_b = pl.pallas_call(
         prepare,
         out_shape=(rows(4, SMALL), rows(3, SMALL), rows(3, SMALL)),
         in_specs=[vmem()] * 4,
         out_specs=(vmem(),) * 3,
+        compiler_params=params(),
         name="prepare",
     )(site_blocks[0, 0], bond_weights[0], bond_gates[0], kept_slots)
 
-    core = send(full, worker(lambda l, i: (l, i + 1)))
-    mirror = send(head, worker(lambda l, i: (l ^ 1, i)))
-    mirror_core = send(full, worker(lambda l, i: (l ^ 1, i + 1)))
-    near = send(full, worker(lambda l, i: (l, i - 1) if l % 2 == 0 else (l, i + 2)))
-    next_one = send(tail, worker(lambda l, i: (l + 1, i + 2) if l % 2 == 0 else (l, i + 3)))
-    next_two = send(tail, worker(lambda l, i: None if l % 2 == 0 else (l - 1, i + 2)))
-
-    iso_msg, iso_three, left, left_three, small = pl.pallas_call(
+    def pick(even, odd):
+        return to_first(lambda l, k: (even if l % 2 == 0 else odd)(l, k))
+
+    edge = send(
+        three_a, pick(lambda l, k: (l, 2 * k - 1), lambda l, k: (l, 2 * k + 3))
+    )
+    cross = send(
+        three_b, pick(lambda l, k: (l + 1, 2 * k + 2), lambda l, k: (l - 1, 2 * k + 2))
+    )
+    mirror_odd = send(full, to_first(lambda l, k: (l ^ 1, 2 * k + 1)))
+    mirror_even = send(three_a, to_first(lambda l, k: (l ^ 1, 2 * k)))
+    beside = send(full, pick(lambda l, k: (l, 2 * k + 1), lambda l, k: (l, 2 * k + 2)))
+
+    iso_msg, iso_three, left, left_three, local = pl.pallas_call(
         first_kernel,
-        out_shape=(
-            rows(4, SMALL), rows(3, SMALL), rows(4), rows(3),
-            jax.ShapeDtypeStruct((2 * SMALL, blocks), BF16),
-        ),
-        in_specs=[hbm()] * 7,
+        out_shape=(rows(4, SMALL), rows(3, SMALL), rows(4), rows(3), rows(6, 3 * SMALL)),
+        in_specs=[hbm()] * 6,
         out_specs=(vmem(),) * 5,
         scratch_shapes=scratch(blocks),
         compiler_params=params(),
         name="first_bond",
-    )(full, core, mirror, mirror_core, near, next_one, next_two)
-
-    iso_1 = send(iso_msg, worker(lambda l, i: (l + 1, i - 2) if l % 2 == 0 else (l - 1, i)))
-    iso_2 = send(iso_three, worker(lambda l, i: (l, i - 2)))
-    left_1 = send(left, worker(lambda l, i: (l + 3, i) if l % 2 == 0 else (l + 1, i + 2)))
-    left_2 = send(left_three, worker(lambda l, i: (l + 2, i + 2)))
-    left_0 = left if loops == 2 else send(left, worker(lambda l, i: (l + 2, i)))
+    )(full, edge, cross, mirror_odd, mirror_even, beside)
+
+    def worker(l, k, d, s):
+        sector = 2 * k + l % 2 + s
+        return (l - l % 2 + 2 * d + sector % 2, sector // 2 * 2 + sector % 2)
+
+    local_r = send(local, to_second(lambda l, k: worker(l, k, 0, 0)))
+    iso_1 = send(iso_msg, to_second(lambda l, k: worker(l, k, 0, -1)))
+    iso_2 = send(iso_three, to_second(lambda l, k: worker(l, k, 0, -2)))
+    left_1 = send(left, to_second(lambda l, k: worker(l, k, 1, 1)))
+    left_2 = send(left_three, to_second(lambda l, k: worker(l, k, 1, 2)))
+    if loops == 2:
+        left_0 = local_r
+    else:
+        left_0 = send(left[: 3 * blocks], to_second(lambda l, k: worker(l, k, 1, 0)))
 
     mid, last, first, whole = pl.pallas_call(
         second_kernel,
         out_shape=(rows(2), rows(1), rows(1, SMALL), rows(4, SMALL)),
-        in_specs=[hbm()] * 6 + [vmem()],
+        in_specs=[hbm()] * 6,
         out_specs=(vmem(),) * 4,
         scratch_shapes=scratch(blocks)
         + [pltpu.VMEM((4 * blocks, blocks), BF16), pltpu.VMEM((4 * blocks, blocks), BF16)],
         compiler_params=params(),
         name="second_bond",
-    )(iso_msg, iso_1, iso_2, left_0, left_1, left_2, small)
-
-    def mid_from(l, i):
-        if l % 2:
-            return None
-        return (l - 1, i - 2) if i % 2 == 0 else (l - 2, i - 1)
-
-    def last_from(l, i):
-        if l % 2:
-            return None
-        return (l - 2, i - 2) if i % 2 == 0 else (l - 1, i - 3)
-
-    def first_from(l, i):
-        return (l - 1, i - 1) if l % 2 == 0 and i % 2 else None
-
-    def whole_from(l, i):
-        if l % 2 == 0:
-            return None
-        return (l - 1, i) if i % 2 == 0 else (l, i - 1)
-
-    mid_r = send(mid, mid_from)
-    last_r = send(last, last_from)
-    first_r = send(first, first_from)
-    whole_r = send(whole, whole_from)
+    )(local_r, iso_1, iso_2, left_0, left_1, left_2)
+
+    def from_second(l, i, d, s):
+        sector = i - s
+        return (l - l % 2 - 2 * d + sector % 2, sector // 2 * 2 + 1 - sector % 2)
+
+    def right_from(s, cores):
+        return lambda l, i: from_second(l, i, 1, s) if l % 2 == 0 and i % 2 in cores else None
+
+    first_r = send(first, right_from(0, (0, 1)))
+    mid_r = send(mid, right_from(1, (0,) if loops == 2 else (0, 1)))
+    last_r = send(last, right_from(2, (0, 1)))
+    whole_r = send(whole, lambda l, i: from_second(l, i, 0, 0) if l % 2 else None)
     if loops == 2:
-        first_mine, level_far = first, first_r
+        mid_mine, level_far = mid, first_r
     else:
-        first_mine = send(first, worker(lambda l, i: (l - 2, i) if l % 2 == 0 else None))
+        mid_mine = mid_r
         level_far = send(
-            iso_msg[4 * blocks :], lambda l, i: (l + 1, i - 1) if l % 2 == 0 and i % 2 else None
+            iso_msg[4 * blocks :], lambda l, i: (l + 1, i) if l % 2 == 0 and i % 2 else None
         )
     sites, weights = pl.pallas_call(
         final_kernel,
@@ -493,8 +504,9 @@
         in_specs=[hbm()] * 7,
         out_specs=(vmem(),) * 2,
         scratch_shapes=[pltpu.VMEM((SMALL, blocks), BF16), pltpu.SemaphoreType.DMA((4,))],
+        compiler_params=params(),
         name="assemble",
-    )(first_mine, mid_r, last_r, first_r, whole_r, iso_msg, level_far)
+    )(first_r, mid_mine, mid_r, last_r, whole_r, iso_msg, level_far)
     return sites.reshape(1, 1, 4, blocks, blocks), weights[None]
 
 

time: 117 us -> 112 us (0.957)
  waiting for transfers between devices: 84 us -> 54.2 us
  Pallas kernels: 4.56 us -> 25.3 us
  local copies, waits for them, and re-layouts: 2.65 us -> 5.39 us
  starting transfers between devices: 23.5 us -> 25.5 us
    ppermute x14, waiting for transfers between devices: 84 us -> 54.2 us  [send(): return lax.ppermute(value, AXES, route)]
    pallas_call x1, Pallas kernels: 0.32 us -> 19.5 us  [per_device(): pl.pallas_call(second_kernel, out_shape=(rows(2), rows(1), rows(1, SMALL)...]
    unnamed x14 -> x28, local copies, waits for them, and re-layouts: 2.65 us -> 5.39 us
    ppermute x14, starting transfers between devices: 23.5 us -> 25.5 us  [send(): return lax.ppermute(value, AXES, route)]
    pallas_call x1, Pallas kernels: 0.13 us -> 1.66 us  [per_device(): pl.pallas_call(first_kernel, out_shape=(rows(4, SMALL), rows(3, SMALL), r...]
  transfers between devices with their start and end apart: 14 -> 14, of which waited for: 2 -> 3; matrix products, arithmetic and copies ran while one was open for 0% -> 0% of each run, Pallas kernels for 0% -> 0%
where the time goes in v2:
time: 112 us
  waiting for transfers between devices  54.2 us (48%)
  starting transfers between devices  25.5 us (23%)
  Pallas kernels  25.3 us (23%)
  local copies, waits for them, and re-layouts  5.39 us (5%)
  between operations  1.68 us (2%)
    ppermute x14, waiting for transfers between devices, send(): return lax.ppermute(value, AXES, route)  54.2 us
    ppermute x14, starting transfers between devices, send(): return lax.ppermute(value, AXES, route)  25.5 us
    pallas_call x1, Pallas kernels, per_device(): pl.pallas_call(second_kernel, out_shape=(rows(2), rows(1), rows(1, SMALL)...  19.5 us
    unnamed x28, local copies, waits for them, and re-layouts  5.39 us
  transfers between devices with their start and end apart: 14, of which 3 were waited for; matrix products, arithmetic and copies ran while one was open for 0% of the time, Pallas kernels for 0%

profile of v2, /device:TPU:1, one launch (start us, length us, event | category | flops | bytes accessed | tf_op | source)
XLA Modules:
  0.0 111.9 jit_solution(15738524621155834069)
XLA Ops:
  1.3 2.2 %prepare.1 = (bf16[1056,256]{1,0:T(8,128)(2,1)}, bf16[800,256]{1,0:T(8,128)(2,1)}, bf16[800,256]{1,0:T(8,128)(2,1)}) custom-call(bf16[4,256,256]{2,1,0:T(8,128)(2,1)} %bitcast.5, f32[1,256]{1,0:T(1,128)} %bitcast.7, f32[16,16]{1,0:T(8,128)} %bitcast.6, s32[1,1]{1,0:T(1,128)S(6)} %copy.6.kept_ref), custom_call_target="tpu_custom_call" | custom-call | tf_op jit(solution)/shard_map/prepare/pallas_call | solution.py:426
  3.5 2.0 %collective-permute-start.4 = (bf16[1056,256]{1,0:T(8,128)(2,1)}, bf16[1056,256]{1,0:T(8,128)(2,1)S(1)}, u32[]{:S(2)}, u32[]{:S(2)}) collective-permute-start(bf16[1056,256]{1,0:T(8,128)(2,1)} %get-tuple-element.16.own), channel_id=1, source_target_pairs={{1,0},{3,2},{5,4},{7,6},{9,8},{11,10},{13,12},{15,14},{18,17},{20,... | collective-permute-start | bytes 1622024 | tf_op jit(solution)/shard_map/ppermute | solution.py:418
  5.5 3.3 %collective-permute-start.2 = (bf16[1056,256]{1,0:T(8,128)(2,1)}, bf16[1056,256]{1,0:T(8,128)(2,1)S(1)}, u32[]{:S(2)}, u32[]{:S(2)}) collective-permute-start(bf16[1056,256]{1,0:T(8,128)(2,1)} %get-tuple-element.16.own), channel_id=1, source_target_pairs={{17,0},{19,2},{21,4},{23,6},{25,8},{27,10},{29,12},{31,14},{1,17},... | collective-permute-start | bytes 1622024 | tf_op jit(solution)/shard_map/ppermute | solution.py:418
  8.8 0.7 collective-permute-start.1
  9.5 0.7 collective-permute-start.3
  10.2 6.1 %collective-permute-start = (bf16[800,256]{1,0:T(8,128)(2,1)}, bf16[800,256]{1,0:T(8,128)(2,1)S(1)}, u32[]{:S(2)}, u32[]{:S(2)}) collective-permute-start(bf16[800,256]{1,0:T(8,128)(2,1)} %get-tuple-element.17), channel_id=1, source_target_pairs={{15,0},{1,2},{3,4},{5,6},{7,8},{9,10},{11,12},{13,14},{19,17},{21,... | collective-permute-start | bytes 1228808 | tf_op jit(solution)/shard_map/ppermute | solution.py:418
  16.2 0.0 collective-permute-done.1.cross
  16.2 0.0 copy-start.8
  16.3 0.0 collective-permute-done.3.mirror_even
  16.3 0.0 copy-start.9
  16.3 8.9 %collective-permute-done.edge = bf16[800,256]{1,0:T(8,128)(2,1)S(1)} collective-permute-done((bf16[800,256]{1,0:T(8,128)(2,1)}, bf16[800,256]{1,0:T(8,128)(2,1)S(1)}, u32[]{:S(2)}, u32[]{:S(2)}) %collective-permute-start) | collective-permute-done | bytes 409632 | tf_op jit(solution)/shard_map/ppermute | solution.py:418
  25.2 0.0 collective-permute-done.4.beside
  25.2 0.0 collective-permute-done.2.mirror_odd
  25.2 0.7 copy-done.10
  25.9 0.2 copy-done.3
  26.1 0.8 copy-done.4
  26.9 1.7 %first_bond.1 = (bf16[1056,256]{1,0:T(8,128)(2,1)}, bf16[800,256]{1,0:T(8,128)(2,1)}, bf16[1024,256]{1,0:T(8,128)(2,1)}, bf16[768,256]{1,0:T(8,128)(2,1)}, bf16[1632,256]{1,0:T(8,128)(2,1)}) custom-call(bf16[1056,256]{1,0:T(8,128)(2,1)} %get-tuple-element.16.own, bf16[800,256]{1,0:T(8,128)(2,1)} %copy-done.10, bf16[800,256]{1,0:T(8,128)(2,1)} %copy-done.8, ...), custom_call_target="tpu_custom_call" | custom-call | tf_op jit(solution)/shard_map/first_bond/pallas_call | solution.py:448
  28.6 1.3 %collective-permute-start.5 = (bf16[1632,256]{1,0:T(8,128)(2,1)}, bf16[1632,256]{1,0:T(8,128)(2,1)S(1)}, u32[]{:S(2)}, u32[]{:S(2)}) collective-permute-start(bf16[1632,256]{1,0:T(8,128)(2,1)} %get-tuple-element.19), channel_id=1, source_target_pairs={{0,1},{2,3},{4,5},{6,7},{8,9},{10,11},{12,13},{14,15},{17,16},{19,... | collective-permute-start | bytes 2506760 | tf_op jit(solution)/shard_map/ppermute | solution.py:418
  29.9 1.3 %collective-permute-start.6 = (bf16[1056,256]{1,0:T(8,128)(2,1)}, bf16[1056,256]{1,0:T(8,128)(2,1)S(1)}, u32[]{:S(2)}, u32[]{:S(2)}) collective-permute-start(bf16[1056,256]{1,0:T(8,128)(2,1)} %get-tuple-element.20.level_mine), channel_id=1, source_target_pairs={{31,1},{17,3},{19,5},{21,7},{23,9},{25,11},{27,13},{29,15},{0,16},... | collective-permute-start | bytes 1622024 | tf_op jit(solution)/shard_map/ppermute | solution.py:418
  31.2 1.3 %collective-permute-start.8 = (bf16[1024,256]{1,0:T(8,128)(2,1)}, bf16[1024,256]{1,0:T(8,128)(2,1)S(1)}, u32[]{:S(2)}, u32[]{:S(2)}) collective-permute-start(bf16[1024,256]{1,0:T(8,128)(2,1)} %get-tuple-element.22), channel_id=1, source_target_pairs={{17,1},{19,3},{21,5},{23,7},{25,9},{27,11},{29,13},{31,15},{2,16},... | collective-permute-start | bytes 1572872 | tf_op jit(solution)/shard_map/ppermute | solution.py:418
  32.5 1.3 %collective-permute-start.7 = (bf16[800,256]{1,0:T(8,128)(2,1)}, bf16[800,256]{1,0:T(8,128)(2,1)S(1)}, u32[]{:S(2)}, u32[]{:S(2)}) collective-permute-start(bf16[800,256]{1,0:T(8,128)(2,1)} %get-tuple-element.21), channel_id=1, source_target_pairs={{14,1},{0,3},{2,5},{4,7},{6,9},{8,11},{10,13},{12,15},{31,16},{17,... | collective-permute-start | bytes 1228808 | tf_op jit(solution)/shard_map/ppermute | solution.py:418
  33.8 1.3 %collective-permute-start.9 = (bf16[768,256]{1,0:T(8,128)(2,1)}, bf16[768,256]{1,0:T(8,128)(2,1)S(1)}, u32[]{:S(2)}, u32[]{:S(2)}) collective-permute-start(bf16[768,256]{1,0:T(8,128)(2,1)} %get-tuple-element.23), channel_id=1, source_target_pairs={{2,1},{4,3},{6,5},{8,7},{10,9},{12,11},{14,13},{0,15},{19,16},{21,... | collective-permute-start | bytes 1179656 | tf_op jit(solution)/shard_map/ppermute | solution.py:418
  35.1 37.1 %collective-permute-done.9.left_2 = bf16[768,256]{1,0:T(8,128)(2,1)S(1)} collective-permute-done((bf16[768,256]{1,0:T(8,128)(2,1)}, bf16[768,256]{1,0:T(8,128)(2,1)S(1)}, u32[]{:S(2)}, u32[]{:S(2)}) %collective-permute-start.9) | collective-permute-done | bytes 393248 | tf_op jit(solution)/shard_map/ppermute | solution.py:418
  72.1 0.0 collective-permute-done.7.iso_2
  72.1 0.0 collective-permute-done.8.left_1
  72.1 0.0 copy-start.6
  72.2 0.0 collective-permute-done.6.iso_1
  72.2 0.0 copy-start.2
  72.2 0.0 collective-permute-done.5.local.left_0
  72.2 0.7 copy-done.11
  72.9 0.2 copy-done.7
  73.0 0.2 copy-done.6
  73.2 0.2 copy-done.2
  73.4 0.9 copy-done
  74.3 19.5 %second_bond.1 = (bf16[512,256]{1,0:T(8,128)(2,1)}, bf16[256,256]{1,0:T(8,128)(2,1)}, bf16[288,256]{1,0:T(8,128)(2,1)}, bf16[1056,256]{1,0:T(8,128)(2,1)}) custom-call(bf16[1632,256]{1,0:T(8,128)(2,1)} %copy-done, bf16[1056,256]{1,0:T(8,128)(2,1)} %copy-done.2, bf16[800,256]{1,0:T(8,128)(2,1)} %copy-done.7, bf16[1632,256]{1,0:T(8,128)(2,1)} %copy-done, ...), custom_call_target="tpu_custom_call" | custom-call | tf_op jit(solution)/shard_map/second_bond/pallas_call | solution.py:472
  93.8 1.8 %collective-permute-start.13 = (bf16[1056,256]{1,0:T(8,128)(2,1)}, bf16[1056,256]{1,0:T(8,128)(2,1)S(1)}, u32[]{:S(2)}, u32[]{:S(2)}) collective-permute-start(bf16[1056,256]{1,0:T(8,128)(2,1)} %get-tuple-element.27), channel_id=1, source_target_pairs={{1,16},{16,17},{3,18},{18,19},{5,20},{20,21},{7,22},{22,23},{9,24}... | collective-permute-start | bytes 1622024 | tf_op jit(solution)/shard_map/ppermute | solution.py:418
  95.6 0.7 collective-permute-start.11
  96.3 1.9 %collective-permute-start.10 = (bf16[288,256]{1,0:T(8,128)(2,1)}, bf16[288,256]{1,0:T(8,128)(2,1)S(1)}, u32[]{:S(2)}, u32[]{:S(2)}) collective-permute-start(bf16[288,256]{1,0:T(8,128)(2,1)} %get-tuple-element.24), channel_id=1, source_target_pairs={{1,0},{16,1},{3,2},{18,3},{5,4},{20,5},{7,6},{22,7},{9,8},{24,9},{... | collective-permute-start | bytes 442376 | tf_op jit(solution)/shard_map/ppermute | solution.py:418
  98.2 1.9 %collective-permute-start.12 = (bf16[256,256]{1,0:T(8,128)(2,1)}, bf16[256,256]{1,0:T(8,128)(2,1)S(1)}, u32[]{:S(2)}, u32[]{:S(2)}) collective-permute-start(bf16[256,256]{1,0:T(8,128)(2,1)} %get-tuple-element.26), channel_id=1, source_target_pairs={{15,0},{30,1},{1,2},{16,3},{3,4},{18,5},{5,6},{20,7},{7,8},{22,9},... | collective-permute-start | bytes 393224 | tf_op jit(solution)/shard_map/ppermute | solution.py:418
  100.1 8.2 %collective-permute-done.12.last = bf16[256,256]{1,0:T(8,128)(2,1)S(1)} collective-permute-done((bf16[256,256]{1,0:T(8,128)(2,1)}, bf16[256,256]{1,0:T(8,128)(2,1)S(1)}, u32[]{:S(2)}, u32[]{:S(2)}) %collective-permute-start.12) | collective-permute-done | bytes 131104 | tf_op jit(solution)/shard_map/ppermute | solution.py:418
  108.3 0.0 collective-permute-done.10.first.level_far
  108.3 0.0 collective-permute-done.11.mid
  108.3 0.0 collective-permute-done.13.whole
  108.3 0.6 copy-done.13
  108.9 0.1 copy-done.1
  109.0 0.1 copy-done.12
  109.1 0.8 copy-done.5
  109.9 1.9 %assemble.1 = (bf16[1024,256]{1,0:T(8,128)(2,1)}, f32[1,256]{1,0:T(1,128)}) custom-call(bf16[288,256]{1,0:T(8,128)(2,1)} %copy-done.1, bf16[512,256]{1,0:T(8,128)(2,1)} %get-tuple-element.25.mid_mine, bf16[512,256]{1,0:T(8,128)(2,1)} %copy-done.12, bf16[256,256]{1,0:T(8,128)(2,1)} %copy-done.13, bf16[1056,256]{1,0:T(8,128)(2,1)} %copy-done.5, ...), custom_call_target="tpu_custom_call" | custom-call | tf_op jit(solution)/shard_map/assemble/pallas_call | solution.py:501
  (12 shorter events, 0.0 us)
Async XLA Ops:
  3.5 21.7 %collective-permute-start.4 = (bf16[1056,256]{1,0:T(8,128)(2,1)}, bf16[1056,256]{1,0:T(8,128)(2,1)S(1)}, u32[]{:S(2)}, u32[]{:S(2)}) collective-permute-start(bf16[1056,256]{1,0:T(8,128)(2,1)} %get-tuple-element.16.own), channel_id=1, source_target_pairs={{1,0},{3,2},{5,4},{7,6},{9,8},{11,10},{13,12},{15,14},{18,17},{20,... | collective-permute-start | bytes 1622024 | tf_op jit(solution)/shard_map/ppermute | solution.py:418
  5.5 19.7 %collective-permute-start.2 = (bf16[1056,256]{1,0:T(8,128)(2,1)}, bf16[1056,256]{1,0:T(8,128)(2,1)S(1)}, u32[]{:S(2)}, u32[]{:S(2)}) collective-permute-start(bf16[1056,256]{1,0:T(8,128)(2,1)} %get-tuple-element.16.own), channel_id=1, source_target_pairs={{17,0},{19,2},{21,4},{23,6},{25,8},{27,10},{29,12},{31,14},{1,17},... | collective-permute-start | bytes 1622024 | tf_op jit(solution)/shard_map/ppermute | solution.py:418
  8.8 7.5 %collective-permute-start.1 = (bf16[800,256]{1,0:T(8,128)(2,1)}, bf16[800,256]{1,0:T(8,128)(2,1)S(1)}, u32[]{:S(2)}, u32[]{:S(2)}) collective-permute-start(bf16[800,256]{1,0:T(8,128)(2,1)} %get-tuple-element.18), channel_id=1, source_target_pairs={{18,0},{20,2},{22,4},{24,6},{26,8},{28,10},{30,12},{16,14},{2,17},... | collective-permute-start | bytes 1228808 | tf_op jit(solution)/shard_map/ppermute | solution.py:418
  9.5 6.8 %collective-permute-start.3 = (bf16[800,256]{1,0:T(8,128)(2,1)}, bf16[800,256]{1,0:T(8,128)(2,1)S(1)}, u32[]{:S(2)}, u32[]{:S(2)}) collective-permute-start(bf16[800,256]{1,0:T(8,128)(2,1)} %get-tuple-element.17), channel_id=1, source_target_pairs={{16,0},{18,2},{20,4},{22,6},{24,8},{26,10},{28,12},{30,14},{0,17},... | collective-permute-start | bytes 1228808 | tf_op jit(solution)/shard_map/ppermute | solution.py:418
  10.2 15.0 %collective-permute-start = (bf16[800,256]{1,0:T(8,128)(2,1)}, bf16[800,256]{1,0:T(8,128)(2,1)S(1)}, u32[]{:S(2)}, u32[]{:S(2)}) collective-permute-start(bf16[800,256]{1,0:T(8,128)(2,1)} %get-tuple-element.17), channel_id=1, source_target_pairs={{15,0},{1,2},{3,4},{5,6},{7,8},{9,10},{11,12},{13,14},{19,17},{21,... | collective-permute-start | bytes 1228808 | tf_op jit(solution)/shard_map/ppermute | solution.py:418
  16.2 8.9 %copy-start.8 = (bf16[800,256]{1,0:T(8,128)(2,1)}, bf16[800,256]{1,0:T(8,128)(2,1)S(1)}, u32[]{:S(2)}) copy-start(bf16[800,256]{1,0:T(8,128)(2,1)S(1)} %collective-permute-done.1.cross) | copy-start | bytes 1228804
  16.3 8.9 %copy-start.9 = (bf16[800,256]{1,0:T(8,128)(2,1)}, bf16[800,256]{1,0:T(8,128)(2,1)S(1)}, u32[]{:S(2)}) copy-start(bf16[800,256]{1,0:T(8,128)(2,1)S(1)} %collective-permute-done.3.mirror_even) | copy-start | bytes 1228804
  25.2 0.7 copy-start.10
  25.2 0.9 copy-start.3
  26.1 0.8 copy-start.4
  28.6 43.6 %collective-permute-start.5 = (bf16[1632,256]{1,0:T(8,128)(2,1)}, bf16[1632,256]{1,0:T(8,128)(2,1)S(1)}, u32[]{:S(2)}, u32[]{:S(2)}) collective-permute-start(bf16[1632,256]{1,0:T(8,128)(2,1)} %get-tuple-element.19), channel_id=1, source_target_pairs={{0,1},{2,3},{4,5},{6,7},{8,9},{10,11},{12,13},{14,15},{17,16},{19,... | collective-permute-start | bytes 2506760 | tf_op jit(solution)/shard_map/ppermute | solution.py:418
  29.9 42.3 %collective-permute-start.6 = (bf16[1056,256]{1,0:T(8,128)(2,1)}, bf16[1056,256]{1,0:T(8,128)(2,1)S(1)}, u32[]{:S(2)}, u32[]{:S(2)}) collective-permute-start(bf16[1056,256]{1,0:T(8,128)(2,1)} %get-tuple-element.20.level_mine), channel_id=1, source_target_pairs={{31,1},{17,3},{19,5},{21,7},{23,9},{25,11},{27,13},{29,15},{0,16},... | collective-permute-start | bytes 1622024 | tf_op jit(solution)/shard_map/ppermute | solution.py:418
  31.2 41.0 %collective-permute-start.8 = (bf16[1024,256]{1,0:T(8,128)(2,1)}, bf16[1024,256]{1,0:T(8,128)(2,1)S(1)}, u32[]{:S(2)}, u32[]{:S(2)}) collective-permute-start(bf16[1024,256]{1,0:T(8,128)(2,1)} %get-tuple-element.22), channel_id=1, source_target_pairs={{17,1},{19,3},{21,5},{23,7},{25,9},{27,11},{29,13},{31,15},{2,16},... | collective-permute-start | bytes 1572872 | tf_op jit(solution)/shard_map/ppermute | solution.py:418
  32.5 39.7 %collective-permute-start.7 = (bf16[800,256]{1,0:T(8,128)(2,1)}, bf16[800,256]{1,0:T(8,128)(2,1)S(1)}, u32[]{:S(2)}, u32[]{:S(2)}) collective-permute-start(bf16[800,256]{1,0:T(8,128)(2,1)} %get-tuple-element.21), channel_id=1, source_target_pairs={{14,1},{0,3},{2,5},{4,7},{6,9},{8,11},{10,13},{12,15},{31,16},{17,... | collective-permute-start | bytes 1228808 | tf_op jit(solution)/shard_map/ppermute | solution.py:418
  33.8 38.4 %collective-permute-start.9 = (bf16[768,256]{1,0:T(8,128)(2,1)}, bf16[768,256]{1,0:T(8,128)(2,1)S(1)}, u32[]{:S(2)}, u32[]{:S(2)}) collective-permute-start(bf16[768,256]{1,0:T(8,128)(2,1)} %get-tuple-element.23), channel_id=1, source_target_pairs={{2,1},{4,3},{6,5},{8,7},{10,9},{12,11},{14,13},{0,15},{19,16},{21,... | collective-permute-start | bytes 1179656 | tf_op jit(solution)/shard_map/ppermute | solution.py:418
  72.1 0.7 copy-start.11
  72.1 0.9 copy-start.7
  72.1 1.0 copy-start.6
  72.2 1.2 %copy-start.2 = (bf16[1056,256]{1,0:T(8,128)(2,1)}, bf16[1056,256]{1,0:T(8,128)(2,1)S(1)}, u32[]{:S(2)}) copy-start(bf16[1056,256]{1,0:T(8,128)(2,1)S(1)} %collective-permute-done.6.iso_1) | copy-start | bytes 1622020
  73.4 0.9 copy-start
  93.8 14.5 %collective-permute-start.13 = (bf16[1056,256]{1,0:T(8,128)(2,1)}, bf16[1056,256]{1,0:T(8,128)(2,1)S(1)}, u32[]{:S(2)}, u32[]{:S(2)}) collective-permute-start(bf16[1056,256]{1,0:T(8,128)(2,1)} %get-tuple-element.27), channel_id=1, source_target_pairs={{1,16},{16,17},{3,18},{18,19},{5,20},{20,21},{7,22},{22,23},{9,24}... | collective-permute-start | bytes 1622024 | tf_op jit(solution)/shard_map/ppermute | solution.py:418
  95.6 12.7 %collective-permute-start.11 = (bf16[512,256]{1,0:T(8,128)(2,1)}, bf16[512,256]{1,0:T(8,128)(2,1)S(1)}, u32[]{:S(2)}, u32[]{:S(2)}) collective-permute-start(bf16[512,256]{1,0:T(8,128)(2,1)} %get-tuple-element.25.mid_mine), channel_id=1, source_target_pairs={{30,0},{16,2},{18,4},{20,6},{22,8},{24,10},{26,12},{28,14}} | collective-permute-start | bytes 786440 | tf_op jit(solution)/shard_map/ppermute | solution.py:418
  96.3 12.0 %collective-permute-start.10 = (bf16[288,256]{1,0:T(8,128)(2,1)}, bf16[288,256]{1,0:T(8,128)(2,1)S(1)}, u32[]{:S(2)}, u32[]{:S(2)}) collective-permute-start(bf16[288,256]{1,0:T(8,128)(2,1)} %get-tuple-element.24), channel_id=1, source_target_pairs={{1,0},{16,1},{3,2},{18,3},{5,4},{20,5},{7,6},{22,7},{9,8},{24,9},{... | collective-permute-start | bytes 442376 | tf_op jit(solution)/shard_map/ppermute | solution.py:418
  98.2 10.1 %collective-permute-start.12 = (bf16[256,256]{1,0:T(8,128)(2,1)}, bf16[256,256]{1,0:T(8,128)(2,1)S(1)}, u32[]{:S(2)}, u32[]{:S(2)}) collective-permute-start(bf16[256,256]{1,0:T(8,128)(2,1)} %get-tuple-element.26), channel_id=1, source_target_pairs={{15,0},{30,1},{1,2},{16,3},{3,4},{18,5},{5,6},{20,7},{7,8},{22,9},... | collective-permute-start | bytes 393224 | tf_op jit(solution)/shard_map/ppermute | solution.py:418
  108.3 0.6 copy-start.13
  108.3 0.7 copy-start.1
  108.3 0.8 copy-start.12
  109.1 0.8 copy-start.5

commit v3 on v2

--- a/solution.py
+++ b/solution.py
@@ -12,7 +12,7 @@
 CHARGE = (0, 1, 1, 2)
 AXES = ("loop", "inner")
 BF16, F32 = jnp.bfloat16, jnp.float32
-VMEM_BYTES = 60 << 20
+VMEM_BYTES = 64 << 20
 HIGHEST = lax.Precision.HIGHEST
 
 
@@ -69,33 +69,74 @@
 
 
 def factor_rows(work, size, panel=32):
-    rowid = lax.broadcasted_iota(jnp.int32, (panel, 128), 0)
+    tiles = panel // 8
+    sub = lax.broadcasted_iota(jnp.int32, (8, 128), 0)
     for start in range(0, size, panel):
         low = start < size // 2
         chunks = [0, 1, 2] if low else [1, 2, 3]
-        rows = [work[start : start + panel, 128 * c : 128 * c + 128] for c in chunks]
-        pivots = jnp.ones((panel, 128), F32)
-        for group in range(panel // 8):
-            base = start % 128 + 8 * group
-            cols = [
-                jnp.broadcast_to(rows[0][:, base + k : base + k + 1], (panel, 128))
-                for k in range(8)
-            ]
-            for j in range(8):
-                at = 8 * group + j
-                pivot = cols[j][at : at + 1, :]
-                factor = jnp.where(rowid > at, cols[j], 0.0) * (1.0 / pivot)
-                for k in range(j + 1, 8):
-                    cols[k] = cols[k] - factor * cols[k][at : at + 1, :]
-                rows = [x - factor * x[at : at + 1, :] for x in rows]
-                pivots = jnp.where(rowid == at, pivot, pivots)
-        scale = lax.rsqrt(pivots)
-        rows = [x * scale for x in rows]
-        for c, x in zip(chunks, rows):
-            work[start : start + panel, 128 * c : 128 * c + 128] = x
+        base = start % 128
+        rows = [
+            [work[start + 8 * t : start + 8 * t + 8, 128 * c : 128 * c + 128] for c in chunks]
+            for t in range(tiles)
+        ]
+
+        def column(k):
+            return {
+                t: jnp.broadcast_to(rows[t][0][:, base + k : base + k + 1], (8, 128))
+                for t in range(k // 8, tiles)
+            }
+
+        def at(col, k):
+            return jnp.broadcast_to(col[k // 8][k % 8 : k % 8 + 1, :], (8, 128))
+
+        pivots = [jnp.ones((8, 128), F32) for _ in range(tiles)]
+        cols = {k: column(k) for k in range(8)}
+        for g in range(tiles):
+            if g + 1 < tiles:
+                cols.update({k: column(k) for k in range(8 * g + 8, 8 * g + 16)})
+
+            def below(col, j):
+                return {
+                    t: (jnp.where(sub > j % 8, v, 0.0) if t == j // 8 else v)
+                    for t, v in col.items()
+                    if t >= g
+                }
+
+            for j in range(8 * g, 8 * g + 8, 2):
+                one, two = cols[j], cols[j + 1]
+                a, b, c = at(one, j), at(one, j + 1), at(two, j + 1)
+                det = a * c - b * b
+                ra, rd = 1.0 / a, 1.0 / det
+                first = {t: v * ra for t, v in below(one, j).items()}
+                ratio = b * ra
+                two = {t: two[t] - one[t] * ratio for t in one if t >= g}
+                second = {t: v * (a * rd) for t, v in below(two, j + 1).items()}
+                for k in cols:
+                    if k > j + 1:
+                        e1, e2 = at(one, k), at(two, k)
+                        cols[k] = {
+                            t: v - (first[t] * e1 + second[t] * e2) for t, v in cols[k].items()
+                        }
+                for i in range(len(chunks)):
+                    r = j % 8
+                    x0 = jnp.broadcast_to(rows[g][i][r : r + 1, :], (8, 128))
+                    x1 = jnp.broadcast_to(rows[g][i][r + 1 : r + 2, :], (8, 128)) - ratio * x0
+                    for t in range(g, tiles):
+                        rows[t][i] = rows[t][i] - (first[t] * x0 + second[t] * x1)
+                pivots[g] = jnp.where(
+                    sub == j % 8, a, jnp.where(sub == j % 8 + 1, det * ra, pivots[g])
+                )
+        done = []
+        for t in range(tiles):
+            scale = lax.rsqrt(pivots[t])
+            done.append([x * scale for x in rows[t]])
+            for c, x in zip(chunks, done[t]):
+                work[start + 8 * t : start + 8 * t + 8, 128 * c : 128 * c + 128] = x
         after = start + panel
         if after < size:
-            h, m, l = split3(jnp.concatenate(rows, axis=1))
+            h, m, l = split3(
+                jnp.concatenate([jnp.concatenate(xs, axis=1) for xs in done], axis=0)
+            )
             right = jnp.concatenate([h, m, h, l, h, m], axis=0)
             left = jnp.concatenate([h, h, m, h, l, m], axis=0)
             first = 128 * chunks[0]
@@ -121,39 +162,48 @@
     return (h + m) + l
 
 
-def prepare(block_ref, weight_ref, gate_ref, kept_ref, full, three_a, three_b):
+def prepare(block_ref, weight_ref, gate_ref, kept_ref, full, three_a, three_b, rows, small, sems):
     x = lax.axis_index("loop") % 2
     c = lax.axis_index("inner") % 2
-    blocks = block_ref.shape[-1]
-    small = jnp.zeros((SMALL, blocks), F32)
+    blocks = rows.shape[-1]
+    load = pltpu.make_async_copy(block_ref, rows, sems.at[0])
+    load.start()
+    values = jnp.zeros((SMALL, blocks), F32)
     rowid = lax.broadcasted_iota(jnp.int32, (SMALL, blocks), 0)
     for n, part in enumerate(split3(weight_ref[...])):
-        small = jnp.where(rowid == W_ROW + n, part.astype(F32), small)
-    small = jnp.where(rowid == K_ROW, kept_ref[...].astype(F32), small).astype(BF16)
-    shift = jnp.where(jnp.logical_and(x == 1, c == 1), 1, 0)
-    for n in range(4):
-        full[n * blocks : (n + 1) * blocks, :] = block_ref[n]
-    for n in range(3):
-        three_a[n * blocks : (n + 1) * blocks, :] = block_ref[n + shift]
-        three_b[n * blocks : (n + 1) * blocks, :] = block_ref[n + 1]
-    for ref in (full, three_a, three_b):
-        base = ref.shape[0] - SMALL
-        ref[base : base + SMALL, :] = small
-        ref[base : base + 16, 0:16] = gate_ref[...].astype(BF16)
+        values = jnp.where(rowid == W_ROW + n, part.astype(F32), values)
+    small[...] = jnp.where(rowid == K_ROW, kept_ref[...].astype(F32), values).astype(BF16)
+    small[0:16, 0:16] = gate_ref[...].astype(BF16)
+    load.wait()
+    shift = pl.multiple_of(jnp.where(jnp.logical_and(x == 1, c == 1), blocks, 0), blocks)
+    copies = []
+    for n, (ref, at) in enumerate(((full, 0), (three_a, shift), (three_b, blocks))):
+        size = ref.shape[0] - SMALL
+        copies.append(
+            pltpu.make_async_copy(rows.at[pl.ds(at, size)], ref.at[pl.ds(0, size)], sems.at[1 + n])
+        )
+        copies.append(
+            pltpu.make_async_copy(small, ref.at[pl.ds(size, SMALL)], sems.at[4 + n])
+        )
+    for copy in copies:
+        copy.start()
+    for copy in copies:
+        copy.wait()
 
 
 def bond_body(
     a_ref, b_ref, below, here, above, kept, gate_rows, scaled, theta, matrix, proj, work, iso, left,
-    gate_stage, gates, sem
+    gate_stage, gates, sem, right_ready, iso_ready
 ):
     blocks = b_ref.shape[-1]
     gate_stage[...] = gate_rows.astype(F32)
     copy = pltpu.make_async_copy(gate_stage, gates, sem)
     copy.start()
-    copy.wait()
-    for first, count, w in ((0, 3, below), (3, 4, here), (7, 3, above)):
+    for first, count, w in ((3, 4, here), (0, 3, below), (7, 3, above)):
         rows = slice(first * blocks, (first + count) * blocks)
         scaled[rows, :] = (a_ref[rows, :].astype(F32) * w).astype(BF16)
+    basis = a_ref[3 * blocks : 7 * blocks, :].T
+    right_ready()
     for (distance, q), (right, first_row, count, first) in PIECES.items():
         product = dot(
             scaled[first_row * blocks : (first_row + count) * blocks, :],
@@ -164,6 +214,7 @@
         theta[slot * blocks : (slot + count) * blocks, :] = (
             product * (1.0 / math.sqrt(blocks))
         ).astype(BF16)
+    copy.wait()
 
     def gate(a, b, p, q):
         return gates[4 * a + b, 4 * p + q]
@@ -199,31 +250,42 @@
                         ] = value.astype(BF16)
                 held.clear()
 
-    basis = a_ref[3 * blocks : 7 * blocks, :]
-    projected = dot(basis, matrix[...], ((0,), (0,)))
+    projected = dot(basis, matrix[...], ((1,), (0,)))
     slot_id = lax.broadcasted_iota(jnp.int32, projected.shape, 0).astype(F32)
-    projected = jnp.where(slot_id < kept, projected, 0.0)
-    proj[...] = projected
+    h, m, l = split3(jnp.where(slot_id < kept, projected, 0.0))
+    for n, part in enumerate((h, m, l)):
+        proj[n * blocks : (n + 1) * blocks, :] = part
     ri = lax.broadcasted_iota(jnp.int32, (blocks, blocks), 0)
     ci = lax.broadcasted_iota(jnp.int32, (blocks, blocks), 1)
     eye = jnp.where(ri == ci, 1.0, 0.0).astype(F32)
-    work[:, :blocks] = dot(projected, projected, ((1,), (1,)), HIGHEST) + eye
+    outer = ((1,), (1,))
+    mixed = dot(h, m, outer) + dot(h, l, outer)
+    work[:, :blocks] = (dot(h, h, outer) + dot(m, m, outer)) + (mixed + mixed.T) + eye
     work[:, blocks:] = eye
     factor_rows(work, blocks)
-    ortho = dot(work[:, blocks:], proj[...], ((1,), (0,)), HIGHEST)
+    wh, wm, wl = split3(work[:, blocks:])
+    h, m, l = (proj[n * blocks : (n + 1) * blocks, :] for n in range(3))
+    inner = ((1,), (0,))
+    ortho = (
+        dot(jnp.concatenate([wh, wm, wl], axis=1), jnp.concatenate([h, h, h], axis=0), inner)
+        + dot(jnp.concatenate([wh, wm], axis=1), jnp.concatenate([m, m], axis=0), inner)
+        + dot(wh, l, inner)
+    )
     ortho = (ortho * math.sqrt(4 * blocks)).astype(BF16)
     for p in range(4):
         iso[p * blocks : (p + 1) * blocks, :] = ortho[:, p * blocks : (p + 1) * blocks]
-    carried = dot(matrix[...], ortho, ((1,), (1,))) * (1.0 / math.sqrt(4 * blocks))
+    iso_ready()
+    carried = dot(matrix[...], ortho, outer) * (1.0 / math.sqrt(4 * blocks))
     level = jnp.sqrt(jnp.mean(carried * carried, axis=0, keepdims=True) + 1e-06)
-    left[...] = (carried / level).astype(BF16)
+    left[...] = (carried * (1.0 / level)).astype(BF16)
     return level
 
 
 def first_kernel(
     own, edge, cross, mirror_odd, mirror_even, beside,
-    iso_msg, iso_three, left, left_three, local,
+    iso_msg, iso_three, left_msg, left_three, local,
     a_ref, b_ref, small, scaled, theta, matrix, proj, work, gate_stage, gates, sems, sem,
+    iso, left, pack,
 ):
     x = lax.axis_index("loop") % 2
     c = lax.axis_index("inner") % 2
@@ -239,8 +301,8 @@
         ],
     }
     smalls = {
-        0: [edge, own, beside, mirror_even, mirror_odd],
-        1: [mirror_even, mirror_odd, cross, own, beside],
+        0: [mirror_even, mirror_odd, edge, own, beside],
+        1: [own, beside, mirror_even, mirror_odd, cross],
     }
 
     def move(source, at, target, to, rows, n):
@@ -259,26 +321,46 @@
                 for n, source in enumerate(smalls[role]):
                     move(source, source.shape[0] - SMALL, small, n * SMALL, SMALL, 6 + n).start()
 
-        for n, (target, to, _, _, count) in enumerate(plans[0]):
-            move(own, 0, target, to * blocks, count * blocks, n).wait()
+        def arrived(chosen):
+            for n, (target, to, _, _, count) in enumerate(plans[0]):
+                if target is chosen:
+                    move(own, 0, target, to * blocks, count * blocks, n).wait()
+
+        copies = []
+
+        def out(source, at, target, to, count, rest=0):
+            rows = count * blocks + rest
+            copies.append(move(source, at * blocks, target, to * blocks, rows, 11 + len(copies)))
+            copies[-1].start()
+
+        def iso_ready():
+            out(iso, 0, iso_msg, 0, 4)
+            out(iso, 1, iso_three, 0, 3)
+            out(iso, 0, local, 0, 3)
+
         for n in range(5):
             move(own, 0, small, n * SMALL, SMALL, 6 + n).wait()
-        below, here, above = (get_split(small, n * SMALL + W_ROW) for n in range(3))
-        kept = small[SMALL + K_ROW : SMALL + K_ROW + 1, 0:1].astype(F32)
+        out(small, 0, local, 6, 0, 2 * SMALL)
+        below, here, above = (get_split(small, (2 + n) * SMALL + W_ROW) for n in range(3))
+        kept = small[3 * SMALL + K_ROW : 3 * SMALL + K_ROW + 1, 0:1].astype(F32)
+        arrived(a_ref)
         level = bond_body(
-            a_ref, b_ref, below, here, above, kept, small[SMALL : SMALL + 16, 0:128],
-            scaled, theta, matrix, proj, work, iso_msg, left, gate_stage, gates, sem,
-        )
-        iso_three[0 : 3 * blocks, :] = iso_msg[blocks : 4 * blocks, :]
-        left_three[...] = left[blocks : 4 * blocks, :]
-        local[0 : 3 * blocks, :] = iso_msg[0 : 3 * blocks, :]
-        local[3 * blocks : 6 * blocks, :] = left[0 : 3 * blocks, :]
-        local[6 * blocks : 6 * blocks + 2 * SMALL, :] = small[3 * SMALL : 5 * SMALL, :]
+            a_ref, b_ref, below, here, above, kept, small[3 * SMALL : 3 * SMALL + 16, 0:128],
+            scaled, theta, matrix, proj, work, iso, left, gate_stage, gates, sem,
+            lambda: arrived(b_ref), iso_ready,
+        )
+        out(left, 0, left_msg, 0, 4)
+        out(left, 1, left_three, 0, 3)
+        out(left, 0, local, 3, 3)
+        pack[...] = jnp.zeros((SMALL, blocks), BF16)
+        put_split(pack, 0, get_split(small, W_ROW))
+        put_split(pack, LEVEL_ROW, level)
         for ref in (iso_msg, iso_three, local):
             base = ref.shape[0] - SMALL
-            ref[base : base + SMALL, :] = jnp.zeros((SMALL, blocks), BF16)
-            put_split(ref, base, get_split(small, 3 * SMALL + W_ROW))
-            put_split(ref, base + LEVEL_ROW, level)
+            copies.append(move(pack, 0, ref, base, SMALL, 11 + len(copies)))
+            copies[-1].start()
+        for copy in copies:
+            copy.wait()
 
 
 def as_column(row):
@@ -317,14 +399,20 @@
         ]
         for copy in copies:
             copy.start()
-        for copy in copies:
-            copy.wait()
+
+        def arrived(right):
+            for copy, (_, _, target, _, _) in zip(copies, moves):
+                if (target is b_ref) == right:
+                    copy.wait()
+
+        arrived(False)
         below = get_split(small, 3 * SMALL)
         here, above = (get_split(small, n * SMALL + W_ROW) for n in range(2))
         kept = small[K_ROW : K_ROW + 1, 0:1].astype(F32)
         level = bond_body(
             a_ref, b_ref, below, here, above, kept, small[0:16, 0:128],
             scaled, theta, matrix, proj, work, iso, left, gate_stage, gates, sem,
+            lambda: arrived(True), lambda: None,
         )
         scales = [as_column(get_split(small, n * SMALL + LEVEL_ROW)) for n in range(2, 5)]
         column = as_column(level)
@@ -380,12 +468,14 @@
         pltpu.VMEM((10 * blocks, blocks), BF16),
         pltpu.VMEM((SLOT_COUNT * blocks, blocks), BF16),
         pltpu.VMEM((4 * blocks, 4 * blocks), BF16),
-        pltpu.VMEM((blocks, 4 * blocks), F32),
+        pltpu.VMEM((3 * blocks, 4 * blocks), BF16),
         pltpu.VMEM((blocks, 2 * blocks), F32),
         pltpu.VMEM((16, 128), F32),
         pltpu.SMEM((16, 128), F32),
-        pltpu.SemaphoreType.DMA((13,)),
+        pltpu.SemaphoreType.DMA((22,)),
         pltpu.SemaphoreType.DMA,
+        pltpu.VMEM((4 * blocks, blocks), BF16),
+        pltpu.VMEM((4 * blocks, blocks), BF16),
     ]
 
 
@@ -394,7 +484,7 @@
 
 
 def hbm():
-    return pl.BlockSpec(memory_space=pl.ANY)
+    return pl.BlockSpec(memory_space=pltpu.HBM)
 
 
 def params():
@@ -426,11 +516,16 @@
     full, three_a, three_b = pl.pallas_call(
         prepare,
         out_shape=(rows(4, SMALL), rows(3, SMALL), rows(3, SMALL)),
-        in_specs=[vmem()] * 4,
-        out_specs=(vmem(),) * 3,
+        in_specs=[hbm()] + [vmem()] * 3,
+        out_specs=(hbm(),) * 3,
+        scratch_shapes=[
+            pltpu.VMEM((4 * blocks, blocks), BF16),
+            pltpu.VMEM((SMALL, blocks), BF16),
+            pltpu.SemaphoreType.DMA((7,)),
+        ],
         compiler_params=params(),
         name="prepare",
-    )(site_blocks[0, 0], bond_weights[0], bond_gates[0], kept_slots)
+    )(site_blocks.reshape(4 * blocks, blocks), bond_weights[0], bond_gates[0], kept_slots)
 
     def pick(even, odd):
         return to_first(lambda l, k: (even if l % 2 == 0 else odd)(l, k))
@@ -445,12 +540,12 @@
     mirror_even = send(three_a, to_first(lambda l, k: (l ^ 1, 2 * k)))
     beside = send(full, pick(lambda l, k: (l, 2 * k + 1), lambda l, k: (l, 2 * k + 2)))
 
-    iso_msg, iso_three, left, left_three, local = pl.pallas_call(
+    iso_msg, iso_three, left_msg, left_three, local = pl.pallas_call(
         first_kernel,
         out_shape=(rows(4, SMALL), rows(3, SMALL), rows(4), rows(3), rows(6, 3 * SMALL)),
         in_specs=[hbm()] * 6,
-        out_specs=(vmem(),) * 5,
-        scratch_shapes=scratch(blocks),
+        out_specs=(hbm(),) * 5,
+        scratch_shapes=scratch(blocks) + [pltpu.VMEM((SMALL, blocks), BF16)],
         compiler_params=params(),
         name="first_bond",
     )(full, edge, cross, mirror_odd, mirror_even, beside)
@@ -462,20 +557,19 @@
     local_r = send(local, to_second(lambda l, k: worker(l, k, 0, 0)))
     iso_1 = send(iso_msg, to_second(lambda l, k: worker(l, k, 0, -1)))
     iso_2 = send(iso_three, to_second(lambda l, k: worker(l, k, 0, -2)))
-    left_1 = send(left, to_second(lambda l, k: worker(l, k, 1, 1)))
+    left_1 = send(left_msg, to_second(lambda l, k: worker(l, k, 1, 1)))
     left_2 = send(left_three, to_second(lambda l, k: worker(l, k, 1, 2)))
     if loops == 2:
         left_0 = local_r
     else:
-        left_0 = send(left[: 3 * blocks], to_second(lambda l, k: worker(l, k, 1, 0)))
+        left_0 = send(left_msg[: 3 * blocks], to_second(lambda l, k: worker(l, k, 1, 0)))
 
     mid, last, first, whole = pl.pallas_call(
         second_kernel,
         out_shape=(rows(2), rows(1), rows(1, SMALL), rows(4, SMALL)),
         in_specs=[hbm()] * 6,
         out_specs=(vmem(),) * 4,
-        scratch_shapes=scratch(blocks)
-        + [pltpu.VMEM((4 * blocks, blocks), BF16), pltpu.VMEM((4 * blocks, blocks), BF16)],
+        scratch_shapes=scratch(blocks),
         compiler_params=params(),
         name="second_bond",
     )(local_r, iso_1, iso_2, left_0, left_1, left_2)

time: 112 us -> 106 us (0.946)
  local copies, waits for them, and re-layouts: 5.39 us -> 0 us
  starting transfers between devices: 25.5 us -> 29.4 us
  Pallas kernels: 25.3 us -> 21.5 us
  waiting for transfers between devices: 54.2 us -> 52.9 us
    unnamed x28 -> x0, local copies, waits for them, and re-layouts: 5.39 us -> none
    ppermute x14, starting transfers between devices: 25.5 us -> 29.4 us  [send(): return lax.ppermute(value, AXES, route)]
    pallas_call x1, Pallas kernels: 19.5 us -> 16.5 us  [per_device(): pl.pallas_call(second_kernel, out_shape=(rows(2), rows(1), rows(1, SMALL)...]
    pallas_call x1, Pallas kernels: 1.66 us -> 0.21 us  [per_device(): pl.pallas_call(first_kernel, out_shape=(rows(4, SMALL), rows(3, SMALL), r...]
    ppermute x14, waiting for transfers between devices: 54.2 us -> 52.9 us  [send(): return lax.ppermute(value, AXES, route)]
where the time goes in v3:
time: 106 us; the launch traced here: 105 us
  waiting for transfers between devices  52.9 us (50%)
  starting transfers between devices  29.4 us (28%)
  Pallas kernels  21.5 us (20%)
  between operations  1.54 us (1%)
    ppermute x14, waiting for transfers between devices, send(): return lax.ppermute(value, AXES, route)  52.9 us
    ppermute x14, starting transfers between devices, send(): return lax.ppermute(value, AXES, route)  29.4 us
    pallas_call x1, Pallas kernels, per_device(): pl.pallas_call(second_kernel, out_shape=(rows(2), rows(1), rows(1, SMALL)...  16.5 us
    pallas_call x1, Pallas kernels, per_device(): pl.pallas_call(prepare, out_shape=(rows(4, SMALL), rows(3, SMALL), rows(3...  2.89 us
  transfers between devices with their start and end apart: 14, of which 3 were waited for; matrix products, arithmetic and copies ran while one was open for 0% of the time, Pallas kernels for 0%

profile of v3, /device:TPU:1, one launch (start us, length us, event | category | flops | bytes accessed | tf_op | source)
XLA Modules:
  0.0 105.3 jit_solution(8654293094177811278)
XLA Ops:
  1.3 2.9 %prepare.1 = (bf16[1056,256]{1,0:T(8,128)(2,1)}, bf16[800,256]{1,0:T(8,128)(2,1)}, bf16[800,256]{1,0:T(8,128)(2,1)}) custom-call(bf16[1024,256]{1,0:T(8,128)(2,1)} %bitcast.5, f32[1,256]{1,0:T(1,128)} %bitcast.7, f32[16,16]{1,0:T(8,128)} %bitcast.6, s32[1,1]{1,0:T(1,128)S(6)} %copy.6.kept_ref), custom_call_target="tpu_custom_call" | custom-call | tf_op jit(solution)/shard_map/prepare/pallas_call | solution.py:516
  4.2 2.8 %collective-permute-start.4 = (bf16[1056,256]{1,0:T(8,128)(2,1)}, bf16[1056,256]{1,0:T(8,128)(2,1)}, u32[]{:S(2)}, u32[]{:S(2)}) collective-permute-start(bf16[1056,256]{1,0:T(8,128)(2,1)} %get-tuple-element.16.own), channel_id=1, source_target_pairs={{1,0},{3,2},{5,4},{7,6},{9,8},{11,10},{13,12},{15,14},{18,17},{20,... | collective-permute-start | bytes 1622024 | tf_op jit(solution)/shard_map/ppermute | solution.py:508
  6.9 3.3 %collective-permute-start.2 = (bf16[1056,256]{1,0:T(8,128)(2,1)}, bf16[1056,256]{1,0:T(8,128)(2,1)}, u32[]{:S(2)}, u32[]{:S(2)}) collective-permute-start(bf16[1056,256]{1,0:T(8,128)(2,1)} %get-tuple-element.16.own), channel_id=1, source_target_pairs={{17,0},{19,2},{21,4},{23,6},{25,8},{27,10},{29,12},{31,14},{1,17},... | collective-permute-start | bytes 1622024 | tf_op jit(solution)/shard_map/ppermute | solution.py:508
  10.2 1.4 %collective-permute-start.1 = (bf16[800,256]{1,0:T(8,128)(2,1)}, bf16[800,256]{1,0:T(8,128)(2,1)}, u32[]{:S(2)}, u32[]{:S(2)}) collective-permute-start(bf16[800,256]{1,0:T(8,128)(2,1)} %get-tuple-element.18), channel_id=1, source_target_pairs={{18,0},{20,2},{22,4},{24,6},{26,8},{28,10},{30,12},{16,14},{2,17},... | collective-permute-start | bytes 1228808 | tf_op jit(solution)/shard_map/ppermute | solution.py:508
  11.6 1.4 %collective-permute-start.3 = (bf16[800,256]{1,0:T(8,128)(2,1)}, bf16[800,256]{1,0:T(8,128)(2,1)}, u32[]{:S(2)}, u32[]{:S(2)}) collective-permute-start(bf16[800,256]{1,0:T(8,128)(2,1)} %get-tuple-element.17), channel_id=1, source_target_pairs={{16,0},{18,2},{20,4},{22,6},{24,8},{26,10},{28,12},{30,14},{0,17},... | collective-permute-start | bytes 1228808 | tf_op jit(solution)/shard_map/ppermute | solution.py:508
  13.1 4.6 %collective-permute-start = (bf16[800,256]{1,0:T(8,128)(2,1)}, bf16[800,256]{1,0:T(8,128)(2,1)}, u32[]{:S(2)}, u32[]{:S(2)}) collective-permute-start(bf16[800,256]{1,0:T(8,128)(2,1)} %get-tuple-element.17), channel_id=1, source_target_pairs={{15,0},{1,2},{3,4},{5,6},{7,8},{9,10},{11,12},{13,14},{19,17},{21,... | collective-permute-start | bytes 1228808 | tf_op jit(solution)/shard_map/ppermute | solution.py:508
  17.6 0.0 collective-permute-done.1.cross
  17.6 0.0 collective-permute-done.3.mirror_even
  17.6 8.2 %collective-permute-done.edge = bf16[800,256]{1,0:T(8,128)(2,1)} collective-permute-done((bf16[800,256]{1,0:T(8,128)(2,1)}, bf16[800,256]{1,0:T(8,128)(2,1)}, u32[]{:S(2)}, u32[]{:S(2)}) %collective-permute-start) | collective-permute-done | bytes 409632 | tf_op jit(solution)/shard_map/ppermute | solution.py:508
  25.9 0.0 collective-permute-done.4.beside
  25.9 0.0 collective-permute-done.2.mirror_odd
  25.9 0.2 first_bond.1
  26.1 1.3 %collective-permute-start.5 = (bf16[1632,256]{1,0:T(8,128)(2,1)}, bf16[1632,256]{1,0:T(8,128)(2,1)}, u32[]{:S(2)}, u32[]{:S(2)}) collective-permute-start(bf16[1632,256]{1,0:T(8,128)(2,1)} %get-tuple-element.19), channel_id=1, source_target_pairs={{0,1},{2,3},{4,5},{6,7},{8,9},{10,11},{12,13},{14,15},{17,16},{19,... | collective-permute-start | bytes 2506760 | tf_op jit(solution)/shard_map/ppermute | solution.py:508
  27.4 1.3 %collective-permute-start.6 = (bf16[1056,256]{1,0:T(8,128)(2,1)}, bf16[1056,256]{1,0:T(8,128)(2,1)}, u32[]{:S(2)}, u32[]{:S(2)}) collective-permute-start(bf16[1056,256]{1,0:T(8,128)(2,1)} %get-tuple-element.20.level_mine), channel_id=1, source_target_pairs={{31,1},{17,3},{19,5},{21,7},{23,9},{25,11},{27,13},{29,15},{0,16},... | collective-permute-start | bytes 1622024 | tf_op jit(solution)/shard_map/ppermute | solution.py:508
  28.7 1.3 %collective-permute-start.8 = (bf16[1024,256]{1,0:T(8,128)(2,1)}, bf16[1024,256]{1,0:T(8,128)(2,1)}, u32[]{:S(2)}, u32[]{:S(2)}) collective-permute-start(bf16[1024,256]{1,0:T(8,128)(2,1)} %get-tuple-element.22), channel_id=1, source_target_pairs={{17,1},{19,3},{21,5},{23,7},{25,9},{27,11},{29,13},{31,15},{2,16},... | collective-permute-start | bytes 1572872 | tf_op jit(solution)/shard_map/ppermute | solution.py:508
  30.0 1.3 %collective-permute-start.7 = (bf16[800,256]{1,0:T(8,128)(2,1)}, bf16[800,256]{1,0:T(8,128)(2,1)}, u32[]{:S(2)}, u32[]{:S(2)}) collective-permute-start(bf16[800,256]{1,0:T(8,128)(2,1)} %get-tuple-element.21), channel_id=1, source_target_pairs={{14,1},{0,3},{2,5},{4,7},{6,9},{8,11},{10,13},{12,15},{31,16},{17,... | collective-permute-start | bytes 1228808 | tf_op jit(solution)/shard_map/ppermute | solution.py:508
  31.3 1.3 %collective-permute-start.9 = (bf16[768,256]{1,0:T(8,128)(2,1)}, bf16[768,256]{1,0:T(8,128)(2,1)}, u32[]{:S(2)}, u32[]{:S(2)}) collective-permute-start(bf16[768,256]{1,0:T(8,128)(2,1)} %get-tuple-element.23), channel_id=1, source_target_pairs={{2,1},{4,3},{6,5},{8,7},{10,9},{12,11},{14,13},{0,15},{19,16},{21,... | collective-permute-start | bytes 1179656 | tf_op jit(solution)/shard_map/ppermute | solution.py:508
  32.6 36.4 %collective-permute-done.9.left_2 = bf16[768,256]{1,0:T(8,128)(2,1)} collective-permute-done((bf16[768,256]{1,0:T(8,128)(2,1)}, bf16[768,256]{1,0:T(8,128)(2,1)}, u32[]{:S(2)}, u32[]{:S(2)}) %collective-permute-start.9) | collective-permute-done | bytes 393248 | tf_op jit(solution)/shard_map/ppermute | solution.py:508
  68.9 0.0 collective-permute-done.7.iso_2
  68.9 0.0 collective-permute-done.8.left_1
  68.9 0.0 collective-permute-done.6.iso_1
  69.0 0.0 collective-permute-done.5.local.left_0
  69.0 16.5 %second_bond.1 = (bf16[512,256]{1,0:T(8,128)(2,1)}, bf16[256,256]{1,0:T(8,128)(2,1)}, bf16[288,256]{1,0:T(8,128)(2,1)}, bf16[1056,256]{1,0:T(8,128)(2,1)}) custom-call(bf16[1632,256]{1,0:T(8,128)(2,1)} %collective-permute-done.5.local.left_0, bf16[1056,256]{1,0:T(8,128)(2,1)} %collective-permute-done.6.iso_1, bf16[800,256]{1,0:T(8,128)(2,1)} %collective-permute-done.7.iso_2, ...), custom_call_target="tpu_custom_call" | custom-call | tf_op jit(solution)/shard_map/second_bond/pallas_call | solution.py:567
  85.5 4.3 %collective-permute-start.13 = (bf16[1056,256]{1,0:T(8,128)(2,1)}, bf16[1056,256]{1,0:T(8,128)(2,1)}, u32[]{:S(2)}, u32[]{:S(2)}) collective-permute-start(bf16[1056,256]{1,0:T(8,128)(2,1)} %get-tuple-element.27), channel_id=1, source_target_pairs={{1,16},{16,17},{3,18},{18,19},{5,20},{20,21},{7,22},{22,23},{9,24}... | collective-permute-start | bytes 1622024 | tf_op jit(solution)/shard_map/ppermute | solution.py:508
  89.8 1.3 %collective-permute-start.11 = (bf16[512,256]{1,0:T(8,128)(2,1)}, bf16[512,256]{1,0:T(8,128)(2,1)}, u32[]{:S(2)}, u32[]{:S(2)}) collective-permute-start(bf16[512,256]{1,0:T(8,128)(2,1)} %get-tuple-element.25.mid_mine), channel_id=1, source_target_pairs={{30,0},{16,2},{18,4},{20,6},{22,8},{24,10},{26,12},{28,14}} | collective-permute-start | bytes 786440 | tf_op jit(solution)/shard_map/ppermute | solution.py:508
  91.1 1.9 %collective-permute-start.10 = (bf16[288,256]{1,0:T(8,128)(2,1)}, bf16[288,256]{1,0:T(8,128)(2,1)}, u32[]{:S(2)}, u32[]{:S(2)}) collective-permute-start(bf16[288,256]{1,0:T(8,128)(2,1)} %get-tuple-element.24), channel_id=1, source_target_pairs={{1,0},{16,1},{3,2},{18,3},{5,4},{20,5},{7,6},{22,7},{9,8},{24,9},{... | collective-permute-start | bytes 442376 | tf_op jit(solution)/shard_map/ppermute | solution.py:508
  93.0 1.9 %collective-permute-start.12 = (bf16[256,256]{1,0:T(8,128)(2,1)}, bf16[256,256]{1,0:T(8,128)(2,1)}, u32[]{:S(2)}, u32[]{:S(2)}) collective-permute-start(bf16[256,256]{1,0:T(8,128)(2,1)} %get-tuple-element.26), channel_id=1, source_target_pairs={{15,0},{30,1},{1,2},{16,3},{3,4},{18,5},{5,6},{20,7},{7,8},{22,9},... | collective-permute-start | bytes 393224 | tf_op jit(solution)/shard_map/ppermute | solution.py:508
  95.0 8.3 %collective-permute-done.12.last = bf16[256,256]{1,0:T(8,128)(2,1)} collective-permute-done((bf16[256,256]{1,0:T(8,128)(2,1)}, bf16[256,256]{1,0:T(8,128)(2,1)}, u32[]{:S(2)}, u32[]{:S(2)}) %collective-permute-start.12) | collective-permute-done | bytes 131104 | tf_op jit(solution)/shard_map/ppermute | solution.py:508
  103.2 0.0 collective-permute-done.10.first.level_far
  103.2 0.0 collective-permute-done.11.mid
  103.2 0.0 collective-permute-done.13.whole
  103.2 1.9 %assemble.1 = (bf16[1024,256]{1,0:T(8,128)(2,1)}, f32[1,256]{1,0:T(1,128)}) custom-call(bf16[288,256]{1,0:T(8,128)(2,1)} %collective-permute-done.10.first.level_far, bf16[512,256]{1,0:T(8,128)(2,1)} %get-tuple-element.25.mid_mine, bf16[512,256]{1,0:T(8,128)(2,1)} %collective-permute-done.11.mid, bf16[256,256]{1,0:T(8,128)(2,1)} %collective-permute-done.12.last, ...), custom_call_target="tpu_custom_call" | custom-call | tf_op jit(solution)/shard_map/assemble/pallas_call | solution.py:595
Async XLA Ops:
  4.2 21.7 %collective-permute-start.4 = (bf16[1056,256]{1,0:T(8,128)(2,1)}, bf16[1056,256]{1,0:T(8,128)(2,1)}, u32[]{:S(2)}, u32[]{:S(2)}) collective-permute-start(bf16[1056,256]{1,0:T(8,128)(2,1)} %get-tuple-element.16.own), channel_id=1, source_target_pairs={{1,0},{3,2},{5,4},{7,6},{9,8},{11,10},{13,12},{15,14},{18,17},{20,... | collective-permute-start | bytes 1622024 | tf_op jit(solution)/shard_map/ppermute | solution.py:508
  6.9 18.9 %collective-permute-start.2 = (bf16[1056,256]{1,0:T(8,128)(2,1)}, bf16[1056,256]{1,0:T(8,128)(2,1)}, u32[]{:S(2)}, u32[]{:S(2)}) collective-permute-start(bf16[1056,256]{1,0:T(8,128)(2,1)} %get-tuple-element.16.own), channel_id=1, source_target_pairs={{17,0},{19,2},{21,4},{23,6},{25,8},{27,10},{29,12},{31,14},{1,17},... | collective-permute-start | bytes 1622024 | tf_op jit(solution)/shard_map/ppermute | solution.py:508
  10.2 7.4 %collective-permute-start.1 = (bf16[800,256]{1,0:T(8,128)(2,1)}, bf16[800,256]{1,0:T(8,128)(2,1)}, u32[]{:S(2)}, u32[]{:S(2)}) collective-permute-start(bf16[800,256]{1,0:T(8,128)(2,1)} %get-tuple-element.18), channel_id=1, source_target_pairs={{18,0},{20,2},{22,4},{24,6},{26,8},{28,10},{30,12},{16,14},{2,17},... | collective-permute-start | bytes 1228808 | tf_op jit(solution)/shard_map/ppermute | solution.py:508
  11.6 6.0 %collective-permute-start.3 = (bf16[800,256]{1,0:T(8,128)(2,1)}, bf16[800,256]{1,0:T(8,128)(2,1)}, u32[]{:S(2)}, u32[]{:S(2)}) collective-permute-start(bf16[800,256]{1,0:T(8,128)(2,1)} %get-tuple-element.17), channel_id=1, source_target_pairs={{16,0},{18,2},{20,4},{22,6},{24,8},{26,10},{28,12},{30,14},{0,17},... | collective-permute-start | bytes 1228808 | tf_op jit(solution)/shard_map/ppermute | solution.py:508
  13.1 12.8 %collective-permute-start = (bf16[800,256]{1,0:T(8,128)(2,1)}, bf16[800,256]{1,0:T(8,128)(2,1)}, u32[]{:S(2)}, u32[]{:S(2)}) collective-permute-start(bf16[800,256]{1,0:T(8,128)(2,1)} %get-tuple-element.17), channel_id=1, source_target_pairs={{15,0},{1,2},{3,4},{5,6},{7,8},{9,10},{11,12},{13,14},{19,17},{21,... | collective-permute-start | bytes 1228808 | tf_op jit(solution)/shard_map/ppermute | solution.py:508
  26.1 42.9 %collective-permute-start.5 = (bf16[1632,256]{1,0:T(8,128)(2,1)}, bf16[1632,256]{1,0:T(8,128)(2,1)}, u32[]{:S(2)}, u32[]{:S(2)}) collective-permute-start(bf16[1632,256]{1,0:T(8,128)(2,1)} %get-tuple-element.19), channel_id=1, source_target_pairs={{0,1},{2,3},{4,5},{6,7},{8,9},{10,11},{12,13},{14,15},{17,16},{19,... | collective-permute-start | bytes 2506760 | tf_op jit(solution)/shard_map/ppermute | solution.py:508
  27.4 41.6 %collective-permute-start.6 = (bf16[1056,256]{1,0:T(8,128)(2,1)}, bf16[1056,256]{1,0:T(8,128)(2,1)}, u32[]{:S(2)}, u32[]{:S(2)}) collective-permute-start(bf16[1056,256]{1,0:T(8,128)(2,1)} %get-tuple-element.20.level_mine), channel_id=1, source_target_pairs={{31,1},{17,3},{19,5},{21,7},{23,9},{25,11},{27,13},{29,15},{0,16},... | collective-permute-start | bytes 1622024 | tf_op jit(solution)/shard_map/ppermute | solution.py:508
  28.7 40.3 %collective-permute-start.8 = (bf16[1024,256]{1,0:T(8,128)(2,1)}, bf16[1024,256]{1,0:T(8,128)(2,1)}, u32[]{:S(2)}, u32[]{:S(2)}) collective-permute-start(bf16[1024,256]{1,0:T(8,128)(2,1)} %get-tuple-element.22), channel_id=1, source_target_pairs={{17,1},{19,3},{21,5},{23,7},{25,9},{27,11},{29,13},{31,15},{2,16},... | collective-permute-start | bytes 1572872 | tf_op jit(solution)/shard_map/ppermute | solution.py:508
  30.0 39.0 %collective-permute-start.7 = (bf16[800,256]{1,0:T(8,128)(2,1)}, bf16[800,256]{1,0:T(8,128)(2,1)}, u32[]{:S(2)}, u32[]{:S(2)}) collective-permute-start(bf16[800,256]{1,0:T(8,128)(2,1)} %get-tuple-element.21), channel_id=1, source_target_pairs={{14,1},{0,3},{2,5},{4,7},{6,9},{8,11},{10,13},{12,15},{31,16},{17,... | collective-permute-start | bytes 1228808 | tf_op jit(solution)/shard_map/ppermute | solution.py:508
  31.3 37.7 %collective-permute-start.9 = (bf16[768,256]{1,0:T(8,128)(2,1)}, bf16[768,256]{1,0:T(8,128)(2,1)}, u32[]{:S(2)}, u32[]{:S(2)}) collective-permute-start(bf16[768,256]{1,0:T(8,128)(2,1)} %get-tuple-element.23), channel_id=1, source_target_pairs={{2,1},{4,3},{6,5},{8,7},{10,9},{12,11},{14,13},{0,15},{19,16},{21,... | collective-permute-start | bytes 1179656 | tf_op jit(solution)/shard_map/ppermute | solution.py:508
  85.5 17.8 %collective-permute-start.13 = (bf16[1056,256]{1,0:T(8,128)(2,1)}, bf16[1056,256]{1,0:T(8,128)(2,1)}, u32[]{:S(2)}, u32[]{:S(2)}) collective-permute-start(bf16[1056,256]{1,0:T(8,128)(2,1)} %get-tuple-element.27), channel_id=1, source_target_pairs={{1,16},{16,17},{3,18},{18,19},{5,20},{20,21},{7,22},{22,23},{9,24}... | collective-permute-start | bytes 1622024 | tf_op jit(solution)/shard_map/ppermute | solution.py:508
  89.8 13.5 %collective-permute-start.11 = (bf16[512,256]{1,0:T(8,128)(2,1)}, bf16[512,256]{1,0:T(8,128)(2,1)}, u32[]{:S(2)}, u32[]{:S(2)}) collective-permute-start(bf16[512,256]{1,0:T(8,128)(2,1)} %get-tuple-element.25.mid_mine), channel_id=1, source_target_pairs={{30,0},{16,2},{18,4},{20,6},{22,8},{24,10},{26,12},{28,14}} | collective-permute-start | bytes 786440 | tf_op jit(solution)/shard_map/ppermute | solution.py:508
  91.1 12.1 %collective-permute-start.10 = (bf16[288,256]{1,0:T(8,128)(2,1)}, bf16[288,256]{1,0:T(8,128)(2,1)}, u32[]{:S(2)}, u32[]{:S(2)}) collective-permute-start(bf16[288,256]{1,0:T(8,128)(2,1)} %get-tuple-element.24), channel_id=1, source_target_pairs={{1,0},{16,1},{3,2},{18,3},{5,4},{20,5},{7,6},{22,7},{9,8},{24,9},{... | collective-permute-start | bytes 442376 | tf_op jit(solution)/shard_map/ppermute | solution.py:508
  93.0 10.2 %collective-permute-start.12 = (bf16[256,256]{1,0:T(8,128)(2,1)}, bf16[256,256]{1,0:T(8,128)(2,1)}, u32[]{:S(2)}, u32[]{:S(2)}) collective-permute-start(bf16[256,256]{1,0:T(8,128)(2,1)} %get-tuple-element.26), channel_id=1, source_target_pairs={{15,0},{30,1},{1,2},{16,3},{3,4},{18,5},{5,6},{20,7},{7,8},{22,9},... | collective-permute-start | bytes 393224 | tf_op jit(solution)/shard_map/ppermute | solution.py:508

commit v4 on v3

--- a/solution.py
+++ b/solution.py
@@ -12,7 +12,7 @@
 CHARGE = (0, 1, 1, 2)
 AXES = ("loop", "inner")
 BF16, F32 = jnp.bfloat16, jnp.float32
-VMEM_BYTES = 64 << 20
+VMEM_BYTES = 24 << 20
 HIGHEST = lax.Precision.HIGHEST
 
 
@@ -162,28 +162,24 @@
     return (h + m) + l
 
 
-def prepare(block_ref, weight_ref, gate_ref, kept_ref, full, three_a, three_b, rows, small, sems):
-    x = lax.axis_index("loop") % 2
-    c = lax.axis_index("inner") % 2
-    blocks = rows.shape[-1]
-    load = pltpu.make_async_copy(block_ref, rows, sems.at[0])
-    load.start()
+def prepare(block_ref, weight_ref, gate_ref, kept_ref, full, head, tail, small, sems):
+    blocks = block_ref.shape[-1]
     values = jnp.zeros((SMALL, blocks), F32)
     rowid = lax.broadcasted_iota(jnp.int32, (SMALL, blocks), 0)
     for n, part in enumerate(split3(weight_ref[...])):
         values = jnp.where(rowid == W_ROW + n, part.astype(F32), values)
     small[...] = jnp.where(rowid == K_ROW, kept_ref[...].astype(F32), values).astype(BF16)
     small[0:16, 0:16] = gate_ref[...].astype(BF16)
-    load.wait()
-    shift = pl.multiple_of(jnp.where(jnp.logical_and(x == 1, c == 1), blocks, 0), blocks)
     copies = []
-    for n, (ref, at) in enumerate(((full, 0), (three_a, shift), (three_b, blocks))):
+    for n, (ref, at) in enumerate(((full, 0), (tail, blocks), (head, 0))):
         size = ref.shape[0] - SMALL
         copies.append(
-            pltpu.make_async_copy(rows.at[pl.ds(at, size)], ref.at[pl.ds(0, size)], sems.at[1 + n])
+            pltpu.make_async_copy(
+                block_ref.at[pl.ds(at, size)], ref.at[pl.ds(0, size)], sems.at[n]
+            )
         )
         copies.append(
-            pltpu.make_async_copy(small, ref.at[pl.ds(size, SMALL)], sems.at[4 + n])
+            pltpu.make_async_copy(small, ref.at[pl.ds(size, SMALL)], sems.at[3 + n])
         )
     for copy in copies:
         copy.start()
@@ -282,7 +278,7 @@
 
 
 def first_kernel(
-    own, edge, cross, mirror_odd, mirror_even, beside,
+    own, here_full, next_full, next_tail, after_tail, here_head,
     iso_msg, iso_three, left_msg, left_three, local,
     a_ref, b_ref, small, scaled, theta, matrix, proj, work, gate_stage, gates, sems, sem,
     iso, left, pack,
@@ -292,17 +288,17 @@
     blocks = a_ref.shape[-1]
     plans = {
         0: [
-            (a_ref, 0, edge, 0, 3), (a_ref, 3, own, 0, 4), (a_ref, 7, beside, 1, 3),
-            (b_ref, 0, mirror_even, 0, 3), (b_ref, 3, mirror_odd, 0, 4), (b_ref, 7, cross, 0, 3),
+            (a_ref, 0, own, 0, 3), (a_ref, 3, here_full, 0, 4), (a_ref, 7, next_tail, 0, 3),
+            (b_ref, 0, here_head, 0, 3), (b_ref, 3, next_full, 0, 4), (b_ref, 7, after_tail, 0, 3),
         ],
         1: [
-            (a_ref, 0, mirror_even, 0, 3), (a_ref, 3, mirror_odd, 0, 4), (a_ref, 7, cross, 0, 3),
-            (b_ref, 0, own, 0, 3), (b_ref, 3, beside, 0, 4), (b_ref, 7, edge, 0, 3),
+            (a_ref, 0, next_full, 0, 3), (a_ref, 3, here_full, 0, 4), (a_ref, 7, after_tail, 0, 3),
+            (b_ref, 0, here_head, 0, 3), (b_ref, 3, own, 0, 4), (b_ref, 7, next_tail, 0, 3),
         ],
     }
     smalls = {
-        0: [mirror_even, mirror_odd, edge, own, beside],
-        1: [own, beside, mirror_even, mirror_odd, cross],
+        0: [here_head, next_full, own, here_full, next_tail],
+        1: [here_head, own, next_full, here_full, after_tail],
     }
 
     def move(source, at, target, to, rows, n):
@@ -430,15 +426,15 @@
 
 
 def final_kernel(
-    first, mid_mine, mid, last, whole, level_mine, level_far, out, weights, small, sems
+    first_mine, first, mid, last, whole_mine, whole, level_mine, level_far, out, weights, small, sems
 ):
     x = lax.axis_index("loop") % 2
     c = lax.axis_index("inner") % 2
     blocks = out.shape[-1]
     plans = {
-        (0, 0): [(first, 0, 1), (mid, 1, 2), (last, 3, 1), (level_mine, 0, 0)],
-        (0, 1): [(first, 0, 1), (mid_mine, 1, 2), (last, 3, 1), (level_far, 0, 0)],
-        (1, 0): [(whole, 0, 4), (whole, 0, 0)],
+        (0, 0): [(first, 0, 1), (mid, 1, 2), (last, 3, 1), (level_far, 0, 0)],
+        (0, 1): [(first_mine, 0, 1), (mid, 1, 2), (last, 3, 1), (level_mine, 0, 0)],
+        (1, 0): [(whole_mine, 0, 4), (whole_mine, 0, 0)],
         (1, 1): [(whole, 0, 4), (whole, 0, 0)],
     }
     for (role, core), plan in plans.items():
@@ -484,7 +480,7 @@
 
 
 def hbm():
-    return pl.BlockSpec(memory_space=pltpu.HBM)
+    return pl.BlockSpec(memory_space=pl.ANY)
 
 
 def params():
@@ -507,38 +503,31 @@
                     route.append(((sl % loops) * inners + si % inners, l * inners + i))
         return lax.ppermute(value, AXES, route)
 
-    def to_first(where):
-        return lambda l, i: where(l, i // 2) if i % 2 == l % 2 else None
+    def to_first(even, odd):
+        return lambda l, i: (even, odd)[l % 2](l, i // 2) if i % 2 == l % 2 else None
 
     def to_second(where):
         return lambda l, i: where(l, i // 2) if i % 2 != l % 2 else None
 
-    full, three_a, three_b = pl.pallas_call(
+    full, head, tail = pl.pallas_call(
         prepare,
         out_shape=(rows(4, SMALL), rows(3, SMALL), rows(3, SMALL)),
-        in_specs=[hbm()] + [vmem()] * 3,
+        in_specs=[vmem()] * 4,
         out_specs=(hbm(),) * 3,
-        scratch_shapes=[
-            pltpu.VMEM((4 * blocks, blocks), BF16),
-            pltpu.VMEM((SMALL, blocks), BF16),
-            pltpu.SemaphoreType.DMA((7,)),
-        ],
+        scratch_shapes=[pltpu.VMEM((SMALL, blocks), BF16), pltpu.SemaphoreType.DMA((6,))],
         compiler_params=params(),
         name="prepare",
     )(site_blocks.reshape(4 * blocks, blocks), bond_weights[0], bond_gates[0], kept_slots)
 
-    def pick(even, odd):
-        return to_first(lambda l, k: (even if l % 2 == 0 else odd)(l, k))
-
-    edge = send(
-        three_a, pick(lambda l, k: (l, 2 * k - 1), lambda l, k: (l, 2 * k + 3))
+    next_full = send(
+        full, to_first(lambda l, k: (l + 1, 2 * k + 2), lambda l, k: (l - 1, 2 * k - 1))
     )
-    cross = send(
-        three_b, pick(lambda l, k: (l + 1, 2 * k + 2), lambda l, k: (l - 1, 2 * k + 2))
+    here_full = send(full, to_first(lambda l, k: (l, 2 * k + 1), lambda l, k: (l - 1, 2 * k)))
+    next_tail = send(tail, to_first(lambda l, k: (l, 2 * k + 2), lambda l, k: (l, 2 * k + 2)))
+    after_tail = send(
+        tail, to_first(lambda l, k: (l + 1, 2 * k + 3), lambda l, k: (l - 1, 2 * k + 1))
     )
-    mirror_odd = send(full, to_first(lambda l, k: (l ^ 1, 2 * k + 1)))
-    mirror_even = send(three_a, to_first(lambda l, k: (l ^ 1, 2 * k)))
-    beside = send(full, pick(lambda l, k: (l, 2 * k + 1), lambda l, k: (l, 2 * k + 2)))
+    here_head = send(head, to_first(lambda l, k: (l + 1, 2 * k + 1), lambda l, k: (l, 2 * k)))
 
     iso_msg, iso_three, left_msg, left_three, local = pl.pallas_call(
         first_kernel,
@@ -548,11 +537,12 @@
         scratch_shapes=scratch(blocks) + [pltpu.VMEM((SMALL, blocks), BF16)],
         compiler_params=params(),
         name="first_bond",
-    )(full, edge, cross, mirror_odd, mirror_even, beside)
+    )(full, here_full, next_full, next_tail, after_tail, here_head)
 
     def worker(l, k, d, s):
-        sector = 2 * k + l % 2 + s
-        return (l - l % 2 + 2 * d + sector % 2, sector // 2 * 2 + sector % 2)
+        sector = 2 * k + 1 - l % 2 + s
+        site = 1 - sector % 2
+        return (l - l % 2 + 2 * d + site, sector // 2 * 2 + site)
 
     local_r = send(local, to_second(lambda l, k: worker(l, k, 0, 0)))
     iso_1 = send(iso_msg, to_second(lambda l, k: worker(l, k, 0, -1)))
@@ -576,31 +566,32 @@
 
     def from_second(l, i, d, s):
         sector = i - s
-        return (l - l % 2 - 2 * d + sector % 2, sector // 2 * 2 + 1 - sector % 2)
+        site = 1 - sector % 2
+        return (l - l % 2 - 2 * d + site, sector // 2 * 2 + 1 - site)
 
     def right_from(s, cores):
         return lambda l, i: from_second(l, i, 1, s) if l % 2 == 0 and i % 2 in cores else None
 
-    first_r = send(first, right_from(0, (0, 1)))
-    mid_r = send(mid, right_from(1, (0,) if loops == 2 else (0, 1)))
+    first_r = send(first, right_from(0, (0,) if loops == 2 else (0, 1)))
+    mid_r = send(mid, right_from(1, (0, 1)))
     last_r = send(last, right_from(2, (0, 1)))
-    whole_r = send(whole, lambda l, i: from_second(l, i, 0, 0) if l % 2 else None)
+    whole_r = send(whole, lambda l, i: from_second(l, i, 0, 0) if l % 2 and i % 2 else None)
     if loops == 2:
-        mid_mine, level_far = mid, first_r
+        first_mine, level_far = first, first_r
     else:
-        mid_mine = mid_r
+        first_mine = first_r
         level_far = send(
-            iso_msg[4 * blocks :], lambda l, i: (l + 1, i) if l % 2 == 0 and i % 2 else None
+            iso_msg[4 * blocks :], lambda l, i: (l + 1, i + 1) if l % 2 == 0 and i % 2 == 0 else None
         )
     sites, weights = pl.pallas_call(
         final_kernel,
         out_shape=(rows(4), jax.ShapeDtypeStruct((1, blocks), F32)),
-        in_specs=[hbm()] * 7,
+        in_specs=[hbm()] * 8,
         out_specs=(vmem(),) * 2,
         scratch_shapes=[pltpu.VMEM((SMALL, blocks), BF16), pltpu.SemaphoreType.DMA((4,))],
         compiler_params=params(),
         name="assemble",
-    )(first_r, mid_mine, mid_r, last_r, whole_r, iso_msg, level_far)
+    )(first_mine, first_r, mid_r, last_r, whole, whole_r, local_r, level_far)
     return sites.reshape(1, 1, 4, blocks, blocks), weights[None]
 
 

time: 106 us -> 96.5 us (0.910)
  starting transfers between devices: 29.4 us -> 23.8 us
  Pallas kernels: 21.5 us -> 17.2 us
  waiting for transfers between devices: 52.9 us -> 50.4 us
  local copies, waits for them, and re-layouts: 0 us -> 2.41 us
    ppermute x14, starting transfers between devices: 29.4 us -> 23.8 us  [send(): return lax.ppermute(value, AXES, route)]
    ppermute x14, waiting for transfers between devices: 52.9 us -> 50.4 us  [send(): return lax.ppermute(value, AXES, route)]
    unnamed x0 -> x6, local copies, waits for them, and re-layouts: none -> 2.41 us
    pallas_call x1, Pallas kernels: 2.89 us -> 0.61 us  [per_device(): pl.pallas_call(prepare, out_shape=(rows(4, SMALL), rows(3, SMALL), rows(3...]
    pallas_call x1, Pallas kernels: 16.5 us -> 15.1 us  [per_device(): pl.pallas_call(second_kernel, out_shape=(rows(2), rows(1), rows(1, SMALL)...]
where the time goes in v4:
time: 96.5 us; the launch traced here: 95.4 us
  waiting for transfers between devices  50.4 us (52%)
  starting transfers between devices  23.8 us (25%)
  Pallas kernels  17.2 us (18%)
  local copies, waits for them, and re-layouts  2.41 us (2%)
  between operations  1.61 us (2%)
    ppermute x14, waiting for transfers between devices, send(): return lax.ppermute(value, AXES, route)  50.4 us
    ppermute x14, starting transfers between devices, send(): return lax.ppermute(value, AXES, route)  23.8 us
    pallas_call x1, Pallas kernels, per_device(): pl.pallas_call(second_kernel, out_shape=(rows(2), rows(1), rows(1, SMALL)...  15.1 us
    unnamed x6, local copies, waits for them, and re-layouts  2.41 us
  transfers between devices with their start and end apart: 14, of which 3 were waited for; matrix products, arithmetic and copies ran while one was open for 0% of the time, Pallas kernels for 0%

profile of v4, /device:TPU:1, one launch (start us, length us, event | category | flops | bytes accessed | tf_op | source)
XLA Modules:
  0.0 95.4 jit_solution(16899037172417776339)
XLA Ops:
  1.3 0.0 copy-start.2
  1.3 0.7 copy-done.2
  2.0 0.0 copy-start
  2.0 1.0 %copy-done = bf16[1,1,4,256,256]{4,3,2,1,0:T(8,128)(2,1)S(1)} copy-done((bf16[1,1,4,256,256]{4,3,2,1,0:T(8,128)(2,1)S(1)}, bf16[1,1,4,256,256]{4,3,2,1,0:T(8,128)(2,1)}, u32[]{:S(2)}) %copy-start) | copy-done | bytes 524312
  3.0 0.0 copy-start.1
  3.0 0.7 copy-done.1
  3.7 0.6 prepare.1
  4.3 4.9 %collective-permute-start.1 = (bf16[1056,256]{1,0:T(8,128)(2,1)S(1)}, bf16[1056,256]{1,0:T(8,128)(2,1)S(1)}, u32[]{:S(2)}, u32[]{:S(2)}) collective-permute-start(bf16[1056,256]{1,0:T(8,128)(2,1)S(1)} %get-tuple-element.16.own), channel_id=1, source_target_pairs={{18,0},{20,2},{22,4},{24,6},{26,8},{28,10},{30,12},{16,14},{15,17}... | collective-permute-start | bytes 1622024 | tf_op jit(solution)/shard_map/ppermute | solution.py:504
  9.3 1.3 %collective-permute-start = (bf16[1056,256]{1,0:T(8,128)(2,1)S(1)}, bf16[1056,256]{1,0:T(8,128)(2,1)S(1)}, u32[]{:S(2)}, u32[]{:S(2)}) collective-permute-start(bf16[1056,256]{1,0:T(8,128)(2,1)S(1)} %get-tuple-element.16.own), channel_id=1, source_target_pairs={{1,0},{3,2},{5,4},{7,6},{9,8},{11,10},{13,12},{15,14},{0,17},{2,19... | collective-permute-start | bytes 1622024 | tf_op jit(solution)/shard_map/ppermute | solution.py:504
  10.6 0.7 collective-permute-start.4
  11.3 3.9 %collective-permute-start.3 = (bf16[800,256]{1,0:T(8,128)(2,1)S(1)}, bf16[800,256]{1,0:T(8,128)(2,1)S(1)}, u32[]{:S(2)}, u32[]{:S(2)}) collective-permute-start(bf16[800,256]{1,0:T(8,128)(2,1)S(1)} %get-tuple-element.17), channel_id=1, source_target_pairs={{19,0},{21,2},{23,4},{25,6},{27,8},{29,10},{31,12},{17,14},{1,17},... | collective-permute-start | bytes 1228808 | tf_op jit(solution)/shard_map/ppermute | solution.py:504
  15.2 0.7 collective-permute-start.2
  15.9 0.0 collective-permute-done.4.here_head
  15.9 9.8 %collective-permute-done.3.after_tail = bf16[800,256]{1,0:T(8,128)(2,1)S(1)} collective-permute-done((bf16[800,256]{1,0:T(8,128)(2,1)S(1)}, bf16[800,256]{1,0:T(8,128)(2,1)S(1)}, u32[]{:S(2)}, u32[]{:S(2)}) %collective-permute-start.3) | collective-permute-done | bytes 409632 | tf_op jit(solution)/shard_map/ppermute | solution.py:504
  25.7 0.0 collective-permute-done.2.next_tail
  25.7 0.0 collective-permute-done.1.next_full
  25.7 0.0 collective-permute-done.here_full
  25.7 0.2 first_bond.1
  25.9 1.3 %collective-permute-start.5 = (bf16[1632,256]{1,0:T(8,128)(2,1)S(1)}, bf16[1632,256]{1,0:T(8,128)(2,1)S(1)}, u32[]{:S(2)}, u32[]{:S(2)}) collective-permute-start(bf16[1632,256]{1,0:T(8,128)(2,1)S(1)} %get-tuple-element.19), channel_id=1, source_target_pairs={{0,1},{2,3},{4,5},{6,7},{8,9},{10,11},{12,13},{14,15},{17,16},{19,... | collective-permute-start | bytes 2506760 | tf_op jit(solution)/shard_map/ppermute | solution.py:504
  27.2 1.3 %collective-permute-start.6 = (bf16[1056,256]{1,0:T(8,128)(2,1)S(1)}, bf16[1056,256]{1,0:T(8,128)(2,1)S(1)}, u32[]{:S(2)}, u32[]{:S(2)}) collective-permute-start(bf16[1056,256]{1,0:T(8,128)(2,1)S(1)} %get-tuple-element.20), channel_id=1, source_target_pairs={{17,1},{19,3},{21,5},{23,7},{25,9},{27,11},{29,13},{31,15},{14,16}... | collective-permute-start | bytes 1622024 | tf_op jit(solution)/shard_map/ppermute | solution.py:504
  28.5 1.3 %collective-permute-start.8 = (bf16[1024,256]{1,0:T(8,128)(2,1)S(1)}, bf16[1024,256]{1,0:T(8,128)(2,1)S(1)}, u32[]{:S(2)}, u32[]{:S(2)}) collective-permute-start(bf16[1024,256]{1,0:T(8,128)(2,1)S(1)} %get-tuple-element.22), channel_id=1, source_target_pairs={{19,1},{21,3},{23,5},{25,7},{27,9},{29,11},{31,13},{17,15},{0,16},... | collective-permute-start | bytes 1572872 | tf_op jit(solution)/shard_map/ppermute | solution.py:504
  29.8 1.3 %collective-permute-start.7 = (bf16[800,256]{1,0:T(8,128)(2,1)S(1)}, bf16[800,256]{1,0:T(8,128)(2,1)S(1)}, u32[]{:S(2)}, u32[]{:S(2)}) collective-permute-start(bf16[800,256]{1,0:T(8,128)(2,1)S(1)} %get-tuple-element.21), channel_id=1, source_target_pairs={{14,1},{0,3},{2,5},{4,7},{6,9},{8,11},{10,13},{12,15},{31,16},{17,... | collective-permute-start | bytes 1228808 | tf_op jit(solution)/shard_map/ppermute | solution.py:504
  31.1 1.3 %collective-permute-start.9 = (bf16[768,256]{1,0:T(8,128)(2,1)S(1)}, bf16[768,256]{1,0:T(8,128)(2,1)S(1)}, u32[]{:S(2)}, u32[]{:S(2)}) collective-permute-start(bf16[768,256]{1,0:T(8,128)(2,1)S(1)} %get-tuple-element.23), channel_id=1, source_target_pairs={{2,1},{4,3},{6,5},{8,7},{10,9},{12,11},{14,13},{0,15},{19,16},{21,... | collective-permute-start | bytes 1179656 | tf_op jit(solution)/shard_map/ppermute | solution.py:504
  32.4 34.0 %collective-permute-done.9.left_2 = bf16[768,256]{1,0:T(8,128)(2,1)S(1)} collective-permute-done((bf16[768,256]{1,0:T(8,128)(2,1)S(1)}, bf16[768,256]{1,0:T(8,128)(2,1)S(1)}, u32[]{:S(2)}, u32[]{:S(2)}) %collective-permute-start.9) | collective-permute-done | bytes 393248 | tf_op jit(solution)/shard_map/ppermute | solution.py:504
  66.5 0.0 collective-permute-done.7.iso_2
  66.5 0.0 collective-permute-done.8.left_1
  66.5 0.0 collective-permute-done.6.iso_1
  66.5 0.0 collective-permute-done.5.local.left_0.level_mine
  66.5 15.1 %second_bond.1 = (bf16[512,256]{1,0:T(8,128)(2,1)S(1)}, bf16[256,256]{1,0:T(8,128)(2,1)S(1)}, bf16[288,256]{1,0:T(8,128)(2,1)S(1)}, bf16[1056,256]{1,0:T(8,128)(2,1)S(1)}) custom-call(bf16[1632,256]{1,0:T(8,128)(2,1)S(1)} %collective-permute-done.5.local.left_0.level_mine, bf16[1056,256]{1,0:T(8,128)(2,1)S(1)} %collective-permute-done.6.iso_1, ...), custom_call_target="tpu_custom_call" | custom-call | tf_op jit(solution)/shard_map/second_bond/pallas_call | solution.py:557
  81.6 1.3 %collective-permute-start.13 = (bf16[1056,256]{1,0:T(8,128)(2,1)S(1)}, bf16[1056,256]{1,0:T(8,128)(2,1)S(1)}, u32[]{:S(2)}, u32[]{:S(2)}) collective-permute-start(bf16[1056,256]{1,0:T(8,128)(2,1)S(1)} %get-tuple-element.27.whole_mine), channel_id=1, source_target_pairs={{1,17},{3,19},{5,21},{7,23},{9,25},{11,27},{13,29},{15,31}} | collective-permute-start | bytes 1622024 | tf_op jit(solution)/shard_map/ppermute | solution.py:504
  83.0 1.9 %collective-permute-start.11 = (bf16[512,256]{1,0:T(8,128)(2,1)S(1)}, bf16[512,256]{1,0:T(8,128)(2,1)S(1)}, u32[]{:S(2)}, u32[]{:S(2)}) collective-permute-start(bf16[512,256]{1,0:T(8,128)(2,1)S(1)} %get-tuple-element.25), channel_id=1, source_target_pairs={{15,0},{16,1},{1,2},{18,3},{3,4},{20,5},{5,6},{22,7},{7,8},{24,9},... | collective-permute-start | bytes 786440 | tf_op jit(solution)/shard_map/ppermute | solution.py:504
  84.9 0.7 collective-permute-start.10
  85.6 1.9 %collective-permute-start.12 = (bf16[256,256]{1,0:T(8,128)(2,1)S(1)}, bf16[256,256]{1,0:T(8,128)(2,1)S(1)}, u32[]{:S(2)}, u32[]{:S(2)}) collective-permute-start(bf16[256,256]{1,0:T(8,128)(2,1)S(1)} %get-tuple-element.26), channel_id=1, source_target_pairs={{30,0},{15,1},{16,2},{1,3},{18,4},{3,5},{20,6},{5,7},{22,8},{7,9},... | collective-permute-start | bytes 393224 | tf_op jit(solution)/shard_map/ppermute | solution.py:504
  87.5 6.5 %collective-permute-done.12.last = bf16[256,256]{1,0:T(8,128)(2,1)S(1)} collective-permute-done((bf16[256,256]{1,0:T(8,128)(2,1)S(1)}, bf16[256,256]{1,0:T(8,128)(2,1)S(1)}, u32[]{:S(2)}, u32[]{:S(2)}) %collective-permute-start.12) | collective-permute-done | bytes 131104 | tf_op jit(solution)/shard_map/ppermute | solution.py:504
  94.0 0.0 collective-permute-done.10.first.level_far
  94.0 0.0 collective-permute-done.11.mid
  94.0 0.0 collective-permute-done.13.whole
  94.0 1.2 %assemble.1 = (bf16[1024,256]{1,0:T(8,128)(2,1)}, f32[1,256]{1,0:T(1,128)}) custom-call(bf16[288,256]{1,0:T(8,128)(2,1)S(1)} %get-tuple-element.24.first_mine, bf16[288,256]{1,0:T(8,128)(2,1)S(1)} %collective-permute-done.10.first.level_far, bf16[512,256]{1,0:T(8,128)(2,1)S(1)} %collective-permute-done.11.mid, ...), custom_call_target="tpu_custom_call" | custom-call | tf_op jit(solution)/shard_map/assemble/pallas_call | solution.py:586
Async XLA Ops:
  1.3 0.7 copy-start.2
  2.0 1.0 %copy-start = (bf16[1,1,4,256,256]{4,3,2,1,0:T(8,128)(2,1)S(1)}, bf16[1,1,4,256,256]{4,3,2,1,0:T(8,128)(2,1)}, u32[]{:S(2)}) copy-start(bf16[1,1,4,256,256]{4,3,2,1,0:T(8,128)(2,1)} %param.4) | copy-start | bytes 1572868
  3.0 0.7 copy-start.1
  4.3 21.4 %collective-permute-start.1 = (bf16[1056,256]{1,0:T(8,128)(2,1)S(1)}, bf16[1056,256]{1,0:T(8,128)(2,1)S(1)}, u32[]{:S(2)}, u32[]{:S(2)}) collective-permute-start(bf16[1056,256]{1,0:T(8,128)(2,1)S(1)} %get-tuple-element.16.own), channel_id=1, source_target_pairs={{18,0},{20,2},{22,4},{24,6},{26,8},{28,10},{30,12},{16,14},{15,17}... | collective-permute-start | bytes 1622024 | tf_op jit(solution)/shard_map/ppermute | solution.py:504
  9.3 16.4 %collective-permute-start = (bf16[1056,256]{1,0:T(8,128)(2,1)S(1)}, bf16[1056,256]{1,0:T(8,128)(2,1)S(1)}, u32[]{:S(2)}, u32[]{:S(2)}) collective-permute-start(bf16[1056,256]{1,0:T(8,128)(2,1)S(1)} %get-tuple-element.16.own), channel_id=1, source_target_pairs={{1,0},{3,2},{5,4},{7,6},{9,8},{11,10},{13,12},{15,14},{0,17},{2,19... | collective-permute-start | bytes 1622024 | tf_op jit(solution)/shard_map/ppermute | solution.py:504
  10.6 5.3 %collective-permute-start.4 = (bf16[800,256]{1,0:T(8,128)(2,1)S(1)}, bf16[800,256]{1,0:T(8,128)(2,1)S(1)}, u32[]{:S(2)}, u32[]{:S(2)}) collective-permute-start(bf16[800,256]{1,0:T(8,128)(2,1)S(1)} %get-tuple-element.18), channel_id=1, source_target_pairs={{17,0},{19,2},{21,4},{23,6},{25,8},{27,10},{29,12},{31,14},{16,17}... | collective-permute-start | bytes 1228808 | tf_op jit(solution)/shard_map/ppermute | solution.py:504
  11.3 14.4 %collective-permute-start.3 = (bf16[800,256]{1,0:T(8,128)(2,1)S(1)}, bf16[800,256]{1,0:T(8,128)(2,1)S(1)}, u32[]{:S(2)}, u32[]{:S(2)}) collective-permute-start(bf16[800,256]{1,0:T(8,128)(2,1)S(1)} %get-tuple-element.17), channel_id=1, source_target_pairs={{19,0},{21,2},{23,4},{25,6},{27,8},{29,10},{31,12},{17,14},{1,17},... | collective-permute-start | bytes 1228808 | tf_op jit(solution)/shard_map/ppermute | solution.py:504
  15.2 10.5 %collective-permute-start.2 = (bf16[800,256]{1,0:T(8,128)(2,1)S(1)}, bf16[800,256]{1,0:T(8,128)(2,1)S(1)}, u32[]{:S(2)}, u32[]{:S(2)}) collective-permute-start(bf16[800,256]{1,0:T(8,128)(2,1)S(1)} %get-tuple-element.17), channel_id=1, source_target_pairs={{2,0},{4,2},{6,4},{8,6},{10,8},{12,10},{14,12},{0,14},{18,17},{20,... | collective-permute-start | bytes 1228808 | tf_op jit(solution)/shard_map/ppermute | solution.py:504
  25.9 40.6 %collective-permute-start.5 = (bf16[1632,256]{1,0:T(8,128)(2,1)S(1)}, bf16[1632,256]{1,0:T(8,128)(2,1)S(1)}, u32[]{:S(2)}, u32[]{:S(2)}) collective-permute-start(bf16[1632,256]{1,0:T(8,128)(2,1)S(1)} %get-tuple-element.19), channel_id=1, source_target_pairs={{0,1},{2,3},{4,5},{6,7},{8,9},{10,11},{12,13},{14,15},{17,16},{19,... | collective-permute-start | bytes 2506760 | tf_op jit(solution)/shard_map/ppermute | solution.py:504
  27.2 39.2 %collective-permute-start.6 = (bf16[1056,256]{1,0:T(8,128)(2,1)S(1)}, bf16[1056,256]{1,0:T(8,128)(2,1)S(1)}, u32[]{:S(2)}, u32[]{:S(2)}) collective-permute-start(bf16[1056,256]{1,0:T(8,128)(2,1)S(1)} %get-tuple-element.20), channel_id=1, source_target_pairs={{17,1},{19,3},{21,5},{23,7},{25,9},{27,11},{29,13},{31,15},{14,16}... | collective-permute-start | bytes 1622024 | tf_op jit(solution)/shard_map/ppermute | solution.py:504
  28.5 37.9 %collective-permute-start.8 = (bf16[1024,256]{1,0:T(8,128)(2,1)S(1)}, bf16[1024,256]{1,0:T(8,128)(2,1)S(1)}, u32[]{:S(2)}, u32[]{:S(2)}) collective-permute-start(bf16[1024,256]{1,0:T(8,128)(2,1)S(1)} %get-tuple-element.22), channel_id=1, source_target_pairs={{19,1},{21,3},{23,5},{25,7},{27,9},{29,11},{31,13},{17,15},{0,16},... | collective-permute-start | bytes 1572872 | tf_op jit(solution)/shard_map/ppermute | solution.py:504
  29.8 36.6 %collective-permute-start.7 = (bf16[800,256]{1,0:T(8,128)(2,1)S(1)}, bf16[800,256]{1,0:T(8,128)(2,1)S(1)}, u32[]{:S(2)}, u32[]{:S(2)}) collective-permute-start(bf16[800,256]{1,0:T(8,128)(2,1)S(1)} %get-tuple-element.21), channel_id=1, source_target_pairs={{14,1},{0,3},{2,5},{4,7},{6,9},{8,11},{10,13},{12,15},{31,16},{17,... | collective-permute-start | bytes 1228808 | tf_op jit(solution)/shard_map/ppermute | solution.py:504
  31.1 35.3 %collective-permute-start.9 = (bf16[768,256]{1,0:T(8,128)(2,1)S(1)}, bf16[768,256]{1,0:T(8,128)(2,1)S(1)}, u32[]{:S(2)}, u32[]{:S(2)}) collective-permute-start(bf16[768,256]{1,0:T(8,128)(2,1)S(1)} %get-tuple-element.23), channel_id=1, source_target_pairs={{2,1},{4,3},{6,5},{8,7},{10,9},{12,11},{14,13},{0,15},{19,16},{21,... | collective-permute-start | bytes 1179656 | tf_op jit(solution)/shard_map/ppermute | solution.py:504
  81.6 12.4 %collective-permute-start.13 = (bf16[1056,256]{1,0:T(8,128)(2,1)S(1)}, bf16[1056,256]{1,0:T(8,128)(2,1)S(1)}, u32[]{:S(2)}, u32[]{:S(2)}) collective-permute-start(bf16[1056,256]{1,0:T(8,128)(2,1)S(1)} %get-tuple-element.27.whole_mine), channel_id=1, source_target_pairs={{1,17},{3,19},{5,21},{7,23},{9,25},{11,27},{13,29},{15,31}} | collective-permute-start | bytes 1622024 | tf_op jit(solution)/shard_map/ppermute | solution.py:504
  83.0 11.0 %collective-permute-start.11 = (bf16[512,256]{1,0:T(8,128)(2,1)S(1)}, bf16[512,256]{1,0:T(8,128)(2,1)S(1)}, u32[]{:S(2)}, u32[]{:S(2)}) collective-permute-start(bf16[512,256]{1,0:T(8,128)(2,1)S(1)} %get-tuple-element.25), channel_id=1, source_target_pairs={{15,0},{16,1},{1,2},{18,3},{3,4},{20,5},{5,6},{22,7},{7,8},{24,9},... | collective-permute-start | bytes 786440 | tf_op jit(solution)/shard_map/ppermute | solution.py:504
  84.9 9.1 %collective-permute-start.10 = (bf16[288,256]{1,0:T(8,128)(2,1)S(1)}, bf16[288,256]{1,0:T(8,128)(2,1)S(1)}, u32[]{:S(2)}, u32[]{:S(2)}) collective-permute-start(bf16[288,256]{1,0:T(8,128)(2,1)S(1)} %get-tuple-element.24.first_mine), channel_id=1, source_target_pairs={{16,0},{18,2},{20,4},{22,6},{24,8},{26,10},{28,12},{30,14}} | collective-permute-start | bytes 442376 | tf_op jit(solution)/shard_map/ppermute | solution.py:504
  85.6 8.4 %collective-permute-start.12 = (bf16[256,256]{1,0:T(8,128)(2,1)S(1)}, bf16[256,256]{1,0:T(8,128)(2,1)S(1)}, u32[]{:S(2)}, u32[]{:S(2)}) collective-permute-start(bf16[256,256]{1,0:T(8,128)(2,1)S(1)} %get-tuple-element.26), channel_id=1, source_target_pairs={{30,0},{15,1},{16,2},{1,3},{18,4},{3,5},{20,6},{5,7},{22,8},{7,9},... | collective-permute-start | bytes 393224 | tf_op jit(solution)/shard_map/ppermute | solution.py:504

commit v5 on v4

--- a/solution.py
+++ b/solution.py
@@ -187,30 +187,37 @@
         copy.wait()
 
 
-def bond_body(
-    a_ref, b_ref, below, here, above, kept, gate_rows, scaled, theta, matrix, proj, work, iso, left,
-    gate_stage, gates, sem, right_ready, iso_ready
-):
-    blocks = b_ref.shape[-1]
-    gate_stage[...] = gate_rows.astype(F32)
-    copy = pltpu.make_async_copy(gate_stage, gates, sem)
-    copy.start()
-    for first, count, w in ((3, 4, here), (0, 3, below), (7, 3, above)):
-        rows = slice(first * blocks, (first + count) * blocks)
-        scaled[rows, :] = (a_ref[rows, :].astype(F32) * w).astype(BF16)
-    basis = a_ref[3 * blocks : 7 * blocks, :].T
-    right_ready()
+def products(a_blocks, b_blocks, weights, scaled, theta):
+    blocks = scaled.shape[-1]
+
+    def block(place):
+        ref, n = place
+        return ref[n * blocks : (n + 1) * blocks, :]
+
+    for n, place in enumerate(a_blocks):
+        w = weights[0 if n < 3 else 1 if n < 7 else 2]
+        scaled[n * blocks : (n + 1) * blocks, :] = (block(place).astype(F32) * w).astype(BF16)
     for (distance, q), (right, first_row, count, first) in PIECES.items():
         product = dot(
             scaled[first_row * blocks : (first_row + count) * blocks, :],
-            b_ref[right * blocks : (right + 1) * blocks, :],
+            block(b_blocks[right]),
             ((1,), (0,)),
         )
         slot = SLOTS[distance, first, q]
         theta[slot * blocks : (slot + count) * blocks, :] = (
             product * (1.0 / math.sqrt(blocks))
         ).astype(BF16)
-    copy.wait()
+
+
+def load_gates(gate_rows, gate_stage, gates, sem):
+    gate_stage[...] = gate_rows.astype(F32)
+    copy = pltpu.make_async_copy(gate_stage, gates, sem)
+    copy.start()
+    return copy
+
+
+def bond_body(basis, kept, theta, matrix, proj, work, iso, left, gates, iso_ready):
+    blocks = theta.shape[-1]
 
     def gate(a, b, p, q):
         return gates[4 * a + b, 4 * p + q]
@@ -278,83 +285,68 @@
 
 
 def first_kernel(
-    own, here_full, next_full, next_tail, after_tail, here_head,
-    iso_msg, iso_three, left_msg, left_three, local,
-    a_ref, b_ref, small, scaled, theta, matrix, proj, work, gate_stage, gates, sems, sem,
-    iso, left, pack,
+    own, here_full, next_full, here_head, after_tail, next_tail,
+    iso, iso_three, left, left_three, local,
+    scaled, theta, matrix, proj, work, gate_stage, gates, sems,
 ):
     x = lax.axis_index("loop") % 2
     c = lax.axis_index("inner") % 2
-    blocks = a_ref.shape[-1]
-    plans = {
-        0: [
-            (a_ref, 0, own, 0, 3), (a_ref, 3, here_full, 0, 4), (a_ref, 7, next_tail, 0, 3),
-            (b_ref, 0, here_head, 0, 3), (b_ref, 3, next_full, 0, 4), (b_ref, 7, after_tail, 0, 3),
-        ],
-        1: [
-            (a_ref, 0, next_full, 0, 3), (a_ref, 3, here_full, 0, 4), (a_ref, 7, after_tail, 0, 3),
-            (b_ref, 0, here_head, 0, 3), (b_ref, 3, own, 0, 4), (b_ref, 7, next_tail, 0, 3),
-        ],
-    }
-    smalls = {
-        0: [here_head, next_full, own, here_full, next_tail],
-        1: [here_head, own, next_full, here_full, after_tail],
-    }
-
-    def move(source, at, target, to, rows, n):
-        return pltpu.make_async_copy(
-            source.at[pl.ds(at, rows)], target.at[pl.ds(to, rows)], sems.at[n]
-        )
+    blocks = scaled.shape[-1]
+
+    def small(ref):
+        return ref.shape[0] - SMALL
+
+    def span(ref, count):
+        return [(ref, n) for n in range(count)]
 
     @pl.when(x == c)
     def _():
-        for role in (0, 1):
+        base = small(here_full)
+        kept = here_full[base + K_ROW : base + K_ROW + 1, 0:1].astype(F32)
+        gates_copy = load_gates(here_full[base : base + 16, 0:128], gate_stage, gates, sems.at[0])
+        rest = 6 * blocks
+        for role, (one, two, three, four) in enumerate(
+            ((own, next_full, next_tail, after_tail), (next_full, own, after_tail, next_tail))
+        ):
 
             @pl.when(x == role)
-            def _(role=role):
-                for n, (target, to, source, at, count) in enumerate(plans[role]):
-                    move(source, at * blocks, target, to * blocks, count * blocks, n).start()
-                for n, source in enumerate(smalls[role]):
-                    move(source, source.shape[0] - SMALL, small, n * SMALL, SMALL, 6 + n).start()
-
-        def arrived(chosen):
-            for n, (target, to, _, _, count) in enumerate(plans[0]):
-                if target is chosen:
-                    move(own, 0, target, to * blocks, count * blocks, n).wait()
-
+            def _(one=one, two=two, three=three, four=four):
+                products(
+                    span(one, 3) + span(here_full, 4) + span(three, 3),
+                    span(here_head, 3) + span(two, 4) + span(four, 3),
+                    [get_split(ref, small(ref) + W_ROW) for ref in (one, here_full, three)],
+                    scaled,
+                    theta,
+                )
+                for n, ref in enumerate((here_head, two)):
+                    local[rest + n * SMALL : rest + (n + 1) * SMALL, :] = ref[small(ref) :, :]
+
+        basis = here_full[0 : 4 * blocks, :].T
+        gates_copy.wait()
         copies = []
 
-        def out(source, at, target, to, count, rest=0):
-            rows = count * blocks + rest
-            copies.append(move(source, at * blocks, target, to * blocks, rows, 11 + len(copies)))
+        def out(source, at, target, to, count):
+            copies.append(
+                pltpu.make_async_copy(
+                    source.at[pl.ds(at * blocks, count * blocks)],
+                    target.at[pl.ds(to * blocks, count * blocks)],
+                    sems.at[1 + len(copies)],
+                )
+            )
             copies[-1].start()
 
         def iso_ready():
-            out(iso, 0, iso_msg, 0, 4)
             out(iso, 1, iso_three, 0, 3)
             out(iso, 0, local, 0, 3)
 
-        for n in range(5):
-            move(own, 0, small, n * SMALL, SMALL, 6 + n).wait()
-        out(small, 0, local, 6, 0, 2 * SMALL)
-        below, here, above = (get_split(small, (2 + n) * SMALL + W_ROW) for n in range(3))
-        kept = small[3 * SMALL + K_ROW : 3 * SMALL + K_ROW + 1, 0:1].astype(F32)
-        arrived(a_ref)
-        level = bond_body(
-            a_ref, b_ref, below, here, above, kept, small[3 * SMALL : 3 * SMALL + 16, 0:128],
-            scaled, theta, matrix, proj, work, iso, left, gate_stage, gates, sem,
-            lambda: arrived(b_ref), iso_ready,
-        )
-        out(left, 0, left_msg, 0, 4)
+        level = bond_body(basis, kept, theta, matrix, proj, work, iso, left, gates, iso_ready)
         out(left, 1, left_three, 0, 3)
         out(left, 0, local, 3, 3)
-        pack[...] = jnp.zeros((SMALL, blocks), BF16)
-        put_split(pack, 0, get_split(small, W_ROW))
-        put_split(pack, LEVEL_ROW, level)
-        for ref in (iso_msg, iso_three, local):
-            base = ref.shape[0] - SMALL
-            copies.append(move(pack, 0, ref, base, SMALL, 11 + len(copies)))
-            copies[-1].start()
+        weights = get_split(local, rest + W_ROW)
+        for ref in (iso, iso_three, local):
+            ref[small(ref) :, :] = jnp.zeros((SMALL, blocks), BF16)
+            put_split(ref, small(ref), weights)
+            put_split(ref, small(ref) + LEVEL_ROW, level)
         for copy in copies:
             copy.wait()
 
@@ -366,101 +358,96 @@
 def second_kernel(
     local, iso_1, iso_2, left_0, left_1, left_2,
     mid, last, first, whole,
-    a_ref, b_ref, small, scaled, theta, matrix, proj, work, gate_stage, gates, sems, sem,
-    iso, left,
+    scaled, theta, matrix, proj, work, gate_stage, gates, sems, iso, left,
 ):
     x = lax.axis_index("loop") % 2
     c = lax.axis_index("inner") % 2
-    blocks = a_ref.shape[-1]
-    moves = [
-        (source, at * blocks, target, to * blocks, count * blocks)
-        for source, at, target, to, count in (
-            (iso_1, 0, a_ref, 0, 1), (iso_2, 0, a_ref, 1, 2), (local, 0, a_ref, 3, 1),
-            (iso_1, 1, a_ref, 4, 2), (iso_2, 2, a_ref, 6, 1), (local, 1, a_ref, 7, 2),
-            (iso_1, 3, a_ref, 9, 1), (left_0, left_0.shape[0] // blocks - 3, b_ref, 0, 3),
-            (left_1, 0, b_ref, 3, 4), (left_2, 0, b_ref, 7, 3),
-        )
-    ]
-    moves.append((local, 6 * blocks, small, 0, 3 * SMALL))
-    for n, source in enumerate((iso_1, iso_2)):
-        moves.append((source, source.shape[0] - SMALL, small, (3 + n) * SMALL, SMALL))
+    blocks = scaled.shape[-1]
+    rest = 6 * blocks
+    near = left_0.shape[0] // blocks - 3
+
+    def small(ref):
+        return ref.shape[0] - SMALL
 
     @pl.when(x != c)
     def _():
-        copies = [
-            pltpu.make_async_copy(
-                source.at[pl.ds(at, rows)], target.at[pl.ds(to, rows)], sems.at[n]
-            )
-            for n, (source, at, target, to, rows) in enumerate(moves)
-        ]
-        for copy in copies:
-            copy.start()
-
-        def arrived(right):
-            for copy, (_, _, target, _, _) in zip(copies, moves):
-                if (target is b_ref) == right:
-                    copy.wait()
-
-        arrived(False)
-        below = get_split(small, 3 * SMALL)
-        here, above = (get_split(small, n * SMALL + W_ROW) for n in range(2))
-        kept = small[K_ROW : K_ROW + 1, 0:1].astype(F32)
+        kept = local[rest + K_ROW : rest + K_ROW + 1, 0:1].astype(F32)
+        gates_copy = load_gates(local[rest : rest + 16, 0:128], gate_stage, gates, sems.at[0])
+        here = [(local, 0), (iso_1, 1), (iso_1, 2), (iso_2, 2)]
+        products(
+            [(iso_1, 0), (iso_2, 0), (iso_2, 1)] + here + [(local, 1), (local, 2), (iso_1, 3)],
+            [(left_0, near + n) for n in range(3)]
+            + [(left_1, n) for n in range(4)]
+            + [(left_2, n) for n in range(3)],
+            [
+                get_split(iso_1, small(iso_1)),
+                get_split(local, rest + W_ROW),
+                get_split(local, rest + SMALL + W_ROW),
+            ],
+            scaled,
+            theta,
+        )
+        basis = jnp.concatenate(
+            [ref[n * blocks : (n + 1) * blocks, :] for ref, n in here], axis=0
+        ).T
+        gates_copy.wait()
         level = bond_body(
-            a_ref, b_ref, below, here, above, kept, small[0:16, 0:128],
-            scaled, theta, matrix, proj, work, iso, left, gate_stage, gates, sem,
-            lambda: arrived(True), lambda: None,
-        )
-        scales = [as_column(get_split(small, n * SMALL + LEVEL_ROW)) for n in range(2, 5)]
+            basis, kept, theta, matrix, proj, work, iso, left, gates, lambda: None
+        )
+        levels = [get_split(ref, small(ref) + LEVEL_ROW) for ref in (local, iso_1, iso_2)]
         column = as_column(level)
+        for ref, lo, hi in ((last, 3, 4), (mid, 1, 3), (first, 0, 1)):
+            for p in range(lo, hi):
+                value = iso[p * blocks : (p + 1) * blocks, :].astype(F32) * column
+                ref[(p - lo) * blocks : (p - lo + 1) * blocks, :] = value.astype(BF16)
+        scales = [as_column(value) for value in levels]
         for p in range(4):
             rows = slice(p * blocks, (p + 1) * blocks)
             whole[rows, :] = (left[rows, :].astype(F32) * scales[CHARGE[p]]).astype(BF16)
-        for ref, lo, hi in ((first, 0, 1), (mid, 1, 3), (last, 3, 4)):
-            for p in range(lo, hi):
-                value = iso[p * blocks : (p + 1) * blocks, :].astype(F32) * column
-                ref[(p - lo) * blocks : (p - lo + 1) * blocks, :] = value.astype(BF16)
-        for ref, value in ((first, get_split(small, 2 * SMALL + LEVEL_ROW)), (whole, level)):
-            base = ref.shape[0] - SMALL
-            ref[base : base + SMALL, :] = jnp.zeros((SMALL, blocks), BF16)
-            put_split(ref, base + LEVEL_ROW, value)
-
-
-def final_kernel(
-    first_mine, first, mid, last, whole_mine, whole, level_mine, level_far, out, weights, small, sems
+        for ref, value in ((first, levels[0]), (whole, level)):
+            ref[small(ref) :, :] = jnp.zeros((SMALL, blocks), BF16)
+            put_split(ref, small(ref) + LEVEL_ROW, value)
+
+
+def place(plan, out, sems):
+    blocks = out.shape[-1]
+    copies = []
+    for n, (source, to, count) in enumerate(plan):
+        copies.append(
+            pltpu.make_async_copy(
+                source.at[pl.ds(0, count * blocks)],
+                out.at[pl.ds(to * blocks, count * blocks)],
+                sems.at[n],
+            )
+        )
+    for copy in copies:
+        copy.start()
+    return copies
+
+
+def assemble(
+    first_mine, first, mid, last, whole_mine, whole, level_mine, level_far, out, weights, sems
 ):
     x = lax.axis_index("loop") % 2
     c = lax.axis_index("inner") % 2
-    blocks = out.shape[-1]
-    plans = {
-        (0, 0): [(first, 0, 1), (mid, 1, 2), (last, 3, 1), (level_far, 0, 0)],
-        (0, 1): [(first_mine, 0, 1), (mid, 1, 2), (last, 3, 1), (level_mine, 0, 0)],
-        (1, 0): [(whole_mine, 0, 4), (whole_mine, 0, 0)],
-        (1, 1): [(whole, 0, 4), (whole, 0, 0)],
-    }
-    for (role, core), plan in plans.items():
+    even = [(mid, 1, 2), (last, 3, 1)]
+    for role, core, plan, level in (
+        (0, 0, [(first, 0, 1)] + even, level_far),
+        (0, 1, [(first_mine, 0, 1)] + even, level_mine),
+        (1, 0, [(whole_mine, 0, 4)], whole_mine),
+        (1, 1, [(whole, 0, 4)], whole),
+    ):
 
         @pl.when(jnp.logical_and(x == role, c == core))
-        def _(plan=plan):
-            copies = []
-            for n, (source, to, count) in enumerate(plan):
-                if count:
-                    rows, goal = pl.ds(0, count * blocks), out.at[pl.ds(to * blocks, count * blocks)]
-                else:
-                    rows, goal = pl.ds(source.shape[0] - SMALL, SMALL), small
-                copies.append(pltpu.make_async_copy(source.at[rows], goal, sems.at[n]))
-            for copy in copies:
-                copy.start()
+        def _(plan=plan, level=level):
+            copies = place(plan, out, sems)
+            weights[...] = get_split(level, level.shape[0] - SMALL + LEVEL_ROW)
             for copy in copies:
                 copy.wait()
 
-    weights[...] = get_split(small, LEVEL_ROW)
-
 
 def scratch(blocks):
     return [
-        pltpu.VMEM((10 * blocks, blocks), BF16),
-        pltpu.VMEM((10 * blocks, blocks), BF16),
-        pltpu.VMEM((5 * SMALL, blocks), BF16),
         pltpu.VMEM((10 * blocks, blocks), BF16),
         pltpu.VMEM((SLOT_COUNT * blocks, blocks), BF16),
         pltpu.VMEM((4 * blocks, 4 * blocks), BF16),
@@ -468,10 +455,7 @@
         pltpu.VMEM((blocks, 2 * blocks), F32),
         pltpu.VMEM((16, 128), F32),
         pltpu.SMEM((16, 128), F32),
-        pltpu.SemaphoreType.DMA((22,)),
-        pltpu.SemaphoreType.DMA,
-        pltpu.VMEM((4 * blocks, blocks), BF16),
-        pltpu.VMEM((4 * blocks, blocks), BF16),
+        pltpu.SemaphoreType.DMA((5,)),
     ]
 
 
@@ -532,12 +516,12 @@
     iso_msg, iso_three, left_msg, left_three, local = pl.pallas_call(
         first_kernel,
         out_shape=(rows(4, SMALL), rows(3, SMALL), rows(4), rows(3), rows(6, 3 * SMALL)),
-        in_specs=[hbm()] * 6,
-        out_specs=(hbm(),) * 5,
-        scratch_shapes=scratch(blocks) + [pltpu.VMEM((SMALL, blocks), BF16)],
+        in_specs=[vmem()] * 6,
+        out_specs=(vmem(),) * 5,
+        scratch_shapes=scratch(blocks),
         compiler_params=params(),
         name="first_bond",
-    )(full, here_full, next_full, next_tail, after_tail, here_head)
+    )(full, here_full, next_full, here_head, after_tail, next_tail)
 
     def worker(l, k, d, s):
         sector = 2 * k + 1 - l % 2 + s
@@ -557,9 +541,9 @@
     mid, last, first, whole = pl.pallas_call(
         second_kernel,
         out_shape=(rows(2), rows(1), rows(1, SMALL), rows(4, SMALL)),
-        in_specs=[hbm()] * 6,
+        in_specs=[vmem()] * 6,
         out_specs=(vmem(),) * 4,
-        scratch_shapes=scratch(blocks),
+        scratch_shapes=scratch(blocks) + [pltpu.VMEM((4 * blocks, blocks), BF16)] * 2,
         compiler_params=params(),
         name="second_bond",
     )(local_r, iso_1, iso_2, left_0, left_1, left_2)
@@ -584,11 +568,11 @@
             iso_msg[4 * blocks :], lambda l, i: (l + 1, i + 1) if l % 2 == 0 and i % 2 == 0 else None
         )
     sites, weights = pl.pallas_call(
-        final_kernel,
+        assemble,
         out_shape=(rows(4), jax.ShapeDtypeStruct((1, blocks), F32)),
-        in_specs=[hbm()] * 8,
-        out_specs=(vmem(),) * 2,
-        scratch_shapes=[pltpu.VMEM((SMALL, blocks), BF16), pltpu.SemaphoreType.DMA((4,))],
+        in_specs=[vmem()] * 8,
+        out_specs=(hbm(), vmem()),
+        scratch_shapes=[pltpu.SemaphoreType.DMA((3,))],
         compiler_params=params(),
         name="assemble",
     )(first_mine, first_r, mid_r, last_r, whole, whole_r, local_r, level_far)

time: 96.5 us -> 93.3 us (0.967)
  waiting for transfers between devices: 50.4 us -> 48.3 us
  Pallas kernels: 17.2 us -> 15.9 us
    ppermute x14, waiting for transfers between devices: 50.4 us -> 48.3 us  [send(): return lax.ppermute(value, AXES, route)]
    pallas_call x1, Pallas kernels: 15.1 us -> 13.9 us  [per_device(): pl.pallas_call(second_kernel, out_shape=(rows(2), rows(1), rows(1, SMALL)...]
  transfers between devices with their start and end apart: 14 -> 14, of which waited for: 3 -> 4; matrix products, arithmetic and copies ran while one was open for 0% -> 0% of each run, Pallas kernels for 0% -> 0%
where the time goes in v5:
time: 93.3 us; the launch traced here: 92.7 us
  waiting for transfers between devices  48.3 us (52%)
  starting transfers between devices  24.4 us (26%)
  Pallas kernels  15.9 us (17%)
  local copies, waits for them, and re-layouts  2.41 us (3%)
  between operations  1.61 us (2%)
    ppermute x14, waiting for transfers between devices, send(): return lax.ppermute(value, AXES, route)  48.3 us
    ppermute x14, starting transfers between devices, send(): return lax.ppermute(value, AXES, route)  24.4 us
    pallas_call x1, Pallas kernels, per_device(): pl.pallas_call(second_kernel, out_shape=(rows(2), rows(1), rows(1, SMALL)...  13.9 us
    unnamed x6, local copies, waits for them, and re-layouts  2.41 us
  transfers between devices with their start and end apart: 14, of which 4 were waited for; matrix products, arithmetic and copies ran while one was open for 0% of the time, Pallas kernels for 0%

profile of v5, /device:TPU:1, one launch (start us, length us, event | category | flops | bytes accessed | tf_op | source)
XLA Modules:
  0.0 92.7 jit_solution(2038059334163740659)
XLA Ops:
  1.3 0.0 copy-start.2
  1.3 0.7 copy-done.2
  2.0 0.0 copy-start
  2.0 1.0 %copy-done = bf16[1,1,4,256,256]{4,3,2,1,0:T(8,128)(2,1)S(1)} copy-done((bf16[1,1,4,256,256]{4,3,2,1,0:T(8,128)(2,1)S(1)}, bf16[1,1,4,256,256]{4,3,2,1,0:T(8,128)(2,1)}, u32[]{:S(2)}) %copy-start) | copy-done | bytes 524312
  3.0 0.0 copy-start.1
  3.0 0.7 copy-done.1
  3.7 0.6 prepare.1
  4.3 4.9 %collective-permute-start.1 = (bf16[1056,256]{1,0:T(8,128)(2,1)S(1)}, bf16[1056,256]{1,0:T(8,128)(2,1)S(1)}, u32[]{:S(2)}, u32[]{:S(2)}) collective-permute-start(bf16[1056,256]{1,0:T(8,128)(2,1)S(1)} %get-tuple-element.16.own), channel_id=1, source_target_pairs={{18,0},{20,2},{22,4},{24,6},{26,8},{28,10},{30,12},{16,14},{15,17}... | collective-permute-start | bytes 1622024 | tf_op jit(solution)/shard_map/ppermute | solution.py:488
  9.3 1.3 %collective-permute-start = (bf16[1056,256]{1,0:T(8,128)(2,1)S(1)}, bf16[1056,256]{1,0:T(8,128)(2,1)S(1)}, u32[]{:S(2)}, u32[]{:S(2)}) collective-permute-start(bf16[1056,256]{1,0:T(8,128)(2,1)S(1)} %get-tuple-element.16.own), channel_id=1, source_target_pairs={{1,0},{3,2},{5,4},{7,6},{9,8},{11,10},{13,12},{15,14},{0,17},{2,19... | collective-permute-start | bytes 1622024 | tf_op jit(solution)/shard_map/ppermute | solution.py:488
  10.6 0.7 collective-permute-start.2
  11.3 0.7 collective-permute-start.4
  12.0 4.5 %collective-permute-start.3 = (bf16[800,256]{1,0:T(8,128)(2,1)S(1)}, bf16[800,256]{1,0:T(8,128)(2,1)S(1)}, u32[]{:S(2)}, u32[]{:S(2)}) collective-permute-start(bf16[800,256]{1,0:T(8,128)(2,1)S(1)} %get-tuple-element.18), channel_id=1, source_target_pairs={{19,0},{21,2},{23,4},{25,6},{27,8},{29,10},{31,12},{17,14},{1,17},... | collective-permute-start | bytes 1228808 | tf_op jit(solution)/shard_map/ppermute | solution.py:488
  16.5 0.0 collective-permute-done.2.here_head
  16.5 0.0 collective-permute-done.4.next_tail
  16.5 9.2 %collective-permute-done.3.after_tail = bf16[800,256]{1,0:T(8,128)(2,1)S(1)} collective-permute-done((bf16[800,256]{1,0:T(8,128)(2,1)S(1)}, bf16[800,256]{1,0:T(8,128)(2,1)S(1)}, u32[]{:S(2)}, u32[]{:S(2)}) %collective-permute-start.3) | collective-permute-done | bytes 409632 | tf_op jit(solution)/shard_map/ppermute | solution.py:488
  25.7 0.0 collective-permute-done.1.next_full
  25.7 0.0 collective-permute-done.here_full
  25.8 1.3 %collective-permute-start.5 = (bf16[1632,256]{1,0:T(8,128)(2,1)S(1)}, bf16[1632,256]{1,0:T(8,128)(2,1)S(1)}, u32[]{:S(2)}, u32[]{:S(2)}) collective-permute-start(bf16[1632,256]{1,0:T(8,128)(2,1)S(1)} %get-tuple-element.19), channel_id=1, source_target_pairs={{0,1},{2,3},{4,5},{6,7},{8,9},{10,11},{12,13},{14,15},{17,16},{19,... | collective-permute-start | bytes 2506760 | tf_op jit(solution)/shard_map/ppermute | solution.py:488
  27.1 1.3 %collective-permute-start.6 = (bf16[1056,256]{1,0:T(8,128)(2,1)S(1)}, bf16[1056,256]{1,0:T(8,128)(2,1)S(1)}, u32[]{:S(2)}, u32[]{:S(2)}) collective-permute-start(bf16[1056,256]{1,0:T(8,128)(2,1)S(1)} %get-tuple-element.20), channel_id=1, source_target_pairs={{17,1},{19,3},{21,5},{23,7},{25,9},{27,11},{29,13},{31,15},{14,16}... | collective-permute-start | bytes 1622024 | tf_op jit(solution)/shard_map/ppermute | solution.py:488
  28.4 1.3 %collective-permute-start.8 = (bf16[1024,256]{1,0:T(8,128)(2,1)S(1)}, bf16[1024,256]{1,0:T(8,128)(2,1)S(1)}, u32[]{:S(2)}, u32[]{:S(2)}) collective-permute-start(bf16[1024,256]{1,0:T(8,128)(2,1)S(1)} %get-tuple-element.22), channel_id=1, source_target_pairs={{19,1},{21,3},{23,5},{25,7},{27,9},{29,11},{31,13},{17,15},{0,16},... | collective-permute-start | bytes 1572872 | tf_op jit(solution)/shard_map/ppermute | solution.py:488
  29.6 1.3 %collective-permute-start.7 = (bf16[800,256]{1,0:T(8,128)(2,1)S(1)}, bf16[800,256]{1,0:T(8,128)(2,1)S(1)}, u32[]{:S(2)}, u32[]{:S(2)}) collective-permute-start(bf16[800,256]{1,0:T(8,128)(2,1)S(1)} %get-tuple-element.21), channel_id=1, source_target_pairs={{14,1},{0,3},{2,5},{4,7},{6,9},{8,11},{10,13},{12,15},{31,16},{17,... | collective-permute-start | bytes 1228808 | tf_op jit(solution)/shard_map/ppermute | solution.py:488
  30.9 1.3 %collective-permute-start.9 = (bf16[768,256]{1,0:T(8,128)(2,1)S(1)}, bf16[768,256]{1,0:T(8,128)(2,1)S(1)}, u32[]{:S(2)}, u32[]{:S(2)}) collective-permute-start(bf16[768,256]{1,0:T(8,128)(2,1)S(1)} %get-tuple-element.23), channel_id=1, source_target_pairs={{2,1},{4,3},{6,5},{8,7},{10,9},{12,11},{14,13},{0,15},{19,16},{21,... | collective-permute-start | bytes 1179656 | tf_op jit(solution)/shard_map/ppermute | solution.py:488
  32.2 27.8 %collective-permute-done.9.left_2 = bf16[768,256]{1,0:T(8,128)(2,1)S(1)} collective-permute-done((bf16[768,256]{1,0:T(8,128)(2,1)S(1)}, bf16[768,256]{1,0:T(8,128)(2,1)S(1)}, u32[]{:S(2)}, u32[]{:S(2)}) %collective-permute-start.9) | collective-permute-done | bytes 393248 | tf_op jit(solution)/shard_map/ppermute | solution.py:488
  60.0 4.9 %collective-permute-done.7.iso_2 = bf16[800,256]{1,0:T(8,128)(2,1)S(1)} collective-permute-done((bf16[800,256]{1,0:T(8,128)(2,1)S(1)}, bf16[800,256]{1,0:T(8,128)(2,1)S(1)}, u32[]{:S(2)}, u32[]{:S(2)}) %collective-permute-start.7) | collective-permute-done | bytes 409632 | tf_op jit(solution)/shard_map/ppermute | solution.py:488
  64.9 0.0 collective-permute-done.8.left_1
  64.9 0.0 collective-permute-done.6.iso_1
  64.9 0.0 collective-permute-done.5.local.left_0.level_mine
  64.9 13.9 %second_bond.1 = (bf16[512,256]{1,0:T(8,128)(2,1)S(1)}, bf16[256,256]{1,0:T(8,128)(2,1)S(1)}, bf16[288,256]{1,0:T(8,128)(2,1)S(1)}, bf16[1056,256]{1,0:T(8,128)(2,1)S(1)}) custom-call(bf16[1632,256]{1,0:T(8,128)(2,1)S(1)} %collective-permute-done.5.local.left_0.level_mine, bf16[1056,256]{1,0:T(8,128)(2,1)S(1)} %collective-permute-done.6.iso_1, ...), custom_call_target="tpu_custom_call" | custom-call | tf_op jit(solution)/shard_map/second_bond/pallas_call | solution.py:541
  78.8 1.3 %collective-permute-start.13 = (bf16[1056,256]{1,0:T(8,128)(2,1)S(1)}, bf16[1056,256]{1,0:T(8,128)(2,1)S(1)}, u32[]{:S(2)}, u32[]{:S(2)}) collective-permute-start(bf16[1056,256]{1,0:T(8,128)(2,1)S(1)} %get-tuple-element.27.whole_mine), channel_id=1, source_target_pairs={{1,17},{3,19},{5,21},{7,23},{9,25},{11,27},{13,29},{15,31}} | collective-permute-start | bytes 1622024 | tf_op jit(solution)/shard_map/ppermute | solution.py:488
  80.1 1.9 %collective-permute-start.11 = (bf16[512,256]{1,0:T(8,128)(2,1)S(1)}, bf16[512,256]{1,0:T(8,128)(2,1)S(1)}, u32[]{:S(2)}, u32[]{:S(2)}) collective-permute-start(bf16[512,256]{1,0:T(8,128)(2,1)S(1)} %get-tuple-element.25), channel_id=1, source_target_pairs={{15,0},{16,1},{1,2},{18,3},{3,4},{20,5},{5,6},{22,7},{7,8},{24,9},... | collective-permute-start | bytes 786440 | tf_op jit(solution)/shard_map/ppermute | solution.py:488
  82.0 0.7 collective-permute-start.10
  82.7 1.9 %collective-permute-start.12 = (bf16[256,256]{1,0:T(8,128)(2,1)S(1)}, bf16[256,256]{1,0:T(8,128)(2,1)S(1)}, u32[]{:S(2)}, u32[]{:S(2)}) collective-permute-start(bf16[256,256]{1,0:T(8,128)(2,1)S(1)} %get-tuple-element.26), channel_id=1, source_target_pairs={{30,0},{15,1},{16,2},{1,3},{18,4},{3,5},{20,6},{5,7},{22,8},{7,9},... | collective-permute-start | bytes 393224 | tf_op jit(solution)/shard_map/ppermute | solution.py:488
  84.6 6.5 %collective-permute-done.12.last = bf16[256,256]{1,0:T(8,128)(2,1)S(1)} collective-permute-done((bf16[256,256]{1,0:T(8,128)(2,1)S(1)}, bf16[256,256]{1,0:T(8,128)(2,1)S(1)}, u32[]{:S(2)}, u32[]{:S(2)}) %collective-permute-start.12) | collective-permute-done | bytes 131104 | tf_op jit(solution)/shard_map/ppermute | solution.py:488
  91.1 0.0 collective-permute-done.10.first.level_far
  91.1 0.0 collective-permute-done.11.mid
  91.1 0.0 collective-permute-done.13.whole
  91.1 1.4 %assemble.1 = (bf16[1024,256]{1,0:T(8,128)(2,1)}, f32[1,256]{1,0:T(1,128)}) custom-call(bf16[288,256]{1,0:T(8,128)(2,1)S(1)} %get-tuple-element.24.first_mine, bf16[288,256]{1,0:T(8,128)(2,1)S(1)} %collective-permute-done.10.first.level_far, bf16[512,256]{1,0:T(8,128)(2,1)S(1)} %collective-permute-done.11.mid, ...), custom_call_target="tpu_custom_call" | custom-call | tf_op jit(solution)/shard_map/assemble/pallas_call | solution.py:570
  (1 shorter events, 0.0 us)
Async XLA Ops:
  1.3 0.7 copy-start.2
  2.0 1.0 %copy-start = (bf16[1,1,4,256,256]{4,3,2,1,0:T(8,128)(2,1)S(1)}, bf16[1,1,4,256,256]{4,3,2,1,0:T(8,128)(2,1)}, u32[]{:S(2)}) copy-start(bf16[1,1,4,256,256]{4,3,2,1,0:T(8,128)(2,1)} %param.4) | copy-start | bytes 1572868
  3.0 0.7 copy-start.1
  4.3 21.4 %collective-permute-start.1 = (bf16[1056,256]{1,0:T(8,128)(2,1)S(1)}, bf16[1056,256]{1,0:T(8,128)(2,1)S(1)}, u32[]{:S(2)}, u32[]{:S(2)}) collective-permute-start(bf16[1056,256]{1,0:T(8,128)(2,1)S(1)} %get-tuple-element.16.own), channel_id=1, source_target_pairs={{18,0},{20,2},{22,4},{24,6},{26,8},{28,10},{30,12},{16,14},{15,17}... | collective-permute-start | bytes 1622024 | tf_op jit(solution)/shard_map/ppermute | solution.py:488
  9.3 16.4 %collective-permute-start = (bf16[1056,256]{1,0:T(8,128)(2,1)S(1)}, bf16[1056,256]{1,0:T(8,128)(2,1)S(1)}, u32[]{:S(2)}, u32[]{:S(2)}) collective-permute-start(bf16[1056,256]{1,0:T(8,128)(2,1)S(1)} %get-tuple-element.16.own), channel_id=1, source_target_pairs={{1,0},{3,2},{5,4},{7,6},{9,8},{11,10},{13,12},{15,14},{0,17},{2,19... | collective-permute-start | bytes 1622024 | tf_op jit(solution)/shard_map/ppermute | solution.py:488
  10.6 5.9 %collective-permute-start.2 = (bf16[800,256]{1,0:T(8,128)(2,1)S(1)}, bf16[800,256]{1,0:T(8,128)(2,1)S(1)}, u32[]{:S(2)}, u32[]{:S(2)}) collective-permute-start(bf16[800,256]{1,0:T(8,128)(2,1)S(1)} %get-tuple-element.17), channel_id=1, source_target_pairs={{17,0},{19,2},{21,4},{23,6},{25,8},{27,10},{29,12},{31,14},{16,17}... | collective-permute-start | bytes 1228808 | tf_op jit(solution)/shard_map/ppermute | solution.py:488
  11.3 5.2 %collective-permute-start.4 = (bf16[800,256]{1,0:T(8,128)(2,1)S(1)}, bf16[800,256]{1,0:T(8,128)(2,1)S(1)}, u32[]{:S(2)}, u32[]{:S(2)}) collective-permute-start(bf16[800,256]{1,0:T(8,128)(2,1)S(1)} %get-tuple-element.18), channel_id=1, source_target_pairs={{2,0},{4,2},{6,4},{8,6},{10,8},{12,10},{14,12},{0,14},{18,17},{20,... | collective-permute-start | bytes 1228808 | tf_op jit(solution)/shard_map/ppermute | solution.py:488
  12.0 13.7 %collective-permute-start.3 = (bf16[800,256]{1,0:T(8,128)(2,1)S(1)}, bf16[800,256]{1,0:T(8,128)(2,1)S(1)}, u32[]{:S(2)}, u32[]{:S(2)}) collective-permute-start(bf16[800,256]{1,0:T(8,128)(2,1)S(1)} %get-tuple-element.18), channel_id=1, source_target_pairs={{19,0},{21,2},{23,4},{25,6},{27,8},{29,10},{31,12},{17,14},{1,17},... | collective-permute-start | bytes 1228808 | tf_op jit(solution)/shard_map/ppermute | solution.py:488
  25.8 39.1 %collective-permute-start.5 = (bf16[1632,256]{1,0:T(8,128)(2,1)S(1)}, bf16[1632,256]{1,0:T(8,128)(2,1)S(1)}, u32[]{:S(2)}, u32[]{:S(2)}) collective-permute-start(bf16[1632,256]{1,0:T(8,128)(2,1)S(1)} %get-tuple-element.19), channel_id=1, source_target_pairs={{0,1},{2,3},{4,5},{6,7},{8,9},{10,11},{12,13},{14,15},{17,16},{19,... | collective-permute-start | bytes 2506760 | tf_op jit(solution)/shard_map/ppermute | solution.py:488
  27.1 37.8 %collective-permute-start.6 = (bf16[1056,256]{1,0:T(8,128)(2,1)S(1)}, bf16[1056,256]{1,0:T(8,128)(2,1)S(1)}, u32[]{:S(2)}, u32[]{:S(2)}) collective-permute-start(bf16[1056,256]{1,0:T(8,128)(2,1)S(1)} %get-tuple-element.20), channel_id=1, source_target_pairs={{17,1},{19,3},{21,5},{23,7},{25,9},{27,11},{29,13},{31,15},{14,16}... | collective-permute-start | bytes 1622024 | tf_op jit(solution)/shard_map/ppermute | solution.py:488
  28.4 36.5 %collective-permute-start.8 = (bf16[1024,256]{1,0:T(8,128)(2,1)S(1)}, bf16[1024,256]{1,0:T(8,128)(2,1)S(1)}, u32[]{:S(2)}, u32[]{:S(2)}) collective-permute-start(bf16[1024,256]{1,0:T(8,128)(2,1)S(1)} %get-tuple-element.22), channel_id=1, source_target_pairs={{19,1},{21,3},{23,5},{25,7},{27,9},{29,11},{31,13},{17,15},{0,16},... | collective-permute-start | bytes 1572872 | tf_op jit(solution)/shard_map/ppermute | solution.py:488
  29.6 35.2 %collective-permute-start.7 = (bf16[800,256]{1,0:T(8,128)(2,1)S(1)}, bf16[800,256]{1,0:T(8,128)(2,1)S(1)}, u32[]{:S(2)}, u32[]{:S(2)}) collective-permute-start(bf16[800,256]{1,0:T(8,128)(2,1)S(1)} %get-tuple-element.21), channel_id=1, source_target_pairs={{14,1},{0,3},{2,5},{4,7},{6,9},{8,11},{10,13},{12,15},{31,16},{17,... | collective-permute-start | bytes 1228808 | tf_op jit(solution)/shard_map/ppermute | solution.py:488
  30.9 29.1 %collective-permute-start.9 = (bf16[768,256]{1,0:T(8,128)(2,1)S(1)}, bf16[768,256]{1,0:T(8,128)(2,1)S(1)}, u32[]{:S(2)}, u32[]{:S(2)}) collective-permute-start(bf16[768,256]{1,0:T(8,128)(2,1)S(1)} %get-tuple-element.23), channel_id=1, source_target_pairs={{2,1},{4,3},{6,5},{8,7},{10,9},{12,11},{14,13},{0,15},{19,16},{21,... | collective-permute-start | bytes 1179656 | tf_op jit(solution)/shard_map/ppermute | solution.py:488
  78.8 12.4 %collective-permute-start.13 = (bf16[1056,256]{1,0:T(8,128)(2,1)S(1)}, bf16[1056,256]{1,0:T(8,128)(2,1)S(1)}, u32[]{:S(2)}, u32[]{:S(2)}) collective-permute-start(bf16[1056,256]{1,0:T(8,128)(2,1)S(1)} %get-tuple-element.27.whole_mine), channel_id=1, source_target_pairs={{1,17},{3,19},{5,21},{7,23},{9,25},{11,27},{13,29},{15,31}} | collective-permute-start | bytes 1622024 | tf_op jit(solution)/shard_map/ppermute | solution.py:488
  80.1 11.0 %collective-permute-start.11 = (bf16[512,256]{1,0:T(8,128)(2,1)S(1)}, bf16[512,256]{1,0:T(8,128)(2,1)S(1)}, u32[]{:S(2)}, u32[]{:S(2)}) collective-permute-start(bf16[512,256]{1,0:T(8,128)(2,1)S(1)} %get-tuple-element.25), channel_id=1, source_target_pairs={{15,0},{16,1},{1,2},{18,3},{3,4},{20,5},{5,6},{22,7},{7,8},{24,9},... | collective-permute-start | bytes 786440 | tf_op jit(solution)/shard_map/ppermute | solution.py:488
  82.0 9.1 %collective-permute-start.10 = (bf16[288,256]{1,0:T(8,128)(2,1)S(1)}, bf16[288,256]{1,0:T(8,128)(2,1)S(1)}, u32[]{:S(2)}, u32[]{:S(2)}) collective-permute-start(bf16[288,256]{1,0:T(8,128)(2,1)S(1)} %get-tuple-element.24.first_mine), channel_id=1, source_target_pairs={{16,0},{18,2},{20,4},{22,6},{24,8},{26,10},{28,12},{30,14}} | collective-permute-start | bytes 442376 | tf_op jit(solution)/shard_map/ppermute | solution.py:488
  82.7 8.4 %collective-permute-start.12 = (bf16[256,256]{1,0:T(8,128)(2,1)S(1)}, bf16[256,256]{1,0:T(8,128)(2,1)S(1)}, u32[]{:S(2)}, u32[]{:S(2)}) collective-permute-start(bf16[256,256]{1,0:T(8,128)(2,1)S(1)} %get-tuple-element.26), channel_id=1, source_target_pairs={{30,0},{15,1},{16,2},{1,3},{18,4},{3,5},{20,6},{5,7},{22,8},{7,9},... | collective-permute-start | bytes 393224 | tf_op jit(solution)/shard_map/ppermute | solution.py:488

commit v6 on v5

--- a/solution.py
+++ b/solution.py
@@ -162,7 +162,7 @@
     return (h + m) + l
 
 
-def prepare(block_ref, weight_ref, gate_ref, kept_ref, full, head, tail, small, sems):
+def prepare(block_ref, weight_ref, gate_ref, kept_ref, full, head, tail, tail_too, small, sems):
     blocks = block_ref.shape[-1]
     values = jnp.zeros((SMALL, blocks), F32)
     rowid = lax.broadcasted_iota(jnp.int32, (SMALL, blocks), 0)
@@ -171,7 +171,7 @@
     small[...] = jnp.where(rowid == K_ROW, kept_ref[...].astype(F32), values).astype(BF16)
     small[0:16, 0:16] = gate_ref[...].astype(BF16)
     copies = []
-    for n, (ref, at) in enumerate(((full, 0), (tail, blocks), (head, 0))):
+    for n, (ref, at) in enumerate(((full, 0), (tail, blocks), (head, 0), (tail_too, blocks))):
         size = ref.shape[0] - SMALL
         copies.append(
             pltpu.make_async_copy(
@@ -179,7 +179,7 @@
             )
         )
         copies.append(
-            pltpu.make_async_copy(small, ref.at[pl.ds(size, SMALL)], sems.at[3 + n])
+            pltpu.make_async_copy(small, ref.at[pl.ds(size, SMALL)], sems.at[4 + n])
         )
     for copy in copies:
         copy.start()
@@ -285,7 +285,7 @@
 
 
 def first_kernel(
-    own, here_full, next_full, here_head, after_tail, next_tail,
+    own, here_full, next_full, next_tail, after_tail, here_head,
     iso, iso_three, left, left_three, local,
     scaled, theta, matrix, proj, work, gate_stage, gates, sems,
 ):
@@ -493,12 +493,12 @@
     def to_second(where):
         return lambda l, i: where(l, i // 2) if i % 2 != l % 2 else None
 
-    full, head, tail = pl.pallas_call(
+    full, head, tail, tail_too = pl.pallas_call(
         prepare,
-        out_shape=(rows(4, SMALL), rows(3, SMALL), rows(3, SMALL)),
+        out_shape=(rows(4, SMALL), rows(3, SMALL), rows(3, SMALL), rows(3, SMALL)),
         in_specs=[vmem()] * 4,
-        out_specs=(hbm(),) * 3,
-        scratch_shapes=[pltpu.VMEM((SMALL, blocks), BF16), pltpu.SemaphoreType.DMA((6,))],
+        out_specs=(hbm(),) * 4,
+        scratch_shapes=[pltpu.VMEM((SMALL, blocks), BF16), pltpu.SemaphoreType.DMA((8,))],
         compiler_params=params(),
         name="prepare",
     )(site_blocks.reshape(4 * blocks, blocks), bond_weights[0], bond_gates[0], kept_slots)
@@ -509,7 +509,7 @@
     here_full = send(full, to_first(lambda l, k: (l, 2 * k + 1), lambda l, k: (l - 1, 2 * k)))
     next_tail = send(tail, to_first(lambda l, k: (l, 2 * k + 2), lambda l, k: (l, 2 * k + 2)))
     after_tail = send(
-        tail, to_first(lambda l, k: (l + 1, 2 * k + 3), lambda l, k: (l - 1, 2 * k + 1))
+        tail_too, to_first(lambda l, k: (l + 1, 2 * k + 3), lambda l, k: (l - 1, 2 * k + 1))
     )
     here_head = send(head, to_first(lambda l, k: (l + 1, 2 * k + 1), lambda l, k: (l, 2 * k)))
 
@@ -521,7 +521,7 @@
         scratch_shapes=scratch(blocks),
         compiler_params=params(),
         name="first_bond",
-    )(full, here_full, next_full, here_head, after_tail, next_tail)
+    )(full, here_full, next_full, next_tail, after_tail, here_head)
 
     def worker(l, k, d, s):
         sector = 2 * k + 1 - l % 2 + s
@@ -540,7 +540,7 @@
 
     mid, last, first, whole = pl.pallas_call(
         second_kernel,
-        out_shape=(rows(2), rows(1), rows(1, SMALL), rows(4, SMALL)),
+        out_shape=(rows(2), rows(1, SMALL + 16), rows(1, SMALL), rows(4, SMALL)),
         in_specs=[vmem()] * 6,
         out_specs=(vmem(),) * 4,
         scratch_shapes=scratch(blocks) + [pltpu.VMEM((4 * blocks, blocks), BF16)] * 2,

time: 93.3 us -> 95.3 us (1.021)
  waiting for transfers between devices: 48.3 us -> 52.4 us
  starting transfers between devices: 24.4 us -> 21.2 us
    ppermute x14, waiting for transfers between devices: 48.3 us -> 52.4 us  [send(): return lax.ppermute(value, AXES, route)]
    ppermute x14, starting transfers between devices: 24.4 us -> 21.2 us  [send(): return lax.ppermute(value, AXES, route)]
  transfers between devices with their start and end apart: 14 -> 14, of which waited for: 4 -> 3; matrix products, arithmetic and copies ran while one was open for 0% -> 0% of each run, Pallas kernels for 0% -> 0%
where the time goes in v6:
time: 95.3 us; the launch traced here: 93.9 us
  waiting for transfers between devices  52.4 us (55%)
  starting transfers between devices  21.2 us (22%)
  Pallas kernels  16.1 us (17%)
  local copies, waits for them, and re-layouts  2.41 us (3%)
  between operations  1.62 us (2%)
    ppermute x14, waiting for transfers between devices, send(): return lax.ppermute(value, AXES, route)  52.4 us
    ppermute x14, starting transfers between devices, send(): return lax.ppermute(value, AXES, route)  21.2 us
    pallas_call x1, Pallas kernels, per_device(): pl.pallas_call(second_kernel, out_shape=(rows(2), rows(1, SMALL + 16), ro...  13.9 us
    unnamed x6, local copies, waits for them, and re-layouts  2.41 us
  transfers between devices with their start and end apart: 14, of which 3 were waited for; matrix products, arithmetic and copies ran while one was open for 0% of the time, Pallas kernels for 0%

profile of v6, /device:TPU:1, one launch (start us, length us, event | category | flops | bytes accessed | tf_op | source)
XLA Modules:
  0.0 93.9 jit_solution(7576059862630449417)
XLA Ops:
  1.3 0.0 copy-start.2
  1.3 0.7 copy-done.2
  2.0 0.0 copy-start
  2.0 1.0 %copy-done = bf16[1,1,4,256,256]{4,3,2,1,0:T(8,128)(2,1)S(1)} copy-done((bf16[1,1,4,256,256]{4,3,2,1,0:T(8,128)(2,1)S(1)}, bf16[1,1,4,256,256]{4,3,2,1,0:T(8,128)(2,1)}, u32[]{:S(2)}) %copy-start) | copy-done | bytes 524312
  3.0 0.0 copy-start.1
  3.0 0.7 copy-done.1
  3.7 0.8 prepare.1
  4.5 4.9 %collective-permute-start.1 = (bf16[1056,256]{1,0:T(8,128)(2,1)S(1)}, bf16[1056,256]{1,0:T(8,128)(2,1)S(1)}, u32[]{:S(2)}, u32[]{:S(2)}) collective-permute-start(bf16[1056,256]{1,0:T(8,128)(2,1)S(1)} %get-tuple-element.17.own), channel_id=1, source_target_pairs={{18,0},{20,2},{22,4},{24,6},{26,8},{28,10},{30,12},{16,14},{15,17}... | collective-permute-start | bytes 1622024 | tf_op jit(solution)/shard_map/ppermute | solution.py:488
  9.5 1.3 %collective-permute-start = (bf16[1056,256]{1,0:T(8,128)(2,1)S(1)}, bf16[1056,256]{1,0:T(8,128)(2,1)S(1)}, u32[]{:S(2)}, u32[]{:S(2)}) collective-permute-start(bf16[1056,256]{1,0:T(8,128)(2,1)S(1)} %get-tuple-element.17.own), channel_id=1, source_target_pairs={{1,0},{3,2},{5,4},{7,6},{9,8},{11,10},{13,12},{15,14},{0,17},{2,19... | collective-permute-start | bytes 1622024 | tf_op jit(solution)/shard_map/ppermute | solution.py:488
  10.8 0.7 collective-permute-start.2
  11.5 1.3 %collective-permute-start.3 = (bf16[800,256]{1,0:T(8,128)(2,1)S(1)}, bf16[800,256]{1,0:T(8,128)(2,1)S(1)}, u32[]{:S(2)}, u32[]{:S(2)}) collective-permute-start(bf16[800,256]{1,0:T(8,128)(2,1)S(1)} %get-tuple-element.19), channel_id=1, source_target_pairs={{19,0},{21,2},{23,4},{25,6},{27,8},{29,10},{31,12},{17,14},{1,17},... | collective-permute-start | bytes 1228808 | tf_op jit(solution)/shard_map/ppermute | solution.py:488
  12.8 0.7 collective-permute-start.4
  13.5 0.0 collective-permute-done.2.next_tail
  13.5 12.4 %collective-permute-done.3.after_tail = bf16[800,256]{1,0:T(8,128)(2,1)S(1)} collective-permute-done((bf16[800,256]{1,0:T(8,128)(2,1)S(1)}, bf16[800,256]{1,0:T(8,128)(2,1)S(1)}, u32[]{:S(2)}, u32[]{:S(2)}) %collective-permute-start.3) | collective-permute-done | bytes 409632 | tf_op jit(solution)/shard_map/ppermute | solution.py:488
  25.9 0.0 collective-permute-done.4.here_head
  25.9 0.0 collective-permute-done.1.next_full
  25.9 0.0 collective-permute-done.here_full
  25.9 0.1 first_bond.1
  26.0 1.3 %collective-permute-start.5 = (bf16[1632,256]{1,0:T(8,128)(2,1)S(1)}, bf16[1632,256]{1,0:T(8,128)(2,1)S(1)}, u32[]{:S(2)}, u32[]{:S(2)}) collective-permute-start(bf16[1632,256]{1,0:T(8,128)(2,1)S(1)} %get-tuple-element.21), channel_id=1, source_target_pairs={{0,1},{2,3},{4,5},{6,7},{8,9},{10,11},{12,13},{14,15},{17,16},{19,... | collective-permute-start | bytes 2506760 | tf_op jit(solution)/shard_map/ppermute | solution.py:488
  27.3 1.3 %collective-permute-start.6 = (bf16[1056,256]{1,0:T(8,128)(2,1)S(1)}, bf16[1056,256]{1,0:T(8,128)(2,1)S(1)}, u32[]{:S(2)}, u32[]{:S(2)}) collective-permute-start(bf16[1056,256]{1,0:T(8,128)(2,1)S(1)} %get-tuple-element.22), channel_id=1, source_target_pairs={{17,1},{19,3},{21,5},{23,7},{25,9},{27,11},{29,13},{31,15},{14,16}... | collective-permute-start | bytes 1622024 | tf_op jit(solution)/shard_map/ppermute | solution.py:488
  28.6 1.3 %collective-permute-start.8 = (bf16[1024,256]{1,0:T(8,128)(2,1)S(1)}, bf16[1024,256]{1,0:T(8,128)(2,1)S(1)}, u32[]{:S(2)}, u32[]{:S(2)}) collective-permute-start(bf16[1024,256]{1,0:T(8,128)(2,1)S(1)} %get-tuple-element.24), channel_id=1, source_target_pairs={{19,1},{21,3},{23,5},{25,7},{27,9},{29,11},{31,13},{17,15},{0,16},... | collective-permute-start | bytes 1572872 | tf_op jit(solution)/shard_map/ppermute | solution.py:488
  29.9 1.3 %collective-permute-start.7 = (bf16[800,256]{1,0:T(8,128)(2,1)S(1)}, bf16[800,256]{1,0:T(8,128)(2,1)S(1)}, u32[]{:S(2)}, u32[]{:S(2)}) collective-permute-start(bf16[800,256]{1,0:T(8,128)(2,1)S(1)} %get-tuple-element.23), channel_id=1, source_target_pairs={{14,1},{0,3},{2,5},{4,7},{6,9},{8,11},{10,13},{12,15},{31,16},{17,... | collective-permute-start | bytes 1228808 | tf_op jit(solution)/shard_map/ppermute | solution.py:488
  31.2 1.3 %collective-permute-start.9 = (bf16[768,256]{1,0:T(8,128)(2,1)S(1)}, bf16[768,256]{1,0:T(8,128)(2,1)S(1)}, u32[]{:S(2)}, u32[]{:S(2)}) collective-permute-start(bf16[768,256]{1,0:T(8,128)(2,1)S(1)} %get-tuple-element.25), channel_id=1, source_target_pairs={{2,1},{4,3},{6,5},{8,7},{10,9},{12,11},{14,13},{0,15},{19,16},{21,... | collective-permute-start | bytes 1179656 | tf_op jit(solution)/shard_map/ppermute | solution.py:488
  32.5 34.0 %collective-permute-done.9.left_2 = bf16[768,256]{1,0:T(8,128)(2,1)S(1)} collective-permute-done((bf16[768,256]{1,0:T(8,128)(2,1)S(1)}, bf16[768,256]{1,0:T(8,128)(2,1)S(1)}, u32[]{:S(2)}, u32[]{:S(2)}) %collective-permute-start.9) | collective-permute-done | bytes 393248 | tf_op jit(solution)/shard_map/ppermute | solution.py:488
  66.5 0.0 collective-permute-done.7.iso_2
  66.5 0.0 collective-permute-done.8.left_1
  66.5 0.0 collective-permute-done.6.iso_1
  66.5 0.0 collective-permute-done.5.local.left_0.level_mine
  66.5 13.9 %second_bond.1 = (bf16[512,256]{1,0:T(8,128)(2,1)S(1)}, bf16[304,256]{1,0:T(8,128)(2,1)S(1)}, bf16[288,256]{1,0:T(8,128)(2,1)S(1)}, bf16[1056,256]{1,0:T(8,128)(2,1)S(1)}) custom-call(bf16[1632,256]{1,0:T(8,128)(2,1)S(1)} %collective-permute-done.5.local.left_0.level_mine, bf16[1056,256]{1,0:T(8,128)(2,1)S(1)} %collective-permute-done.6.iso_1, ...), custom_call_target="tpu_custom_call" | custom-call | tf_op jit(solution)/shard_map/second_bond/pallas_call | solution.py:541
  80.4 1.3 %collective-permute-start.13 = (bf16[1056,256]{1,0:T(8,128)(2,1)S(1)}, bf16[1056,256]{1,0:T(8,128)(2,1)S(1)}, u32[]{:S(2)}, u32[]{:S(2)}) collective-permute-start(bf16[1056,256]{1,0:T(8,128)(2,1)S(1)} %get-tuple-element.29.whole_mine), channel_id=1, source_target_pairs={{1,17},{3,19},{5,21},{7,23},{9,25},{11,27},{13,29},{15,31}} | collective-permute-start | bytes 1622024 | tf_op jit(solution)/shard_map/ppermute | solution.py:488
  81.7 1.9 %collective-permute-start.11 = (bf16[512,256]{1,0:T(8,128)(2,1)S(1)}, bf16[512,256]{1,0:T(8,128)(2,1)S(1)}, u32[]{:S(2)}, u32[]{:S(2)}) collective-permute-start(bf16[512,256]{1,0:T(8,128)(2,1)S(1)} %get-tuple-element.27), channel_id=1, source_target_pairs={{15,0},{16,1},{1,2},{18,3},{3,4},{20,5},{5,6},{22,7},{7,8},{24,9},... | collective-permute-start | bytes 786440 | tf_op jit(solution)/shard_map/ppermute | solution.py:488
  83.6 1.9 %collective-permute-start.12 = (bf16[304,256]{1,0:T(8,128)(2,1)S(1)}, bf16[304,256]{1,0:T(8,128)(2,1)S(1)}, u32[]{:S(2)}, u32[]{:S(2)}) collective-permute-start(bf16[304,256]{1,0:T(8,128)(2,1)S(1)} %get-tuple-element.28), channel_id=1, source_target_pairs={{30,0},{15,1},{16,2},{1,3},{18,4},{3,5},{20,6},{5,7},{22,8},{7,9},... | collective-permute-start | bytes 466952 | tf_op jit(solution)/shard_map/ppermute | solution.py:488
  85.6 0.7 collective-permute-start.10
  86.3 0.0 collective-permute-done.10.first.level_far
  86.3 6.1 %collective-permute-done.12.last = bf16[304,256]{1,0:T(8,128)(2,1)S(1)} collective-permute-done((bf16[304,256]{1,0:T(8,128)(2,1)S(1)}, bf16[304,256]{1,0:T(8,128)(2,1)S(1)}, u32[]{:S(2)}, u32[]{:S(2)}) %collective-permute-start.12) | collective-permute-done | bytes 155680 | tf_op jit(solution)/shard_map/ppermute | solution.py:488
  92.3 0.0 collective-permute-done.11.mid
  92.3 0.0 collective-permute-done.13.whole
  92.3 1.4 %assemble.1 = (bf16[1024,256]{1,0:T(8,128)(2,1)}, f32[1,256]{1,0:T(1,128)}) custom-call(bf16[288,256]{1,0:T(8,128)(2,1)S(1)} %get-tuple-element.26.first_mine, bf16[288,256]{1,0:T(8,128)(2,1)S(1)} %collective-permute-done.10.first.level_far, bf16[512,256]{1,0:T(8,128)(2,1)S(1)} %collective-permute-done.11.mid, ...), custom_call_target="tpu_custom_call" | custom-call | tf_op jit(solution)/shard_map/assemble/pallas_call | solution.py:570
Async XLA Ops:
  1.3 0.7 copy-start.2
  2.0 1.0 %copy-start = (bf16[1,1,4,256,256]{4,3,2,1,0:T(8,128)(2,1)S(1)}, bf16[1,1,4,256,256]{4,3,2,1,0:T(8,128)(2,1)}, u32[]{:S(2)}) copy-start(bf16[1,1,4,256,256]{4,3,2,1,0:T(8,128)(2,1)} %param.4) | copy-start | bytes 1572868
  3.0 0.7 copy-start.1
  4.5 21.4 %collective-permute-start.1 = (bf16[1056,256]{1,0:T(8,128)(2,1)S(1)}, bf16[1056,256]{1,0:T(8,128)(2,1)S(1)}, u32[]{:S(2)}, u32[]{:S(2)}) collective-permute-start(bf16[1056,256]{1,0:T(8,128)(2,1)S(1)} %get-tuple-element.17.own), channel_id=1, source_target_pairs={{18,0},{20,2},{22,4},{24,6},{26,8},{28,10},{30,12},{16,14},{15,17}... | collective-permute-start | bytes 1622024 | tf_op jit(solution)/shard_map/ppermute | solution.py:488
  9.5 16.4 %collective-permute-start = (bf16[1056,256]{1,0:T(8,128)(2,1)S(1)}, bf16[1056,256]{1,0:T(8,128)(2,1)S(1)}, u32[]{:S(2)}, u32[]{:S(2)}) collective-permute-start(bf16[1056,256]{1,0:T(8,128)(2,1)S(1)} %get-tuple-element.17.own), channel_id=1, source_target_pairs={{1,0},{3,2},{5,4},{7,6},{9,8},{11,10},{13,12},{15,14},{0,17},{2,19... | collective-permute-start | bytes 1622024 | tf_op jit(solution)/shard_map/ppermute | solution.py:488
  10.8 2.7 %collective-permute-start.2 = (bf16[800,256]{1,0:T(8,128)(2,1)S(1)}, bf16[800,256]{1,0:T(8,128)(2,1)S(1)}, u32[]{:S(2)}, u32[]{:S(2)}) collective-permute-start(bf16[800,256]{1,0:T(8,128)(2,1)S(1)} %get-tuple-element.18), channel_id=1, source_target_pairs={{2,0},{4,2},{6,4},{8,6},{10,8},{12,10},{14,12},{0,14},{18,17},{20,... | collective-permute-start | bytes 1228808 | tf_op jit(solution)/shard_map/ppermute | solution.py:488
  11.5 14.4 %collective-permute-start.3 = (bf16[800,256]{1,0:T(8,128)(2,1)S(1)}, bf16[800,256]{1,0:T(8,128)(2,1)S(1)}, u32[]{:S(2)}, u32[]{:S(2)}) collective-permute-start(bf16[800,256]{1,0:T(8,128)(2,1)S(1)} %get-tuple-element.19), channel_id=1, source_target_pairs={{19,0},{21,2},{23,4},{25,6},{27,8},{29,10},{31,12},{17,14},{1,17},... | collective-permute-start | bytes 1228808 | tf_op jit(solution)/shard_map/ppermute | solution.py:488
  12.8 13.1 %collective-permute-start.4 = (bf16[800,256]{1,0:T(8,128)(2,1)S(1)}, bf16[800,256]{1,0:T(8,128)(2,1)S(1)}, u32[]{:S(2)}, u32[]{:S(2)}) collective-permute-start(bf16[800,256]{1,0:T(8,128)(2,1)S(1)} %get-tuple-element.20), channel_id=1, source_target_pairs={{17,0},{19,2},{21,4},{23,6},{25,8},{27,10},{29,12},{31,14},{16,17}... | collective-permute-start | bytes 1228808 | tf_op jit(solution)/shard_map/ppermute | solution.py:488
  26.0 40.5 %collective-permute-start.5 = (bf16[1632,256]{1,0:T(8,128)(2,1)S(1)}, bf16[1632,256]{1,0:T(8,128)(2,1)S(1)}, u32[]{:S(2)}, u32[]{:S(2)}) collective-permute-start(bf16[1632,256]{1,0:T(8,128)(2,1)S(1)} %get-tuple-element.21), channel_id=1, source_target_pairs={{0,1},{2,3},{4,5},{6,7},{8,9},{10,11},{12,13},{14,15},{17,16},{19,... | collective-permute-start | bytes 2506760 | tf_op jit(solution)/shard_map/ppermute | solution.py:488
  27.3 39.2 %collective-permute-start.6 = (bf16[1056,256]{1,0:T(8,128)(2,1)S(1)}, bf16[1056,256]{1,0:T(8,128)(2,1)S(1)}, u32[]{:S(2)}, u32[]{:S(2)}) collective-permute-start(bf16[1056,256]{1,0:T(8,128)(2,1)S(1)} %get-tuple-element.22), channel_id=1, source_target_pairs={{17,1},{19,3},{21,5},{23,7},{25,9},{27,11},{29,13},{31,15},{14,16}... | collective-permute-start | bytes 1622024 | tf_op jit(solution)/shard_map/ppermute | solution.py:488
  28.6 37.9 %collective-permute-start.8 = (bf16[1024,256]{1,0:T(8,128)(2,1)S(1)}, bf16[1024,256]{1,0:T(8,128)(2,1)S(1)}, u32[]{:S(2)}, u32[]{:S(2)}) collective-permute-start(bf16[1024,256]{1,0:T(8,128)(2,1)S(1)} %get-tuple-element.24), channel_id=1, source_target_pairs={{19,1},{21,3},{23,5},{25,7},{27,9},{29,11},{31,13},{17,15},{0,16},... | collective-permute-start | bytes 1572872 | tf_op jit(solution)/shard_map/ppermute | solution.py:488
  29.9 36.6 %collective-permute-start.7 = (bf16[800,256]{1,0:T(8,128)(2,1)S(1)}, bf16[800,256]{1,0:T(8,128)(2,1)S(1)}, u32[]{:S(2)}, u32[]{:S(2)}) collective-permute-start(bf16[800,256]{1,0:T(8,128)(2,1)S(1)} %get-tuple-element.23), channel_id=1, source_target_pairs={{14,1},{0,3},{2,5},{4,7},{6,9},{8,11},{10,13},{12,15},{31,16},{17,... | collective-permute-start | bytes 1228808 | tf_op jit(solution)/shard_map/ppermute | solution.py:488
  31.2 35.3 %collective-permute-start.9 = (bf16[768,256]{1,0:T(8,128)(2,1)S(1)}, bf16[768,256]{1,0:T(8,128)(2,1)S(1)}, u32[]{:S(2)}, u32[]{:S(2)}) collective-permute-start(bf16[768,256]{1,0:T(8,128)(2,1)S(1)} %get-tuple-element.25), channel_id=1, source_target_pairs={{2,1},{4,3},{6,5},{8,7},{10,9},{12,11},{14,13},{0,15},{19,16},{21,... | collective-permute-start | bytes 1179656 | tf_op jit(solution)/shard_map/ppermute | solution.py:488
  80.4 11.9 %collective-permute-start.13 = (bf16[1056,256]{1,0:T(8,128)(2,1)S(1)}, bf16[1056,256]{1,0:T(8,128)(2,1)S(1)}, u32[]{:S(2)}, u32[]{:S(2)}) collective-permute-start(bf16[1056,256]{1,0:T(8,128)(2,1)S(1)} %get-tuple-element.29.whole_mine), channel_id=1, source_target_pairs={{1,17},{3,19},{5,21},{7,23},{9,25},{11,27},{13,29},{15,31}} | collective-permute-start | bytes 1622024 | tf_op jit(solution)/shard_map/ppermute | solution.py:488
  81.7 10.6 %collective-permute-start.11 = (bf16[512,256]{1,0:T(8,128)(2,1)S(1)}, bf16[512,256]{1,0:T(8,128)(2,1)S(1)}, u32[]{:S(2)}, u32[]{:S(2)}) collective-permute-start(bf16[512,256]{1,0:T(8,128)(2,1)S(1)} %get-tuple-element.27), channel_id=1, source_target_pairs={{15,0},{16,1},{1,2},{18,3},{3,4},{20,5},{5,6},{22,7},{7,8},{24,9},... | collective-permute-start | bytes 786440 | tf_op jit(solution)/shard_map/ppermute | solution.py:488
  83.6 8.7 %collective-permute-start.12 = (bf16[304,256]{1,0:T(8,128)(2,1)S(1)}, bf16[304,256]{1,0:T(8,128)(2,1)S(1)}, u32[]{:S(2)}, u32[]{:S(2)}) collective-permute-start(bf16[304,256]{1,0:T(8,128)(2,1)S(1)} %get-tuple-element.28), channel_id=1, source_target_pairs={{30,0},{15,1},{16,2},{1,3},{18,4},{3,5},{20,6},{5,7},{22,8},{7,9},... | collective-permute-start | bytes 466952 | tf_op jit(solution)/shard_map/ppermute | solution.py:488
  85.6 0.7 collective-permute-start.10

commit v7 on v5

--- a/solution.py
+++ b/solution.py
@@ -278,9 +278,16 @@
     for p in range(4):
         iso[p * blocks : (p + 1) * blocks, :] = ortho[:, p * blocks : (p + 1) * blocks]
     iso_ready()
-    carried = dot(matrix[...], ortho, outer) * (1.0 / math.sqrt(4 * blocks))
-    level = jnp.sqrt(jnp.mean(carried * carried, axis=0, keepdims=True) + 1e-06)
-    left[...] = (carried * (1.0 / level)).astype(BF16)
+    flipped = ortho.T
+    parts, total = [], 0.0
+    for p in range(4):
+        rows = matrix[p * blocks : (p + 1) * blocks, :]
+        parts.append(dot(rows, flipped, inner) * (1.0 / math.sqrt(4 * blocks)))
+        total = total + jnp.sum(parts[p] * parts[p], axis=0, keepdims=True)
+    level = jnp.sqrt(total * (1.0 / (4 * blocks)) + 1e-06)
+    scale = 1.0 / level
+    for p in range(4):
+        left[p * blocks : (p + 1) * blocks, :] = (parts[p] * scale).astype(BF16)
     return level
 
 
@@ -411,17 +418,18 @@
 
 def place(plan, out, sems):
     blocks = out.shape[-1]
+    half = blocks // 2
     copies = []
-    for n, (source, to, count) in enumerate(plan):
-        copies.append(
-            pltpu.make_async_copy(
-                source.at[pl.ds(0, count * blocks)],
-                out.at[pl.ds(to * blocks, count * blocks)],
-                sems.at[n],
+    for source, to, count in plan:
+        for n in range(2 * count):
+            copies.append(
+                pltpu.make_async_copy(
+                    source.at[pl.ds(n * half, half)],
+                    out.at[pl.ds(to * blocks + n * half, half)],
+                    sems.at[len(copies)],
+                )
             )
-        )
-    for copy in copies:
-        copy.start()
+            copies[-1].start()
     return copies
 
 
@@ -572,7 +580,7 @@
         out_shape=(rows(4), jax.ShapeDtypeStruct((1, blocks), F32)),
         in_specs=[vmem()] * 8,
         out_specs=(hbm(), vmem()),
-        scratch_shapes=[pltpu.SemaphoreType.DMA((3,))],
+        scratch_shapes=[pltpu.SemaphoreType.DMA((8,))],
         compiler_params=params(),
         name="assemble",
     )(first_mine, first_r, mid_r, last_r, whole, whole_r, local_r, level_far)

time: 93.3 us -> 92.3 us (0.989)
  Pallas kernels: 15.9 us -> 14.9 us
    pallas_call x1, Pallas kernels: 13.9 us -> 12.8 us  [per_device(): pl.pallas_call(second_kernel, out_shape=(rows(2), rows(1), rows(1, SMALL)...]
where the time goes in v7:
time: 92.3 us; the launch traced here: 91.6 us
  waiting for transfers between devices  48.3 us (52%)
  starting transfers between devices  24.4 us (26%)
  Pallas kernels  14.9 us (16%)
  local copies, waits for them, and re-layouts  2.41 us (3%)
  between operations  1.61 us (2%)
    ppermute x14, waiting for transfers between devices, send(): return lax.ppermute(value, AXES, route)  48.3 us
    ppermute x14, starting transfers between devices, send(): return lax.ppermute(value, AXES, route)  24.4 us
    pallas_call x1, Pallas kernels, per_device(): pl.pallas_call(second_kernel, out_shape=(rows(2), rows(1), rows(1, SMALL)...  12.8 us
    unnamed x6, local copies, waits for them, and re-layouts  2.41 us
  transfers between devices with their start and end apart: 14, of which 4 were waited for; matrix products, arithmetic and copies ran while one was open for 0% of the time, Pallas kernels for 0%

profile of v7, /device:TPU:1, one launch (start us, length us, event | category | flops | bytes accessed | tf_op | source)
XLA Modules:
  0.0 91.6 jit_solution(2440640064107550462)
XLA Ops:
  1.3 0.0 copy-start.2
  1.3 0.7 copy-done.2
  2.0 0.0 copy-start
  2.0 1.0 %copy-done = bf16[1,1,4,256,256]{4,3,2,1,0:T(8,128)(2,1)S(1)} copy-done((bf16[1,1,4,256,256]{4,3,2,1,0:T(8,128)(2,1)S(1)}, bf16[1,1,4,256,256]{4,3,2,1,0:T(8,128)(2,1)}, u32[]{:S(2)}) %copy-start) | copy-done | bytes 524312
  3.0 0.0 copy-start.1
  3.0 0.7 copy-done.1
  3.7 0.6 prepare.1
  4.3 4.9 %collective-permute-start.1 = (bf16[1056,256]{1,0:T(8,128)(2,1)S(1)}, bf16[1056,256]{1,0:T(8,128)(2,1)S(1)}, u32[]{:S(2)}, u32[]{:S(2)}) collective-permute-start(bf16[1056,256]{1,0:T(8,128)(2,1)S(1)} %get-tuple-element.16.own), channel_id=1, source_target_pairs={{18,0},{20,2},{22,4},{24,6},{26,8},{28,10},{30,12},{16,14},{15,17}... | collective-permute-start | bytes 1622024 | tf_op jit(solution)/shard_map/ppermute | solution.py:496
  9.3 1.3 %collective-permute-start = (bf16[1056,256]{1,0:T(8,128)(2,1)S(1)}, bf16[1056,256]{1,0:T(8,128)(2,1)S(1)}, u32[]{:S(2)}, u32[]{:S(2)}) collective-permute-start(bf16[1056,256]{1,0:T(8,128)(2,1)S(1)} %get-tuple-element.16.own), channel_id=1, source_target_pairs={{1,0},{3,2},{5,4},{7,6},{9,8},{11,10},{13,12},{15,14},{0,17},{2,19... | collective-permute-start | bytes 1622024 | tf_op jit(solution)/shard_map/ppermute | solution.py:496
  10.6 0.7 collective-permute-start.2
  11.3 0.7 collective-permute-start.4
  12.0 4.5 %collective-permute-start.3 = (bf16[800,256]{1,0:T(8,128)(2,1)S(1)}, bf16[800,256]{1,0:T(8,128)(2,1)S(1)}, u32[]{:S(2)}, u32[]{:S(2)}) collective-permute-start(bf16[800,256]{1,0:T(8,128)(2,1)S(1)} %get-tuple-element.18), channel_id=1, source_target_pairs={{19,0},{21,2},{23,4},{25,6},{27,8},{29,10},{31,12},{17,14},{1,17},... | collective-permute-start | bytes 1228808 | tf_op jit(solution)/shard_map/ppermute | solution.py:496
  16.5 0.0 collective-permute-done.2.here_head
  16.5 0.0 collective-permute-done.4.next_tail
  16.5 9.2 %collective-permute-done.3.after_tail = bf16[800,256]{1,0:T(8,128)(2,1)S(1)} collective-permute-done((bf16[800,256]{1,0:T(8,128)(2,1)S(1)}, bf16[800,256]{1,0:T(8,128)(2,1)S(1)}, u32[]{:S(2)}, u32[]{:S(2)}) %collective-permute-start.3) | collective-permute-done | bytes 409632 | tf_op jit(solution)/shard_map/ppermute | solution.py:496
  25.7 0.0 collective-permute-done.1.next_full
  25.7 0.0 collective-permute-done.here_full
  25.8 1.3 %collective-permute-start.5 = (bf16[1632,256]{1,0:T(8,128)(2,1)S(1)}, bf16[1632,256]{1,0:T(8,128)(2,1)S(1)}, u32[]{:S(2)}, u32[]{:S(2)}) collective-permute-start(bf16[1632,256]{1,0:T(8,128)(2,1)S(1)} %get-tuple-element.19), channel_id=1, source_target_pairs={{0,1},{2,3},{4,5},{6,7},{8,9},{10,11},{12,13},{14,15},{17,16},{19,... | collective-permute-start | bytes 2506760 | tf_op jit(solution)/shard_map/ppermute | solution.py:496
  27.1 1.3 %collective-permute-start.6 = (bf16[1056,256]{1,0:T(8,128)(2,1)S(1)}, bf16[1056,256]{1,0:T(8,128)(2,1)S(1)}, u32[]{:S(2)}, u32[]{:S(2)}) collective-permute-start(bf16[1056,256]{1,0:T(8,128)(2,1)S(1)} %get-tuple-element.20), channel_id=1, source_target_pairs={{17,1},{19,3},{21,5},{23,7},{25,9},{27,11},{29,13},{31,15},{14,16}... | collective-permute-start | bytes 1622024 | tf_op jit(solution)/shard_map/ppermute | solution.py:496
  28.4 1.3 %collective-permute-start.8 = (bf16[1024,256]{1,0:T(8,128)(2,1)S(1)}, bf16[1024,256]{1,0:T(8,128)(2,1)S(1)}, u32[]{:S(2)}, u32[]{:S(2)}) collective-permute-start(bf16[1024,256]{1,0:T(8,128)(2,1)S(1)} %get-tuple-element.22), channel_id=1, source_target_pairs={{19,1},{21,3},{23,5},{25,7},{27,9},{29,11},{31,13},{17,15},{0,16},... | collective-permute-start | bytes 1572872 | tf_op jit(solution)/shard_map/ppermute | solution.py:496
  29.6 1.3 %collective-permute-start.7 = (bf16[800,256]{1,0:T(8,128)(2,1)S(1)}, bf16[800,256]{1,0:T(8,128)(2,1)S(1)}, u32[]{:S(2)}, u32[]{:S(2)}) collective-permute-start(bf16[800,256]{1,0:T(8,128)(2,1)S(1)} %get-tuple-element.21), channel_id=1, source_target_pairs={{14,1},{0,3},{2,5},{4,7},{6,9},{8,11},{10,13},{12,15},{31,16},{17,... | collective-permute-start | bytes 1228808 | tf_op jit(solution)/shard_map/ppermute | solution.py:496
  30.9 1.3 %collective-permute-start.9 = (bf16[768,256]{1,0:T(8,128)(2,1)S(1)}, bf16[768,256]{1,0:T(8,128)(2,1)S(1)}, u32[]{:S(2)}, u32[]{:S(2)}) collective-permute-start(bf16[768,256]{1,0:T(8,128)(2,1)S(1)} %get-tuple-element.23), channel_id=1, source_target_pairs={{2,1},{4,3},{6,5},{8,7},{10,9},{12,11},{14,13},{0,15},{19,16},{21,... | collective-permute-start | bytes 1179656 | tf_op jit(solution)/shard_map/ppermute | solution.py:496
  32.2 27.8 %collective-permute-done.9.left_2 = bf16[768,256]{1,0:T(8,128)(2,1)S(1)} collective-permute-done((bf16[768,256]{1,0:T(8,128)(2,1)S(1)}, bf16[768,256]{1,0:T(8,128)(2,1)S(1)}, u32[]{:S(2)}, u32[]{:S(2)}) %collective-permute-start.9) | collective-permute-done | bytes 393248 | tf_op jit(solution)/shard_map/ppermute | solution.py:496
  60.0 4.9 %collective-permute-done.7.iso_2 = bf16[800,256]{1,0:T(8,128)(2,1)S(1)} collective-permute-done((bf16[800,256]{1,0:T(8,128)(2,1)S(1)}, bf16[800,256]{1,0:T(8,128)(2,1)S(1)}, u32[]{:S(2)}, u32[]{:S(2)}) %collective-permute-start.7) | collective-permute-done | bytes 409632 | tf_op jit(solution)/shard_map/ppermute | solution.py:496
  64.9 0.0 collective-permute-done.8.left_1
  64.9 0.0 collective-permute-done.6.iso_1
  64.9 0.0 collective-permute-done.5.local.left_0.level_mine
  64.9 12.8 %second_bond.1 = (bf16[512,256]{1,0:T(8,128)(2,1)S(1)}, bf16[256,256]{1,0:T(8,128)(2,1)S(1)}, bf16[288,256]{1,0:T(8,128)(2,1)S(1)}, bf16[1056,256]{1,0:T(8,128)(2,1)S(1)}) custom-call(bf16[1632,256]{1,0:T(8,128)(2,1)S(1)} %collective-permute-done.5.local.left_0.level_mine, bf16[1056,256]{1,0:T(8,128)(2,1)S(1)} %collective-permute-done.6.iso_1, ...), custom_call_target="tpu_custom_call" | custom-call | tf_op jit(solution)/shard_map/second_bond/pallas_call | solution.py:549
  77.7 1.3 %collective-permute-start.13 = (bf16[1056,256]{1,0:T(8,128)(2,1)S(1)}, bf16[1056,256]{1,0:T(8,128)(2,1)S(1)}, u32[]{:S(2)}, u32[]{:S(2)}) collective-permute-start(bf16[1056,256]{1,0:T(8,128)(2,1)S(1)} %get-tuple-element.27.whole_mine), channel_id=1, source_target_pairs={{1,17},{3,19},{5,21},{7,23},{9,25},{11,27},{13,29},{15,31}} | collective-permute-start | bytes 1622024 | tf_op jit(solution)/shard_map/ppermute | solution.py:496
  79.0 1.9 %collective-permute-start.11 = (bf16[512,256]{1,0:T(8,128)(2,1)S(1)}, bf16[512,256]{1,0:T(8,128)(2,1)S(1)}, u32[]{:S(2)}, u32[]{:S(2)}) collective-permute-start(bf16[512,256]{1,0:T(8,128)(2,1)S(1)} %get-tuple-element.25), channel_id=1, source_target_pairs={{15,0},{16,1},{1,2},{18,3},{3,4},{20,5},{5,6},{22,7},{7,8},{24,9},... | collective-permute-start | bytes 786440 | tf_op jit(solution)/shard_map/ppermute | solution.py:496
  81.0 0.7 collective-permute-start.10
  81.6 1.9 %collective-permute-start.12 = (bf16[256,256]{1,0:T(8,128)(2,1)S(1)}, bf16[256,256]{1,0:T(8,128)(2,1)S(1)}, u32[]{:S(2)}, u32[]{:S(2)}) collective-permute-start(bf16[256,256]{1,0:T(8,128)(2,1)S(1)} %get-tuple-element.26), channel_id=1, source_target_pairs={{30,0},{15,1},{16,2},{1,3},{18,4},{3,5},{20,6},{5,7},{22,8},{7,9},... | collective-permute-start | bytes 393224 | tf_op jit(solution)/shard_map/ppermute | solution.py:496
  83.6 6.5 %collective-permute-done.12.last = bf16[256,256]{1,0:T(8,128)(2,1)S(1)} collective-permute-done((bf16[256,256]{1,0:T(8,128)(2,1)S(1)}, bf16[256,256]{1,0:T(8,128)(2,1)S(1)}, u32[]{:S(2)}, u32[]{:S(2)}) %collective-permute-start.12) | collective-permute-done | bytes 131104 | tf_op jit(solution)/shard_map/ppermute | solution.py:496
  90.0 0.0 collective-permute-done.10.first.level_far
  90.0 0.0 collective-permute-done.11.mid
  90.0 0.0 collective-permute-done.13.whole
  90.1 1.4 %assemble.1 = (bf16[1024,256]{1,0:T(8,128)(2,1)}, f32[1,256]{1,0:T(1,128)}) custom-call(bf16[288,256]{1,0:T(8,128)(2,1)S(1)} %get-tuple-element.24.first_mine, bf16[288,256]{1,0:T(8,128)(2,1)S(1)} %collective-permute-done.10.first.level_far, bf16[512,256]{1,0:T(8,128)(2,1)S(1)} %collective-permute-done.11.mid, ...), custom_call_target="tpu_custom_call" | custom-call | tf_op jit(solution)/shard_map/assemble/pallas_call | solution.py:578
  (1 shorter events, 0.0 us)
Async XLA Ops:
  1.3 0.7 copy-start.2
  2.0 1.0 %copy-start = (bf16[1,1,4,256,256]{4,3,2,1,0:T(8,128)(2,1)S(1)}, bf16[1,1,4,256,256]{4,3,2,1,0:T(8,128)(2,1)}, u32[]{:S(2)}) copy-start(bf16[1,1,4,256,256]{4,3,2,1,0:T(8,128)(2,1)} %param.4) | copy-start | bytes 1572868
  3.0 0.7 copy-start.1
  4.3 21.4 %collective-permute-start.1 = (bf16[1056,256]{1,0:T(8,128)(2,1)S(1)}, bf16[1056,256]{1,0:T(8,128)(2,1)S(1)}, u32[]{:S(2)}, u32[]{:S(2)}) collective-permute-start(bf16[1056,256]{1,0:T(8,128)(2,1)S(1)} %get-tuple-element.16.own), channel_id=1, source_target_pairs={{18,0},{20,2},{22,4},{24,6},{26,8},{28,10},{30,12},{16,14},{15,17}... | collective-permute-start | bytes 1622024 | tf_op jit(solution)/shard_map/ppermute | solution.py:496
  9.3 16.4 %collective-permute-start = (bf16[1056,256]{1,0:T(8,128)(2,1)S(1)}, bf16[1056,256]{1,0:T(8,128)(2,1)S(1)}, u32[]{:S(2)}, u32[]{:S(2)}) collective-permute-start(bf16[1056,256]{1,0:T(8,128)(2,1)S(1)} %get-tuple-element.16.own), channel_id=1, source_target_pairs={{1,0},{3,2},{5,4},{7,6},{9,8},{11,10},{13,12},{15,14},{0,17},{2,19... | collective-permute-start | bytes 1622024 | tf_op jit(solution)/shard_map/ppermute | solution.py:496
  10.6 5.9 %collective-permute-start.2 = (bf16[800,256]{1,0:T(8,128)(2,1)S(1)}, bf16[800,256]{1,0:T(8,128)(2,1)S(1)}, u32[]{:S(2)}, u32[]{:S(2)}) collective-permute-start(bf16[800,256]{1,0:T(8,128)(2,1)S(1)} %get-tuple-element.17), channel_id=1, source_target_pairs={{17,0},{19,2},{21,4},{23,6},{25,8},{27,10},{29,12},{31,14},{16,17}... | collective-permute-start | bytes 1228808 | tf_op jit(solution)/shard_map/ppermute | solution.py:496
  11.3 5.2 %collective-permute-start.4 = (bf16[800,256]{1,0:T(8,128)(2,1)S(1)}, bf16[800,256]{1,0:T(8,128)(2,1)S(1)}, u32[]{:S(2)}, u32[]{:S(2)}) collective-permute-start(bf16[800,256]{1,0:T(8,128)(2,1)S(1)} %get-tuple-element.18), channel_id=1, source_target_pairs={{2,0},{4,2},{6,4},{8,6},{10,8},{12,10},{14,12},{0,14},{18,17},{20,... | collective-permute-start | bytes 1228808 | tf_op jit(solution)/shard_map/ppermute | solution.py:496
  12.0 13.7 %collective-permute-start.3 = (bf16[800,256]{1,0:T(8,128)(2,1)S(1)}, bf16[800,256]{1,0:T(8,128)(2,1)S(1)}, u32[]{:S(2)}, u32[]{:S(2)}) collective-permute-start(bf16[800,256]{1,0:T(8,128)(2,1)S(1)} %get-tuple-element.18), channel_id=1, source_target_pairs={{19,0},{21,2},{23,4},{25,6},{27,8},{29,10},{31,12},{17,14},{1,17},... | collective-permute-start | bytes 1228808 | tf_op jit(solution)/shard_map/ppermute | solution.py:496
  25.8 39.1 %collective-permute-start.5 = (bf16[1632,256]{1,0:T(8,128)(2,1)S(1)}, bf16[1632,256]{1,0:T(8,128)(2,1)S(1)}, u32[]{:S(2)}, u32[]{:S(2)}) collective-permute-start(bf16[1632,256]{1,0:T(8,128)(2,1)S(1)} %get-tuple-element.19), channel_id=1, source_target_pairs={{0,1},{2,3},{4,5},{6,7},{8,9},{10,11},{12,13},{14,15},{17,16},{19,... | collective-permute-start | bytes 2506760 | tf_op jit(solution)/shard_map/ppermute | solution.py:496
  27.1 37.8 %collective-permute-start.6 = (bf16[1056,256]{1,0:T(8,128)(2,1)S(1)}, bf16[1056,256]{1,0:T(8,128)(2,1)S(1)}, u32[]{:S(2)}, u32[]{:S(2)}) collective-permute-start(bf16[1056,256]{1,0:T(8,128)(2,1)S(1)} %get-tuple-element.20), channel_id=1, source_target_pairs={{17,1},{19,3},{21,5},{23,7},{25,9},{27,11},{29,13},{31,15},{14,16}... | collective-permute-start | bytes 1622024 | tf_op jit(solution)/shard_map/ppermute | solution.py:496
  28.4 36.5 %collective-permute-start.8 = (bf16[1024,256]{1,0:T(8,128)(2,1)S(1)}, bf16[1024,256]{1,0:T(8,128)(2,1)S(1)}, u32[]{:S(2)}, u32[]{:S(2)}) collective-permute-start(bf16[1024,256]{1,0:T(8,128)(2,1)S(1)} %get-tuple-element.22), channel_id=1, source_target_pairs={{19,1},{21,3},{23,5},{25,7},{27,9},{29,11},{31,13},{17,15},{0,16},... | collective-permute-start | bytes 1572872 | tf_op jit(solution)/shard_map/ppermute | solution.py:496
  29.6 35.2 %collective-permute-start.7 = (bf16[800,256]{1,0:T(8,128)(2,1)S(1)}, bf16[800,256]{1,0:T(8,128)(2,1)S(1)}, u32[]{:S(2)}, u32[]{:S(2)}) collective-permute-start(bf16[800,256]{1,0:T(8,128)(2,1)S(1)} %get-tuple-element.21), channel_id=1, source_target_pairs={{14,1},{0,3},{2,5},{4,7},{6,9},{8,11},{10,13},{12,15},{31,16},{17,... | collective-permute-start | bytes 1228808 | tf_op jit(solution)/shard_map/ppermute | solution.py:496
  30.9 29.1 %collective-permute-start.9 = (bf16[768,256]{1,0:T(8,128)(2,1)S(1)}, bf16[768,256]{1,0:T(8,128)(2,1)S(1)}, u32[]{:S(2)}, u32[]{:S(2)}) collective-permute-start(bf16[768,256]{1,0:T(8,128)(2,1)S(1)} %get-tuple-element.23), channel_id=1, source_target_pairs={{2,1},{4,3},{6,5},{8,7},{10,9},{12,11},{14,13},{0,15},{19,16},{21,... | collective-permute-start | bytes 1179656 | tf_op jit(solution)/shard_map/ppermute | solution.py:496
  77.7 12.4 %collective-permute-start.13 = (bf16[1056,256]{1,0:T(8,128)(2,1)S(1)}, bf16[1056,256]{1,0:T(8,128)(2,1)S(1)}, u32[]{:S(2)}, u32[]{:S(2)}) collective-permute-start(bf16[1056,256]{1,0:T(8,128)(2,1)S(1)} %get-tuple-element.27.whole_mine), channel_id=1, source_target_pairs={{1,17},{3,19},{5,21},{7,23},{9,25},{11,27},{13,29},{15,31}} | collective-permute-start | bytes 1622024 | tf_op jit(solution)/shard_map/ppermute | solution.py:496
  79.0 11.0 %collective-permute-start.11 = (bf16[512,256]{1,0:T(8,128)(2,1)S(1)}, bf16[512,256]{1,0:T(8,128)(2,1)S(1)}, u32[]{:S(2)}, u32[]{:S(2)}) collective-permute-start(bf16[512,256]{1,0:T(8,128)(2,1)S(1)} %get-tuple-element.25), channel_id=1, source_target_pairs={{15,0},{16,1},{1,2},{18,3},{3,4},{20,5},{5,6},{22,7},{7,8},{24,9},... | collective-permute-start | bytes 786440 | tf_op jit(solution)/shard_map/ppermute | solution.py:496
  81.0 9.1 %collective-permute-start.10 = (bf16[288,256]{1,0:T(8,128)(2,1)S(1)}, bf16[288,256]{1,0:T(8,128)(2,1)S(1)}, u32[]{:S(2)}, u32[]{:S(2)}) collective-permute-start(bf16[288,256]{1,0:T(8,128)(2,1)S(1)} %get-tuple-element.24.first_mine), channel_id=1, source_target_pairs={{16,0},{18,2},{20,4},{22,6},{24,8},{26,10},{28,12},{30,14}} | collective-permute-start | bytes 442376 | tf_op jit(solution)/shard_map/ppermute | solution.py:496
  81.6 8.4 %collective-permute-start.12 = (bf16[256,256]{1,0:T(8,128)(2,1)S(1)}, bf16[256,256]{1,0:T(8,128)(2,1)S(1)}, u32[]{:S(2)}, u32[]{:S(2)}) collective-permute-start(bf16[256,256]{1,0:T(8,128)(2,1)S(1)} %get-tuple-element.26), channel_id=1, source_target_pairs={{30,0},{15,1},{16,2},{1,3},{18,4},{3,5},{20,6},{5,7},{22,8},{7,9},... | collective-permute-start | bytes 393224 | tf_op jit(solution)/shard_map/ppermute | solution.py:496

commit v8 on v7

--- a/solution.py
+++ b/solution.py
@@ -187,7 +187,7 @@
         copy.wait()
 
 
-def products(a_blocks, b_blocks, weights, scaled, theta):
+def products(a_blocks, b_blocks, weights, scaled, theta, basis):
     blocks = scaled.shape[-1]
 
     def block(place):
@@ -197,6 +197,8 @@
     for n, place in enumerate(a_blocks):
         w = weights[0 if n < 3 else 1 if n < 7 else 2]
         scaled[n * blocks : (n + 1) * blocks, :] = (block(place).astype(F32) * w).astype(BF16)
+    for n in range(4):
+        basis[:, n * blocks : (n + 1) * blocks] = block(a_blocks[3 + n]).T
     for (distance, q), (right, first_row, count, first) in PIECES.items():
         product = dot(
             scaled[first_row * blocks : (first_row + count) * blocks, :],
@@ -253,7 +255,7 @@
                         ] = value.astype(BF16)
                 held.clear()
 
-    projected = dot(basis, matrix[...], ((1,), (0,)))
+    projected = dot(basis[...], matrix[...], ((1,), (0,)))
     slot_id = lax.broadcasted_iota(jnp.int32, projected.shape, 0).astype(F32)
     h, m, l = split3(jnp.where(slot_id < kept, projected, 0.0))
     for n, part in enumerate((h, m, l)):
@@ -294,7 +296,7 @@
 def first_kernel(
     own, here_full, next_full, here_head, after_tail, next_tail,
     iso, iso_three, left, left_three, local,
-    scaled, theta, matrix, proj, work, gate_stage, gates, sems,
+    scaled, theta, basis, matrix, proj, work, gate_stage, gates, sems,
 ):
     x = lax.axis_index("loop") % 2
     c = lax.axis_index("inner") % 2
@@ -324,11 +326,11 @@
                     [get_split(ref, small(ref) + W_ROW) for ref in (one, here_full, three)],
                     scaled,
                     theta,
+                    basis,
                 )
                 for n, ref in enumerate((here_head, two)):
                     local[rest + n * SMALL : rest + (n + 1) * SMALL, :] = ref[small(ref) :, :]
 
-        basis = here_full[0 : 4 * blocks, :].T
         gates_copy.wait()
         copies = []
 
@@ -359,13 +361,13 @@
 
 
 def as_column(row):
-    return jnp.broadcast_to(row, (row.shape[1], row.shape[1])).T
+    return jnp.broadcast_to(row, (128, row.shape[1])).T
 
 
 def second_kernel(
     local, iso_1, iso_2, left_0, left_1, left_2,
     mid, last, first, whole,
-    scaled, theta, matrix, proj, work, gate_stage, gates, sems, iso, left,
+    scaled, theta, basis, matrix, proj, work, gate_stage, gates, sems, iso, left, columns,
 ):
     x = lax.axis_index("loop") % 2
     c = lax.axis_index("inner") % 2
@@ -393,21 +395,24 @@
             ],
             scaled,
             theta,
+            basis,
         )
-        basis = jnp.concatenate(
-            [ref[n * blocks : (n + 1) * blocks, :] for ref, n in here], axis=0
-        ).T
+        levels = [get_split(ref, small(ref) + LEVEL_ROW) for ref in (local, iso_1, iso_2)]
+        for n, value in enumerate(levels):
+            columns[n * blocks : (n + 1) * blocks, :] = as_column(value)
         gates_copy.wait()
         level = bond_body(
             basis, kept, theta, matrix, proj, work, iso, left, gates, lambda: None
         )
-        levels = [get_split(ref, small(ref) + LEVEL_ROW) for ref in (local, iso_1, iso_2)]
-        column = as_column(level)
+        column = jnp.concatenate([as_column(level)] * 2, axis=1)
         for ref, lo, hi in ((last, 3, 4), (mid, 1, 3), (first, 0, 1)):
             for p in range(lo, hi):
                 value = iso[p * blocks : (p + 1) * blocks, :].astype(F32) * column
                 ref[(p - lo) * blocks : (p - lo + 1) * blocks, :] = value.astype(BF16)
-        scales = [as_column(value) for value in levels]
+        scales = [
+            jnp.concatenate([columns[n * blocks : (n + 1) * blocks, :]] * 2, axis=1)
+            for n in range(3)
+        ]
         for p in range(4):
             rows = slice(p * blocks, (p + 1) * blocks)
             whole[rows, :] = (left[rows, :].astype(F32) * scales[CHARGE[p]]).astype(BF16)
@@ -458,6 +463,7 @@
     return [
         pltpu.VMEM((10 * blocks, blocks), BF16),
         pltpu.VMEM((SLOT_COUNT * blocks, blocks), BF16),
+        pltpu.VMEM((blocks, 4 * blocks), BF16),
         pltpu.VMEM((4 * blocks, 4 * blocks), BF16),
         pltpu.VMEM((3 * blocks, 4 * blocks), BF16),
         pltpu.VMEM((blocks, 2 * blocks), F32),
@@ -551,7 +557,9 @@
         out_shape=(rows(2), rows(1), rows(1, SMALL), rows(4, SMALL)),
         in_specs=[vmem()] * 6,
         out_specs=(vmem(),) * 4,
-        scratch_shapes=scratch(blocks) + [pltpu.VMEM((4 * blocks, blocks), BF16)] * 2,
+        scratch_shapes=scratch(blocks)
+        + [pltpu.VMEM((4 * blocks, blocks), BF16)] * 2
+        + [pltpu.VMEM((3 * blocks, 128), F32)],
         compiler_params=params(),
         name="second_bond",
     )(local_r, iso_1, iso_2, left_0, left_1, left_2)

time: 92.3 us -> 92.1 us (level)
  no operation moved by 1% of the time
where the time goes in v8:
time: 92.1 us; the launch traced here: 91.5 us
  waiting for transfers between devices  48.1 us (52%)
  starting transfers between devices  24.4 us (26%)
  Pallas kernels  14.9 us (16%)
  local copies, waits for them, and re-layouts  2.41 us (3%)
  between operations  1.61 us (2%)
    ppermute x14, waiting for transfers between devices, send(): return lax.ppermute(value, AXES, route)  48.1 us
    ppermute x14, starting transfers between devices, send(): return lax.ppermute(value, AXES, route)  24.4 us
    pallas_call x1, Pallas kernels, per_device(): pl.pallas_call(second_kernel, out_shape=(rows(2), rows(1), rows(1, SMALL)...  12.9 us
    unnamed x6, local copies, waits for them, and re-layouts  2.41 us
  transfers between devices with their start and end apart: 14, of which 4 were waited for; matrix products, arithmetic and copies ran while one was open for 0% of the time, Pallas kernels for 0%

profile of v8, /device:TPU:1, one launch (start us, length us, event | category | flops | bytes accessed | tf_op | source)
XLA Modules:
  0.0 91.5 jit_solution(1491092814243907927)
XLA Ops:
  1.3 0.0 copy-start.2
  1.3 0.7 copy-done.2
  2.0 0.0 copy-start
  2.0 1.0 %copy-done = bf16[1,1,4,256,256]{4,3,2,1,0:T(8,128)(2,1)S(1)} copy-done((bf16[1,1,4,256,256]{4,3,2,1,0:T(8,128)(2,1)S(1)}, bf16[1,1,4,256,256]{4,3,2,1,0:T(8,128)(2,1)}, u32[]{:S(2)}) %copy-start) | copy-done | bytes 524312
  3.0 0.0 copy-start.1
  3.0 0.7 copy-done.1
  3.7 0.6 prepare.1
  4.3 4.9 %collective-permute-start.1 = (bf16[1056,256]{1,0:T(8,128)(2,1)S(1)}, bf16[1056,256]{1,0:T(8,128)(2,1)S(1)}, u32[]{:S(2)}, u32[]{:S(2)}) collective-permute-start(bf16[1056,256]{1,0:T(8,128)(2,1)S(1)} %get-tuple-element.16.own), channel_id=1, source_target_pairs={{18,0},{20,2},{22,4},{24,6},{26,8},{28,10},{30,12},{16,14},{15,17}... | collective-permute-start | bytes 1622024 | tf_op jit(solution)/shard_map/ppermute | solution.py:502
  9.3 1.3 %collective-permute-start = (bf16[1056,256]{1,0:T(8,128)(2,1)S(1)}, bf16[1056,256]{1,0:T(8,128)(2,1)S(1)}, u32[]{:S(2)}, u32[]{:S(2)}) collective-permute-start(bf16[1056,256]{1,0:T(8,128)(2,1)S(1)} %get-tuple-element.16.own), channel_id=1, source_target_pairs={{1,0},{3,2},{5,4},{7,6},{9,8},{11,10},{13,12},{15,14},{0,17},{2,19... | collective-permute-start | bytes 1622024 | tf_op jit(solution)/shard_map/ppermute | solution.py:502
  10.6 0.7 collective-permute-start.2
  11.3 0.7 collective-permute-start.4
  12.0 4.5 %collective-permute-start.3 = (bf16[800,256]{1,0:T(8,128)(2,1)S(1)}, bf16[800,256]{1,0:T(8,128)(2,1)S(1)}, u32[]{:S(2)}, u32[]{:S(2)}) collective-permute-start(bf16[800,256]{1,0:T(8,128)(2,1)S(1)} %get-tuple-element.18), channel_id=1, source_target_pairs={{19,0},{21,2},{23,4},{25,6},{27,8},{29,10},{31,12},{17,14},{1,17},... | collective-permute-start | bytes 1228808 | tf_op jit(solution)/shard_map/ppermute | solution.py:502
  16.5 0.0 collective-permute-done.2.here_head
  16.5 0.0 collective-permute-done.4.next_tail
  16.5 9.2 %collective-permute-done.3.after_tail = bf16[800,256]{1,0:T(8,128)(2,1)S(1)} collective-permute-done((bf16[800,256]{1,0:T(8,128)(2,1)S(1)}, bf16[800,256]{1,0:T(8,128)(2,1)S(1)}, u32[]{:S(2)}, u32[]{:S(2)}) %collective-permute-start.3) | collective-permute-done | bytes 409632 | tf_op jit(solution)/shard_map/ppermute | solution.py:502
  25.7 0.0 collective-permute-done.1.next_full
  25.7 0.0 collective-permute-done.here_full
  25.8 1.3 %collective-permute-start.5 = (bf16[1632,256]{1,0:T(8,128)(2,1)S(1)}, bf16[1632,256]{1,0:T(8,128)(2,1)S(1)}, u32[]{:S(2)}, u32[]{:S(2)}) collective-permute-start(bf16[1632,256]{1,0:T(8,128)(2,1)S(1)} %get-tuple-element.19), channel_id=1, source_target_pairs={{0,1},{2,3},{4,5},{6,7},{8,9},{10,11},{12,13},{14,15},{17,16},{19,... | collective-permute-start | bytes 2506760 | tf_op jit(solution)/shard_map/ppermute | solution.py:502
  27.1 1.3 %collective-permute-start.6 = (bf16[1056,256]{1,0:T(8,128)(2,1)S(1)}, bf16[1056,256]{1,0:T(8,128)(2,1)S(1)}, u32[]{:S(2)}, u32[]{:S(2)}) collective-permute-start(bf16[1056,256]{1,0:T(8,128)(2,1)S(1)} %get-tuple-element.20), channel_id=1, source_target_pairs={{17,1},{19,3},{21,5},{23,7},{25,9},{27,11},{29,13},{31,15},{14,16}... | collective-permute-start | bytes 1622024 | tf_op jit(solution)/shard_map/ppermute | solution.py:502
  28.4 1.3 %collective-permute-start.8 = (bf16[1024,256]{1,0:T(8,128)(2,1)S(1)}, bf16[1024,256]{1,0:T(8,128)(2,1)S(1)}, u32[]{:S(2)}, u32[]{:S(2)}) collective-permute-start(bf16[1024,256]{1,0:T(8,128)(2,1)S(1)} %get-tuple-element.22), channel_id=1, source_target_pairs={{19,1},{21,3},{23,5},{25,7},{27,9},{29,11},{31,13},{17,15},{0,16},... | collective-permute-start | bytes 1572872 | tf_op jit(solution)/shard_map/ppermute | solution.py:502
  29.6 1.3 %collective-permute-start.7 = (bf16[800,256]{1,0:T(8,128)(2,1)S(1)}, bf16[800,256]{1,0:T(8,128)(2,1)S(1)}, u32[]{:S(2)}, u32[]{:S(2)}) collective-permute-start(bf16[800,256]{1,0:T(8,128)(2,1)S(1)} %get-tuple-element.21), channel_id=1, source_target_pairs={{14,1},{0,3},{2,5},{4,7},{6,9},{8,11},{10,13},{12,15},{31,16},{17,... | collective-permute-start | bytes 1228808 | tf_op jit(solution)/shard_map/ppermute | solution.py:502
  30.9 1.3 %collective-permute-start.9 = (bf16[768,256]{1,0:T(8,128)(2,1)S(1)}, bf16[768,256]{1,0:T(8,128)(2,1)S(1)}, u32[]{:S(2)}, u32[]{:S(2)}) collective-permute-start(bf16[768,256]{1,0:T(8,128)(2,1)S(1)} %get-tuple-element.23), channel_id=1, source_target_pairs={{2,1},{4,3},{6,5},{8,7},{10,9},{12,11},{14,13},{0,15},{19,16},{21,... | collective-permute-start | bytes 1179656 | tf_op jit(solution)/shard_map/ppermute | solution.py:502
  32.2 27.6 %collective-permute-done.9.left_2 = bf16[768,256]{1,0:T(8,128)(2,1)S(1)} collective-permute-done((bf16[768,256]{1,0:T(8,128)(2,1)S(1)}, bf16[768,256]{1,0:T(8,128)(2,1)S(1)}, u32[]{:S(2)}, u32[]{:S(2)}) %collective-permute-start.9) | collective-permute-done | bytes 393248 | tf_op jit(solution)/shard_map/ppermute | solution.py:502
  59.8 4.9 %collective-permute-done.7.iso_2 = bf16[800,256]{1,0:T(8,128)(2,1)S(1)} collective-permute-done((bf16[800,256]{1,0:T(8,128)(2,1)S(1)}, bf16[800,256]{1,0:T(8,128)(2,1)S(1)}, u32[]{:S(2)}, u32[]{:S(2)}) %collective-permute-start.7) | collective-permute-done | bytes 409632 | tf_op jit(solution)/shard_map/ppermute | solution.py:502
  64.7 0.0 collective-permute-done.8.left_1
  64.7 0.0 collective-permute-done.6.iso_1
  64.7 0.0 collective-permute-done.5.local.left_0.level_mine
  64.7 12.9 %second_bond.1 = (bf16[512,256]{1,0:T(8,128)(2,1)S(1)}, bf16[256,256]{1,0:T(8,128)(2,1)S(1)}, bf16[288,256]{1,0:T(8,128)(2,1)S(1)}, bf16[1056,256]{1,0:T(8,128)(2,1)S(1)}) custom-call(bf16[1632,256]{1,0:T(8,128)(2,1)S(1)} %collective-permute-done.5.local.left_0.level_mine, bf16[1056,256]{1,0:T(8,128)(2,1)S(1)} %collective-permute-done.6.iso_1, ...), custom_call_target="tpu_custom_call" | custom-call | tf_op jit(solution)/shard_map/second_bond/pallas_call | solution.py:555
  77.5 1.3 %collective-permute-start.13 = (bf16[1056,256]{1,0:T(8,128)(2,1)S(1)}, bf16[1056,256]{1,0:T(8,128)(2,1)S(1)}, u32[]{:S(2)}, u32[]{:S(2)}) collective-permute-start(bf16[1056,256]{1,0:T(8,128)(2,1)S(1)} %get-tuple-element.27.whole_mine), channel_id=1, source_target_pairs={{1,17},{3,19},{5,21},{7,23},{9,25},{11,27},{13,29},{15,31}} | collective-permute-start | bytes 1622024 | tf_op jit(solution)/shard_map/ppermute | solution.py:502
  78.9 1.9 %collective-permute-start.11 = (bf16[512,256]{1,0:T(8,128)(2,1)S(1)}, bf16[512,256]{1,0:T(8,128)(2,1)S(1)}, u32[]{:S(2)}, u32[]{:S(2)}) collective-permute-start(bf16[512,256]{1,0:T(8,128)(2,1)S(1)} %get-tuple-element.25), channel_id=1, source_target_pairs={{15,0},{16,1},{1,2},{18,3},{3,4},{20,5},{5,6},{22,7},{7,8},{24,9},... | collective-permute-start | bytes 786440 | tf_op jit(solution)/shard_map/ppermute | solution.py:502
  80.8 0.7 collective-permute-start.10
  81.5 1.9 %collective-permute-start.12 = (bf16[256,256]{1,0:T(8,128)(2,1)S(1)}, bf16[256,256]{1,0:T(8,128)(2,1)S(1)}, u32[]{:S(2)}, u32[]{:S(2)}) collective-permute-start(bf16[256,256]{1,0:T(8,128)(2,1)S(1)} %get-tuple-element.26), channel_id=1, source_target_pairs={{30,0},{15,1},{16,2},{1,3},{18,4},{3,5},{20,6},{5,7},{22,8},{7,9},... | collective-permute-start | bytes 393224 | tf_op jit(solution)/shard_map/ppermute | solution.py:502
  83.4 6.5 %collective-permute-done.12.last = bf16[256,256]{1,0:T(8,128)(2,1)S(1)} collective-permute-done((bf16[256,256]{1,0:T(8,128)(2,1)S(1)}, bf16[256,256]{1,0:T(8,128)(2,1)S(1)}, u32[]{:S(2)}, u32[]{:S(2)}) %collective-permute-start.12) | collective-permute-done | bytes 131104 | tf_op jit(solution)/shard_map/ppermute | solution.py:502
  89.9 0.0 collective-permute-done.10.first.level_far
  89.9 0.0 collective-permute-done.11.mid
  89.9 0.0 collective-permute-done.13.whole
  89.9 1.4 %assemble.1 = (bf16[1024,256]{1,0:T(8,128)(2,1)}, f32[1,256]{1,0:T(1,128)}) custom-call(bf16[288,256]{1,0:T(8,128)(2,1)S(1)} %get-tuple-element.24.first_mine, bf16[288,256]{1,0:T(8,128)(2,1)S(1)} %collective-permute-done.10.first.level_far, bf16[512,256]{1,0:T(8,128)(2,1)S(1)} %collective-permute-done.11.mid, ...), custom_call_target="tpu_custom_call" | custom-call | tf_op jit(solution)/shard_map/assemble/pallas_call | solution.py:586
  (1 shorter events, 0.0 us)
Async XLA Ops:
  1.3 0.7 copy-start.2
  2.0 1.0 %copy-start = (bf16[1,1,4,256,256]{4,3,2,1,0:T(8,128)(2,1)S(1)}, bf16[1,1,4,256,256]{4,3,2,1,0:T(8,128)(2,1)}, u32[]{:S(2)}) copy-start(bf16[1,1,4,256,256]{4,3,2,1,0:T(8,128)(2,1)} %param.4) | copy-start | bytes 1572868
  3.0 0.7 copy-start.1
  4.3 21.4 %collective-permute-start.1 = (bf16[1056,256]{1,0:T(8,128)(2,1)S(1)}, bf16[1056,256]{1,0:T(8,128)(2,1)S(1)}, u32[]{:S(2)}, u32[]{:S(2)}) collective-permute-start(bf16[1056,256]{1,0:T(8,128)(2,1)S(1)} %get-tuple-element.16.own), channel_id=1, source_target_pairs={{18,0},{20,2},{22,4},{24,6},{26,8},{28,10},{30,12},{16,14},{15,17}... | collective-permute-start | bytes 1622024 | tf_op jit(solution)/shard_map/ppermute | solution.py:502
  9.3 16.4 %collective-permute-start = (bf16[1056,256]{1,0:T(8,128)(2,1)S(1)}, bf16[1056,256]{1,0:T(8,128)(2,1)S(1)}, u32[]{:S(2)}, u32[]{:S(2)}) collective-permute-start(bf16[1056,256]{1,0:T(8,128)(2,1)S(1)} %get-tuple-element.16.own), channel_id=1, source_target_pairs={{1,0},{3,2},{5,4},{7,6},{9,8},{11,10},{13,12},{15,14},{0,17},{2,19... | collective-permute-start | bytes 1622024 | tf_op jit(solution)/shard_map/ppermute | solution.py:502
  10.6 5.9 %collective-permute-start.2 = (bf16[800,256]{1,0:T(8,128)(2,1)S(1)}, bf16[800,256]{1,0:T(8,128)(2,1)S(1)}, u32[]{:S(2)}, u32[]{:S(2)}) collective-permute-start(bf16[800,256]{1,0:T(8,128)(2,1)S(1)} %get-tuple-element.17), channel_id=1, source_target_pairs={{17,0},{19,2},{21,4},{23,6},{25,8},{27,10},{29,12},{31,14},{16,17}... | collective-permute-start | bytes 1228808 | tf_op jit(solution)/shard_map/ppermute | solution.py:502
  11.3 5.2 %collective-permute-start.4 = (bf16[800,256]{1,0:T(8,128)(2,1)S(1)}, bf16[800,256]{1,0:T(8,128)(2,1)S(1)}, u32[]{:S(2)}, u32[]{:S(2)}) collective-permute-start(bf16[800,256]{1,0:T(8,128)(2,1)S(1)} %get-tuple-element.18), channel_id=1, source_target_pairs={{2,0},{4,2},{6,4},{8,6},{10,8},{12,10},{14,12},{0,14},{18,17},{20,... | collective-permute-start | bytes 1228808 | tf_op jit(solution)/shard_map/ppermute | solution.py:502
  12.0 13.7 %collective-permute-start.3 = (bf16[800,256]{1,0:T(8,128)(2,1)S(1)}, bf16[800,256]{1,0:T(8,128)(2,1)S(1)}, u32[]{:S(2)}, u32[]{:S(2)}) collective-permute-start(bf16[800,256]{1,0:T(8,128)(2,1)S(1)} %get-tuple-element.18), channel_id=1, source_target_pairs={{19,0},{21,2},{23,4},{25,6},{27,8},{29,10},{31,12},{17,14},{1,17},... | collective-permute-start | bytes 1228808 | tf_op jit(solution)/shard_map/ppermute | solution.py:502
  25.8 38.9 %collective-permute-start.5 = (bf16[1632,256]{1,0:T(8,128)(2,1)S(1)}, bf16[1632,256]{1,0:T(8,128)(2,1)S(1)}, u32[]{:S(2)}, u32[]{:S(2)}) collective-permute-start(bf16[1632,256]{1,0:T(8,128)(2,1)S(1)} %get-tuple-element.19), channel_id=1, source_target_pairs={{0,1},{2,3},{4,5},{6,7},{8,9},{10,11},{12,13},{14,15},{17,16},{19,... | collective-permute-start | bytes 2506760 | tf_op jit(solution)/shard_map/ppermute | solution.py:502
  27.1 37.6 %collective-permute-start.6 = (bf16[1056,256]{1,0:T(8,128)(2,1)S(1)}, bf16[1056,256]{1,0:T(8,128)(2,1)S(1)}, u32[]{:S(2)}, u32[]{:S(2)}) collective-permute-start(bf16[1056,256]{1,0:T(8,128)(2,1)S(1)} %get-tuple-element.20), channel_id=1, source_target_pairs={{17,1},{19,3},{21,5},{23,7},{25,9},{27,11},{29,13},{31,15},{14,16}... | collective-permute-start | bytes 1622024 | tf_op jit(solution)/shard_map/ppermute | solution.py:502
  28.4 36.3 %collective-permute-start.8 = (bf16[1024,256]{1,0:T(8,128)(2,1)S(1)}, bf16[1024,256]{1,0:T(8,128)(2,1)S(1)}, u32[]{:S(2)}, u32[]{:S(2)}) collective-permute-start(bf16[1024,256]{1,0:T(8,128)(2,1)S(1)} %get-tuple-element.22), channel_id=1, source_target_pairs={{19,1},{21,3},{23,5},{25,7},{27,9},{29,11},{31,13},{17,15},{0,16},... | collective-permute-start | bytes 1572872 | tf_op jit(solution)/shard_map/ppermute | solution.py:502
  29.6 35.0 %collective-permute-start.7 = (bf16[800,256]{1,0:T(8,128)(2,1)S(1)}, bf16[800,256]{1,0:T(8,128)(2,1)S(1)}, u32[]{:S(2)}, u32[]{:S(2)}) collective-permute-start(bf16[800,256]{1,0:T(8,128)(2,1)S(1)} %get-tuple-element.21), channel_id=1, source_target_pairs={{14,1},{0,3},{2,5},{4,7},{6,9},{8,11},{10,13},{12,15},{31,16},{17,... | collective-permute-start | bytes 1228808 | tf_op jit(solution)/shard_map/ppermute | solution.py:502
  30.9 28.9 %collective-permute-start.9 = (bf16[768,256]{1,0:T(8,128)(2,1)S(1)}, bf16[768,256]{1,0:T(8,128)(2,1)S(1)}, u32[]{:S(2)}, u32[]{:S(2)}) collective-permute-start(bf16[768,256]{1,0:T(8,128)(2,1)S(1)} %get-tuple-element.23), channel_id=1, source_target_pairs={{2,1},{4,3},{6,5},{8,7},{10,9},{12,11},{14,13},{0,15},{19,16},{21,... | collective-permute-start | bytes 1179656 | tf_op jit(solution)/shard_map/ppermute | solution.py:502
  77.5 12.4 %collective-permute-start.13 = (bf16[1056,256]{1,0:T(8,128)(2,1)S(1)}, bf16[1056,256]{1,0:T(8,128)(2,1)S(1)}, u32[]{:S(2)}, u32[]{:S(2)}) collective-permute-start(bf16[1056,256]{1,0:T(8,128)(2,1)S(1)} %get-tuple-element.27.whole_mine), channel_id=1, source_target_pairs={{1,17},{3,19},{5,21},{7,23},{9,25},{11,27},{13,29},{15,31}} | collective-permute-start | bytes 1622024 | tf_op jit(solution)/shard_map/ppermute | solution.py:502
  78.9 11.0 %collective-permute-start.11 = (bf16[512,256]{1,0:T(8,128)(2,1)S(1)}, bf16[512,256]{1,0:T(8,128)(2,1)S(1)}, u32[]{:S(2)}, u32[]{:S(2)}) collective-permute-start(bf16[512,256]{1,0:T(8,128)(2,1)S(1)} %get-tuple-element.25), channel_id=1, source_target_pairs={{15,0},{16,1},{1,2},{18,3},{3,4},{20,5},{5,6},{22,7},{7,8},{24,9},... | collective-permute-start | bytes 786440 | tf_op jit(solution)/shard_map/ppermute | solution.py:502
  80.8 9.1 %collective-permute-start.10 = (bf16[288,256]{1,0:T(8,128)(2,1)S(1)}, bf16[288,256]{1,0:T(8,128)(2,1)S(1)}, u32[]{:S(2)}, u32[]{:S(2)}) collective-permute-start(bf16[288,256]{1,0:T(8,128)(2,1)S(1)} %get-tuple-element.24.first_mine), channel_id=1, source_target_pairs={{16,0},{18,2},{20,4},{22,6},{24,8},{26,10},{28,12},{30,14}} | collective-permute-start | bytes 442376 | tf_op jit(solution)/shard_map/ppermute | solution.py:502
  81.5 8.4 %collective-permute-start.12 = (bf16[256,256]{1,0:T(8,128)(2,1)S(1)}, bf16[256,256]{1,0:T(8,128)(2,1)S(1)}, u32[]{:S(2)}, u32[]{:S(2)}) collective-permute-start(bf16[256,256]{1,0:T(8,128)(2,1)S(1)} %get-tuple-element.26), channel_id=1, source_target_pairs={{30,0},{15,1},{16,2},{1,3},{18,4},{3,5},{20,6},{5,7},{22,8},{7,9},... | collective-permute-start | bytes 393224 | tf_op jit(solution)/shard_map/ppermute | solution.py:502

commit v9 on v8

--- a/solution.py
+++ b/solution.py
@@ -366,7 +366,7 @@
 
 def second_kernel(
     local, iso_1, iso_2, left_0, left_1, left_2,
-    mid, last, first, whole,
+    mid, last, three, whole,
     scaled, theta, basis, matrix, proj, work, gate_stage, gates, sems, iso, left, columns,
 ):
     x = lax.axis_index("loop") % 2
@@ -405,10 +405,12 @@
             basis, kept, theta, matrix, proj, work, iso, left, gates, lambda: None
         )
         column = jnp.concatenate([as_column(level)] * 2, axis=1)
-        for ref, lo, hi in ((last, 3, 4), (mid, 1, 3), (first, 0, 1)):
-            for p in range(lo, hi):
-                value = iso[p * blocks : (p + 1) * blocks, :].astype(F32) * column
-                ref[(p - lo) * blocks : (p - lo + 1) * blocks, :] = value.astype(BF16)
+        for p in range(4):
+            value = iso[p * blocks : (p + 1) * blocks, :].astype(F32) * column
+            value = value.astype(BF16)
+            for ref, lo, hi in ((last, 3, 4), (mid, 1, 3), (three, 0, 3)):
+                if lo <= p < hi:
+                    ref[(p - lo) * blocks : (p - lo + 1) * blocks, :] = value
         scales = [
             jnp.concatenate([columns[n * blocks : (n + 1) * blocks, :]] * 2, axis=1)
             for n in range(3)
@@ -416,7 +418,7 @@
         for p in range(4):
             rows = slice(p * blocks, (p + 1) * blocks)
             whole[rows, :] = (left[rows, :].astype(F32) * scales[CHARGE[p]]).astype(BF16)
-        for ref, value in ((first, levels[0]), (whole, level)):
+        for ref, value in ((three, levels[0]), (whole, level)):
             ref[small(ref) :, :] = jnp.zeros((SMALL, blocks), BF16)
             put_split(ref, small(ref) + LEVEL_ROW, value)
 
@@ -425,11 +427,11 @@
     blocks = out.shape[-1]
     half = blocks // 2
     copies = []
-    for source, to, count in plan:
+    for source, at, to, count in plan:
         for n in range(2 * count):
             copies.append(
                 pltpu.make_async_copy(
-                    source.at[pl.ds(n * half, half)],
+                    source.at[pl.ds(at * blocks + n * half, half)],
                     out.at[pl.ds(to * blocks + n * half, half)],
                     sems.at[len(copies)],
                 )
@@ -439,16 +441,15 @@
 
 
 def assemble(
-    first_mine, first, mid, last, whole_mine, whole, level_mine, level_far, out, weights, sems
+    three_mine, three, mid, handed, last, whole_mine, whole, level_mine, level_far, out, weights, sems
 ):
     x = lax.axis_index("loop") % 2
     c = lax.axis_index("inner") % 2
-    even = [(mid, 1, 2), (last, 3, 1)]
     for role, core, plan, level in (
-        (0, 0, [(first, 0, 1)] + even, level_far),
-        (0, 1, [(first_mine, 0, 1)] + even, level_mine),
-        (1, 0, [(whole_mine, 0, 4)], whole_mine),
-        (1, 1, [(whole, 0, 4)], whole),
+        (0, 0, [(three, 0, 0, 1), (mid, 0, 1, 2), (last, 0, 3, 1)], level_far),
+        (0, 1, [(three_mine, 0, 0, 1), (handed, 1, 1, 2), (last, 0, 3, 1)], level_mine),
+        (1, 0, [(whole_mine, 0, 0, 4)], whole_mine),
+        (1, 1, [(whole, 0, 0, 4)], whole),
     ):
 
         @pl.when(jnp.logical_and(x == role, c == core))
@@ -552,9 +553,9 @@
     else:
         left_0 = send(left_msg[: 3 * blocks], to_second(lambda l, k: worker(l, k, 1, 0)))
 
-    mid, last, first, whole = pl.pallas_call(
+    mid, last, three, whole = pl.pallas_call(
         second_kernel,
-        out_shape=(rows(2), rows(1), rows(1, SMALL), rows(4, SMALL)),
+        out_shape=(rows(2), rows(1), rows(3, SMALL), rows(4, SMALL)),
         in_specs=[vmem()] * 6,
         out_specs=(vmem(),) * 4,
         scratch_shapes=scratch(blocks)
@@ -572,26 +573,27 @@
     def right_from(s, cores):
         return lambda l, i: from_second(l, i, 1, s) if l % 2 == 0 and i % 2 in cores else None
 
-    first_r = send(first, right_from(0, (0,) if loops == 2 else (0, 1)))
-    mid_r = send(mid, right_from(1, (0, 1)))
+    three_r = send(three, right_from(0, (0,)))
+    mid_r = send(mid, right_from(1, (0,)))
     last_r = send(last, right_from(2, (0, 1)))
     whole_r = send(whole, lambda l, i: from_second(l, i, 0, 0) if l % 2 and i % 2 else None)
+    handed = send(three_r, lambda l, i: (l, i - 1) if l % 2 == 0 and i % 2 else None)
     if loops == 2:
-        first_mine, level_far = first, first_r
+        three_mine, level_far = three, three_r
     else:
-        first_mine = first_r
+        three_mine = send(three, right_from(0, (1,)))
         level_far = send(
             iso_msg[4 * blocks :], lambda l, i: (l + 1, i + 1) if l % 2 == 0 and i % 2 == 0 else None
         )
     sites, weights = pl.pallas_call(
         assemble,
         out_shape=(rows(4), jax.ShapeDtypeStruct((1, blocks), F32)),
-        in_specs=[vmem()] * 8,
+        in_specs=[vmem()] * 9,
         out_specs=(hbm(), vmem()),
         scratch_shapes=[pltpu.SemaphoreType.DMA((8,))],
         compiler_params=params(),
         name="assemble",
-    )(first_mine, first_r, mid_r, last_r, whole, whole_r, local_r, level_far)
+    )(three_mine, three_r, mid_r, handed, last_r, whole, whole_r, local_r, level_far)
     return sites.reshape(1, 1, 4, blocks, blocks), weights[None]
 
 

time: 92.1 us -> 102 us (1.11)
  starting transfers between devices: 24.4 us -> 31 us
  waiting for transfers between devices: 48.1 us -> 51 us
    ppermute x14 -> x15, starting transfers between devices: 24.4 us -> 31 us  [send(): return lax.ppermute(value, AXES, route)]
    ppermute x14 -> x15, waiting for transfers between devices: 48.1 us -> 51 us  [send(): return lax.ppermute(value, AXES, route)]
  transfers between devices with their start and end apart: 14 -> 15, of which waited for: 4 -> 4; matrix products, arithmetic and copies ran while one was open for 0% -> 0% of each run, Pallas kernels for 0% -> 0%
where the time goes in v9:
time: 102 us; the launch traced here: 101 us
  waiting for transfers between devices  51 us (50%)
  starting transfers between devices  31 us (30%)
  Pallas kernels  15 us (15%)
  local copies, waits for them, and re-layouts  2.41 us (2%)
  between operations  1.63 us (2%)
    ppermute x15, waiting for transfers between devices, send(): return lax.ppermute(value, AXES, route)  51 us
    ppermute x15, starting transfers between devices, send(): return lax.ppermute(value, AXES, route)  31 us
    pallas_call x1, Pallas kernels, per_device(): pl.pallas_call(second_kernel, out_shape=(rows(2), rows(1), rows(3, SMALL)...  12.9 us
    unnamed x6, local copies, waits for them, and re-layouts  2.41 us
  transfers between devices with their start and end apart: 15, of which 4 were waited for; matrix products, arithmetic and copies ran while one was open for 0% of the time, Pallas kernels for 0%

profile of v9, /device:TPU:1, one launch (start us, length us, event | category | flops | bytes accessed | tf_op | source)
XLA Modules:
  0.0 101.0 jit_solution(2129714179826869344)
XLA Ops:
  1.3 0.0 copy-start.2
  1.3 0.7 copy-done.2
  2.0 0.0 copy-start
  2.0 1.0 %copy-done = bf16[1,1,4,256,256]{4,3,2,1,0:T(8,128)(2,1)S(1)} copy-done((bf16[1,1,4,256,256]{4,3,2,1,0:T(8,128)(2,1)S(1)}, bf16[1,1,4,256,256]{4,3,2,1,0:T(8,128)(2,1)}, u32[]{:S(2)}) %copy-start) | copy-done | bytes 524312
  3.0 0.0 copy-start.1
  3.0 0.7 copy-done.1
  3.7 0.6 prepare.1
  4.3 4.9 %collective-permute-start.1 = (bf16[1056,256]{1,0:T(8,128)(2,1)S(1)}, bf16[1056,256]{1,0:T(8,128)(2,1)S(1)}, u32[]{:S(2)}, u32[]{:S(2)}) collective-permute-start(bf16[1056,256]{1,0:T(8,128)(2,1)S(1)} %get-tuple-element.16.own), channel_id=1, source_target_pairs={{18,0},{20,2},{22,4},{24,6},{26,8},{28,10},{30,12},{16,14},{15,17}... | collective-permute-start | bytes 1622024 | tf_op jit(solution)/shard_map/ppermute | solution.py:503
  9.3 1.3 %collective-permute-start = (bf16[1056,256]{1,0:T(8,128)(2,1)S(1)}, bf16[1056,256]{1,0:T(8,128)(2,1)S(1)}, u32[]{:S(2)}, u32[]{:S(2)}) collective-permute-start(bf16[1056,256]{1,0:T(8,128)(2,1)S(1)} %get-tuple-element.16.own), channel_id=1, source_target_pairs={{1,0},{3,2},{5,4},{7,6},{9,8},{11,10},{13,12},{15,14},{0,17},{2,19... | collective-permute-start | bytes 1622024 | tf_op jit(solution)/shard_map/ppermute | solution.py:503
  10.6 0.7 collective-permute-start.2
  11.3 0.7 collective-permute-start.4
  12.0 4.5 %collective-permute-start.3 = (bf16[800,256]{1,0:T(8,128)(2,1)S(1)}, bf16[800,256]{1,0:T(8,128)(2,1)S(1)}, u32[]{:S(2)}, u32[]{:S(2)}) collective-permute-start(bf16[800,256]{1,0:T(8,128)(2,1)S(1)} %get-tuple-element.18), channel_id=1, source_target_pairs={{19,0},{21,2},{23,4},{25,6},{27,8},{29,10},{31,12},{17,14},{1,17},... | collective-permute-start | bytes 1228808 | tf_op jit(solution)/shard_map/ppermute | solution.py:503
  16.5 0.0 collective-permute-done.2.here_head
  16.5 0.0 collective-permute-done.4.next_tail
  16.5 9.2 %collective-permute-done.3.after_tail = bf16[800,256]{1,0:T(8,128)(2,1)S(1)} collective-permute-done((bf16[800,256]{1,0:T(8,128)(2,1)S(1)}, bf16[800,256]{1,0:T(8,128)(2,1)S(1)}, u32[]{:S(2)}, u32[]{:S(2)}) %collective-permute-start.3) | collective-permute-done | bytes 409632 | tf_op jit(solution)/shard_map/ppermute | solution.py:503
  25.7 0.0 collective-permute-done.1.next_full
  25.7 0.0 collective-permute-done.here_full
  25.8 1.3 %collective-permute-start.5 = (bf16[1632,256]{1,0:T(8,128)(2,1)S(1)}, bf16[1632,256]{1,0:T(8,128)(2,1)S(1)}, u32[]{:S(2)}, u32[]{:S(2)}) collective-permute-start(bf16[1632,256]{1,0:T(8,128)(2,1)S(1)} %get-tuple-element.19), channel_id=1, source_target_pairs={{0,1},{2,3},{4,5},{6,7},{8,9},{10,11},{12,13},{14,15},{17,16},{19,... | collective-permute-start | bytes 2506760 | tf_op jit(solution)/shard_map/ppermute | solution.py:503
  27.1 1.3 %collective-permute-start.6 = (bf16[1056,256]{1,0:T(8,128)(2,1)S(1)}, bf16[1056,256]{1,0:T(8,128)(2,1)S(1)}, u32[]{:S(2)}, u32[]{:S(2)}) collective-permute-start(bf16[1056,256]{1,0:T(8,128)(2,1)S(1)} %get-tuple-element.20), channel_id=1, source_target_pairs={{17,1},{19,3},{21,5},{23,7},{25,9},{27,11},{29,13},{31,15},{14,16}... | collective-permute-start | bytes 1622024 | tf_op jit(solution)/shard_map/ppermute | solution.py:503
  28.4 1.3 %collective-permute-start.8 = (bf16[1024,256]{1,0:T(8,128)(2,1)S(1)}, bf16[1024,256]{1,0:T(8,128)(2,1)S(1)}, u32[]{:S(2)}, u32[]{:S(2)}) collective-permute-start(bf16[1024,256]{1,0:T(8,128)(2,1)S(1)} %get-tuple-element.22), channel_id=1, source_target_pairs={{19,1},{21,3},{23,5},{25,7},{27,9},{29,11},{31,13},{17,15},{0,16},... | collective-permute-start | bytes 1572872 | tf_op jit(solution)/shard_map/ppermute | solution.py:503
  29.6 1.3 %collective-permute-start.7 = (bf16[800,256]{1,0:T(8,128)(2,1)S(1)}, bf16[800,256]{1,0:T(8,128)(2,1)S(1)}, u32[]{:S(2)}, u32[]{:S(2)}) collective-permute-start(bf16[800,256]{1,0:T(8,128)(2,1)S(1)} %get-tuple-element.21), channel_id=1, source_target_pairs={{14,1},{0,3},{2,5},{4,7},{6,9},{8,11},{10,13},{12,15},{31,16},{17,... | collective-permute-start | bytes 1228808 | tf_op jit(solution)/shard_map/ppermute | solution.py:503
  30.9 1.3 %collective-permute-start.9 = (bf16[768,256]{1,0:T(8,128)(2,1)S(1)}, bf16[768,256]{1,0:T(8,128)(2,1)S(1)}, u32[]{:S(2)}, u32[]{:S(2)}) collective-permute-start(bf16[768,256]{1,0:T(8,128)(2,1)S(1)} %get-tuple-element.23), channel_id=1, source_target_pairs={{2,1},{4,3},{6,5},{8,7},{10,9},{12,11},{14,13},{0,15},{19,16},{21,... | collective-permute-start | bytes 1179656 | tf_op jit(solution)/shard_map/ppermute | solution.py:503
  32.2 27.6 %collective-permute-done.9.left_2 = bf16[768,256]{1,0:T(8,128)(2,1)S(1)} collective-permute-done((bf16[768,256]{1,0:T(8,128)(2,1)S(1)}, bf16[768,256]{1,0:T(8,128)(2,1)S(1)}, u32[]{:S(2)}, u32[]{:S(2)}) %collective-permute-start.9) | collective-permute-done | bytes 393248 | tf_op jit(solution)/shard_map/ppermute | solution.py:503
  59.8 4.9 %collective-permute-done.7.iso_2 = bf16[800,256]{1,0:T(8,128)(2,1)S(1)} collective-permute-done((bf16[800,256]{1,0:T(8,128)(2,1)S(1)}, bf16[800,256]{1,0:T(8,128)(2,1)S(1)}, u32[]{:S(2)}, u32[]{:S(2)}) %collective-permute-start.7) | collective-permute-done | bytes 409632 | tf_op jit(solution)/shard_map/ppermute | solution.py:503
  64.7 0.0 collective-permute-done.8.left_1
  64.7 0.0 collective-permute-done.6.iso_1
  64.7 0.0 collective-permute-done.5.local.left_0.level_mine
  64.7 12.9 %second_bond.1 = (bf16[512,256]{1,0:T(8,128)(2,1)S(1)}, bf16[256,256]{1,0:T(8,128)(2,1)S(1)}, bf16[800,256]{1,0:T(8,128)(2,1)S(1)}, bf16[1056,256]{1,0:T(8,128)(2,1)S(1)}) custom-call(bf16[1632,256]{1,0:T(8,128)(2,1)S(1)} %collective-permute-done.5.local.left_0.level_mine, bf16[1056,256]{1,0:T(8,128)(2,1)S(1)} %collective-permute-done.6.iso_1, ...), custom_call_target="tpu_custom_call" | custom-call | tf_op jit(solution)/shard_map/second_bond/pallas_call | solution.py:556
  77.6 0.7 collective-permute-start.10
  78.3 1.3 %collective-permute-start.14 = (bf16[1056,256]{1,0:T(8,128)(2,1)S(1)}, bf16[1056,256]{1,0:T(8,128)(2,1)S(1)}, u32[]{:S(2)}, u32[]{:S(2)}) collective-permute-start(bf16[1056,256]{1,0:T(8,128)(2,1)S(1)} %get-tuple-element.27.whole_mine), channel_id=1, source_target_pairs={{1,17},{3,19},{5,21},{7,23},{9,25},{11,27},{13,29},{15,31}} | collective-permute-start | bytes 1622024 | tf_op jit(solution)/shard_map/ppermute | solution.py:503
  79.6 0.0 collective-permute-done.10.three.level_far
  79.6 1.3 %collective-permute-start.12 = (bf16[800,256]{1,0:T(8,128)(2,1)S(1)}, bf16[800,256]{1,0:T(8,128)(2,1)S(1)}, u32[]{:S(2)}, u32[]{:S(2)}) collective-permute-start(bf16[800,256]{1,0:T(8,128)(2,1)S(1)} %collective-permute-done.10.three.level_far), channel_id=1, source_target_pairs={{0,1},{2,3},{4,5},{6,7},{8,9},{10,11},{12,13},{14,15}} | collective-permute-start | bytes 1228808 | tf_op jit(solution)/shard_map/ppermute | solution.py:503
  80.9 4.8 %collective-permute-start.11 = (bf16[512,256]{1,0:T(8,128)(2,1)S(1)}, bf16[512,256]{1,0:T(8,128)(2,1)S(1)}, u32[]{:S(2)}, u32[]{:S(2)}) collective-permute-start(bf16[512,256]{1,0:T(8,128)(2,1)S(1)} %get-tuple-element.25), channel_id=1, source_target_pairs={{15,0},{1,2},{3,4},{5,6},{7,8},{9,10},{11,12},{13,14}} | collective-permute-start | bytes 786440 | tf_op jit(solution)/shard_map/ppermute | solution.py:503
  85.7 4.4 %collective-permute-start.13 = (bf16[256,256]{1,0:T(8,128)(2,1)S(1)}, bf16[256,256]{1,0:T(8,128)(2,1)S(1)}, u32[]{:S(2)}, u32[]{:S(2)}) collective-permute-start(bf16[256,256]{1,0:T(8,128)(2,1)S(1)} %get-tuple-element.26), channel_id=1, source_target_pairs={{30,0},{15,1},{16,2},{1,3},{18,4},{3,5},{20,6},{5,7},{22,8},{7,9},... | collective-permute-start | bytes 393224 | tf_op jit(solution)/shard_map/ppermute | solution.py:503
  90.1 9.3 %collective-permute-done.13.last = bf16[256,256]{1,0:T(8,128)(2,1)S(1)} collective-permute-done((bf16[256,256]{1,0:T(8,128)(2,1)S(1)}, bf16[256,256]{1,0:T(8,128)(2,1)S(1)}, u32[]{:S(2)}, u32[]{:S(2)}) %collective-permute-start.13) | collective-permute-done | bytes 131104 | tf_op jit(solution)/shard_map/ppermute | solution.py:503
  99.4 0.0 collective-permute-done.11.mid
  99.4 0.0 collective-permute-done.14.whole
  99.4 0.0 collective-permute-done.12.handed
  99.4 1.4 %assemble.1 = (bf16[1024,256]{1,0:T(8,128)(2,1)}, f32[1,256]{1,0:T(1,128)}) custom-call(bf16[800,256]{1,0:T(8,128)(2,1)S(1)} %get-tuple-element.24.three_mine, bf16[800,256]{1,0:T(8,128)(2,1)S(1)} %collective-permute-done.10.three.level_far, bf16[512,256]{1,0:T(8,128)(2,1)S(1)} %collective-permute-done.11.mid, ...), custom_call_target="tpu_custom_call" | custom-call | tf_op jit(solution)/shard_map/assemble/pallas_call | solution.py:588
  (1 shorter events, 0.0 us)
Async XLA Ops:
  1.3 0.7 copy-start.2
  2.0 1.0 %copy-start = (bf16[1,1,4,256,256]{4,3,2,1,0:T(8,128)(2,1)S(1)}, bf16[1,1,4,256,256]{4,3,2,1,0:T(8,128)(2,1)}, u32[]{:S(2)}) copy-start(bf16[1,1,4,256,256]{4,3,2,1,0:T(8,128)(2,1)} %param.4) | copy-start | bytes 1572868
  3.0 0.7 copy-start.1
  4.3 21.4 %collective-permute-start.1 = (bf16[1056,256]{1,0:T(8,128)(2,1)S(1)}, bf16[1056,256]{1,0:T(8,128)(2,1)S(1)}, u32[]{:S(2)}, u32[]{:S(2)}) collective-permute-start(bf16[1056,256]{1,0:T(8,128)(2,1)S(1)} %get-tuple-element.16.own), channel_id=1, source_target_pairs={{18,0},{20,2},{22,4},{24,6},{26,8},{28,10},{30,12},{16,14},{15,17}... | collective-permute-start | bytes 1622024 | tf_op jit(solution)/shard_map/ppermute | solution.py:503
  9.3 16.4 %collective-permute-start = (bf16[1056,256]{1,0:T(8,128)(2,1)S(1)}, bf16[1056,256]{1,0:T(8,128)(2,1)S(1)}, u32[]{:S(2)}, u32[]{:S(2)}) collective-permute-start(bf16[1056,256]{1,0:T(8,128)(2,1)S(1)} %get-tuple-element.16.own), channel_id=1, source_target_pairs={{1,0},{3,2},{5,4},{7,6},{9,8},{11,10},{13,12},{15,14},{0,17},{2,19... | collective-permute-start | bytes 1622024 | tf_op jit(solution)/shard_map/ppermute | solution.py:503
  10.6 5.9 %collective-permute-start.2 = (bf16[800,256]{1,0:T(8,128)(2,1)S(1)}, bf16[800,256]{1,0:T(8,128)(2,1)S(1)}, u32[]{:S(2)}, u32[]{:S(2)}) collective-permute-start(bf16[800,256]{1,0:T(8,128)(2,1)S(1)} %get-tuple-element.17), channel_id=1, source_target_pairs={{17,0},{19,2},{21,4},{23,6},{25,8},{27,10},{29,12},{31,14},{16,17}... | collective-permute-start | bytes 1228808 | tf_op jit(solution)/shard_map/ppermute | solution.py:503
  11.3 5.2 %collective-permute-start.4 = (bf16[800,256]{1,0:T(8,128)(2,1)S(1)}, bf16[800,256]{1,0:T(8,128)(2,1)S(1)}, u32[]{:S(2)}, u32[]{:S(2)}) collective-permute-start(bf16[800,256]{1,0:T(8,128)(2,1)S(1)} %get-tuple-element.18), channel_id=1, source_target_pairs={{2,0},{4,2},{6,4},{8,6},{10,8},{12,10},{14,12},{0,14},{18,17},{20,... | collective-permute-start | bytes 1228808 | tf_op jit(solution)/shard_map/ppermute | solution.py:503
  12.0 13.7 %collective-permute-start.3 = (bf16[800,256]{1,0:T(8,128)(2,1)S(1)}, bf16[800,256]{1,0:T(8,128)(2,1)S(1)}, u32[]{:S(2)}, u32[]{:S(2)}) collective-permute-start(bf16[800,256]{1,0:T(8,128)(2,1)S(1)} %get-tuple-element.18), channel_id=1, source_target_pairs={{19,0},{21,2},{23,4},{25,6},{27,8},{29,10},{31,12},{17,14},{1,17},... | collective-permute-start | bytes 1228808 | tf_op jit(solution)/shard_map/ppermute | solution.py:503
  25.8 38.9 %collective-permute-start.5 = (bf16[1632,256]{1,0:T(8,128)(2,1)S(1)}, bf16[1632,256]{1,0:T(8,128)(2,1)S(1)}, u32[]{:S(2)}, u32[]{:S(2)}) collective-permute-start(bf16[1632,256]{1,0:T(8,128)(2,1)S(1)} %get-tuple-element.19), channel_id=1, source_target_pairs={{0,1},{2,3},{4,5},{6,7},{8,9},{10,11},{12,13},{14,15},{17,16},{19,... | collective-permute-start | bytes 2506760 | tf_op jit(solution)/shard_map/ppermute | solution.py:503
  27.1 37.6 %collective-permute-start.6 = (bf16[1056,256]{1,0:T(8,128)(2,1)S(1)}, bf16[1056,256]{1,0:T(8,128)(2,1)S(1)}, u32[]{:S(2)}, u32[]{:S(2)}) collective-permute-start(bf16[1056,256]{1,0:T(8,128)(2,1)S(1)} %get-tuple-element.20), channel_id=1, source_target_pairs={{17,1},{19,3},{21,5},{23,7},{25,9},{27,11},{29,13},{31,15},{14,16}... | collective-permute-start | bytes 1622024 | tf_op jit(solution)/shard_map/ppermute | solution.py:503
  28.4 36.3 %collective-permute-start.8 = (bf16[1024,256]{1,0:T(8,128)(2,1)S(1)}, bf16[1024,256]{1,0:T(8,128)(2,1)S(1)}, u32[]{:S(2)}, u32[]{:S(2)}) collective-permute-start(bf16[1024,256]{1,0:T(8,128)(2,1)S(1)} %get-tuple-element.22), channel_id=1, source_target_pairs={{19,1},{21,3},{23,5},{25,7},{27,9},{29,11},{31,13},{17,15},{0,16},... | collective-permute-start | bytes 1572872 | tf_op jit(solution)/shard_map/ppermute | solution.py:503
  29.6 35.0 %collective-permute-start.7 = (bf16[800,256]{1,0:T(8,128)(2,1)S(1)}, bf16[800,256]{1,0:T(8,128)(2,1)S(1)}, u32[]{:S(2)}, u32[]{:S(2)}) collective-permute-start(bf16[800,256]{1,0:T(8,128)(2,1)S(1)} %get-tuple-element.21), channel_id=1, source_target_pairs={{14,1},{0,3},{2,5},{4,7},{6,9},{8,11},{10,13},{12,15},{31,16},{17,... | collective-permute-start | bytes 1228808 | tf_op jit(solution)/shard_map/ppermute | solution.py:503
  30.9 28.9 %collective-permute-start.9 = (bf16[768,256]{1,0:T(8,128)(2,1)S(1)}, bf16[768,256]{1,0:T(8,128)(2,1)S(1)}, u32[]{:S(2)}, u32[]{:S(2)}) collective-permute-start(bf16[768,256]{1,0:T(8,128)(2,1)S(1)} %get-tuple-element.23), channel_id=1, source_target_pairs={{2,1},{4,3},{6,5},{8,7},{10,9},{12,11},{14,13},{0,15},{19,16},{21,... | collective-permute-start | bytes 1179656 | tf_op jit(solution)/shard_map/ppermute | solution.py:503
  77.6 2.0 %collective-permute-start.10 = (bf16[800,256]{1,0:T(8,128)(2,1)S(1)}, bf16[800,256]{1,0:T(8,128)(2,1)S(1)}, u32[]{:S(2)}, u32[]{:S(2)}) collective-permute-start(bf16[800,256]{1,0:T(8,128)(2,1)S(1)} %get-tuple-element.24.three_mine), channel_id=1, source_target_pairs={{16,0},{18,2},{20,4},{22,6},{24,8},{26,10},{28,12},{30,14}} | collective-permute-start | bytes 1228808 | tf_op jit(solution)/shard_map/ppermute | solution.py:503
  78.3 21.2 %collective-permute-start.14 = (bf16[1056,256]{1,0:T(8,128)(2,1)S(1)}, bf16[1056,256]{1,0:T(8,128)(2,1)S(1)}, u32[]{:S(2)}, u32[]{:S(2)}) collective-permute-start(bf16[1056,256]{1,0:T(8,128)(2,1)S(1)} %get-tuple-element.27.whole_mine), channel_id=1, source_target_pairs={{1,17},{3,19},{5,21},{7,23},{9,25},{11,27},{13,29},{15,31}} | collective-permute-start | bytes 1622024 | tf_op jit(solution)/shard_map/ppermute | solution.py:503
  79.6 19.8 %collective-permute-start.12 = (bf16[800,256]{1,0:T(8,128)(2,1)S(1)}, bf16[800,256]{1,0:T(8,128)(2,1)S(1)}, u32[]{:S(2)}, u32[]{:S(2)}) collective-permute-start(bf16[800,256]{1,0:T(8,128)(2,1)S(1)} %collective-permute-done.10.three.level_far), channel_id=1, source_target_pairs={{0,1},{2,3},{4,5},{6,7},{8,9},{10,11},{12,13},{14,15}} | collective-permute-start | bytes 1228808 | tf_op jit(solution)/shard_map/ppermute | solution.py:503
  80.9 18.5 %collective-permute-start.11 = (bf16[512,256]{1,0:T(8,128)(2,1)S(1)}, bf16[512,256]{1,0:T(8,128)(2,1)S(1)}, u32[]{:S(2)}, u32[]{:S(2)}) collective-permute-start(bf16[512,256]{1,0:T(8,128)(2,1)S(1)} %get-tuple-element.25), channel_id=1, source_target_pairs={{15,0},{1,2},{3,4},{5,6},{7,8},{9,10},{11,12},{13,14}} | collective-permute-start | bytes 786440 | tf_op jit(solution)/shard_map/ppermute | solution.py:503
  85.7 13.7 %collective-permute-start.13 = (bf16[256,256]{1,0:T(8,128)(2,1)S(1)}, bf16[256,256]{1,0:T(8,128)(2,1)S(1)}, u32[]{:S(2)}, u32[]{:S(2)}) collective-permute-start(bf16[256,256]{1,0:T(8,128)(2,1)S(1)} %get-tuple-element.26), channel_id=1, source_target_pairs={{30,0},{15,1},{16,2},{1,3},{18,4},{3,5},{20,6},{5,7},{22,8},{7,9},... | collective-permute-start | bytes 393224 | tf_op jit(solution)/shard_map/ppermute | solution.py:503

commit v10 on v8

--- a/solution.py
+++ b/solution.py
@@ -218,7 +218,7 @@
     return copy
 
 
-def bond_body(basis, kept, theta, matrix, proj, work, iso, left, gates, iso_ready):
+def bond_body(basis, kept, theta, matrix, proj, work, iso, put_left, gates, iso_ready):
     blocks = theta.shape[-1]
 
     def gate(a, b, p, q):
@@ -289,7 +289,7 @@
     level = jnp.sqrt(total * (1.0 / (4 * blocks)) + 1e-06)
     scale = 1.0 / level
     for p in range(4):
-        left[p * blocks : (p + 1) * blocks, :] = (parts[p] * scale).astype(BF16)
+        put_left(p, (parts[p] * scale).astype(BF16))
     return level
 
 
@@ -348,9 +348,12 @@
             out(iso, 1, iso_three, 0, 3)
             out(iso, 0, local, 0, 3)
 
-        level = bond_body(basis, kept, theta, matrix, proj, work, iso, left, gates, iso_ready)
-        out(left, 1, left_three, 0, 3)
-        out(left, 0, local, 3, 3)
+        def put_left(p, value):
+            for ref, at in ((left, p), (left_three, p - 1), (local, p + 3 if p < 3 else -1)):
+                if at >= 0:
+                    ref[at * blocks : (at + 1) * blocks, :] = value
+
+        level = bond_body(basis, kept, theta, matrix, proj, work, iso, put_left, gates, iso_ready)
         weights = get_split(local, rest + W_ROW)
         for ref in (iso, iso_three, local):
             ref[small(ref) :, :] = jnp.zeros((SMALL, blocks), BF16)
@@ -401,8 +404,11 @@
         for n, value in enumerate(levels):
             columns[n * blocks : (n + 1) * blocks, :] = as_column(value)
         gates_copy.wait()
+        def put_left(p, value):
+            left[p * blocks : (p + 1) * blocks, :] = value
+
         level = bond_body(
-            basis, kept, theta, matrix, proj, work, iso, left, gates, lambda: None
+            basis, kept, theta, matrix, proj, work, iso, put_left, gates, lambda: None
         )
         column = jnp.concatenate([as_column(level)] * 2, axis=1)
         for ref, lo, hi in ((last, 3, 4), (mid, 1, 3), (first, 0, 1)):

time: 92.1 us -> 91.7 us (level)
  no operation moved by 1% of the time
where the time goes in v10:
time: 91.7 us; the launch traced here: 91.1 us
  waiting for transfers between devices  47.8 us (52%)
  starting transfers between devices  24.4 us (27%)
  Pallas kernels  14.9 us (16%)
  local copies, waits for them, and re-layouts  2.41 us (3%)
  between operations  1.61 us (2%)
    ppermute x14, waiting for transfers between devices, send(): return lax.ppermute(value, AXES, route)  47.8 us
    ppermute x14, starting transfers between devices, send(): return lax.ppermute(value, AXES, route)  24.4 us
    pallas_call x1, Pallas kernels, per_device(): pl.pallas_call(second_kernel, out_shape=(rows(2), rows(1), rows(1, SMALL)...  12.8 us
    unnamed x6, local copies, waits for them, and re-layouts  2.41 us
  transfers between devices with their start and end apart: 14, of which 4 were waited for; matrix products, arithmetic and copies ran while one was open for 0% of the time, Pallas kernels for 0%

profile of v10, /device:TPU:1, one launch (start us, length us, event | category | flops | bytes accessed | tf_op | source)
XLA Modules:
  0.0 91.1 jit_solution(4929765434647298496)
XLA Ops:
  1.3 0.0 copy-start.2
  1.3 0.7 copy-done.2
  2.0 0.0 copy-start
  2.0 1.0 %copy-done = bf16[1,1,4,256,256]{4,3,2,1,0:T(8,128)(2,1)S(1)} copy-done((bf16[1,1,4,256,256]{4,3,2,1,0:T(8,128)(2,1)S(1)}, bf16[1,1,4,256,256]{4,3,2,1,0:T(8,128)(2,1)}, u32[]{:S(2)}) %copy-start) | copy-done | bytes 524312
  3.0 0.0 copy-start.1
  3.0 0.7 copy-done.1
  3.7 0.6 prepare.1
  4.3 4.9 %collective-permute-start.1 = (bf16[1056,256]{1,0:T(8,128)(2,1)S(1)}, bf16[1056,256]{1,0:T(8,128)(2,1)S(1)}, u32[]{:S(2)}, u32[]{:S(2)}) collective-permute-start(bf16[1056,256]{1,0:T(8,128)(2,1)S(1)} %get-tuple-element.16.own), channel_id=1, source_target_pairs={{18,0},{20,2},{22,4},{24,6},{26,8},{28,10},{30,12},{16,14},{15,17}... | collective-permute-start | bytes 1622024 | tf_op jit(solution)/shard_map/ppermute | solution.py:508
  9.3 1.3 %collective-permute-start = (bf16[1056,256]{1,0:T(8,128)(2,1)S(1)}, bf16[1056,256]{1,0:T(8,128)(2,1)S(1)}, u32[]{:S(2)}, u32[]{:S(2)}) collective-permute-start(bf16[1056,256]{1,0:T(8,128)(2,1)S(1)} %get-tuple-element.16.own), channel_id=1, source_target_pairs={{1,0},{3,2},{5,4},{7,6},{9,8},{11,10},{13,12},{15,14},{0,17},{2,19... | collective-permute-start | bytes 1622024 | tf_op jit(solution)/shard_map/ppermute | solution.py:508
  10.6 0.7 collective-permute-start.2
  11.3 0.7 collective-permute-start.4
  12.0 4.5 %collective-permute-start.3 = (bf16[800,256]{1,0:T(8,128)(2,1)S(1)}, bf16[800,256]{1,0:T(8,128)(2,1)S(1)}, u32[]{:S(2)}, u32[]{:S(2)}) collective-permute-start(bf16[800,256]{1,0:T(8,128)(2,1)S(1)} %get-tuple-element.18), channel_id=1, source_target_pairs={{19,0},{21,2},{23,4},{25,6},{27,8},{29,10},{31,12},{17,14},{1,17},... | collective-permute-start | bytes 1228808 | tf_op jit(solution)/shard_map/ppermute | solution.py:508
  16.5 0.0 collective-permute-done.2.here_head
  16.5 0.0 collective-permute-done.4.next_tail
  16.5 9.2 %collective-permute-done.3.after_tail = bf16[800,256]{1,0:T(8,128)(2,1)S(1)} collective-permute-done((bf16[800,256]{1,0:T(8,128)(2,1)S(1)}, bf16[800,256]{1,0:T(8,128)(2,1)S(1)}, u32[]{:S(2)}, u32[]{:S(2)}) %collective-permute-start.3) | collective-permute-done | bytes 409632 | tf_op jit(solution)/shard_map/ppermute | solution.py:508
  25.7 0.0 collective-permute-done.1.next_full
  25.7 0.0 collective-permute-done.here_full
  25.8 1.3 %collective-permute-start.5 = (bf16[1632,256]{1,0:T(8,128)(2,1)S(1)}, bf16[1632,256]{1,0:T(8,128)(2,1)S(1)}, u32[]{:S(2)}, u32[]{:S(2)}) collective-permute-start(bf16[1632,256]{1,0:T(8,128)(2,1)S(1)} %get-tuple-element.19), channel_id=1, source_target_pairs={{0,1},{2,3},{4,5},{6,7},{8,9},{10,11},{12,13},{14,15},{17,16},{19,... | collective-permute-start | bytes 2506760 | tf_op jit(solution)/shard_map/ppermute | solution.py:508
  27.1 1.3 %collective-permute-start.6 = (bf16[1056,256]{1,0:T(8,128)(2,1)S(1)}, bf16[1056,256]{1,0:T(8,128)(2,1)S(1)}, u32[]{:S(2)}, u32[]{:S(2)}) collective-permute-start(bf16[1056,256]{1,0:T(8,128)(2,1)S(1)} %get-tuple-element.20), channel_id=1, source_target_pairs={{17,1},{19,3},{21,5},{23,7},{25,9},{27,11},{29,13},{31,15},{14,16}... | collective-permute-start | bytes 1622024 | tf_op jit(solution)/shard_map/ppermute | solution.py:508
  28.4 1.3 %collective-permute-start.8 = (bf16[1024,256]{1,0:T(8,128)(2,1)S(1)}, bf16[1024,256]{1,0:T(8,128)(2,1)S(1)}, u32[]{:S(2)}, u32[]{:S(2)}) collective-permute-start(bf16[1024,256]{1,0:T(8,128)(2,1)S(1)} %get-tuple-element.22), channel_id=1, source_target_pairs={{19,1},{21,3},{23,5},{25,7},{27,9},{29,11},{31,13},{17,15},{0,16},... | collective-permute-start | bytes 1572872 | tf_op jit(solution)/shard_map/ppermute | solution.py:508
  29.6 1.3 %collective-permute-start.7 = (bf16[800,256]{1,0:T(8,128)(2,1)S(1)}, bf16[800,256]{1,0:T(8,128)(2,1)S(1)}, u32[]{:S(2)}, u32[]{:S(2)}) collective-permute-start(bf16[800,256]{1,0:T(8,128)(2,1)S(1)} %get-tuple-element.21), channel_id=1, source_target_pairs={{14,1},{0,3},{2,5},{4,7},{6,9},{8,11},{10,13},{12,15},{31,16},{17,... | collective-permute-start | bytes 1228808 | tf_op jit(solution)/shard_map/ppermute | solution.py:508
  30.9 1.3 %collective-permute-start.9 = (bf16[768,256]{1,0:T(8,128)(2,1)S(1)}, bf16[768,256]{1,0:T(8,128)(2,1)S(1)}, u32[]{:S(2)}, u32[]{:S(2)}) collective-permute-start(bf16[768,256]{1,0:T(8,128)(2,1)S(1)} %get-tuple-element.23), channel_id=1, source_target_pairs={{2,1},{4,3},{6,5},{8,7},{10,9},{12,11},{14,13},{0,15},{19,16},{21,... | collective-permute-start | bytes 1179656 | tf_op jit(solution)/shard_map/ppermute | solution.py:508
  32.2 27.2 %collective-permute-done.9.left_2 = bf16[768,256]{1,0:T(8,128)(2,1)S(1)} collective-permute-done((bf16[768,256]{1,0:T(8,128)(2,1)S(1)}, bf16[768,256]{1,0:T(8,128)(2,1)S(1)}, u32[]{:S(2)}, u32[]{:S(2)}) %collective-permute-start.9) | collective-permute-done | bytes 393248 | tf_op jit(solution)/shard_map/ppermute | solution.py:508
  59.4 4.9 %collective-permute-done.7.iso_2 = bf16[800,256]{1,0:T(8,128)(2,1)S(1)} collective-permute-done((bf16[800,256]{1,0:T(8,128)(2,1)S(1)}, bf16[800,256]{1,0:T(8,128)(2,1)S(1)}, u32[]{:S(2)}, u32[]{:S(2)}) %collective-permute-start.7) | collective-permute-done | bytes 409632 | tf_op jit(solution)/shard_map/ppermute | solution.py:508
  64.3 0.0 collective-permute-done.8.left_1
  64.3 0.0 collective-permute-done.6.iso_1
  64.3 0.0 collective-permute-done.5.local.left_0.level_mine
  64.3 12.8 %second_bond.1 = (bf16[512,256]{1,0:T(8,128)(2,1)S(1)}, bf16[256,256]{1,0:T(8,128)(2,1)S(1)}, bf16[288,256]{1,0:T(8,128)(2,1)S(1)}, bf16[1056,256]{1,0:T(8,128)(2,1)S(1)}) custom-call(bf16[1632,256]{1,0:T(8,128)(2,1)S(1)} %collective-permute-done.5.local.left_0.level_mine, bf16[1056,256]{1,0:T(8,128)(2,1)S(1)} %collective-permute-done.6.iso_1, ...), custom_call_target="tpu_custom_call" | custom-call | tf_op jit(solution)/shard_map/second_bond/pallas_call | solution.py:561
  77.2 1.3 %collective-permute-start.13 = (bf16[1056,256]{1,0:T(8,128)(2,1)S(1)}, bf16[1056,256]{1,0:T(8,128)(2,1)S(1)}, u32[]{:S(2)}, u32[]{:S(2)}) collective-permute-start(bf16[1056,256]{1,0:T(8,128)(2,1)S(1)} %get-tuple-element.27.whole_mine), channel_id=1, source_target_pairs={{1,17},{3,19},{5,21},{7,23},{9,25},{11,27},{13,29},{15,31}} | collective-permute-start | bytes 1622024 | tf_op jit(solution)/shard_map/ppermute | solution.py:508
  78.5 1.9 %collective-permute-start.11 = (bf16[512,256]{1,0:T(8,128)(2,1)S(1)}, bf16[512,256]{1,0:T(8,128)(2,1)S(1)}, u32[]{:S(2)}, u32[]{:S(2)}) collective-permute-start(bf16[512,256]{1,0:T(8,128)(2,1)S(1)} %get-tuple-element.25), channel_id=1, source_target_pairs={{15,0},{16,1},{1,2},{18,3},{3,4},{20,5},{5,6},{22,7},{7,8},{24,9},... | collective-permute-start | bytes 786440 | tf_op jit(solution)/shard_map/ppermute | solution.py:508
  80.4 0.7 collective-permute-start.10
  81.1 1.9 %collective-permute-start.12 = (bf16[256,256]{1,0:T(8,128)(2,1)S(1)}, bf16[256,256]{1,0:T(8,128)(2,1)S(1)}, u32[]{:S(2)}, u32[]{:S(2)}) collective-permute-start(bf16[256,256]{1,0:T(8,128)(2,1)S(1)} %get-tuple-element.26), channel_id=1, source_target_pairs={{30,0},{15,1},{16,2},{1,3},{18,4},{3,5},{20,6},{5,7},{22,8},{7,9},... | collective-permute-start | bytes 393224 | tf_op jit(solution)/shard_map/ppermute | solution.py:508
  83.0 6.5 %collective-permute-done.12.last = bf16[256,256]{1,0:T(8,128)(2,1)S(1)} collective-permute-done((bf16[256,256]{1,0:T(8,128)(2,1)S(1)}, bf16[256,256]{1,0:T(8,128)(2,1)S(1)}, u32[]{:S(2)}, u32[]{:S(2)}) %collective-permute-start.12) | collective-permute-done | bytes 131104 | tf_op jit(solution)/shard_map/ppermute | solution.py:508
  89.5 0.0 collective-permute-done.10.first.level_far
  89.5 0.0 collective-permute-done.11.mid
  89.5 0.0 collective-permute-done.13.whole
  89.5 1.4 %assemble.1 = (bf16[1024,256]{1,0:T(8,128)(2,1)}, f32[1,256]{1,0:T(1,128)}) custom-call(bf16[288,256]{1,0:T(8,128)(2,1)S(1)} %get-tuple-element.24.first_mine, bf16[288,256]{1,0:T(8,128)(2,1)S(1)} %collective-permute-done.10.first.level_far, bf16[512,256]{1,0:T(8,128)(2,1)S(1)} %collective-permute-done.11.mid, ...), custom_call_target="tpu_custom_call" | custom-call | tf_op jit(solution)/shard_map/assemble/pallas_call | solution.py:592
  (1 shorter events, 0.0 us)
Async XLA Ops:
  1.3 0.7 copy-start.2
  2.0 1.0 %copy-start = (bf16[1,1,4,256,256]{4,3,2,1,0:T(8,128)(2,1)S(1)}, bf16[1,1,4,256,256]{4,3,2,1,0:T(8,128)(2,1)}, u32[]{:S(2)}) copy-start(bf16[1,1,4,256,256]{4,3,2,1,0:T(8,128)(2,1)} %param.4) | copy-start | bytes 1572868
  3.0 0.7 copy-start.1
  4.3 21.4 %collective-permute-start.1 = (bf16[1056,256]{1,0:T(8,128)(2,1)S(1)}, bf16[1056,256]{1,0:T(8,128)(2,1)S(1)}, u32[]{:S(2)}, u32[]{:S(2)}) collective-permute-start(bf16[1056,256]{1,0:T(8,128)(2,1)S(1)} %get-tuple-element.16.own), channel_id=1, source_target_pairs={{18,0},{20,2},{22,4},{24,6},{26,8},{28,10},{30,12},{16,14},{15,17}... | collective-permute-start | bytes 1622024 | tf_op jit(solution)/shard_map/ppermute | solution.py:508
  9.3 16.4 %collective-permute-start = (bf16[1056,256]{1,0:T(8,128)(2,1)S(1)}, bf16[1056,256]{1,0:T(8,128)(2,1)S(1)}, u32[]{:S(2)}, u32[]{:S(2)}) collective-permute-start(bf16[1056,256]{1,0:T(8,128)(2,1)S(1)} %get-tuple-element.16.own), channel_id=1, source_target_pairs={{1,0},{3,2},{5,4},{7,6},{9,8},{11,10},{13,12},{15,14},{0,17},{2,19... | collective-permute-start | bytes 1622024 | tf_op jit(solution)/shard_map/ppermute | solution.py:508
  10.6 5.9 %collective-permute-start.2 = (bf16[800,256]{1,0:T(8,128)(2,1)S(1)}, bf16[800,256]{1,0:T(8,128)(2,1)S(1)}, u32[]{:S(2)}, u32[]{:S(2)}) collective-permute-start(bf16[800,256]{1,0:T(8,128)(2,1)S(1)} %get-tuple-element.17), channel_id=1, source_target_pairs={{17,0},{19,2},{21,4},{23,6},{25,8},{27,10},{29,12},{31,14},{16,17}... | collective-permute-start | bytes 1228808 | tf_op jit(solution)/shard_map/ppermute | solution.py:508
  11.3 5.2 %collective-permute-start.4 = (bf16[800,256]{1,0:T(8,128)(2,1)S(1)}, bf16[800,256]{1,0:T(8,128)(2,1)S(1)}, u32[]{:S(2)}, u32[]{:S(2)}) collective-permute-start(bf16[800,256]{1,0:T(8,128)(2,1)S(1)} %get-tuple-element.18), channel_id=1, source_target_pairs={{2,0},{4,2},{6,4},{8,6},{10,8},{12,10},{14,12},{0,14},{18,17},{20,... | collective-permute-start | bytes 1228808 | tf_op jit(solution)/shard_map/ppermute | solution.py:508
  12.0 13.7 %collective-permute-start.3 = (bf16[800,256]{1,0:T(8,128)(2,1)S(1)}, bf16[800,256]{1,0:T(8,128)(2,1)S(1)}, u32[]{:S(2)}, u32[]{:S(2)}) collective-permute-start(bf16[800,256]{1,0:T(8,128)(2,1)S(1)} %get-tuple-element.18), channel_id=1, source_target_pairs={{19,0},{21,2},{23,4},{25,6},{27,8},{29,10},{31,12},{17,14},{1,17},... | collective-permute-start | bytes 1228808 | tf_op jit(solution)/shard_map/ppermute | solution.py:508
  25.8 38.6 %collective-permute-start.5 = (bf16[1632,256]{1,0:T(8,128)(2,1)S(1)}, bf16[1632,256]{1,0:T(8,128)(2,1)S(1)}, u32[]{:S(2)}, u32[]{:S(2)}) collective-permute-start(bf16[1632,256]{1,0:T(8,128)(2,1)S(1)} %get-tuple-element.19), channel_id=1, source_target_pairs={{0,1},{2,3},{4,5},{6,7},{8,9},{10,11},{12,13},{14,15},{17,16},{19,... | collective-permute-start | bytes 2506760 | tf_op jit(solution)/shard_map/ppermute | solution.py:508
  27.1 37.3 %collective-permute-start.6 = (bf16[1056,256]{1,0:T(8,128)(2,1)S(1)}, bf16[1056,256]{1,0:T(8,128)(2,1)S(1)}, u32[]{:S(2)}, u32[]{:S(2)}) collective-permute-start(bf16[1056,256]{1,0:T(8,128)(2,1)S(1)} %get-tuple-element.20), channel_id=1, source_target_pairs={{17,1},{19,3},{21,5},{23,7},{25,9},{27,11},{29,13},{31,15},{14,16}... | collective-permute-start | bytes 1622024 | tf_op jit(solution)/shard_map/ppermute | solution.py:508
  28.4 36.0 %collective-permute-start.8 = (bf16[1024,256]{1,0:T(8,128)(2,1)S(1)}, bf16[1024,256]{1,0:T(8,128)(2,1)S(1)}, u32[]{:S(2)}, u32[]{:S(2)}) collective-permute-start(bf16[1024,256]{1,0:T(8,128)(2,1)S(1)} %get-tuple-element.22), channel_id=1, source_target_pairs={{19,1},{21,3},{23,5},{25,7},{27,9},{29,11},{31,13},{17,15},{0,16},... | collective-permute-start | bytes 1572872 | tf_op jit(solution)/shard_map/ppermute | solution.py:508
  29.6 34.7 %collective-permute-start.7 = (bf16[800,256]{1,0:T(8,128)(2,1)S(1)}, bf16[800,256]{1,0:T(8,128)(2,1)S(1)}, u32[]{:S(2)}, u32[]{:S(2)}) collective-permute-start(bf16[800,256]{1,0:T(8,128)(2,1)S(1)} %get-tuple-element.21), channel_id=1, source_target_pairs={{14,1},{0,3},{2,5},{4,7},{6,9},{8,11},{10,13},{12,15},{31,16},{17,... | collective-permute-start | bytes 1228808 | tf_op jit(solution)/shard_map/ppermute | solution.py:508
  30.9 28.5 %collective-permute-start.9 = (bf16[768,256]{1,0:T(8,128)(2,1)S(1)}, bf16[768,256]{1,0:T(8,128)(2,1)S(1)}, u32[]{:S(2)}, u32[]{:S(2)}) collective-permute-start(bf16[768,256]{1,0:T(8,128)(2,1)S(1)} %get-tuple-element.23), channel_id=1, source_target_pairs={{2,1},{4,3},{6,5},{8,7},{10,9},{12,11},{14,13},{0,15},{19,16},{21,... | collective-permute-start | bytes 1179656 | tf_op jit(solution)/shard_map/ppermute | solution.py:508
  77.2 12.4 %collective-permute-start.13 = (bf16[1056,256]{1,0:T(8,128)(2,1)S(1)}, bf16[1056,256]{1,0:T(8,128)(2,1)S(1)}, u32[]{:S(2)}, u32[]{:S(2)}) collective-permute-start(bf16[1056,256]{1,0:T(8,128)(2,1)S(1)} %get-tuple-element.27.whole_mine), channel_id=1, source_target_pairs={{1,17},{3,19},{5,21},{7,23},{9,25},{11,27},{13,29},{15,31}} | collective-permute-start | bytes 1622024 | tf_op jit(solution)/shard_map/ppermute | solution.py:508
  78.5 11.0 %collective-permute-start.11 = (bf16[512,256]{1,0:T(8,128)(2,1)S(1)}, bf16[512,256]{1,0:T(8,128)(2,1)S(1)}, u32[]{:S(2)}, u32[]{:S(2)}) collective-permute-start(bf16[512,256]{1,0:T(8,128)(2,1)S(1)} %get-tuple-element.25), channel_id=1, source_target_pairs={{15,0},{16,1},{1,2},{18,3},{3,4},{20,5},{5,6},{22,7},{7,8},{24,9},... | collective-permute-start | bytes 786440 | tf_op jit(solution)/shard_map/ppermute | solution.py:508
  80.4 9.1 %collective-permute-start.10 = (bf16[288,256]{1,0:T(8,128)(2,1)S(1)}, bf16[288,256]{1,0:T(8,128)(2,1)S(1)}, u32[]{:S(2)}, u32[]{:S(2)}) collective-permute-start(bf16[288,256]{1,0:T(8,128)(2,1)S(1)} %get-tuple-element.24.first_mine), channel_id=1, source_target_pairs={{16,0},{18,2},{20,4},{22,6},{24,8},{26,10},{28,12},{30,14}} | collective-permute-start | bytes 442376 | tf_op jit(solution)/shard_map/ppermute | solution.py:508
  81.1 8.4 %collective-permute-start.12 = (bf16[256,256]{1,0:T(8,128)(2,1)S(1)}, bf16[256,256]{1,0:T(8,128)(2,1)S(1)}, u32[]{:S(2)}, u32[]{:S(2)}) collective-permute-start(bf16[256,256]{1,0:T(8,128)(2,1)S(1)} %get-tuple-element.26), channel_id=1, source_target_pairs={{30,0},{15,1},{16,2},{1,3},{18,4},{3,5},{20,6},{5,7},{22,8},{7,9},... | collective-permute-start | bytes 393224 | tf_op jit(solution)/shard_map/ppermute | solution.py:508

commit v11 on v10

--- a/solution.py
+++ b/solution.py
@@ -187,6 +187,10 @@
         copy.wait()
 
 
+def exact_root(blocks):
+    return math.log2(blocks) % 2 == 0
+
+
 def products(a_blocks, b_blocks, weights, scaled, theta, basis):
     blocks = scaled.shape[-1]
 
@@ -206,13 +210,14 @@
             ((1,), (0,)),
         )
         slot = SLOTS[distance, first, q]
-        theta[slot * blocks : (slot + count) * blocks, :] = (
-            product * (1.0 / math.sqrt(blocks))
-        ).astype(BF16)
-
-
-def load_gates(gate_rows, gate_stage, gates, sem):
-    gate_stage[...] = gate_rows.astype(F32)
+        if not exact_root(blocks):
+            product = product * (1.0 / math.sqrt(blocks))
+        theta[slot * blocks : (slot + count) * blocks, :] = product.astype(BF16)
+
+
+def load_gates(gate_rows, blocks, gate_stage, gates, sem):
+    factor = 1.0 / math.sqrt(blocks) if exact_root(blocks) else 1.0
+    gate_stage[...] = gate_rows.astype(F32) * factor
     copy = pltpu.make_async_copy(gate_stage, gates, sem)
     copy.start()
     return copy
@@ -268,7 +273,8 @@
     work[:, :blocks] = (dot(h, h, outer) + dot(m, m, outer)) + (mixed + mixed.T) + eye
     work[:, blocks:] = eye
     factor_rows(work, blocks)
-    wh, wm, wl = split3(work[:, blocks:])
+    root = math.sqrt(4 * blocks)
+    wh, wm, wl = split3(work[:, blocks:] * (root if exact_root(blocks) else 1.0))
     h, m, l = (proj[n * blocks : (n + 1) * blocks, :] for n in range(3))
     inner = ((1,), (0,))
     ortho = (
@@ -276,7 +282,7 @@
         + dot(jnp.concatenate([wh, wm], axis=1), jnp.concatenate([m, m], axis=0), inner)
         + dot(wh, l, inner)
     )
-    ortho = (ortho * math.sqrt(4 * blocks)).astype(BF16)
+    ortho = (ortho * (1.0 if exact_root(blocks) else root)).astype(BF16)
     for p in range(4):
         iso[p * blocks : (p + 1) * blocks, :] = ortho[:, p * blocks : (p + 1) * blocks]
     iso_ready()
@@ -312,7 +318,7 @@
     def _():
         base = small(here_full)
         kept = here_full[base + K_ROW : base + K_ROW + 1, 0:1].astype(F32)
-        gates_copy = load_gates(here_full[base : base + 16, 0:128], gate_stage, gates, sems.at[0])
+        gates_copy = load_gates(here_full[base : base + 16, 0:128], blocks, gate_stage, gates, sems.at[0])
         rest = 6 * blocks
         for role, (one, two, three, four) in enumerate(
             ((own, next_full, next_tail, after_tail), (next_full, own, after_tail, next_tail))
@@ -384,7 +390,7 @@
     @pl.when(x != c)
     def _():
         kept = local[rest + K_ROW : rest + K_ROW + 1, 0:1].astype(F32)
-        gates_copy = load_gates(local[rest : rest + 16, 0:128], gate_stage, gates, sems.at[0])
+        gates_copy = load_gates(local[rest : rest + 16, 0:128], blocks, gate_stage, gates, sems.at[0])
         here = [(local, 0), (iso_1, 1), (iso_1, 2), (iso_2, 2)]
         products(
             [(iso_1, 0), (iso_2, 0), (iso_2, 1)] + here + [(local, 1), (local, 2), (iso_1, 3)],

time: 91.7 us -> 91.7 us (level)
  no operation moved by 1% of the time
where the time goes in v11:
time: 91.7 us; the launch traced here: 91.1 us
  waiting for transfers between devices  47.7 us (52%)
  starting transfers between devices  24.4 us (27%)
  Pallas kernels  14.9 us (16%)
  local copies, waits for them, and re-layouts  2.41 us (3%)
  between operations  1.61 us (2%)
    ppermute x14, waiting for transfers between devices, send(): return lax.ppermute(value, AXES, route)  47.7 us
    ppermute x14, starting transfers between devices, send(): return lax.ppermute(value, AXES, route)  24.4 us
    pallas_call x1, Pallas kernels, per_device(): pl.pallas_call(second_kernel, out_shape=(rows(2), rows(1), rows(1, SMALL)...  12.8 us
    unnamed x6, local copies, waits for them, and re-layouts  2.41 us
  transfers between devices with their start and end apart: 14, of which 4 were waited for; matrix products, arithmetic and copies ran while one was open for 0% of the time, Pallas kernels for 0%

profile of v11, /device:TPU:1, one launch (start us, length us, event | category | flops | bytes accessed | tf_op | source)
XLA Modules:
  0.0 91.1 jit_solution(16228550692643471539)
XLA Ops:
  1.3 0.0 copy-start.2
  1.3 0.7 copy-done.2
  2.0 0.0 copy-start
  2.0 1.0 %copy-done = bf16[1,1,4,256,256]{4,3,2,1,0:T(8,128)(2,1)S(1)} copy-done((bf16[1,1,4,256,256]{4,3,2,1,0:T(8,128)(2,1)S(1)}, bf16[1,1,4,256,256]{4,3,2,1,0:T(8,128)(2,1)}, u32[]{:S(2)}) %copy-start) | copy-done | bytes 524312
  3.0 0.0 copy-start.1
  3.0 0.7 copy-done.1
  3.7 0.6 prepare.1
  4.3 4.9 %collective-permute-start.1 = (bf16[1056,256]{1,0:T(8,128)(2,1)S(1)}, bf16[1056,256]{1,0:T(8,128)(2,1)S(1)}, u32[]{:S(2)}, u32[]{:S(2)}) collective-permute-start(bf16[1056,256]{1,0:T(8,128)(2,1)S(1)} %get-tuple-element.16.own), channel_id=1, source_target_pairs={{18,0},{20,2},{22,4},{24,6},{26,8},{28,10},{30,12},{16,14},{15,17}... | collective-permute-start | bytes 1622024 | tf_op jit(solution)/shard_map/ppermute | solution.py:514
  9.3 1.3 %collective-permute-start = (bf16[1056,256]{1,0:T(8,128)(2,1)S(1)}, bf16[1056,256]{1,0:T(8,128)(2,1)S(1)}, u32[]{:S(2)}, u32[]{:S(2)}) collective-permute-start(bf16[1056,256]{1,0:T(8,128)(2,1)S(1)} %get-tuple-element.16.own), channel_id=1, source_target_pairs={{1,0},{3,2},{5,4},{7,6},{9,8},{11,10},{13,12},{15,14},{0,17},{2,19... | collective-permute-start | bytes 1622024 | tf_op jit(solution)/shard_map/ppermute | solution.py:514
  10.6 0.7 collective-permute-start.2
  11.3 0.7 collective-permute-start.4
  12.0 4.5 %collective-permute-start.3 = (bf16[800,256]{1,0:T(8,128)(2,1)S(1)}, bf16[800,256]{1,0:T(8,128)(2,1)S(1)}, u32[]{:S(2)}, u32[]{:S(2)}) collective-permute-start(bf16[800,256]{1,0:T(8,128)(2,1)S(1)} %get-tuple-element.18), channel_id=1, source_target_pairs={{19,0},{21,2},{23,4},{25,6},{27,8},{29,10},{31,12},{17,14},{1,17},... | collective-permute-start | bytes 1228808 | tf_op jit(solution)/shard_map/ppermute | solution.py:514
  16.5 0.0 collective-permute-done.2.here_head
  16.5 0.0 collective-permute-done.4.next_tail
  16.5 9.2 %collective-permute-done.3.after_tail = bf16[800,256]{1,0:T(8,128)(2,1)S(1)} collective-permute-done((bf16[800,256]{1,0:T(8,128)(2,1)S(1)}, bf16[800,256]{1,0:T(8,128)(2,1)S(1)}, u32[]{:S(2)}, u32[]{:S(2)}) %collective-permute-start.3) | collective-permute-done | bytes 409632 | tf_op jit(solution)/shard_map/ppermute | solution.py:514
  25.7 0.0 collective-permute-done.1.next_full
  25.7 0.0 collective-permute-done.here_full
  25.8 1.3 %collective-permute-start.5 = (bf16[1632,256]{1,0:T(8,128)(2,1)S(1)}, bf16[1632,256]{1,0:T(8,128)(2,1)S(1)}, u32[]{:S(2)}, u32[]{:S(2)}) collective-permute-start(bf16[1632,256]{1,0:T(8,128)(2,1)S(1)} %get-tuple-element.19), channel_id=1, source_target_pairs={{0,1},{2,3},{4,5},{6,7},{8,9},{10,11},{12,13},{14,15},{17,16},{19,... | collective-permute-start | bytes 2506760 | tf_op jit(solution)/shard_map/ppermute | solution.py:514
  27.1 1.3 %collective-permute-start.6 = (bf16[1056,256]{1,0:T(8,128)(2,1)S(1)}, bf16[1056,256]{1,0:T(8,128)(2,1)S(1)}, u32[]{:S(2)}, u32[]{:S(2)}) collective-permute-start(bf16[1056,256]{1,0:T(8,128)(2,1)S(1)} %get-tuple-element.20), channel_id=1, source_target_pairs={{17,1},{19,3},{21,5},{23,7},{25,9},{27,11},{29,13},{31,15},{14,16}... | collective-permute-start | bytes 1622024 | tf_op jit(solution)/shard_map/ppermute | solution.py:514
  28.4 1.3 %collective-permute-start.8 = (bf16[1024,256]{1,0:T(8,128)(2,1)S(1)}, bf16[1024,256]{1,0:T(8,128)(2,1)S(1)}, u32[]{:S(2)}, u32[]{:S(2)}) collective-permute-start(bf16[1024,256]{1,0:T(8,128)(2,1)S(1)} %get-tuple-element.22), channel_id=1, source_target_pairs={{19,1},{21,3},{23,5},{25,7},{27,9},{29,11},{31,13},{17,15},{0,16},... | collective-permute-start | bytes 1572872 | tf_op jit(solution)/shard_map/ppermute | solution.py:514
  29.6 1.3 %collective-permute-start.7 = (bf16[800,256]{1,0:T(8,128)(2,1)S(1)}, bf16[800,256]{1,0:T(8,128)(2,1)S(1)}, u32[]{:S(2)}, u32[]{:S(2)}) collective-permute-start(bf16[800,256]{1,0:T(8,128)(2,1)S(1)} %get-tuple-element.21), channel_id=1, source_target_pairs={{14,1},{0,3},{2,5},{4,7},{6,9},{8,11},{10,13},{12,15},{31,16},{17,... | collective-permute-start | bytes 1228808 | tf_op jit(solution)/shard_map/ppermute | solution.py:514
  30.9 1.3 %collective-permute-start.9 = (bf16[768,256]{1,0:T(8,128)(2,1)S(1)}, bf16[768,256]{1,0:T(8,128)(2,1)S(1)}, u32[]{:S(2)}, u32[]{:S(2)}) collective-permute-start(bf16[768,256]{1,0:T(8,128)(2,1)S(1)} %get-tuple-element.23), channel_id=1, source_target_pairs={{2,1},{4,3},{6,5},{8,7},{10,9},{12,11},{14,13},{0,15},{19,16},{21,... | collective-permute-start | bytes 1179656 | tf_op jit(solution)/shard_map/ppermute | solution.py:514
  32.2 27.2 %collective-permute-done.9.left_2 = bf16[768,256]{1,0:T(8,128)(2,1)S(1)} collective-permute-done((bf16[768,256]{1,0:T(8,128)(2,1)S(1)}, bf16[768,256]{1,0:T(8,128)(2,1)S(1)}, u32[]{:S(2)}, u32[]{:S(2)}) %collective-permute-start.9) | collective-permute-done | bytes 393248 | tf_op jit(solution)/shard_map/ppermute | solution.py:514
  59.4 4.9 %collective-permute-done.7.iso_2 = bf16[800,256]{1,0:T(8,128)(2,1)S(1)} collective-permute-done((bf16[800,256]{1,0:T(8,128)(2,1)S(1)}, bf16[800,256]{1,0:T(8,128)(2,1)S(1)}, u32[]{:S(2)}, u32[]{:S(2)}) %collective-permute-start.7) | collective-permute-done | bytes 409632 | tf_op jit(solution)/shard_map/ppermute | solution.py:514
  64.3 0.0 collective-permute-done.8.left_1
  64.3 0.0 collective-permute-done.6.iso_1
  64.3 0.0 collective-permute-done.5.local.left_0.level_mine
  64.3 12.8 %second_bond.1 = (bf16[512,256]{1,0:T(8,128)(2,1)S(1)}, bf16[256,256]{1,0:T(8,128)(2,1)S(1)}, bf16[288,256]{1,0:T(8,128)(2,1)S(1)}, bf16[1056,256]{1,0:T(8,128)(2,1)S(1)}) custom-call(bf16[1632,256]{1,0:T(8,128)(2,1)S(1)} %collective-permute-done.5.local.left_0.level_mine, bf16[1056,256]{1,0:T(8,128)(2,1)S(1)} %collective-permute-done.6.iso_1, ...), custom_call_target="tpu_custom_call" | custom-call | tf_op jit(solution)/shard_map/second_bond/pallas_call | solution.py:567
  77.1 1.3 %collective-permute-start.13 = (bf16[1056,256]{1,0:T(8,128)(2,1)S(1)}, bf16[1056,256]{1,0:T(8,128)(2,1)S(1)}, u32[]{:S(2)}, u32[]{:S(2)}) collective-permute-start(bf16[1056,256]{1,0:T(8,128)(2,1)S(1)} %get-tuple-element.27.whole_mine), channel_id=1, source_target_pairs={{1,17},{3,19},{5,21},{7,23},{9,25},{11,27},{13,29},{15,31}} | collective-permute-start | bytes 1622024 | tf_op jit(solution)/shard_map/ppermute | solution.py:514
  78.4 1.9 %collective-permute-start.11 = (bf16[512,256]{1,0:T(8,128)(2,1)S(1)}, bf16[512,256]{1,0:T(8,128)(2,1)S(1)}, u32[]{:S(2)}, u32[]{:S(2)}) collective-permute-start(bf16[512,256]{1,0:T(8,128)(2,1)S(1)} %get-tuple-element.25), channel_id=1, source_target_pairs={{15,0},{16,1},{1,2},{18,3},{3,4},{20,5},{5,6},{22,7},{7,8},{24,9},... | collective-permute-start | bytes 786440 | tf_op jit(solution)/shard_map/ppermute | solution.py:514
  80.4 0.7 collective-permute-start.10
  81.0 1.9 %collective-permute-start.12 = (bf16[256,256]{1,0:T(8,128)(2,1)S(1)}, bf16[256,256]{1,0:T(8,128)(2,1)S(1)}, u32[]{:S(2)}, u32[]{:S(2)}) collective-permute-start(bf16[256,256]{1,0:T(8,128)(2,1)S(1)} %get-tuple-element.26), channel_id=1, source_target_pairs={{30,0},{15,1},{16,2},{1,3},{18,4},{3,5},{20,6},{5,7},{22,8},{7,9},... | collective-permute-start | bytes 393224 | tf_op jit(solution)/shard_map/ppermute | solution.py:514
  83.0 6.5 %collective-permute-done.12.last = bf16[256,256]{1,0:T(8,128)(2,1)S(1)} collective-permute-done((bf16[256,256]{1,0:T(8,128)(2,1)S(1)}, bf16[256,256]{1,0:T(8,128)(2,1)S(1)}, u32[]{:S(2)}, u32[]{:S(2)}) %collective-permute-start.12) | collective-permute-done | bytes 131104 | tf_op jit(solution)/shard_map/ppermute | solution.py:514
  89.5 0.0 collective-permute-done.10.first.level_far
  89.5 0.0 collective-permute-done.11.mid
  89.5 0.0 collective-permute-done.13.whole
  89.5 1.4 %assemble.1 = (bf16[1024,256]{1,0:T(8,128)(2,1)}, f32[1,256]{1,0:T(1,128)}) custom-call(bf16[288,256]{1,0:T(8,128)(2,1)S(1)} %get-tuple-element.24.first_mine, bf16[288,256]{1,0:T(8,128)(2,1)S(1)} %collective-permute-done.10.first.level_far, bf16[512,256]{1,0:T(8,128)(2,1)S(1)} %collective-permute-done.11.mid, ...), custom_call_target="tpu_custom_call" | custom-call | tf_op jit(solution)/shard_map/assemble/pallas_call | solution.py:598
  (1 shorter events, 0.0 us)
Async XLA Ops:
  1.3 0.7 copy-start.2
  2.0 1.0 %copy-start = (bf16[1,1,4,256,256]{4,3,2,1,0:T(8,128)(2,1)S(1)}, bf16[1,1,4,256,256]{4,3,2,1,0:T(8,128)(2,1)}, u32[]{:S(2)}) copy-start(bf16[1,1,4,256,256]{4,3,2,1,0:T(8,128)(2,1)} %param.4) | copy-start | bytes 1572868
  3.0 0.7 copy-start.1
  4.3 21.4 %collective-permute-start.1 = (bf16[1056,256]{1,0:T(8,128)(2,1)S(1)}, bf16[1056,256]{1,0:T(8,128)(2,1)S(1)}, u32[]{:S(2)}, u32[]{:S(2)}) collective-permute-start(bf16[1056,256]{1,0:T(8,128)(2,1)S(1)} %get-tuple-element.16.own), channel_id=1, source_target_pairs={{18,0},{20,2},{22,4},{24,6},{26,8},{28,10},{30,12},{16,14},{15,17}... | collective-permute-start | bytes 1622024 | tf_op jit(solution)/shard_map/ppermute | solution.py:514
  9.3 16.4 %collective-permute-start = (bf16[1056,256]{1,0:T(8,128)(2,1)S(1)}, bf16[1056,256]{1,0:T(8,128)(2,1)S(1)}, u32[]{:S(2)}, u32[]{:S(2)}) collective-permute-start(bf16[1056,256]{1,0:T(8,128)(2,1)S(1)} %get-tuple-element.16.own), channel_id=1, source_target_pairs={{1,0},{3,2},{5,4},{7,6},{9,8},{11,10},{13,12},{15,14},{0,17},{2,19... | collective-permute-start | bytes 1622024 | tf_op jit(solution)/shard_map/ppermute | solution.py:514
  10.6 5.9 %collective-permute-start.2 = (bf16[800,256]{1,0:T(8,128)(2,1)S(1)}, bf16[800,256]{1,0:T(8,128)(2,1)S(1)}, u32[]{:S(2)}, u32[]{:S(2)}) collective-permute-start(bf16[800,256]{1,0:T(8,128)(2,1)S(1)} %get-tuple-element.17), channel_id=1, source_target_pairs={{17,0},{19,2},{21,4},{23,6},{25,8},{27,10},{29,12},{31,14},{16,17}... | collective-permute-start | bytes 1228808 | tf_op jit(solution)/shard_map/ppermute | solution.py:514
  11.3 5.2 %collective-permute-start.4 = (bf16[800,256]{1,0:T(8,128)(2,1)S(1)}, bf16[800,256]{1,0:T(8,128)(2,1)S(1)}, u32[]{:S(2)}, u32[]{:S(2)}) collective-permute-start(bf16[800,256]{1,0:T(8,128)(2,1)S(1)} %get-tuple-element.18), channel_id=1, source_target_pairs={{2,0},{4,2},{6,4},{8,6},{10,8},{12,10},{14,12},{0,14},{18,17},{20,... | collective-permute-start | bytes 1228808 | tf_op jit(solution)/shard_map/ppermute | solution.py:514
  12.0 13.7 %collective-permute-start.3 = (bf16[800,256]{1,0:T(8,128)(2,1)S(1)}, bf16[800,256]{1,0:T(8,128)(2,1)S(1)}, u32[]{:S(2)}, u32[]{:S(2)}) collective-permute-start(bf16[800,256]{1,0:T(8,128)(2,1)S(1)} %get-tuple-element.18), channel_id=1, source_target_pairs={{19,0},{21,2},{23,4},{25,6},{27,8},{29,10},{31,12},{17,14},{1,17},... | collective-permute-start | bytes 1228808 | tf_op jit(solution)/shard_map/ppermute | solution.py:514
  25.8 38.5 %collective-permute-start.5 = (bf16[1632,256]{1,0:T(8,128)(2,1)S(1)}, bf16[1632,256]{1,0:T(8,128)(2,1)S(1)}, u32[]{:S(2)}, u32[]{:S(2)}) collective-permute-start(bf16[1632,256]{1,0:T(8,128)(2,1)S(1)} %get-tuple-element.19), channel_id=1, source_target_pairs={{0,1},{2,3},{4,5},{6,7},{8,9},{10,11},{12,13},{14,15},{17,16},{19,... | collective-permute-start | bytes 2506760 | tf_op jit(solution)/shard_map/ppermute | solution.py:514
  27.1 37.2 %collective-permute-start.6 = (bf16[1056,256]{1,0:T(8,128)(2,1)S(1)}, bf16[1056,256]{1,0:T(8,128)(2,1)S(1)}, u32[]{:S(2)}, u32[]{:S(2)}) collective-permute-start(bf16[1056,256]{1,0:T(8,128)(2,1)S(1)} %get-tuple-element.20), channel_id=1, source_target_pairs={{17,1},{19,3},{21,5},{23,7},{25,9},{27,11},{29,13},{31,15},{14,16}... | collective-permute-start | bytes 1622024 | tf_op jit(solution)/shard_map/ppermute | solution.py:514
  28.4 35.9 %collective-permute-start.8 = (bf16[1024,256]{1,0:T(8,128)(2,1)S(1)}, bf16[1024,256]{1,0:T(8,128)(2,1)S(1)}, u32[]{:S(2)}, u32[]{:S(2)}) collective-permute-start(bf16[1024,256]{1,0:T(8,128)(2,1)S(1)} %get-tuple-element.22), channel_id=1, source_target_pairs={{19,1},{21,3},{23,5},{25,7},{27,9},{29,11},{31,13},{17,15},{0,16},... | collective-permute-start | bytes 1572872 | tf_op jit(solution)/shard_map/ppermute | solution.py:514
  29.6 34.6 %collective-permute-start.7 = (bf16[800,256]{1,0:T(8,128)(2,1)S(1)}, bf16[800,256]{1,0:T(8,128)(2,1)S(1)}, u32[]{:S(2)}, u32[]{:S(2)}) collective-permute-start(bf16[800,256]{1,0:T(8,128)(2,1)S(1)} %get-tuple-element.21), channel_id=1, source_target_pairs={{14,1},{0,3},{2,5},{4,7},{6,9},{8,11},{10,13},{12,15},{31,16},{17,... | collective-permute-start | bytes 1228808 | tf_op jit(solution)/shard_map/ppermute | solution.py:514
  30.9 28.5 %collective-permute-start.9 = (bf16[768,256]{1,0:T(8,128)(2,1)S(1)}, bf16[768,256]{1,0:T(8,128)(2,1)S(1)}, u32[]{:S(2)}, u32[]{:S(2)}) collective-permute-start(bf16[768,256]{1,0:T(8,128)(2,1)S(1)} %get-tuple-element.23), channel_id=1, source_target_pairs={{2,1},{4,3},{6,5},{8,7},{10,9},{12,11},{14,13},{0,15},{19,16},{21,... | collective-permute-start | bytes 1179656 | tf_op jit(solution)/shard_map/ppermute | solution.py:514
  77.1 12.4 %collective-permute-start.13 = (bf16[1056,256]{1,0:T(8,128)(2,1)S(1)}, bf16[1056,256]{1,0:T(8,128)(2,1)S(1)}, u32[]{:S(2)}, u32[]{:S(2)}) collective-permute-start(bf16[1056,256]{1,0:T(8,128)(2,1)S(1)} %get-tuple-element.27.whole_mine), channel_id=1, source_target_pairs={{1,17},{3,19},{5,21},{7,23},{9,25},{11,27},{13,29},{15,31}} | collective-permute-start | bytes 1622024 | tf_op jit(solution)/shard_map/ppermute | solution.py:514
  78.4 11.0 %collective-permute-start.11 = (bf16[512,256]{1,0:T(8,128)(2,1)S(1)}, bf16[512,256]{1,0:T(8,128)(2,1)S(1)}, u32[]{:S(2)}, u32[]{:S(2)}) collective-permute-start(bf16[512,256]{1,0:T(8,128)(2,1)S(1)} %get-tuple-element.25), channel_id=1, source_target_pairs={{15,0},{16,1},{1,2},{18,3},{3,4},{20,5},{5,6},{22,7},{7,8},{24,9},... | collective-permute-start | bytes 786440 | tf_op jit(solution)/shard_map/ppermute | solution.py:514
  80.4 9.1 %collective-permute-start.10 = (bf16[288,256]{1,0:T(8,128)(2,1)S(1)}, bf16[288,256]{1,0:T(8,128)(2,1)S(1)}, u32[]{:S(2)}, u32[]{:S(2)}) collective-permute-start(bf16[288,256]{1,0:T(8,128)(2,1)S(1)} %get-tuple-element.24.first_mine), channel_id=1, source_target_pairs={{16,0},{18,2},{20,4},{22,6},{24,8},{26,10},{28,12},{30,14}} | collective-permute-start | bytes 442376 | tf_op jit(solution)/shard_map/ppermute | solution.py:514
  81.0 8.4 %collective-permute-start.12 = (bf16[256,256]{1,0:T(8,128)(2,1)S(1)}, bf16[256,256]{1,0:T(8,128)(2,1)S(1)}, u32[]{:S(2)}, u32[]{:S(2)}) collective-permute-start(bf16[256,256]{1,0:T(8,128)(2,1)S(1)} %get-tuple-element.26), channel_id=1, source_target_pairs={{30,0},{15,1},{16,2},{1,3},{18,4},{3,5},{20,6},{5,7},{22,8},{7,9},... | collective-permute-start | bytes 393224 | tf_op jit(solution)/shard_map/ppermute | solution.py:514
